TPU v7x, 32 devices: a whole 2x2x4 slice. The times are simulated.
32 devices in a mesh: group: 2 (over y), res: 4 (over z), seq: 4 (over x, core).
Axes of the slice: x: 2, y: 2, z: 4, core: 2. Of those that a mesh axis runs over, the one named last changes fastest.
Arguments:
- alignment_features: bfloat16 [256, 64, 256], P(('group', 'seq'), 'res'), parts along dimension 0, may hold values from -6 to 6
- occupancy_flags: int32 [256, 64], P(('group', 'seq'), 'res'), parts along dimension 0, may hold values from 0 to 1
- standardize_scale: float32 [256], replicated, may hold values from 0.1 to 1.9
- standardize_shift: float32 [256], replicated, may hold values from -3 to 3
- first_factor_matrix: bfloat16 [256, 32], replicated, may hold values from -0.375 to 0.375
- first_factor_offset: float32 [32], replicated, may hold values from -3 to 3
- second_factor_matrix: bfloat16 [256, 32], replicated, may hold values from -0.375 to 0.375
- second_factor_offset: float32 [32], replicated, may hold values from -3 to 3
- final_matrix: bfloat16 [1024, 128], replicated, may hold values from -1.75 to 1.75
- final_offset: float32 [128], replicated, may hold values from -256 to 256
Outputs:
- pair: bfloat16 [128, 64, 128], P(('group', 'res'), 'seq'), parts along dimension 0
There are 2 independent parts, one for each index of `group`. A program takes and returns all parts, laid end to end along the dimension named above; an argument that names none is the same for every part. Nothing has to cross between parts.
All inputs are finite; a program needn't handle non-finite values.
Results may differ from a plain program's by a relative error of at most 0.004.
Values may be sent and summed in bfloat16 or wider, within the bound.
No kernel may reach another device: no remote copies, remote signals or barrier semaphores. Data moves between devices by JAX's collectives and lax.ppermute only.
A program may use at most 64 MiB of HBM per device.

v0:
```python
import jax
import jax.numpy as jnp
from jax import lax
from jax.sharding import PartitionSpec as P


def standardize_features(alignment_features, standardize_scale, standardize_shift):
    averaged_products = alignment_features.astype(jnp.float32)
    center = jnp.mean(averaged_products, axis=-1, keepdims=True)
    spread = jnp.mean((averaged_products - center) ** 2, axis=-1, keepdims=True)
    return (
        (averaged_products - center) * lax.rsqrt(spread + 1e-05) * standardize_scale
        + standardize_shift
    ).astype(jnp.bfloat16)


def tile_pairs(full_left, full_live, own_right, own_mask, w_full):
    rows = full_left.shape[1]
    proj = full_left.shape[2]
    columns = own_right.shape[1]
    outs = w_full.shape[1]
    outer = jnp.einsum("sic,sje->ijce", full_left, own_right, preferred_element_type=jnp.float32)
    flat = outer.reshape(rows * columns, proj * proj)
    raw = jnp.dot(
        flat, w_full, precision=lax.Precision.HIGHEST, preferred_element_type=jnp.float32
    ).reshape(rows, columns, outs)
    count = jnp.einsum("si,sj->ij", full_live.astype(jnp.float32), own_mask.astype(jnp.float32))
    return (raw, count)


def local(
    alignment_features,
    occupancy_flags,
    standardize_scale,
    standardize_shift,
    first_factor_matrix,
    first_factor_offset,
    second_factor_matrix,
    second_factor_offset,
    final_matrix,
    final_offset,
):
    valid_entries = occupancy_flags.astype(jnp.float32)
    live_wire = occupancy_flags.astype(jnp.bfloat16)
    standardized_alignment = standardize_features(
        alignment_features, standardize_scale, standardize_shift
    )
    first_factor = (
        (
            jnp.dot(standardized_alignment, first_factor_matrix, preferred_element_type=jnp.float32)
            + first_factor_offset
        )
        * valid_entries[:, :, None]
    ).astype(jnp.bfloat16)
    second_factor = (
        (
            jnp.dot(
                standardized_alignment, second_factor_matrix, preferred_element_type=jnp.float32
            )
            + second_factor_offset
        )
        * valid_entries[:, :, None]
    ).astype(jnp.bfloat16)
    w_full = final_matrix.astype(jnp.float32)
    right_cols, mask_cols = (
        lax.all_gather(second_factor, "res", axis=1, tiled=True),
        lax.all_gather(live_wire, "res", axis=1, tiled=True),
    )
    full_left, full_live = (
        lax.all_gather(first_factor, "seq", axis=0, tiled=True),
        lax.all_gather(live_wire, "seq", axis=0, tiled=True),
    )
    own_right, own_mask = (
        lax.all_to_all(right_cols, "seq", split_axis=1, concat_axis=0, tiled=True),
        lax.all_to_all(mask_cols, "seq", split_axis=1, concat_axis=0, tiled=True),
    )
    raw, count = tile_pairs(full_left, full_live, own_right, own_mask, w_full)
    return ((raw + final_offset) / (1.0 + count)[:, :, None]).astype(jnp.bfloat16)


def solution(mesh):
    in_specs = (
        P(("group", "seq"), "res", None),
        P(("group", "seq"), "res"),
        P(),
        P(),
        P(),
        P(),
        P(),
        P(),
        P(),
        P(),
    )
    out_specs = P(("group", "res"), "seq", None)
    return jax.shard_map(local, mesh=mesh, in_specs=in_specs, out_specs=out_specs, check_vma=False)
```

profile of v0, /device:TPU:0, one launch (start us, length us, event | category | flops | bytes accessed | tf_op | source)
XLA Modules:
  0.0 76.8 jit_solution(15684921333127855028)
XLA Ops:
  0.0 0.0 copy-start
  0.0 0.8 %fusion.20 = (bf16[32,16]{0,1:T(8,128)(2,1)S(1)}, f32[32,16]{0,1:T(8,128)S(1)}) fusion(s32[32,16]{0,1:T(8,128)} %param.11), kind=kLoop, calls=%fused_computation.27 | loop fusion | flops 1024 | bytes 5120 | tf_op jit(solution)/shard_map/convert_element_type | solution.py:44
  0.8 14.8 %all_gather.15 = bf16[32,64]{0,1:T(8,128)(2,1)S(1)} all-gather(bf16[32,16]{0,1:T(8,128)(2,1)S(1)} %get-tuple-element.5), channel_id=1, replica_groups=mesh['group'=2,'res'=4,'seq'=4] {'res'}, dimensions={1}, use_global_device_ids=true | all-gather | bytes 5120 | tf_op jit(solution)/shard_map/all_gather | solution.py:67
  15.6 0.7 reshape.36
  16.2 3.2 %all-to-all-start.1 = ((bf16[4,2,256]{2,1,0:T(2,128)(2,1)}), bf16[4,2,256]{2,1,0:T(2,128)(2,1)S(1)}, u32[]{:S(2)}, u32[]{:S(2)}) async-start(bf16[4,2,256]{2,1,0:T(2,128)(2,1)} %reshape.36), calls=%async_computation.1 | async-start | bytes 8192 | tf_op jit(solution)/shard_map/all_to_all | solution.py:75
  19.5 1.1 %convert_reduce_fusion = f32[32,16]{1,0:T(8,128)S(1)} fusion(bf16[32,16,256]{2,1,0:T(8,128)(2,1)} %param.10), kind=kLoop, calls=%fused_computation.12 | loop fusion | flops 261632 | bytes 264192 | tf_op jit(solution)/shard_map/reduce_sum | solution.py:9
  20.6 1.2 %fusion.8 = f32[32,16]{1,0:T(8,128)S(1)} fusion(bf16[32,16,256]{2,1,0:T(8,128)(2,1)} %param.10, f32[32,16]{1,0:T(8,128)S(1)} %broadcast_multiply_fusion), kind=kLoop, calls=%fused_computation.15 | loop fusion | flops 523776 | bytes 266240 | tf_op jit(solution)/shard_map/reduce_sum | solution.py:10
  21.8 0.1 copy.20
  21.9 1.3 %fusion.2 = bf16[32,16,32]{2,1,0:T(8,128)(2,1)S(1)} fusion(f32[32,16]{1,0:T(8,128)S(1)} %copy.20, f32[32]{0:T(128)} %param.17, bf16[32,16,256]{2,1,0:T(8,128)(2,1)} %param.10, f32[256]{0:T(256)} %param.13, f32[256]{0:T(256)} %param.12, f32[32,16]{1,0:T(8,128)S(1)} %add_rsqrt_fusion, f32[32,16]{1,0:T(8,128)S(1)} %broadcast_multiply_fusion, ...), kind=kOutput, calls=%fused_computation.5 | convolution fusion | flops 9224192 | bytes 319616 | tf_op jit(solution)/shard_map/dot_general | solution.py:57
  23.2 16.3 %all_gather.12 = bf16[32,64,32]{2,1,0:T(8,128)(2,1)S(1)} all-gather(bf16[32,16,32]{2,1,0:T(8,128)(2,1)S(1)} %fusion.2), channel_id=1, replica_groups=mesh['group'=2,'res'=4,'seq'=4] {'res'}, dimensions={1}, use_global_device_ids=true | all-gather | bytes 163840 | tf_op jit(solution)/shard_map/all_gather | solution.py:66
  39.5 1.3 %fusion.3 = bf16[32,16,32]{2,1,0:T(8,128)(2,1)S(1)} fusion(f32[32]{0:T(128)} %param.15, f32[32,16]{1,0:T(8,128)S(1)} %copy.20, bf16[32,16,256]{2,1,0:T(8,128)(2,1)} %param.10, f32[256]{0:T(256)} %param.13, f32[256]{0:T(256)} %param.12, f32[32,16]{1,0:T(8,128)S(1)} %add_rsqrt_fusion, f32[32,16]{1,0:T(8,128)S(1)} %broadcast_multiply_fusion, ...), kind=kOutput, calls=%fused_computation.6 | convolution fusion | flops 9224192 | bytes 319616 | tf_op jit(solution)/shard_map/dot_general | solution.py:50
  40.8 7.4 %all_gather.13 = bf16[128,16,32]{2,1,0:T(8,128)(2,1)S(1)} all-gather(bf16[32,16,32]{2,1,0:T(8,128)(2,1)S(1)} %fusion.3), channel_id=1, replica_groups=mesh['group'=2,'res'=4,'seq'=4] {'seq'}, dimensions={0}, use_global_device_ids=true | all-gather | bytes 163840 | tf_op jit(solution)/shard_map/all_gather | solution.py:70
  48.2 0.3 copy.33
  48.5 1.1 %reshape.34 = bf16[4,2,8192]{2,1,0:T(2,128)(2,1)} reshape(bf16[64,32,32]{2,1,0:T(8,128)(2,1)S(1)} %bitcast.41) | data formatting | bytes 262144
  49.7 5.2 %all-gather = bf16[4,32,16]{1,2,0:T(8,128)(2,1)S(1)} all-gather(bf16[1,32,16]{1,2,0:T(8,128)(2,1)S(1)} %bitcast.45), channel_id=1, replica_groups=mesh['group'=2,'res'=4,'seq'=4] {'seq'}, dimensions={0}, use_global_device_ids=true | all-gather | bytes 5120 | tf_op jit(solution)/shard_map/all_gather | solution.py:71
  54.8 0.1 reshape.27
  54.9 0.0 all-to-all-done.1
  54.9 3.3 %all-to-all-start = ((bf16[4,2,8192]{2,1,0:T(2,128)(2,1)}), bf16[4,2,8192]{2,1,0:T(2,128)(2,1)S(1)}, u32[]{:S(2)}, u32[]{:S(2)}) async-start(bf16[4,2,8192]{2,1,0:T(2,128)(2,1)} %reshape.34), calls=%async_computation | async-start | bytes 262144 | tf_op jit(solution)/shard_map/all_to_all | solution.py:74
  58.3 0.1 reshape.37
  58.4 0.1 all_to_all.34
  58.5 0.1 convolution_add_fusion.3
  58.6 4.3 %all-to-all-done = bf16[4,2,8192]{2,1,0:T(2,128)(2,1)S(1)} async-done(((bf16[4,2,8192]{2,1,0:T(2,128)(2,1)}), bf16[4,2,8192]{2,1,0:T(2,128)(2,1)S(1)}, u32[]{:S(2)}, u32[]{:S(2)}) %all-to-all-start) | async-done | bytes 131104 | tf_op jit(solution)/shard_map/all_to_all | solution.py:74
  62.9 0.3 reshape.35
  63.1 0.3 copy.22
  63.4 0.3 reshape.30
  63.7 2.6 %convolution_bitcast_fusion = f32[16,16,32,32]{2,3,0,1:T(8,128)} fusion(bf16[128,16,32]{2,1,0:T(8,128)(2,1)S(1)} %all_gather.13, bf16[128,16,32,1]{0,2,1,3:T(8,128)(2,1)S(1)} %reshape.30), kind=kOutput, calls=%fused_computation | convolution fusion | flops 67108864 | bytes 1310720 | tf_op jit(solution)/shard_map/sic,sje->ijce/dot_general | solution.py:22
  66.4 5.4 %copy.24 = f32[16,16,32,32]{3,2,1,0:T(8,128)} copy(f32[16,16,32,32]{2,3,0,1:T(8,128)} %convolution_bitcast_fusion) | data formatting | bytes 2097152 | tf_op jit(solution)/shard_map/sic,sje->ijce/transpose | solution.py:22
  71.7 0.0 copy-start.1
  71.7 3.8 %dot_general.20 = f32[16,16,1024]{2,1,0:T(8,128)S(1)} reshape(f32[16,16,32,32]{3,2,1,0:T(8,128)} %copy.24) | data formatting | bytes 2097152 | tf_op jit(solution)/shard_map/dot_general | solution.py:24
  75.5 0.0 copy-done
  75.5 0.0 copy-done.1
  75.5 1.2 %fusion.5 = bf16[16,16,128]{2,1,0:T(8,128)(2,1)} fusion(f32[16,16,1024]{2,1,0:T(8,128)S(1)} %dot_general.20, bf16[1024,128]{1,0:T(8,128)(2,1)S(1)} %copy-done, f32[16,16]{1,0:T(8,128)S(1)} %convolution_add_fusion.3, f32[128]{0:T(128)S(1)} %copy-done.1), kind=kOutput, calls=%fused_computation.9 | convolution fusion | flops 402751488 | bytes 1377792 | tf_op jit(solution)/shard_map/dot_general | solution.py:24
  (5 shorter events, 0.0 us)
Async XLA Ops:
  0.0 75.5 %copy-start = (bf16[1024,128]{1,0:T(8,128)(2,1)S(1)}, bf16[1024,128]{1,0:T(8,128)(2,1)}, u32[]{:S(2)}) copy-start(bf16[1024,128]{1,0:T(8,128)(2,1)} %param.18) | copy-start | bytes 786436
  16.2 38.7 %all-to-all-start.1 = ((bf16[4,2,256]{2,1,0:T(2,128)(2,1)}), bf16[4,2,256]{2,1,0:T(2,128)(2,1)S(1)}, u32[]{:S(2)}, u32[]{:S(2)}) async-start(bf16[4,2,256]{2,1,0:T(2,128)(2,1)} %reshape.36), calls=%async_computation.1 | async-start | bytes 8192 | tf_op jit(solution)/shard_map/all_to_all | solution.py:75
  54.9 7.9 %all-to-all-start = ((bf16[4,2,8192]{2,1,0:T(2,128)(2,1)}), bf16[4,2,8192]{2,1,0:T(2,128)(2,1)S(1)}, u32[]{:S(2)}, u32[]{:S(2)}) async-start(bf16[4,2,8192]{2,1,0:T(2,128)(2,1)} %reshape.34), calls=%async_computation | async-start | bytes 262144 | tf_op jit(solution)/shard_map/all_to_all | solution.py:74
  71.7 3.8 %copy-start.1 = (f32[128]{0:T(128)S(1)}, f32[128]{0:T(128)}, u32[]{:S(2)}) copy-start(f32[128]{0:T(128)} %param.19) | copy-start | bytes 1540
where the time goes:
time: 77.3 us; the launch traced here: 76.8 us
  blocking collectives  43.6 us (56%)
  local copies, waits for them, and re-layouts  12.5 us (16%)
  matrix products  6.63 us (9%)
  starting transfers between devices  6.57 us (8%)
  waiting for transfers between devices  4.28 us (6%)
  other arithmetic  3.07 us (4%)
    all_gather x1, blocking collectives, local(): lax.all_gather(second_factor, 'res', axis=1, tiled=True)  16.3 us
    all_gather x1, blocking collectives, local(): lax.all_gather(live_wire, 'res', axis=1, tiled=True)  14.8 us
    all_gather x1, blocking collectives, local(): lax.all_gather(first_factor, 'seq', axis=0, tiled=True)  7.36 us
    transpose x1, local copies, waits for them, and re-layouts, tile_pairs(): jnp.einsum('sic,sje->ijce', full_left, own_right, preferred_element_type=...  5.36 us
    all_gather x1, blocking collectives, local(): lax.all_gather(live_wire, 'seq', axis=0, tiled=True)  5.17 us
    all_to_all x1, waiting for transfers between devices, local(): lax.all_to_all(right_cols, 'seq', split_axis=1, concat_axis=0, tiled=True)  4.28 us
    dot_general x1, local copies, waits for them, and re-layouts, tile_pairs(): jnp.dot(flat, w_full, precision=lax.Precision.HIGHEST, preferred_element_...  3.76 us
    all_to_all x1, starting transfers between devices, local(): lax.all_to_all(right_cols, 'seq', split_axis=1, concat_axis=0, tiled=True)  3.33 us
  transfers between devices with their start and end apart: 2, of which 1 were waited for; matrix products, arithmetic and copies ran while one was open for 9% of the time, Pallas kernels for 0%

commit v1 on v0

v1 whole, which is shorter than its diff:
```python
import functools

import jax
import jax.numpy as jnp
from jax import lax
from jax.experimental import pallas as pl
from jax.experimental.pallas import tpu as pltpu
from jax.sharding import PartitionSpec as P

LANES = 128
F32 = jnp.float32
BF16 = jnp.bfloat16
TN = (((0,), (0,)), ((), ()))
NT = (((1,), (1,)), ((), ()))
NN = (((1,), (0,)), ((), ()))


def dot(a, b, dims=NN):
    return lax.dot_general(a, b, dims, preferred_element_type=F32)


def iota(shape, dim):
    return lax.broadcasted_iota(jnp.int32, shape, dim)


def project_kernel(x_ref, flag_ref, scale_ref, shift_ref, wl_ref, bl_ref, wr_ref, br_ref,
                   left_ref, right_ref, proj_ref):
    seqs, rows, depth = x_ref.shape
    width = wl_ref.shape[0]
    fold = LANES // width
    lanes = rows * width

    x = x_ref[...].astype(F32).reshape(seqs * rows, depth)
    center = jnp.mean(x, axis=-1, keepdims=True)
    x = x - center
    spread = jnp.mean(x * x, axis=-1, keepdims=True)
    normed = x * lax.rsqrt(spread + 1e-05) * scale_ref[...].reshape(1, depth)
    normed = (normed + shift_ref[...].reshape(1, depth)).astype(BF16)
    weight = jnp.concatenate([wl_ref[...]] * fold + [wr_ref[...]] * fold, axis=0)
    bias = jnp.concatenate([bl_ref[...].reshape(1, width)] * fold + [br_ref[...].reshape(1, width)] * fold, axis=1)
    both = dot(normed, weight, NT) + bias
    proj_ref[0] = both[:, :LANES]
    proj_ref[1] = both[:, LANES:]

    lane = iota((rows, lanes + LANES), 1)
    residue = jnp.where(lane < lanes, lane // width, lane - lanes)
    spreader = (residue == iota((rows, lanes + LANES), 0)).astype(BF16)
    mask = dot(flag_ref[...].astype(BF16), spreader, TN)

    place = iota((seqs, LANES), 1) // width
    for half, out_ref in ((0, left_ref), (1, right_ref)):
        for tile in range(rows // fold):
            merged = proj_ref[half, pl.ds(tile * fold, seqs, stride=rows), :]
            for k in range(1, fold):
                part = proj_ref[half, pl.ds(tile * fold + k, seqs, stride=rows), :]
                merged = jnp.where(place == k, part, merged)
            where = slice(tile * LANES, (tile + 1) * LANES)
            out_ref[:, where] = (merged * mask[:, where]).astype(BF16)
        out_ref[:, lanes:] = mask[:, lanes:].astype(BF16)


def pair_kernel(count_of, rows, columns, width, *refs):
    lefts, rights = refs[:count_of], refs[count_of:2 * count_of]
    w_ref, bias_ref, out_ref, left_ref, right_ref, outer_ref, flat_ref, raw_ref = refs[2 * count_of:]
    seqs = lefts[0].shape[0]
    fold = LANES // width
    lanes = rows * width

    me_res, me_seq = lax.axis_index("res"), lax.axis_index("seq")
    for k in range(count_of):
        at = pl.multiple_of(lax.rem(me_seq + count_of - k, count_of) * seqs, seqs)
        left_ref[pl.ds(at, seqs), :] = lefts[k][...]
        at = pl.multiple_of(lax.rem(me_res + count_of - k, count_of) * seqs, seqs)
        right_ref[pl.ds(at, seqs), :] = rights[k][...]

    outer = dot(left_ref[:, :lanes], right_ref[:, :lanes], TN)
    for tile in range(columns // fold):
        outer_ref[tile] = outer[:, tile * LANES:(tile + 1) * LANES]

    place = iota((rows, LANES), 1) // width
    for tile in range(columns // fold):
        for quad in range(width // fold):
            part = [
                outer_ref[tile, pl.ds(quad * fold + k, rows, stride=width), :]
                for k in range(fold)
            ]
            step = fold // 2
            while step:
                keep = (place // step) % 2 == 0
                new = list(part)
                for k in range(fold):
                    if (k // step) % 2 == 0:
                        a, b = part[k], part[k + step]
                        new[k] = jnp.where(keep, a, pltpu.roll(b, step * width, 1))
                        new[k + step] = jnp.where(keep, pltpu.roll(a, LANES - step * width, 1), b)
                part = new
                step //= 2
            for k in range(fold):
                j = tile * fold + k
                flat_ref[j * rows:(j + 1) * rows, quad * LANES:(quad + 1) * LANES] = part[k].astype(BF16)

    raw = dot(flat_ref[...], w_ref[...]) + bias_ref[...].reshape(1, -1)

    pair = rows * columns
    lane, sub = iota((LANES, pair), 1), iota((LANES, pair), 0)
    live_left = dot(left_ref[:, lanes:], (lane % rows == sub).astype(BF16))
    live_right = dot(right_ref[:, lanes:], (lane // rows == sub).astype(BF16))
    both = (live_left * live_right).astype(BF16)
    count = dot(both, jnp.ones((both.shape[0], raw.shape[1]), BF16), TN)
    raw_ref[...] = raw / (1.0 + count)
    for i in range(rows):
        out_ref[i] = raw_ref[pl.ds(i, columns, stride=rows), :].astype(BF16)


def local(n, x, flags, scale, shift, wl, bl, wr, br, w, bias):
    seqs, rows, depth = x.shape
    width = wl.shape[1]
    outs = w.shape[1]
    lanes = rows * width
    wire = jax.ShapeDtypeStruct((seqs, lanes + LANES), BF16)
    left, right = pl.pallas_call(
        project_kernel,
        out_shape=(wire, wire),
        scratch_shapes=[pltpu.VMEM((2, seqs * rows, LANES), F32)],
        compiler_params=pltpu.CompilerParams(vmem_limit_bytes=16 << 20),
        name="project",
    )(x, flags.T, scale, shift, wl.T, bl, wr.T, br)

    lefts = [left] + [
        lax.ppermute(left, "seq", [(p, (p + k) % n) for p in range(n)]) for k in range(1, n)
    ]
    rights = [
        lax.ppermute(
            right, ("res", "seq"),
            [(a * n + p, (p + k) % n * n + a) for a in range(n) for p in range(n)],
        )
        for k in range(n)
    ]
    return pl.pallas_call(
        functools.partial(pair_kernel, n, rows, rows, width),
        out_shape=jax.ShapeDtypeStruct((rows, rows, outs), BF16),
        scratch_shapes=[
            pltpu.VMEM((n * seqs, lanes + LANES), BF16),
            pltpu.VMEM((n * seqs, lanes + LANES), BF16),
            pltpu.VMEM((lanes // LANES, lanes, LANES), F32),
            pltpu.VMEM((rows * rows, width * width), BF16),
            pltpu.VMEM((rows * rows, outs), F32),
        ],
        compiler_params=pltpu.CompilerParams(vmem_limit_bytes=24 << 20),
        name="pair",
    )(*lefts, *rights, w, bias)


def solution(mesh):
    n = mesh.shape["res"]
    assert n == mesh.shape["seq"]
    in_specs = (P(("group", "seq"), "res", None), P(("group", "seq"), "res")) + (P(),) * 8
    return jax.shard_map(
        functools.partial(local, n), mesh=mesh, in_specs=in_specs,
        out_specs=P(("group", "res"), "seq", None), check_vma=False,
    )
```

time: 77.3 us -> 22.5 us (0.29)
  the two profiles are of different devices: /device:TPU:0 before, /device:TPU:2 now
where the time goes in v1:
time: 22.5 us; the launch traced here: 22.1 us
  starting transfers between devices  9.8 us (44%)
  waiting for transfers between devices  5.67 us (25%)
  local copies, waits for them, and re-layouts  3.79 us (17%)
  Pallas kernels  2.74 us (12%)
    ppermute x4, starting transfers between devices, local(): lax.ppermute(right, ('res', 'seq'), [(a * n + p, (p + k) % n * n + a) for...  8.29 us
    ppermute x4, waiting for transfers between devices, local(): lax.ppermute(right, ('res', 'seq'), [(a * n + p, (p + k) % n * n + a) for...  5.66 us
    unnamed x20, local copies, waits for them, and re-layouts  3.79 us
    pallas_call x1, Pallas kernels, local(): pl.pallas_call(functools.partial(pair_kernel, n, rows, rows, width), out_...  2.23 us
    ppermute x3, starting transfers between devices, local(): lax.ppermute(left, 'seq', [(p, (p + k) % n) for p in range(n)])  1.51 us
    pallas_call x1, Pallas kernels, local(): pl.pallas_call(project_kernel, out_shape=(wire, wire), scratch_shapes=[pl...  0.51 us
  transfers between devices with their start and end apart: 7, of which 2 were waited for; matrix products, arithmetic and copies ran while one was open for 0% of the time, Pallas kernels for 0%

profile of v1, /device:TPU:2, one launch (start us, length us, event | category | flops | bytes accessed | tf_op | source)
XLA Modules:
  0.0 22.1 jit_solution(10958538503906063488)
XLA Ops:
  0.0 0.0 copy-start.6
  0.0 0.0 copy-start.8
  0.0 0.0 copy-start.5
  0.0 0.0 copy-start.7
  0.0 0.7 %copy-done.6 = f32[256]{0:T(256)S(1)} copy-done((f32[256]{0:T(256)S(1)}, f32[256]{0:T(256)}, u32[]{:S(2)}) %copy-start.6) | copy-done | bytes 1048
  0.7 0.0 copy-done.8
  0.7 0.0 copy-done.5
  0.7 0.0 copy-done.7
  0.7 0.0 copy-start
  0.7 0.9 %copy-done = bf16[32,16,256]{2,1,0:T(8,128)(2,1)S(1)} copy-done((bf16[32,16,256]{2,1,0:T(8,128)(2,1)S(1)}, bf16[32,16,256]{2,1,0:T(8,128)(2,1)}, u32[]{:S(2)}) %copy-start) | copy-done | bytes 262168
  1.7 0.0 copy-start.2
  1.7 0.7 %copy-done.2 = bf16[256,32]{0,1:T(8,128)(2,1)S(1)} copy-done((bf16[256,32]{0,1:T(8,128)(2,1)S(1)}, bf16[256,32]{0,1:T(8,128)(2,1)}, u32[]{:S(2)}) %copy-start.2) | copy-done | bytes 16408
  2.4 0.0 copy-start.3
  2.4 0.7 %copy-done.3 = bf16[256,32]{0,1:T(8,128)(2,1)S(1)} copy-done((bf16[256,32]{0,1:T(8,128)(2,1)S(1)}, bf16[256,32]{0,1:T(8,128)(2,1)}, u32[]{:S(2)}) %copy-start.3) | copy-done | bytes 16408
  3.1 0.0 copy-start.4
  3.1 0.7 %copy-done.4 = s32[32,16]{0,1:T(8,128)S(1)} copy-done((s32[32,16]{0,1:T(8,128)S(1)}, s32[32,16]{0,1:T(8,128)}, u32[]{:S(2)}) %copy-start.4) | copy-done | bytes 2072
  3.8 0.0 copy-start.1
  3.8 0.5 %project.1 = (bf16[32,640]{1,0:T(8,128)(2,1)S(1)}, bf16[32,640]{1,0:T(8,128)(2,1)S(1)}) custom-call(bf16[32,16,256]{2,1,0:T(8,128)(2,1)S(1)} %copy-done, s32[16,32]{1,0:T(8,128)S(1)} %bitcast.5, f32[256]{0:T(256)S(1)} %copy-done.5, f32[256]{0:T(256)S(1)} %copy-done.6, bf16[32,256]{1,0:T(8,128)(2,1)S(1)} %bitcast.3, f32[32]{0:T(128)S(1)} %copy-done.7, ...), custom_call_target="tpu_custom_call" | custom-call | tf_op jit(solution)/shard_map/project/pallas_call | solution.py:121
  4.3 0.0 copy-start.9
  4.3 0.1 collective-permute-start.2
  4.4 1.5 %collective-permute-start.1 = (bf16[32,640]{1,0:T(8,128)(2,1)S(1)}, bf16[32,640]{1,0:T(8,128)(2,1)S(1)}, u32[]{:S(2)}, u32[]{:S(2)}) collective-permute-start(bf16[32,640]{1,0:T(8,128)(2,1)S(1)} %get-tuple-element.7.refs_0_), channel_id=1, source_target_pairs={{0,2},{1,3},{2,0},{3,1},{4,6},{5,7},{6,4},{7,5},{8,10},{9,11},{10,... | collective-permute-start | bytes 122888 | tf_op jit(solution)/shard_map/ppermute | solution.py:130
  5.8 0.0 collective-permute-start
  5.9 1.8 %collective-permute-start.6 = (bf16[32,640]{1,0:T(8,128)(2,1)S(1)}, bf16[32,640]{1,0:T(8,128)(2,1)S(1)}, u32[]{:S(2)}, u32[]{:S(2)}) collective-permute-start(bf16[32,640]{1,0:T(8,128)(2,1)S(1)} %get-tuple-element.8), channel_id=1, source_target_pairs={{0,12},{1,0},{2,4},{3,8},{4,13},{5,1},{6,5},{7,9},{8,14},{9,2},{10... | collective-permute-start | bytes 122888 | tf_op jit(solution)/shard_map/ppermute | solution.py:133
  7.7 2.6 %collective-permute-start.5 = (bf16[32,640]{1,0:T(8,128)(2,1)S(1)}, bf16[32,640]{1,0:T(8,128)(2,1)S(1)}, u32[]{:S(2)}, u32[]{:S(2)}) collective-permute-start(bf16[32,640]{1,0:T(8,128)(2,1)S(1)} %get-tuple-element.8), channel_id=1, source_target_pairs={{0,8},{1,12},{2,0},{3,4},{4,9},{5,13},{6,1},{7,5},{8,10},{9,14},{1... | collective-permute-start | bytes 122888 | tf_op jit(solution)/shard_map/ppermute | solution.py:133
  10.3 0.0 collective-permute-done.2.refs_3_
  10.3 1.0 %collective-permute-start.4 = (bf16[32,640]{1,0:T(8,128)(2,1)S(1)}, bf16[32,640]{1,0:T(8,128)(2,1)S(1)}, u32[]{:S(2)}, u32[]{:S(2)}) collective-permute-start(bf16[32,640]{1,0:T(8,128)(2,1)S(1)} %get-tuple-element.8), channel_id=1, source_target_pairs={{0,4},{1,8},{2,12},{3,0},{4,5},{5,9},{6,13},{7,1},{8,6},{9,10},{10... | collective-permute-start | bytes 122888 | tf_op jit(solution)/shard_map/ppermute | solution.py:133
  11.3 0.0 collective-permute-done.1.refs_2_
  11.3 2.9 %collective-permute-start.3 = (bf16[32,640]{1,0:T(8,128)(2,1)S(1)}, bf16[32,640]{1,0:T(8,128)(2,1)S(1)}, u32[]{:S(2)}, u32[]{:S(2)}) collective-permute-start(bf16[32,640]{1,0:T(8,128)(2,1)S(1)} %get-tuple-element.8), channel_id=1, source_target_pairs={{0,0},{1,4},{2,8},{3,12},{4,1},{5,5},{6,9},{7,13},{8,2},{9,6},{10,... | collective-permute-start | bytes 122888 | tf_op jit(solution)/shard_map/ppermute | solution.py:133
  14.2 0.0 collective-permute-done.refs_1_
  14.2 0.0 collective-permute-done.6.refs_7_
  14.2 0.0 collective-permute-done.5.refs_6_
  14.2 0.5 %collective-permute-done.4.refs_5_ = bf16[32,640]{1,0:T(8,128)(2,1)S(1)} collective-permute-done((bf16[32,640]{1,0:T(8,128)(2,1)S(1)}, bf16[32,640]{1,0:T(8,128)(2,1)S(1)}, u32[]{:S(2)}, u32[]{:S(2)}) %collective-permute-start.4) | collective-permute-done | bytes 40992 | tf_op jit(solution)/shard_map/ppermute | solution.py:133
  14.7 5.1 %collective-permute-done.3.refs_4_ = bf16[32,640]{1,0:T(8,128)(2,1)S(1)} collective-permute-done((bf16[32,640]{1,0:T(8,128)(2,1)S(1)}, bf16[32,640]{1,0:T(8,128)(2,1)S(1)}, u32[]{:S(2)}, u32[]{:S(2)}) %collective-permute-start.3) | collective-permute-done | bytes 40992 | tf_op jit(solution)/shard_map/ppermute | solution.py:133
  19.8 0.0 copy-done.1
  19.8 0.0 copy-done.9
  19.9 2.2 %pair.1 = bf16[16,16,128]{2,1,0:T(8,128)(2,1)} custom-call(bf16[32,640]{1,0:T(8,128)(2,1)S(1)} %get-tuple-element.7.refs_0_, bf16[32,640]{1,0:T(8,128)(2,1)S(1)} %collective-permute-done.refs_1_, bf16[32,640]{1,0:T(8,128)(2,1)S(1)} %collective-permute-done.1.refs_2_, bf16[32,640]{1,0:T(8,128)(2,1)S(1)} %collective-permute-done.2.refs_3_, ...), custom_call_target="tpu_custom_call" | custom-call | tf_op jit(solution)/shard_map/pair/pallas_call | solution.py:139
Async XLA Ops:
  0.0 0.7 %copy-start.6 = (f32[256]{0:T(256)S(1)}, f32[256]{0:T(256)}, u32[]{:S(2)}) copy-start(f32[256]{0:T(256)} %shift_ref.1) | copy-start | bytes 3076
  0.0 0.7 %copy-start.8 = (f32[32]{0:T(128)S(1)}, f32[32]{0:T(128)}, u32[]{:S(2)}) copy-start(f32[32]{0:T(128)} %br_ref.1) | copy-start | bytes 388
  0.0 0.7 %copy-start.5 = (f32[256]{0:T(256)S(1)}, f32[256]{0:T(256)}, u32[]{:S(2)}) copy-start(f32[256]{0:T(256)} %scale_ref.1) | copy-start | bytes 3076
  0.0 0.7 %copy-start.7 = (f32[32]{0:T(128)S(1)}, f32[32]{0:T(128)}, u32[]{:S(2)}) copy-start(f32[32]{0:T(128)} %bl_ref.1) | copy-start | bytes 388
  0.7 1.0 %copy-start = (bf16[32,16,256]{2,1,0:T(8,128)(2,1)S(1)}, bf16[32,16,256]{2,1,0:T(8,128)(2,1)}, u32[]{:S(2)}) copy-start(bf16[32,16,256]{2,1,0:T(8,128)(2,1)} %x_ref.1) | copy-start | bytes 786436
  1.7 0.7 %copy-start.2 = (bf16[256,32]{0,1:T(8,128)(2,1)S(1)}, bf16[256,32]{0,1:T(8,128)(2,1)}, u32[]{:S(2)}) copy-start(bf16[256,32]{0,1:T(8,128)(2,1)} %param.14) | copy-start | bytes 49156
  2.4 0.7 %copy-start.3 = (bf16[256,32]{0,1:T(8,128)(2,1)S(1)}, bf16[256,32]{0,1:T(8,128)(2,1)}, u32[]{:S(2)}) copy-start(bf16[256,32]{0,1:T(8,128)(2,1)} %param.16) | copy-start | bytes 49156
  3.1 0.7 %copy-start.4 = (s32[32,16]{0,1:T(8,128)S(1)}, s32[32,16]{0,1:T(8,128)}, u32[]{:S(2)}) copy-start(s32[32,16]{0,1:T(8,128)} %param.11) | copy-start | bytes 6148
  3.8 16.0 %copy-start.1 = (bf16[1024,128]{1,0:T(8,128)(2,1)S(1)}, bf16[1024,128]{1,0:T(8,128)(2,1)}, u32[]{:S(2)}) copy-start(bf16[1024,128]{1,0:T(8,128)(2,1)} %refs_8_.1) | copy-start | bytes 786436
  4.3 15.5 %copy-start.9 = (f32[128]{0:T(128)S(1)}, f32[128]{0:T(128)}, u32[]{:S(2)}) copy-start(f32[128]{0:T(128)} %refs_9_.1) | copy-start | bytes 1540
  4.3 5.9 %collective-permute-start.2 = (bf16[32,640]{1,0:T(8,128)(2,1)S(1)}, bf16[32,640]{1,0:T(8,128)(2,1)S(1)}, u32[]{:S(2)}, u32[]{:S(2)}) collective-permute-start(bf16[32,640]{1,0:T(8,128)(2,1)S(1)} %get-tuple-element.7.refs_0_), channel_id=1, source_target_pairs={{0,3},{1,0},{2,1},{3,2},{4,7},{5,4},{6,5},{7,6},{8,11},{9,8},{10,9... | collective-permute-start | bytes 122888 | tf_op jit(solution)/shard_map/ppermute | solution.py:130
  4.4 6.9 %collective-permute-start.1 = (bf16[32,640]{1,0:T(8,128)(2,1)S(1)}, bf16[32,640]{1,0:T(8,128)(2,1)S(1)}, u32[]{:S(2)}, u32[]{:S(2)}) collective-permute-start(bf16[32,640]{1,0:T(8,128)(2,1)S(1)} %get-tuple-element.7.refs_0_), channel_id=1, source_target_pairs={{0,2},{1,3},{2,0},{3,1},{4,6},{5,7},{6,4},{7,5},{8,10},{9,11},{10,... | collective-permute-start | bytes 122888 | tf_op jit(solution)/shard_map/ppermute | solution.py:130
  5.8 8.3 %collective-permute-start = (bf16[32,640]{1,0:T(8,128)(2,1)S(1)}, bf16[32,640]{1,0:T(8,128)(2,1)S(1)}, u32[]{:S(2)}, u32[]{:S(2)}) collective-permute-start(bf16[32,640]{1,0:T(8,128)(2,1)S(1)} %get-tuple-element.7.refs_0_), channel_id=1, source_target_pairs={{0,1},{1,2},{2,3},{3,0},{4,5},{5,6},{6,7},{7,4},{8,9},{9,10},{10,1... | collective-permute-start | bytes 122888 | tf_op jit(solution)/shard_map/ppermute | solution.py:130
  5.9 8.3 %collective-permute-start.6 = (bf16[32,640]{1,0:T(8,128)(2,1)S(1)}, bf16[32,640]{1,0:T(8,128)(2,1)S(1)}, u32[]{:S(2)}, u32[]{:S(2)}) collective-permute-start(bf16[32,640]{1,0:T(8,128)(2,1)S(1)} %get-tuple-element.8), channel_id=1, source_target_pairs={{0,12},{1,0},{2,4},{3,8},{4,13},{5,1},{6,5},{7,9},{8,14},{9,2},{10... | collective-permute-start | bytes 122888 | tf_op jit(solution)/shard_map/ppermute | solution.py:133
  7.7 6.5 %collective-permute-start.5 = (bf16[32,640]{1,0:T(8,128)(2,1)S(1)}, bf16[32,640]{1,0:T(8,128)(2,1)S(1)}, u32[]{:S(2)}, u32[]{:S(2)}) collective-permute-start(bf16[32,640]{1,0:T(8,128)(2,1)S(1)} %get-tuple-element.8), channel_id=1, source_target_pairs={{0,8},{1,12},{2,0},{3,4},{4,9},{5,13},{6,1},{7,5},{8,10},{9,14},{1... | collective-permute-start | bytes 122888 | tf_op jit(solution)/shard_map/ppermute | solution.py:133
  10.3 4.5 %collective-permute-start.4 = (bf16[32,640]{1,0:T(8,128)(2,1)S(1)}, bf16[32,640]{1,0:T(8,128)(2,1)S(1)}, u32[]{:S(2)}, u32[]{:S(2)}) collective-permute-start(bf16[32,640]{1,0:T(8,128)(2,1)S(1)} %get-tuple-element.8), channel_id=1, source_target_pairs={{0,4},{1,8},{2,12},{3,0},{4,5},{5,9},{6,13},{7,1},{8,6},{9,10},{10... | collective-permute-start | bytes 122888 | tf_op jit(solution)/shard_map/ppermute | solution.py:133
  11.3 8.6 %collective-permute-start.3 = (bf16[32,640]{1,0:T(8,128)(2,1)S(1)}, bf16[32,640]{1,0:T(8,128)(2,1)S(1)}, u32[]{:S(2)}, u32[]{:S(2)}) collective-permute-start(bf16[32,640]{1,0:T(8,128)(2,1)S(1)} %get-tuple-element.8), channel_id=1, source_target_pairs={{0,0},{1,4},{2,8},{3,12},{4,1},{5,5},{6,9},{7,13},{8,2},{9,6},{10,... | collective-permute-start | bytes 122888 | tf_op jit(solution)/shard_map/ppermute | solution.py:133

commit v2 on v1

v2 whole, which is shorter than its diff:
```python
import functools

import jax
import jax.numpy as jnp
from jax import lax
from jax.experimental import pallas as pl
from jax.experimental.pallas import tpu as pltpu
from jax.sharding import PartitionSpec as P

LANES = 128
F32 = jnp.float32
BF16 = jnp.bfloat16
TN = (((0,), (0,)), ((), ()))
NT = (((1,), (1,)), ((), ()))
NN = (((1,), (0,)), ((), ()))


def dot(a, b, dims=NN):
    return lax.dot_general(a, b, dims, preferred_element_type=F32)


def iota(shape, dim):
    return lax.broadcasted_iota(jnp.int32, shape, dim)


def project_kernel(x_hbm, flag_hbm, scale_hbm, shift_hbm, wl_hbm, bl_hbm, wr_hbm, br_hbm,
                   left_ref, right_ref,
                   x_ref, flag_ref, scale_ref, shift_ref, wl_ref, bl_ref, wr_ref, br_ref, proj_ref, sems):
    copies = [
        pltpu.make_async_copy(src, dst, sems.at[k])
        for k, (src, dst) in enumerate((
            (x_hbm, x_ref), (flag_hbm, flag_ref), (scale_hbm, scale_ref), (shift_hbm, shift_ref),
            (wl_hbm, wl_ref), (bl_hbm, bl_ref), (wr_hbm, wr_ref), (br_hbm, br_ref),
        ))
    ]
    for copy in copies:
        copy.start()
    seqs, rows, depth = x_ref.shape
    width = wl_ref.shape[0]
    fold = LANES // width
    lanes = rows * width
    data = lanes // LANES * seqs
    for copy in copies:
        copy.wait()

    x = x_ref[...].astype(F32).reshape(seqs * rows, depth)
    center = jnp.mean(x, axis=-1, keepdims=True)
    x = x - center
    spread = jnp.mean(x * x, axis=-1, keepdims=True)
    normed = x * lax.rsqrt(spread + 1e-05) * scale_ref[...].reshape(1, depth)
    normed = (normed + shift_ref[...].reshape(1, depth)).astype(BF16)
    weight = jnp.concatenate([wl_ref[...]] * fold + [wr_ref[...]] * fold, axis=0)
    bias = jnp.concatenate([bl_ref[...].reshape(1, width)] * fold + [br_ref[...].reshape(1, width)] * fold, axis=1)
    both = dot(normed, weight, NT) + bias
    proj_ref[0] = both[:, :LANES]
    proj_ref[1] = both[:, LANES:]

    flags = flag_ref[...].astype(F32)
    spreader = (iota((rows, lanes), 1) // width == iota((rows, lanes), 0)).astype(BF16)
    mask = dot(flags.astype(BF16), spreader, TN)
    flags = jnp.concatenate([flags, jnp.zeros((rows, LANES - seqs), F32)], axis=1).astype(BF16)

    place = iota((seqs, LANES), 1) // width
    for half, out_ref in ((0, left_ref), (1, right_ref)):
        for tile in range(rows // fold):
            merged = proj_ref[half, pl.ds(tile * fold, seqs, stride=rows), :]
            for k in range(1, fold):
                part = proj_ref[half, pl.ds(tile * fold + k, seqs, stride=rows), :]
                merged = jnp.where(place == k, part, merged)
            merged = merged * mask[:, tile * LANES:(tile + 1) * LANES]
            out_ref[tile * seqs:(tile + 1) * seqs, :] = merged.astype(BF16)
        out_ref[data:, :] = flags


def whole_factor(pieces, seqs, data):
    return jnp.concatenate(
        [
            jnp.concatenate([p[t * seqs:(t + 1) * seqs, :] for t in range(data // seqs)], axis=1)
            for p in pieces
        ],
        axis=0,
    )


def whole_mask(pieces, seqs, data):
    each = LANES // seqs
    tiles = []
    for first in range(0, len(pieces), each):
        total = pieces[first][data:, :].astype(F32)
        for k in range(1, min(each, len(pieces) - first)):
            total = total + pltpu.roll(pieces[first + k][data:, :].astype(F32), k * seqs, 1)
        tiles.append(total)
    return jnp.concatenate(tiles, axis=1).astype(BF16)


def pair_kernel(pieces, seqs, rows, columns, width, *refs):
    lefts, rights = refs[:pieces], refs[pieces:2 * pieces]
    w_ref, bias_ref, out_ref, outer_ref, flat_ref, raw_ref = refs[2 * pieces:]
    fold = LANES // width
    data = rows * width // LANES * seqs

    outer = dot(whole_factor(lefts, seqs, data), whole_factor(rights, seqs, data), TN)
    for tile in range(columns // fold):
        outer_ref[tile] = outer[:, tile * LANES:(tile + 1) * LANES]

    place = iota((rows, LANES), 1) // width
    for tile in range(columns // fold):
        for quad in range(width // fold):
            part = [
                outer_ref[tile, pl.ds(quad * fold + k, rows, stride=width), :]
                for k in range(fold)
            ]
            step = fold // 2
            while step:
                keep = (place // step) % 2 == 0
                new = list(part)
                for k in range(fold):
                    if (k // step) % 2 == 0:
                        a, b = part[k], part[k + step]
                        new[k] = jnp.where(keep, a, pltpu.roll(b, step * width, 1))
                        new[k + step] = jnp.where(keep, pltpu.roll(a, LANES - step * width, 1), b)
                part = new
                step //= 2
            for k in range(fold):
                j = tile * fold + k
                flat_ref[j * rows:(j + 1) * rows, quad * LANES:(quad + 1) * LANES] = part[k].astype(BF16)

    raw = dot(flat_ref[...], w_ref[...]) + bias_ref[...].reshape(1, -1)

    pair = rows * columns
    row = iota((pair, rows), 0)
    live_left = dot((row % rows == iota((pair, rows), 1)).astype(BF16), whole_mask(lefts, seqs, data))
    row = iota((pair, columns), 0)
    live_right = dot((row // rows == iota((pair, columns), 1)).astype(BF16), whole_mask(rights, seqs, data))
    count = jnp.sum(live_left * live_right, axis=1, keepdims=True)
    raw_ref[...] = raw / (1.0 + count)
    for i in range(rows):
        out_ref[i] = raw_ref[pl.ds(i, columns, stride=rows), :].astype(BF16)


def local(n, x, flags, scale, shift, wl, bl, wr, br, w, bias):
    seqs, rows, depth = x.shape
    width = wl.shape[1]
    outs = w.shape[1]
    lanes = rows * width
    data = lanes // LANES * seqs
    operands = (x, flags.T, scale, shift, wl.T, bl, wr.T, br)
    wire = jax.ShapeDtypeStruct((data + rows, LANES), BF16)
    left, right = pl.pallas_call(
        project_kernel,
        out_shape=(wire, wire),
        in_specs=[pl.BlockSpec(memory_space=pltpu.HBM)] * len(operands),
        scratch_shapes=[pltpu.VMEM(o.shape, o.dtype) for o in operands] + [
            pltpu.VMEM((2, seqs * rows, LANES), F32),
            pltpu.SemaphoreType.DMA((len(operands),)),
        ],
        compiler_params=pltpu.CompilerParams(vmem_limit_bytes=16 << 20),
        name="project",
    )(*operands)

    other = (lambda a, b, m: a ^ b ^ m) if n & (n - 1) == 0 else (lambda a, b, m: (m - a - b) % n)
    both = [(a, b) for a in range(n) for b in range(n)]
    along_res = [[(a * n + b, other(a, b, m) * n + b) for a, b in both] for m in range(n)]
    along_seq = [[(a * n + b, a * n + other(a, b, m)) for a, b in both] for m in range(n)]
    axes = ("res", "seq")
    brought = [lax.ppermute(right, axes, pairs) for pairs in along_res]
    lefts = [lax.ppermute(left, axes, pairs) for pairs in along_seq]
    rights = [lax.ppermute(block, axes, pairs) for block, pairs in zip(brought, along_seq)]
    return pl.pallas_call(
        functools.partial(pair_kernel, n, seqs, rows, rows, width),
        out_shape=jax.ShapeDtypeStruct((rows, rows, outs), BF16),
        scratch_shapes=[
            pltpu.VMEM((lanes // LANES, lanes, LANES), F32),
            pltpu.VMEM((rows * rows, width * width), BF16),
            pltpu.VMEM((rows * rows, outs), F32),
        ],
        compiler_params=pltpu.CompilerParams(vmem_limit_bytes=24 << 20),
        name="pair",
    )(*lefts, *rights, w, bias)


def solution(mesh):
    n = mesh.shape["res"]
    assert n == mesh.shape["seq"]
    in_specs = (P(("group", "seq"), "res", None), P(("group", "seq"), "res")) + (P(),) * 8
    return jax.shard_map(
        functools.partial(local, n), mesh=mesh, in_specs=in_specs,
        out_specs=P(("group", "res"), "seq", None), check_vma=False,
    )
```

time: 22.5 us -> 38.5 us (1.71)
  the two profiles are of different devices: /device:TPU:2 before, /device:TPU:29 now
where the time goes in v2:
time: 38.5 us; the launch traced here: 37.8 us
  starting transfers between devices  27.5 us (71%)
  local copies, waits for them, and re-layouts  3.79 us (10%)
  waiting for transfers between devices  3.55 us (9%)
  Pallas kernels  2.78 us (7%)
    ppermute x4, starting transfers between devices, local(): lefts = [lax.ppermute(left, axes, pairs) for pairs in along_seq]  9.55 us
    ppermute x4, starting transfers between devices, local(): brought = [lax.ppermute(right, axes, pairs) for pairs in along_res]  9.04 us
    ppermute x4, starting transfers between devices, local(): lax.ppermute(block, axes, pairs)  8.91 us
    unnamed x20, local copies, waits for them, and re-layouts  3.79 us
    ppermute x4, waiting for transfers between devices, local(): lax.ppermute(block, axes, pairs)  3.53 us
    pallas_call x1, Pallas kernels, local(): pl.pallas_call(functools.partial(pair_kernel, n, seqs, rows, rows, width)...  2.11 us
  transfers between devices with their start and end apart: 12, of which 1 were waited for; matrix products, arithmetic and copies ran while one was open for 0% of the time, Pallas kernels for 0%

profile of v2, /device:TPU:29, one launch (start us, length us, event | category | flops | bytes accessed | tf_op | source)
XLA Modules:
  0.0 37.8 jit_solution(17101358334598179207)
XLA Ops:
  0.0 0.0 copy-start.6
  0.0 0.0 copy-start.8
  0.0 0.0 copy-start.5
  0.0 0.0 copy-start.7
  0.0 0.7 %copy-done.6 = f32[256]{0:T(256)S(1)} copy-done((f32[256]{0:T(256)S(1)}, f32[256]{0:T(256)}, u32[]{:S(2)}) %copy-start.6) | copy-done | bytes 1048
  0.7 0.0 copy-done.8
  0.7 0.0 copy-done.5
  0.7 0.0 copy-done.7
  0.7 0.0 copy-start
  0.7 0.9 %copy-done = bf16[32,16,256]{2,1,0:T(8,128)(2,1)S(1)} copy-done((bf16[32,16,256]{2,1,0:T(8,128)(2,1)S(1)}, bf16[32,16,256]{2,1,0:T(8,128)(2,1)}, u32[]{:S(2)}) %copy-start) | copy-done | bytes 262168
  1.7 0.0 copy-start.2
  1.7 0.7 %copy-done.2 = bf16[256,32]{0,1:T(8,128)(2,1)S(1)} copy-done((bf16[256,32]{0,1:T(8,128)(2,1)S(1)}, bf16[256,32]{0,1:T(8,128)(2,1)}, u32[]{:S(2)}) %copy-start.2) | copy-done | bytes 16408
  2.4 0.0 copy-start.3
  2.4 0.7 %copy-done.3 = bf16[256,32]{0,1:T(8,128)(2,1)S(1)} copy-done((bf16[256,32]{0,1:T(8,128)(2,1)S(1)}, bf16[256,32]{0,1:T(8,128)(2,1)}, u32[]{:S(2)}) %copy-start.3) | copy-done | bytes 16408
  3.1 0.0 copy-start.4
  3.1 0.7 %copy-done.4 = s32[32,16]{0,1:T(8,128)S(1)} copy-done((s32[32,16]{0,1:T(8,128)S(1)}, s32[32,16]{0,1:T(8,128)}, u32[]{:S(2)}) %copy-start.4) | copy-done | bytes 2072
  3.8 0.0 copy-start.1
  3.8 0.7 %project.1 = (bf16[144,128]{1,0:T(8,128)(2,1)S(1)}, bf16[144,128]{1,0:T(8,128)(2,1)S(1)}) custom-call(bf16[32,16,256]{2,1,0:T(8,128)(2,1)S(1)} %copy-done, s32[16,32]{1,0:T(8,128)S(1)} %bitcast.5, f32[256]{0:T(256)S(1)} %copy-done.5, f32[256]{0:T(256)S(1)} %copy-done.6, bf16[32,256]{1,0:T(8,128)(2,1)S(1)} %bitcast.3, f32[32]{0:T(128)S(1)} %copy-done.7, ...), custom_call_target="tpu_custom_call" | custom-call | tf_op jit(solution)/shard_map/project/pallas_call | solution.py:149
  4.5 0.0 copy-start.9
  4.5 0.7 %collective-permute-start.3 = (bf16[144,128]{1,0:T(8,128)(2,1)S(1)}, bf16[144,128]{1,0:T(8,128)(2,1)S(1)}, u32[]{:S(2)}, u32[]{:S(2)}) collective-permute-start(bf16[144,128]{1,0:T(8,128)(2,1)S(1)} %get-tuple-element.7), channel_id=1, source_target_pairs={{0,3},{1,2},{2,1},{3,0},{4,6},{5,7},{6,4},{7,5},{8,9},{9,8},{10,11... | collective-permute-start | bytes 110600 | tf_op jit(solution)/shard_map/ppermute | solution.py:167
  5.2 2.6 %collective-permute-start.2 = (bf16[144,128]{1,0:T(8,128)(2,1)S(1)}, bf16[144,128]{1,0:T(8,128)(2,1)S(1)}, u32[]{:S(2)}, u32[]{:S(2)}) collective-permute-start(bf16[144,128]{1,0:T(8,128)(2,1)S(1)} %get-tuple-element.7), channel_id=1, source_target_pairs={{0,2},{1,3},{2,0},{3,1},{4,7},{5,6},{6,5},{7,4},{8,8},{9,9},{10,10... | collective-permute-start | bytes 110600 | tf_op jit(solution)/shard_map/ppermute | solution.py:167
  7.8 3.1 %collective-permute-start.1 = (bf16[144,128]{1,0:T(8,128)(2,1)S(1)}, bf16[144,128]{1,0:T(8,128)(2,1)S(1)}, u32[]{:S(2)}, u32[]{:S(2)}) collective-permute-start(bf16[144,128]{1,0:T(8,128)(2,1)S(1)} %get-tuple-element.7), channel_id=1, source_target_pairs={{0,1},{1,0},{2,3},{3,2},{4,4},{5,5},{6,6},{7,7},{8,11},{9,10},{10,... | collective-permute-start | bytes 110600 | tf_op jit(solution)/shard_map/ppermute | solution.py:167
  10.9 2.4 %collective-permute-start.10 = (bf16[144,128]{1,0:T(8,128)(2,1)S(1)}, bf16[144,128]{1,0:T(8,128)(2,1)S(1)}, u32[]{:S(2)}, u32[]{:S(2)}) collective-permute-start(bf16[144,128]{1,0:T(8,128)(2,1)S(1)} %get-tuple-element.8), channel_id=1, source_target_pairs={{0,12},{1,9},{2,6},{3,3},{4,8},{5,13},{6,2},{7,7},{8,4},{9,1},{10,... | collective-permute-start | bytes 110600 | tf_op jit(solution)/shard_map/ppermute | solution.py:166
  13.3 3.6 %collective-permute-start.8 = (bf16[144,128]{1,0:T(8,128)(2,1)S(1)}, bf16[144,128]{1,0:T(8,128)(2,1)S(1)}, u32[]{:S(2)}, u32[]{:S(2)}) collective-permute-start(bf16[144,128]{1,0:T(8,128)(2,1)S(1)} %get-tuple-element.8), channel_id=1, source_target_pairs={{0,8},{1,13},{2,2},{3,7},{4,12},{5,9},{6,6},{7,3},{8,0},{9,5},{10,... | collective-permute-start | bytes 110600 | tf_op jit(solution)/shard_map/ppermute | solution.py:166
  16.9 0.0 collective-permute-done.3.refs_3_
  16.9 0.7 %collective-permute-start.6 = (bf16[144,128]{1,0:T(8,128)(2,1)S(1)}, bf16[144,128]{1,0:T(8,128)(2,1)S(1)}, u32[]{:S(2)}, u32[]{:S(2)}) collective-permute-start(bf16[144,128]{1,0:T(8,128)(2,1)S(1)} %get-tuple-element.8), channel_id=1, source_target_pairs={{0,4},{1,1},{2,14},{3,11},{4,0},{5,5},{6,10},{7,15},{8,12},{9,9},{... | collective-permute-start | bytes 110600 | tf_op jit(solution)/shard_map/ppermute | solution.py:166
  17.5 0.0 collective-permute-done.2.refs_2_
  17.6 2.4 %collective-permute-start.4 = (bf16[144,128]{1,0:T(8,128)(2,1)S(1)}, bf16[144,128]{1,0:T(8,128)(2,1)S(1)}, u32[]{:S(2)}, u32[]{:S(2)}) collective-permute-start(bf16[144,128]{1,0:T(8,128)(2,1)S(1)} %get-tuple-element.8), channel_id=1, source_target_pairs={{0,0},{1,5},{2,10},{3,15},{4,4},{5,1},{6,14},{7,11},{8,8},{9,13},{... | collective-permute-start | bytes 110600 | tf_op jit(solution)/shard_map/ppermute | solution.py:166
  20.0 0.0 collective-permute-done.1.refs_1_
  20.0 3.2 %collective-permute-start = (bf16[144,128]{1,0:T(8,128)(2,1)S(1)}, bf16[144,128]{1,0:T(8,128)(2,1)S(1)}, u32[]{:S(2)}, u32[]{:S(2)}) collective-permute-start(bf16[144,128]{1,0:T(8,128)(2,1)S(1)} %get-tuple-element.7), channel_id=1, source_target_pairs={{0,0},{1,1},{2,2},{3,3},{4,5},{5,4},{6,7},{7,6},{8,10},{9,11},{10,... | collective-permute-start | bytes 110600 | tf_op jit(solution)/shard_map/ppermute | solution.py:167
  23.2 0.0 collective-permute-done.10
  23.2 0.7 %collective-permute-start.11 = (bf16[144,128]{1,0:T(8,128)(2,1)S(1)}, bf16[144,128]{1,0:T(8,128)(2,1)S(1)}, u32[]{:S(2)}, u32[]{:S(2)}) collective-permute-start(bf16[144,128]{1,0:T(8,128)(2,1)S(1)} %collective-permute-done.10), channel_id=1, source_target_pairs={{0,3},{1,2},{2,1},{3,0},{4,6},{5,7},{6,4},{7,5},{8,9},{9,8},{10,11... | collective-permute-start | bytes 110600 | tf_op jit(solution)/shard_map/ppermute | solution.py:168
  23.9 0.0 collective-permute-done.8
  23.9 2.7 %collective-permute-start.9 = (bf16[144,128]{1,0:T(8,128)(2,1)S(1)}, bf16[144,128]{1,0:T(8,128)(2,1)S(1)}, u32[]{:S(2)}, u32[]{:S(2)}) collective-permute-start(bf16[144,128]{1,0:T(8,128)(2,1)S(1)} %collective-permute-done.8), channel_id=1, source_target_pairs={{0,2},{1,3},{2,0},{3,1},{4,7},{5,6},{6,5},{7,4},{8,8},{9,9},{10,10... | collective-permute-start | bytes 110600 | tf_op jit(solution)/shard_map/ppermute | solution.py:168
  26.6 0.0 collective-permute-done.6
  26.6 3.3 %collective-permute-start.7 = (bf16[144,128]{1,0:T(8,128)(2,1)S(1)}, bf16[144,128]{1,0:T(8,128)(2,1)S(1)}, u32[]{:S(2)}, u32[]{:S(2)}) collective-permute-start(bf16[144,128]{1,0:T(8,128)(2,1)S(1)} %collective-permute-done.6), channel_id=1, source_target_pairs={{0,1},{1,0},{2,3},{3,2},{4,4},{5,5},{6,6},{7,7},{8,11},{9,10},{10,... | collective-permute-start | bytes 110600 | tf_op jit(solution)/shard_map/ppermute | solution.py:168
  29.8 0.0 collective-permute-done.4
  29.8 2.3 %collective-permute-start.5 = (bf16[144,128]{1,0:T(8,128)(2,1)S(1)}, bf16[144,128]{1,0:T(8,128)(2,1)S(1)}, u32[]{:S(2)}, u32[]{:S(2)}) collective-permute-start(bf16[144,128]{1,0:T(8,128)(2,1)S(1)} %collective-permute-done.4), channel_id=1, source_target_pairs={{0,0},{1,1},{2,2},{3,3},{4,5},{5,4},{6,7},{7,6},{8,10},{9,11},{10,... | collective-permute-start | bytes 110600 | tf_op jit(solution)/shard_map/ppermute | solution.py:168
  32.2 0.0 collective-permute-done.refs_0_
  32.2 0.0 collective-permute-done.11.refs_7_
  32.2 0.0 collective-permute-done.9.refs_6_
  32.2 0.0 collective-permute-done.7.refs_5_
  32.2 3.5 %collective-permute-done.5.refs_4_ = bf16[144,128]{1,0:T(8,128)(2,1)S(1)} collective-permute-done((bf16[144,128]{1,0:T(8,128)(2,1)S(1)}, bf16[144,128]{1,0:T(8,128)(2,1)S(1)}, u32[]{:S(2)}, u32[]{:S(2)}) %collective-permute-start.5) | collective-permute-done | bytes 36896 | tf_op jit(solution)/shard_map/ppermute | solution.py:168
  35.7 0.0 copy-done.1
  35.7 0.0 copy-done.9
  35.7 2.1 %pair.1 = bf16[16,16,128]{2,1,0:T(8,128)(2,1)} custom-call(bf16[144,128]{1,0:T(8,128)(2,1)S(1)} %collective-permute-done.refs_0_, bf16[144,128]{1,0:T(8,128)(2,1)S(1)} %collective-permute-done.1.refs_1_, bf16[144,128]{1,0:T(8,128)(2,1)S(1)} %collective-permute-done.2.refs_2_, bf16[144,128]{1,0:T(8,128)(2,1)S(1)} %collective-permute-done.3.refs_3_, ...), custom_call_target="tpu_custom_call" | custom-call | tf_op jit(solution)/shard_map/pair/pallas_call | solution.py:169
Async XLA Ops:
  0.0 0.7 %copy-start.6 = (f32[256]{0:T(256)S(1)}, f32[256]{0:T(256)}, u32[]{:S(2)}) copy-start(f32[256]{0:T(256)} %shift_hbm.1) | copy-start | bytes 3076
  0.0 0.7 %copy-start.8 = (f32[32]{0:T(128)S(1)}, f32[32]{0:T(128)}, u32[]{:S(2)}) copy-start(f32[32]{0:T(128)} %br_hbm.1) | copy-start | bytes 388
  0.0 0.7 %copy-start.5 = (f32[256]{0:T(256)S(1)}, f32[256]{0:T(256)}, u32[]{:S(2)}) copy-start(f32[256]{0:T(256)} %scale_hbm.1) | copy-start | bytes 3076
  0.0 0.7 %copy-start.7 = (f32[32]{0:T(128)S(1)}, f32[32]{0:T(128)}, u32[]{:S(2)}) copy-start(f32[32]{0:T(128)} %bl_hbm.1) | copy-start | bytes 388
  0.7 1.0 %copy-start = (bf16[32,16,256]{2,1,0:T(8,128)(2,1)S(1)}, bf16[32,16,256]{2,1,0:T(8,128)(2,1)}, u32[]{:S(2)}) copy-start(bf16[32,16,256]{2,1,0:T(8,128)(2,1)} %x_hbm.1) | copy-start | bytes 786436
  1.7 0.7 %copy-start.2 = (bf16[256,32]{0,1:T(8,128)(2,1)S(1)}, bf16[256,32]{0,1:T(8,128)(2,1)}, u32[]{:S(2)}) copy-start(bf16[256,32]{0,1:T(8,128)(2,1)} %param.14) | copy-start | bytes 49156
  2.4 0.7 %copy-start.3 = (bf16[256,32]{0,1:T(8,128)(2,1)S(1)}, bf16[256,32]{0,1:T(8,128)(2,1)}, u32[]{:S(2)}) copy-start(bf16[256,32]{0,1:T(8,128)(2,1)} %param.16) | copy-start | bytes 49156
  3.1 0.7 %copy-start.4 = (s32[32,16]{0,1:T(8,128)S(1)}, s32[32,16]{0,1:T(8,128)}, u32[]{:S(2)}) copy-start(s32[32,16]{0,1:T(8,128)} %param.11) | copy-start | bytes 6148
  3.8 31.9 %copy-start.1 = (bf16[1024,128]{1,0:T(8,128)(2,1)S(1)}, bf16[1024,128]{1,0:T(8,128)(2,1)}, u32[]{:S(2)}) copy-start(bf16[1024,128]{1,0:T(8,128)(2,1)} %refs_8_.1) | copy-start | bytes 786436
  4.5 31.2 %copy-start.9 = (f32[128]{0:T(128)S(1)}, f32[128]{0:T(128)}, u32[]{:S(2)}) copy-start(f32[128]{0:T(128)} %refs_9_.1) | copy-start | bytes 1540
  4.5 12.4 %collective-permute-start.3 = (bf16[144,128]{1,0:T(8,128)(2,1)S(1)}, bf16[144,128]{1,0:T(8,128)(2,1)S(1)}, u32[]{:S(2)}, u32[]{:S(2)}) collective-permute-start(bf16[144,128]{1,0:T(8,128)(2,1)S(1)} %get-tuple-element.7), channel_id=1, source_target_pairs={{0,3},{1,2},{2,1},{3,0},{4,6},{5,7},{6,4},{7,5},{8,9},{9,8},{10,11... | collective-permute-start | bytes 110600 | tf_op jit(solution)/shard_map/ppermute | solution.py:167
  5.2 12.4 %collective-permute-start.2 = (bf16[144,128]{1,0:T(8,128)(2,1)S(1)}, bf16[144,128]{1,0:T(8,128)(2,1)S(1)}, u32[]{:S(2)}, u32[]{:S(2)}) collective-permute-start(bf16[144,128]{1,0:T(8,128)(2,1)S(1)} %get-tuple-element.7), channel_id=1, source_target_pairs={{0,2},{1,3},{2,0},{3,1},{4,7},{5,6},{6,5},{7,4},{8,8},{9,9},{10,10... | collective-permute-start | bytes 110600 | tf_op jit(solution)/shard_map/ppermute | solution.py:167
  7.8 12.2 %collective-permute-start.1 = (bf16[144,128]{1,0:T(8,128)(2,1)S(1)}, bf16[144,128]{1,0:T(8,128)(2,1)S(1)}, u32[]{:S(2)}, u32[]{:S(2)}) collective-permute-start(bf16[144,128]{1,0:T(8,128)(2,1)S(1)} %get-tuple-element.7), channel_id=1, source_target_pairs={{0,1},{1,0},{2,3},{3,2},{4,4},{5,5},{6,6},{7,7},{8,11},{9,10},{10,... | collective-permute-start | bytes 110600 | tf_op jit(solution)/shard_map/ppermute | solution.py:167
  10.9 12.3 %collective-permute-start.10 = (bf16[144,128]{1,0:T(8,128)(2,1)S(1)}, bf16[144,128]{1,0:T(8,128)(2,1)S(1)}, u32[]{:S(2)}, u32[]{:S(2)}) collective-permute-start(bf16[144,128]{1,0:T(8,128)(2,1)S(1)} %get-tuple-element.8), channel_id=1, source_target_pairs={{0,12},{1,9},{2,6},{3,3},{4,8},{5,13},{6,2},{7,7},{8,4},{9,1},{10,... | collective-permute-start | bytes 110600 | tf_op jit(solution)/shard_map/ppermute | solution.py:166
  13.3 10.6 %collective-permute-start.8 = (bf16[144,128]{1,0:T(8,128)(2,1)S(1)}, bf16[144,128]{1,0:T(8,128)(2,1)S(1)}, u32[]{:S(2)}, u32[]{:S(2)}) collective-permute-start(bf16[144,128]{1,0:T(8,128)(2,1)S(1)} %get-tuple-element.8), channel_id=1, source_target_pairs={{0,8},{1,13},{2,2},{3,7},{4,12},{5,9},{6,6},{7,3},{8,0},{9,5},{10,... | collective-permute-start | bytes 110600 | tf_op jit(solution)/shard_map/ppermute | solution.py:166
  16.9 9.7 %collective-permute-start.6 = (bf16[144,128]{1,0:T(8,128)(2,1)S(1)}, bf16[144,128]{1,0:T(8,128)(2,1)S(1)}, u32[]{:S(2)}, u32[]{:S(2)}) collective-permute-start(bf16[144,128]{1,0:T(8,128)(2,1)S(1)} %get-tuple-element.8), channel_id=1, source_target_pairs={{0,4},{1,1},{2,14},{3,11},{4,0},{5,5},{6,10},{7,15},{8,12},{9,9},{... | collective-permute-start | bytes 110600 | tf_op jit(solution)/shard_map/ppermute | solution.py:166
  17.6 12.3 %collective-permute-start.4 = (bf16[144,128]{1,0:T(8,128)(2,1)S(1)}, bf16[144,128]{1,0:T(8,128)(2,1)S(1)}, u32[]{:S(2)}, u32[]{:S(2)}) collective-permute-start(bf16[144,128]{1,0:T(8,128)(2,1)S(1)} %get-tuple-element.8), channel_id=1, source_target_pairs={{0,0},{1,5},{2,10},{3,15},{4,4},{5,1},{6,14},{7,11},{8,8},{9,13},{... | collective-permute-start | bytes 110600 | tf_op jit(solution)/shard_map/ppermute | solution.py:166
  20.0 12.2 %collective-permute-start = (bf16[144,128]{1,0:T(8,128)(2,1)S(1)}, bf16[144,128]{1,0:T(8,128)(2,1)S(1)}, u32[]{:S(2)}, u32[]{:S(2)}) collective-permute-start(bf16[144,128]{1,0:T(8,128)(2,1)S(1)} %get-tuple-element.7), channel_id=1, source_target_pairs={{0,0},{1,1},{2,2},{3,3},{4,5},{5,4},{6,7},{7,6},{8,10},{9,11},{10,... | collective-permute-start | bytes 110600 | tf_op jit(solution)/shard_map/ppermute | solution.py:167
  23.2 9.0 %collective-permute-start.11 = (bf16[144,128]{1,0:T(8,128)(2,1)S(1)}, bf16[144,128]{1,0:T(8,128)(2,1)S(1)}, u32[]{:S(2)}, u32[]{:S(2)}) collective-permute-start(bf16[144,128]{1,0:T(8,128)(2,1)S(1)} %collective-permute-done.10), channel_id=1, source_target_pairs={{0,3},{1,2},{2,1},{3,0},{4,6},{5,7},{6,4},{7,5},{8,9},{9,8},{10,11... | collective-permute-start | bytes 110600 | tf_op jit(solution)/shard_map/ppermute | solution.py:168
  23.9 8.3 %collective-permute-start.9 = (bf16[144,128]{1,0:T(8,128)(2,1)S(1)}, bf16[144,128]{1,0:T(8,128)(2,1)S(1)}, u32[]{:S(2)}, u32[]{:S(2)}) collective-permute-start(bf16[144,128]{1,0:T(8,128)(2,1)S(1)} %collective-permute-done.8), channel_id=1, source_target_pairs={{0,2},{1,3},{2,0},{3,1},{4,7},{5,6},{6,5},{7,4},{8,8},{9,9},{10,10... | collective-permute-start | bytes 110600 | tf_op jit(solution)/shard_map/ppermute | solution.py:168
  26.6 5.6 %collective-permute-start.7 = (bf16[144,128]{1,0:T(8,128)(2,1)S(1)}, bf16[144,128]{1,0:T(8,128)(2,1)S(1)}, u32[]{:S(2)}, u32[]{:S(2)}) collective-permute-start(bf16[144,128]{1,0:T(8,128)(2,1)S(1)} %collective-permute-done.6), channel_id=1, source_target_pairs={{0,1},{1,0},{2,3},{3,2},{4,4},{5,5},{6,6},{7,7},{8,11},{9,10},{10,... | collective-permute-start | bytes 110600 | tf_op jit(solution)/shard_map/ppermute | solution.py:168
  29.8 5.9 %collective-permute-start.5 = (bf16[144,128]{1,0:T(8,128)(2,1)S(1)}, bf16[144,128]{1,0:T(8,128)(2,1)S(1)}, u32[]{:S(2)}, u32[]{:S(2)}) collective-permute-start(bf16[144,128]{1,0:T(8,128)(2,1)S(1)} %collective-permute-done.4), channel_id=1, source_target_pairs={{0,0},{1,1},{2,2},{3,3},{4,5},{5,4},{6,7},{7,6},{8,10},{9,11},{10,... | collective-permute-start | bytes 110600 | tf_op jit(solution)/shard_map/ppermute | solution.py:168

commit v3 on v2

--- a/solution.py
+++ b/solution.py
@@ -58,7 +58,9 @@
     flags = flag_ref[...].astype(F32)
     spreader = (iota((rows, lanes), 1) // width == iota((rows, lanes), 0)).astype(BF16)
     mask = dot(flags.astype(BF16), spreader, TN)
-    flags = jnp.concatenate([flags, jnp.zeros((rows, LANES - seqs), F32)], axis=1).astype(BF16)
+    flags = jnp.concatenate([flags] * (LANES // seqs), axis=1)
+    block = iota((rows, LANES), 1) // seqs
+    me = lax.axis_index("seq")
 
     place = iota((seqs, LANES), 1) // width
     for half, out_ref in ((0, left_ref), (1, right_ref)):
@@ -69,37 +71,31 @@
                 merged = jnp.where(place == k, part, merged)
             merged = merged * mask[:, tile * LANES:(tile + 1) * LANES]
             out_ref[tile * seqs:(tile + 1) * seqs, :] = merged.astype(BF16)
-        out_ref[data:, :] = flags
+        for tile in range((out_ref.shape[0] - data) // rows):
+            mine = jnp.where(block + tile * (LANES // seqs) == me, flags, 0.0)
+            out_ref[data + tile * rows:data + (tile + 1) * rows, :] = mine.astype(BF16)
 
 
-def whole_factor(pieces, seqs, data):
-    return jnp.concatenate(
-        [
-            jnp.concatenate([p[t * seqs:(t + 1) * seqs, :] for t in range(data // seqs)], axis=1)
-            for p in pieces
-        ],
-        axis=0,
-    )
+def whole_mask(pieces, rows, data):
+    total = functools.reduce(jnp.add, [p[data:, :] for p in pieces])
+    return jnp.concatenate([total[k:k + rows] for k in range(0, total.shape[0], rows)], axis=1)
 
 
-def whole_mask(pieces, seqs, data):
-    each = LANES // seqs
-    tiles = []
-    for first in range(0, len(pieces), each):
-        total = pieces[first][data:, :].astype(F32)
-        for k in range(1, min(each, len(pieces) - first)):
-            total = total + pltpu.roll(pieces[first + k][data:, :].astype(F32), k * seqs, 1)
-        tiles.append(total)
-    return jnp.concatenate(tiles, axis=1).astype(BF16)
-
-
-def pair_kernel(pieces, seqs, rows, columns, width, *refs):
-    lefts, rights = refs[:pieces], refs[pieces:2 * pieces]
-    w_ref, bias_ref, out_ref, outer_ref, flat_ref, raw_ref = refs[2 * pieces:]
+def pair_kernel(n, seqs, rows, columns, width, *refs):
+    lefts, rights, own_ref = refs[:n], refs[n:2 * n], refs[2 * n]
+    w_ref, bias_ref, out_ref, left_ref, right_ref, outer_ref, flat_ref, raw_ref = refs[2 * n + 1:]
     fold = LANES // width
     data = rows * width // LANES * seqs
 
-    outer = dot(whole_factor(lefts, seqs, data), whole_factor(rights, seqs, data), TN)
+    me_res, me_seq = lax.axis_index("res"), lax.axis_index("seq")
+    rights = [jnp.where(me_res == me_seq, own_ref[...], rights[0][...])] + list(rights[1:])
+    for k in range(n):
+        for pieces, me, whole_ref in ((lefts, me_seq, left_ref), (rights, me_res, right_ref)):
+            at = pl.multiple_of((me ^ k) * seqs, seqs)
+            for tile in range(data // seqs):
+                whole_ref[pl.ds(at, seqs), tile * LANES:(tile + 1) * LANES] = pieces[k][tile * seqs:(tile + 1) * seqs, :]
+
+    outer = dot(left_ref[...], right_ref[...], TN)
     for tile in range(columns // fold):
         outer_ref[tile] = outer[:, tile * LANES:(tile + 1) * LANES]
 
@@ -129,9 +125,9 @@
 
     pair = rows * columns
     row = iota((pair, rows), 0)
-    live_left = dot((row % rows == iota((pair, rows), 1)).astype(BF16), whole_mask(lefts, seqs, data))
+    live_left = dot((row % rows == iota((pair, rows), 1)).astype(BF16), whole_mask(lefts, rows, data))
     row = iota((pair, columns), 0)
-    live_right = dot((row // rows == iota((pair, columns), 1)).astype(BF16), whole_mask(rights, seqs, data))
+    live_right = dot((row // rows == iota((pair, columns), 1)).astype(BF16), whole_mask(rights, rows, data))
     count = jnp.sum(live_left * live_right, axis=1, keepdims=True)
     raw_ref[...] = raw / (1.0 + count)
     for i in range(rows):
@@ -144,8 +140,11 @@
     outs = w.shape[1]
     lanes = rows * width
     data = lanes // LANES * seqs
-    operands = (x, flags.T, scale, shift, wl.T, bl, wr.T, br)
-    wire = jax.ShapeDtypeStruct((data + rows, LANES), BF16)
+    operands = [
+        pltpu.with_memory_space_constraint(o, pltpu.HBM)
+        for o in (x, flags.T, scale, shift, wl.T, bl, wr.T, br)
+    ]
+    wire = jax.ShapeDtypeStruct((data + rows * pl.cdiv(n * seqs, LANES), LANES), BF16)
     left, right = pl.pallas_call(
         project_kernel,
         out_shape=(wire, wire),
@@ -158,30 +157,35 @@
         name="project",
     )(*operands)
 
-    other = (lambda a, b, m: a ^ b ^ m) if n & (n - 1) == 0 else (lambda a, b, m: (m - a - b) % n)
-    both = [(a, b) for a in range(n) for b in range(n)]
-    along_res = [[(a * n + b, other(a, b, m) * n + b) for a, b in both] for m in range(n)]
-    along_seq = [[(a * n + b, a * n + other(a, b, m)) for a, b in both] for m in range(n)]
     axes = ("res", "seq")
-    brought = [lax.ppermute(right, axes, pairs) for pairs in along_res]
-    lefts = [lax.ppermute(left, axes, pairs) for pairs in along_seq]
-    rights = [lax.ppermute(block, axes, pairs) for block, pairs in zip(brought, along_seq)]
+    rights = []
+    for k in range(n):
+        pairs = []
+        for a in range(n):
+            for p in range(n):
+                r = p ^ k
+                to = ((a + 1) % n, (a + 1) % n) if (r, a) == (a, p) else (r, a)
+                pairs.append((a * n + p, to[0] * n + to[1]))
+        rights.append(lax.ppermute(right, axes, pairs))
+    lefts = [left] + [lax.ppermute(left, "seq", [(p, p ^ k) for p in range(n)]) for k in range(1, n)]
     return pl.pallas_call(
         functools.partial(pair_kernel, n, seqs, rows, rows, width),
         out_shape=jax.ShapeDtypeStruct((rows, rows, outs), BF16),
         scratch_shapes=[
+            pltpu.VMEM((n * seqs, lanes), BF16),
+            pltpu.VMEM((n * seqs, lanes), BF16),
             pltpu.VMEM((lanes // LANES, lanes, LANES), F32),
             pltpu.VMEM((rows * rows, width * width), BF16),
             pltpu.VMEM((rows * rows, outs), F32),
         ],
         compiler_params=pltpu.CompilerParams(vmem_limit_bytes=24 << 20),
         name="pair",
-    )(*lefts, *rights, w, bias)
+    )(*lefts, *rights, right, w, bias)
 
 
 def solution(mesh):
     n = mesh.shape["res"]
-    assert n == mesh.shape["seq"]
+    assert n == mesh.shape["seq"] and n & (n - 1) == 0
     in_specs = (P(("group", "seq"), "res", None), P(("group", "seq"), "res")) + (P(),) * 8
     return jax.shard_map(
         functools.partial(local, n), mesh=mesh, in_specs=in_specs,

time: 38.5 us -> 18.5 us (0.48)
  the two profiles are of different devices: /device:TPU:29 before, /device:TPU:0 now
where the time goes in v3:
time: 18.5 us; the launch traced here: 18.4 us
  starting transfers between devices  9.65 us (52%)
  waiting for transfers between devices  4.95 us (27%)
  Pallas kernels  3.74 us (20%)
    ppermute x4, starting transfers between devices, local(): rights.append(lax.ppermute(right, axes, pairs))  6.53 us
    ppermute x4, waiting for transfers between devices, local(): rights.append(lax.ppermute(right, axes, pairs))  4.95 us
    ppermute x3, starting transfers between devices, local(): lax.ppermute(left, 'seq', [(p, p ^ k) for p in range(n)])  3.12 us
    pallas_call x1, Pallas kernels, local(): pl.pallas_call(functools.partial(pair_kernel, n, seqs, rows, rows, width)...  2.15 us
    pallas_call x1, Pallas kernels, local(): pl.pallas_call(project_kernel, out_shape=(wire, wire), in_specs=[pl.Block...  1.59 us
  transfers between devices with their start and end apart: 7, of which 2 were waited for; matrix products, arithmetic and copies ran while one was open for 0% of the time, Pallas kernels for 0%

profile of v3, /device:TPU:0, one launch (start us, length us, event | category | flops | bytes accessed | tf_op | source)
XLA Modules:
  0.0 18.4 jit_solution(15396198544476305793)
XLA Ops:
  0.0 0.0 copy-start
  0.0 1.6 %project.1 = (bf16[144,128]{1,0:T(8,128)(2,1)S(1)}, bf16[144,128]{1,0:T(8,128)(2,1)S(1)}) custom-call(bf16[32,16,256]{2,1,0:T(8,128)(2,1)} %x_hbm.1, s32[16,32]{1,0:T(8,128)} %bitcast.5, f32[256]{0:T(256)} %scale_hbm.1, f32[256]{0:T(256)} %shift_hbm.1, bf16[32,256]{1,0:T(8,128)(2,1)} %bitcast.3, f32[32]{0:T(128)} %bl_hbm.1, bf16[32,256]{1,0:T(8,128)(2,1)} %bitcast.4, ...), custom_call_target="tpu_custom_call" | custom-call | tf_op jit(solution)/shard_map/project/pallas_call | solution.py:148
  1.6 0.0 copy-start.1
  1.6 2.4 %collective-permute-start.2 = (bf16[144,128]{1,0:T(8,128)(2,1)S(1)}, bf16[144,128]{1,0:T(8,128)(2,1)S(1)}, u32[]{:S(2)}, u32[]{:S(2)}) collective-permute-start(bf16[144,128]{1,0:T(8,128)(2,1)S(1)} %get-tuple-element.7.refs_0_), channel_id=1, source_target_pairs={{0,3},{1,2},{2,1},{3,0},{4,7},{5,6},{6,5},{7,4},{8,11},{9,10},{10,... | collective-permute-start | bytes 110600 | tf_op jit(solution)/shard_map/ppermute | solution.py:170
  4.1 0.6 %collective-permute-start.1 = (bf16[144,128]{1,0:T(8,128)(2,1)S(1)}, bf16[144,128]{1,0:T(8,128)(2,1)S(1)}, u32[]{:S(2)}, u32[]{:S(2)}) collective-permute-start(bf16[144,128]{1,0:T(8,128)(2,1)S(1)} %get-tuple-element.7.refs_0_), channel_id=1, source_target_pairs={{0,2},{1,3},{2,0},{3,1},{4,6},{5,7},{6,4},{7,5},{8,10},{9,11},{10,... | collective-permute-start | bytes 110600 | tf_op jit(solution)/shard_map/ppermute | solution.py:170
  4.7 0.0 collective-permute-start
  4.7 3.9 %collective-permute-start.6 = (bf16[144,128]{1,0:T(8,128)(2,1)S(1)}, bf16[144,128]{1,0:T(8,128)(2,1)S(1)}, u32[]{:S(2)}, u32[]{:S(2)}) collective-permute-start(bf16[144,128]{1,0:T(8,128)(2,1)S(1)} %get-tuple-element.8.refs_8_), channel_id=1, source_target_pairs={{0,12},{1,8},{2,4},{3,0},{4,13},{5,9},{6,5},{7,1},{8,14},{9,10},{1... | collective-permute-start | bytes 110600 | tf_op jit(solution)/shard_map/ppermute | solution.py:169
  8.6 1.5 %collective-permute-start.5 = (bf16[144,128]{1,0:T(8,128)(2,1)S(1)}, bf16[144,128]{1,0:T(8,128)(2,1)S(1)}, u32[]{:S(2)}, u32[]{:S(2)}) collective-permute-start(bf16[144,128]{1,0:T(8,128)(2,1)S(1)} %get-tuple-element.8.refs_8_), channel_id=1, source_target_pairs={{0,8},{1,12},{2,0},{3,4},{4,9},{5,13},{6,1},{7,5},{8,10},{9,14},{1... | collective-permute-start | bytes 110600 | tf_op jit(solution)/shard_map/ppermute | solution.py:169
  10.1 0.0 collective-permute-done.2.refs_3_
  10.1 0.0 collective-permute-start.4
  10.1 0.0 collective-permute-done.1.refs_2_
  10.1 1.2 %collective-permute-start.3 = (bf16[144,128]{1,0:T(8,128)(2,1)S(1)}, bf16[144,128]{1,0:T(8,128)(2,1)S(1)}, u32[]{:S(2)}, u32[]{:S(2)}) collective-permute-start(bf16[144,128]{1,0:T(8,128)(2,1)S(1)} %get-tuple-element.8.refs_8_), channel_id=1, source_target_pairs={{0,5},{1,4},{2,8},{3,12},{4,1},{5,10},{6,9},{7,13},{8,2},{9,6},{10... | collective-permute-start | bytes 110600 | tf_op jit(solution)/shard_map/ppermute | solution.py:169
  11.3 0.0 collective-permute-done.refs_1_
  11.3 0.0 collective-permute-done.6.refs_7_
  11.3 1.6 %collective-permute-done.5.refs_6_ = bf16[144,128]{1,0:T(8,128)(2,1)S(1)} collective-permute-done((bf16[144,128]{1,0:T(8,128)(2,1)S(1)}, bf16[144,128]{1,0:T(8,128)(2,1)S(1)}, u32[]{:S(2)}, u32[]{:S(2)}) %collective-permute-start.5) | collective-permute-done | bytes 36896 | tf_op jit(solution)/shard_map/ppermute | solution.py:169
  12.8 0.0 collective-permute-done.4.refs_5_
  12.8 3.4 %collective-permute-done.3.refs_4_ = bf16[144,128]{1,0:T(8,128)(2,1)S(1)} collective-permute-done((bf16[144,128]{1,0:T(8,128)(2,1)S(1)}, bf16[144,128]{1,0:T(8,128)(2,1)S(1)}, u32[]{:S(2)}, u32[]{:S(2)}) %collective-permute-start.3) | collective-permute-done | bytes 36896 | tf_op jit(solution)/shard_map/ppermute | solution.py:169
  16.2 0.0 copy-done
  16.2 0.0 copy-done.1
  16.2 2.1 %pair.1 = bf16[16,16,128]{2,1,0:T(8,128)(2,1)} custom-call(bf16[144,128]{1,0:T(8,128)(2,1)S(1)} %get-tuple-element.7.refs_0_, bf16[144,128]{1,0:T(8,128)(2,1)S(1)} %collective-permute-done.refs_1_, bf16[144,128]{1,0:T(8,128)(2,1)S(1)} %collective-permute-done.1.refs_2_, bf16[144,128]{1,0:T(8,128)(2,1)S(1)} %collective-permute-done.2.refs_3_, ...), custom_call_target="tpu_custom_call" | custom-call | tf_op jit(solution)/shard_map/pair/pallas_call | solution.py:171
Async XLA Ops:
  0.0 16.2 %copy-start = (bf16[1024,128]{1,0:T(8,128)(2,1)S(1)}, bf16[1024,128]{1,0:T(8,128)(2,1)}, u32[]{:S(2)}) copy-start(bf16[1024,128]{1,0:T(8,128)(2,1)} %refs_9_.1) | copy-start | bytes 786436
  1.6 14.6 %copy-start.1 = (f32[128]{0:T(128)S(1)}, f32[128]{0:T(128)}, u32[]{:S(2)}) copy-start(f32[128]{0:T(128)} %refs_10_.1) | copy-start | bytes 1540
  1.6 8.5 %collective-permute-start.2 = (bf16[144,128]{1,0:T(8,128)(2,1)S(1)}, bf16[144,128]{1,0:T(8,128)(2,1)S(1)}, u32[]{:S(2)}, u32[]{:S(2)}) collective-permute-start(bf16[144,128]{1,0:T(8,128)(2,1)S(1)} %get-tuple-element.7.refs_0_), channel_id=1, source_target_pairs={{0,3},{1,2},{2,1},{3,0},{4,7},{5,6},{6,5},{7,4},{8,11},{9,10},{10,... | collective-permute-start | bytes 110600 | tf_op jit(solution)/shard_map/ppermute | solution.py:170
  4.1 6.0 %collective-permute-start.1 = (bf16[144,128]{1,0:T(8,128)(2,1)S(1)}, bf16[144,128]{1,0:T(8,128)(2,1)S(1)}, u32[]{:S(2)}, u32[]{:S(2)}) collective-permute-start(bf16[144,128]{1,0:T(8,128)(2,1)S(1)} %get-tuple-element.7.refs_0_), channel_id=1, source_target_pairs={{0,2},{1,3},{2,0},{3,1},{4,6},{5,7},{6,4},{7,5},{8,10},{9,11},{10,... | collective-permute-start | bytes 110600 | tf_op jit(solution)/shard_map/ppermute | solution.py:170
  4.7 6.6 %collective-permute-start = (bf16[144,128]{1,0:T(8,128)(2,1)S(1)}, bf16[144,128]{1,0:T(8,128)(2,1)S(1)}, u32[]{:S(2)}, u32[]{:S(2)}) collective-permute-start(bf16[144,128]{1,0:T(8,128)(2,1)S(1)} %get-tuple-element.7.refs_0_), channel_id=1, source_target_pairs={{0,1},{1,0},{2,3},{3,2},{4,5},{5,4},{6,7},{7,6},{8,9},{9,8},{10,11... | collective-permute-start | bytes 110600 | tf_op jit(solution)/shard_map/ppermute | solution.py:170
  4.7 6.5 %collective-permute-start.6 = (bf16[144,128]{1,0:T(8,128)(2,1)S(1)}, bf16[144,128]{1,0:T(8,128)(2,1)S(1)}, u32[]{:S(2)}, u32[]{:S(2)}) collective-permute-start(bf16[144,128]{1,0:T(8,128)(2,1)S(1)} %get-tuple-element.8.refs_8_), channel_id=1, source_target_pairs={{0,12},{1,8},{2,4},{3,0},{4,13},{5,9},{6,5},{7,1},{8,14},{9,10},{1... | collective-permute-start | bytes 110600 | tf_op jit(solution)/shard_map/ppermute | solution.py:169
  8.6 4.2 %collective-permute-start.5 = (bf16[144,128]{1,0:T(8,128)(2,1)S(1)}, bf16[144,128]{1,0:T(8,128)(2,1)S(1)}, u32[]{:S(2)}, u32[]{:S(2)}) collective-permute-start(bf16[144,128]{1,0:T(8,128)(2,1)S(1)} %get-tuple-element.8.refs_8_), channel_id=1, source_target_pairs={{0,8},{1,12},{2,0},{3,4},{4,9},{5,13},{6,1},{7,5},{8,10},{9,14},{1... | collective-permute-start | bytes 110600 | tf_op jit(solution)/shard_map/ppermute | solution.py:169
  10.1 2.8 %collective-permute-start.4 = (bf16[144,128]{1,0:T(8,128)(2,1)S(1)}, bf16[144,128]{1,0:T(8,128)(2,1)S(1)}, u32[]{:S(2)}, u32[]{:S(2)}) collective-permute-start(bf16[144,128]{1,0:T(8,128)(2,1)S(1)} %get-tuple-element.8.refs_8_), channel_id=1, source_target_pairs={{0,4},{1,0},{2,12},{3,8},{4,5},{5,1},{6,13},{7,9},{8,6},{9,2},{10,... | collective-permute-start | bytes 110600 | tf_op jit(solution)/shard_map/ppermute | solution.py:169
  10.1 6.1 %collective-permute-start.3 = (bf16[144,128]{1,0:T(8,128)(2,1)S(1)}, bf16[144,128]{1,0:T(8,128)(2,1)S(1)}, u32[]{:S(2)}, u32[]{:S(2)}) collective-permute-start(bf16[144,128]{1,0:T(8,128)(2,1)S(1)} %get-tuple-element.8.refs_8_), channel_id=1, source_target_pairs={{0,5},{1,4},{2,8},{3,12},{4,1},{5,10},{6,9},{7,13},{8,2},{9,6},{10... | collective-permute-start | bytes 110600 | tf_op jit(solution)/shard_map/ppermute | solution.py:169

commit v4 on v3

--- a/solution.py
+++ b/solution.py
@@ -24,7 +24,7 @@
 
 
 def project_kernel(x_hbm, flag_hbm, scale_hbm, shift_hbm, wl_hbm, bl_hbm, wr_hbm, br_hbm,
-                   left_ref, right_ref,
+                   both_ref,
                    x_ref, flag_ref, scale_ref, shift_ref, wl_ref, bl_ref, wr_ref, br_ref, proj_ref, sems):
     copies = [
         pltpu.make_async_copy(src, dst, sems.at[k])
@@ -63,7 +63,9 @@
     me = lax.axis_index("seq")
 
     place = iota((seqs, LANES), 1) // width
-    for half, out_ref in ((0, left_ref), (1, right_ref)):
+    size = both_ref.shape[0] // 2
+    for half in range(2):
+        out_ref = both_ref.at[half * size:(half + 1) * size]
         for tile in range(rows // fold):
             merged = proj_ref[half, pl.ds(tile * fold, seqs, stride=rows), :]
             for k in range(1, fold):
@@ -81,21 +83,26 @@
     return jnp.concatenate([total[k:k + rows] for k in range(0, total.shape[0], rows)], axis=1)
 
 
-def pair_kernel(n, seqs, rows, columns, width, *refs):
-    lefts, rights, own_ref = refs[:n], refs[n:2 * n], refs[2 * n]
-    w_ref, bias_ref, out_ref, left_ref, right_ref, outer_ref, flat_ref, raw_ref = refs[2 * n + 1:]
+def pair_kernel(n, seqs, rows, columns, width, all_ref, w_ref, bias_ref, out_ref, outer_ref, flat_ref, raw_ref):
     fold = LANES // width
     data = rows * width // LANES * seqs
+    size = all_ref.shape[0] // (2 * n * n)
 
-    me_res, me_seq = lax.axis_index("res"), lax.axis_index("seq")
-    rights = [jnp.where(me_res == me_seq, own_ref[...], rights[0][...])] + list(rights[1:])
-    for k in range(n):
-        for pieces, me, whole_ref in ((lefts, me_seq, left_ref), (rights, me_res, right_ref)):
-            at = pl.multiple_of((me ^ k) * seqs, seqs)
-            for tile in range(data // seqs):
-                whole_ref[pl.ds(at, seqs), tile * LANES:(tile + 1) * LANES] = pieces[k][tile * seqs:(tile + 1) * seqs, :]
+    def pieces(block, half):
+        at = [pl.multiple_of(((block * n + p) * 2 + half) * size, size) for p in range(n)]
+        return [all_ref[pl.ds(k, size), :] for k in at]
 
-    outer = dot(left_ref[...], right_ref[...], TN)
+    def factor(pieces):
+        return jnp.concatenate(
+            [
+                jnp.concatenate([p[t * seqs:(t + 1) * seqs] for t in range(data // seqs)], axis=1)
+                for p in pieces
+            ],
+            axis=0,
+        )
+
+    lefts, rights = pieces(lax.axis_index("res"), 0), pieces(lax.axis_index("seq"), 1)
+    outer = dot(factor(lefts), factor(rights), TN)
     for tile in range(columns // fold):
         outer_ref[tile] = outer[:, tile * LANES:(tile + 1) * LANES]
 
@@ -144,10 +151,10 @@
         pltpu.with_memory_space_constraint(o, pltpu.HBM)
         for o in (x, flags.T, scale, shift, wl.T, bl, wr.T, br)
     ]
-    wire = jax.ShapeDtypeStruct((data + rows * pl.cdiv(n * seqs, LANES), LANES), BF16)
-    left, right = pl.pallas_call(
+    wire = jax.ShapeDtypeStruct((2 * (data + rows * pl.cdiv(n * seqs, LANES)), LANES), BF16)
+    both = pl.pallas_call(
         project_kernel,
-        out_shape=(wire, wire),
+        out_shape=wire,
         in_specs=[pl.BlockSpec(memory_space=pltpu.HBM)] * len(operands),
         scratch_shapes=[pltpu.VMEM(o.shape, o.dtype) for o in operands] + [
             pltpu.VMEM((2, seqs * rows, LANES), F32),
@@ -157,30 +164,18 @@
         name="project",
     )(*operands)
 
-    axes = ("res", "seq")
-    rights = []
-    for k in range(n):
-        pairs = []
-        for a in range(n):
-            for p in range(n):
-                r = p ^ k
-                to = ((a + 1) % n, (a + 1) % n) if (r, a) == (a, p) else (r, a)
-                pairs.append((a * n + p, to[0] * n + to[1]))
-        rights.append(lax.ppermute(right, axes, pairs))
-    lefts = [left] + [lax.ppermute(left, "seq", [(p, p ^ k) for p in range(n)]) for k in range(1, n)]
+    gathered = lax.all_gather(both, ("res", "seq"), axis=0, tiled=True)
     return pl.pallas_call(
         functools.partial(pair_kernel, n, seqs, rows, rows, width),
         out_shape=jax.ShapeDtypeStruct((rows, rows, outs), BF16),
         scratch_shapes=[
-            pltpu.VMEM((n * seqs, lanes), BF16),
-            pltpu.VMEM((n * seqs, lanes), BF16),
             pltpu.VMEM((lanes // LANES, lanes, LANES), F32),
             pltpu.VMEM((rows * rows, width * width), BF16),
             pltpu.VMEM((rows * rows, outs), F32),
         ],
         compiler_params=pltpu.CompilerParams(vmem_limit_bytes=24 << 20),
         name="pair",
-    )(*lefts, *rights, right, w, bias)
+    )(gathered, w, bias)
 
 
 def solution(mesh):

time: 18.5 us -> 62.7 us (3.39)
  waiting for transfers between devices: 4.95 us -> 42 us
  between operations: 0.03 us -> 13.4 us
  starting transfers between devices: 9.65 us -> 0.01 us
  local copies, waits for them, and re-layouts: 0.01 us -> 2.87 us
    all_gather x0 -> x1, waiting for transfers between devices: none -> 41.9 us  [local(): gathered = lax.all_gather(both, ('res', 'seq'), axis=0, tiled=True)]
    ppermute x7 -> x0, starting transfers between devices: 9.65 us -> none  [the longest x4 6.53 us: local(): rights.append(lax.ppermute(right, axes, pairs))]
    ppermute x7 -> x0, waiting for transfers between devices: 4.95 us -> none  [the longest x4 4.95 us: local(): rights.append(lax.ppermute(right, axes, pairs))]
    unnamed x4 -> x6, local copies, waits for them, and re-layouts: 0.01 us -> 2.87 us
  transfers between devices with their start and end apart: 7 -> 1, of which waited for: 2 -> 1; matrix products, arithmetic and copies ran while one was open for 0% -> 0% of each run, Pallas kernels for 0% -> 0%
where the time goes in v4:
time: 62.7 us; the launch traced here: 62.5 us
  waiting for transfers between devices  42 us (67%)
  between operations  13.4 us (21%)
  Pallas kernels  4.29 us (7%)
  local copies, waits for them, and re-layouts  2.87 us (5%)
    all_gather x1, waiting for transfers between devices, local(): gathered = lax.all_gather(both, ('res', 'seq'), axis=0, tiled=True)  41.9 us
    unnamed x6, local copies, waits for them, and re-layouts  2.87 us
    pallas_call x1, Pallas kernels, local(): pl.pallas_call(project_kernel, out_shape=wire, in_specs=[pl.BlockSpec(mem...  2.18 us
    pallas_call x1, Pallas kernels, local(): pl.pallas_call(functools.partial(pair_kernel, n, seqs, rows, rows, width)...  2.11 us
  transfers between devices with their start and end apart: 1, of which 1 were waited for; matrix products, arithmetic and copies ran while one was open for 0% of the time, Pallas kernels for 0%

profile of v4, /device:TPU:0, one launch (start us, length us, event | category | flops | bytes accessed | tf_op | source)
XLA Modules:
  0.0 62.5 jit_solution(4630416679662674067)
XLA Ops:
  6.5 0.0 all-gather.2.cloned.1.call-start
  6.5 2.2 %project.1 = bf16[288,128]{1,0:T(8,128)(2,1)} custom-call(bf16[32,16,256]{2,1,0:T(8,128)(2,1)} %x_hbm.1, s32[16,32]{1,0:T(8,128)} %bitcast.5, f32[256]{0:T(256)} %scale_hbm.1, f32[256]{0:T(256)} %shift_hbm.1, bf16[32,256]{1,0:T(8,128)(2,1)} %bitcast.3, f32[32]{0:T(128)} %bl_hbm.1, bf16[32,256]{1,0:T(8,128)(2,1)} %bitcast.4, f32[32]{0:T(128)} %br_hbm.1), custom_call_target="tpu_custom_call" | custom-call | tf_op jit(solution)/shard_map/project/pallas_call | solution.py:155
  8.7 0.0 all-gather.2.cloned.1.call-update
  8.7 41.9 %all-gather.2.cloned.1.call-done.all_ref = bf16[4608,128]{1,0:T(8,128)(2,1)} async-done(((bf16[288,128]{1,0:T(8,128)(2,1)}), bf16[4608,128]{1,0:T(8,128)(2,1)}) %all-gather.2.cloned.1.call-update) | async-done | bytes 1179664 | tf_op jit(solution)/shard_map/all_gather | solution.py:167
  50.7 0.0 copy-start
  50.7 1.3 %copy-done = bf16[4608,128]{1,0:T(8,128)(2,1)S(1)} copy-done((bf16[4608,128]{1,0:T(8,128)(2,1)S(1)}, bf16[4608,128]{1,0:T(8,128)(2,1)}, u32[]{:S(2)}) %copy-start) | copy-done | bytes 1179672
  52.0 0.0 copy-start.1
  52.0 0.9 %copy-done.1 = bf16[1024,128]{1,0:T(8,128)(2,1)S(1)} copy-done((bf16[1024,128]{1,0:T(8,128)(2,1)S(1)}, bf16[1024,128]{1,0:T(8,128)(2,1)}, u32[]{:S(2)}) %copy-start.1) | copy-done | bytes 262168
  52.9 0.0 copy-start.2
  52.9 0.7 %copy-done.2 = f32[128]{0:T(128)S(1)} copy-done((f32[128]{0:T(128)S(1)}, f32[128]{0:T(128)}, u32[]{:S(2)}) %copy-start.2) | copy-done | bytes 536
  53.6 2.1 %pair.1 = bf16[16,16,128]{2,1,0:T(8,128)(2,1)} custom-call(bf16[4608,128]{1,0:T(8,128)(2,1)S(1)} %copy-done, bf16[1024,128]{1,0:T(8,128)(2,1)S(1)} %copy-done.1, f32[128]{0:T(128)S(1)} %copy-done.2), custom_call_target="tpu_custom_call" | custom-call | tf_op jit(solution)/shard_map/pair/pallas_call | solution.py:168
Async XLA Ops:
  6.5 44.2 %all-gather.2.cloned.1.call-start = ((), (), s32[]{:S(2)}) async-start(), calls=%async_computation | async-start | bytes 1253376 | tf_op jit(solution)/shard_map/all_gather | solution.py:167
  50.7 1.3 %copy-start = (bf16[4608,128]{1,0:T(8,128)(2,1)S(1)}, bf16[4608,128]{1,0:T(8,128)(2,1)}, u32[]{:S(2)}) copy-start(bf16[4608,128]{1,0:T(8,128)(2,1)} %all-gather.2.cloned.1.call-done.all_ref) | copy-start | bytes 3538948
  52.0 0.9 %copy-start.1 = (bf16[1024,128]{1,0:T(8,128)(2,1)S(1)}, bf16[1024,128]{1,0:T(8,128)(2,1)}, u32[]{:S(2)}) copy-start(bf16[1024,128]{1,0:T(8,128)(2,1)} %w_ref.1) | copy-start | bytes 786436
  52.9 0.7 %copy-start.2 = (f32[128]{0:T(128)S(1)}, f32[128]{0:T(128)}, u32[]{:S(2)}) copy-start(f32[128]{0:T(128)} %bias_ref.1) | copy-start | bytes 1540
Sparse Core Ops, SparseCore 0:
  9.6 41.0 all-gather.1

commit v5 on v3

--- a/solution.py
+++ b/solution.py
@@ -8,6 +8,7 @@
 from jax.sharding import PartitionSpec as P
 
 LANES = 128
+CORES = 2
 F32 = jnp.float32
 BF16 = jnp.bfloat16
 TN = (((0,), (0,)), ((), ()))
@@ -23,35 +24,17 @@
     return lax.broadcasted_iota(jnp.int32, shape, dim)
 
 
-def project_kernel(x_hbm, flag_hbm, scale_hbm, shift_hbm, wl_hbm, bl_hbm, wr_hbm, br_hbm,
-                   left_ref, right_ref,
-                   x_ref, flag_ref, scale_ref, shift_ref, wl_ref, bl_ref, wr_ref, br_ref, proj_ref, sems):
-    copies = [
-        pltpu.make_async_copy(src, dst, sems.at[k])
-        for k, (src, dst) in enumerate((
-            (x_hbm, x_ref), (flag_hbm, flag_ref), (scale_hbm, scale_ref), (shift_hbm, shift_ref),
-            (wl_hbm, wl_ref), (bl_hbm, bl_ref), (wr_hbm, wr_ref), (br_hbm, br_ref),
-        ))
-    ]
-    for copy in copies:
-        copy.start()
+def project_block(width, x_ref, flag_ref, weight, vectors, block, left_ref, right_ref, proj_ref):
     seqs, rows, depth = x_ref.shape
-    width = wl_ref.shape[0]
     fold = LANES // width
     lanes = rows * width
     data = lanes // LANES * seqs
-    for copy in copies:
-        copy.wait()
-
     x = x_ref[...].astype(F32).reshape(seqs * rows, depth)
     center = jnp.mean(x, axis=-1, keepdims=True)
     x = x - center
     spread = jnp.mean(x * x, axis=-1, keepdims=True)
-    normed = x * lax.rsqrt(spread + 1e-05) * scale_ref[...].reshape(1, depth)
-    normed = (normed + shift_ref[...].reshape(1, depth)).astype(BF16)
-    weight = jnp.concatenate([wl_ref[...]] * fold + [wr_ref[...]] * fold, axis=0)
-    bias = jnp.concatenate([bl_ref[...].reshape(1, width)] * fold + [br_ref[...].reshape(1, width)] * fold, axis=1)
-    both = dot(normed, weight, NT) + bias
+    normed = x * lax.rsqrt(spread + 1e-05) * vectors[0:1] + vectors[1:2]
+    both = dot(normed.astype(BF16), weight, NT) + vectors[2:3]
     proj_ref[0] = both[:, :LANES]
     proj_ref[1] = both[:, LANES:]
 
@@ -59,8 +42,7 @@
     spreader = (iota((rows, lanes), 1) // width == iota((rows, lanes), 0)).astype(BF16)
     mask = dot(flags.astype(BF16), spreader, TN)
     flags = jnp.concatenate([flags] * (LANES // seqs), axis=1)
-    block = iota((rows, LANES), 1) // seqs
-    me = lax.axis_index("seq")
+    lane_block = iota((rows, LANES), 1) // seqs
 
     place = iota((seqs, LANES), 1) // width
     for half, out_ref in ((0, left_ref), (1, right_ref)):
@@ -72,16 +54,61 @@
             merged = merged * mask[:, tile * LANES:(tile + 1) * LANES]
             out_ref[tile * seqs:(tile + 1) * seqs, :] = merged.astype(BF16)
         for tile in range((out_ref.shape[0] - data) // rows):
-            mine = jnp.where(block + tile * (LANES // seqs) == me, flags, 0.0)
+            mine = jnp.where(lane_block + tile * (LANES // seqs) == block, flags, 0.0)
             out_ref[data + tile * rows:data + (tile + 1) * rows, :] = mine.astype(BF16)
 
 
+def own_kernel(x_hbm, flag_hbm, scale_hbm, shift_hbm, wl_hbm, bl_hbm, wr_hbm, br_hbm,
+               left_ref, right_ref, weight_ref, vector_ref,
+               x_ref, flag_ref, scale_ref, shift_ref, wl_ref, bl_ref, wr_ref, br_ref, proj_ref, sems):
+    copies = [
+        pltpu.make_async_copy(src, dst, sems.at[k])
+        for k, (src, dst) in enumerate((
+            (x_hbm, x_ref), (flag_hbm, flag_ref), (scale_hbm, scale_ref), (shift_hbm, shift_ref),
+            (wl_hbm, wl_ref), (bl_hbm, bl_ref), (wr_hbm, wr_ref), (br_hbm, br_ref),
+        ))
+    ]
+    for copy in copies:
+        copy.start()
+    for copy in copies:
+        copy.wait()
+    width, depth = wl_ref.shape
+    fold = LANES // width
+    weight = jnp.concatenate([wl_ref[...]] * fold + [wr_ref[...]] * fold, axis=0)
+    bias = [bl_ref[...].reshape(1, width)] * fold + [br_ref[...].reshape(1, width)] * fold
+    vectors = jnp.concatenate(
+        [
+            scale_ref[...].reshape(1, depth),
+            shift_ref[...].reshape(1, depth),
+            jnp.concatenate(bias, axis=1),
+            jnp.zeros((5, depth), F32),
+        ],
+        axis=0,
+    )
+    weight_ref[...] = weight
+    vector_ref[...] = vectors
+    project_block(width, x_ref, flag_ref, weight, vectors, lax.axis_index("seq"), left_ref, right_ref, proj_ref)
+
+
+def both_kernel(width, x_ref, flag_ref, weight_ref, vector_ref, own_left_ref, own_right_ref, left_ref, right_ref, proj_ref):
+    block = lax.axis_index("seq")
+    core = block % CORES
+    left_ref[core] = own_left_ref[...]
+    right_ref[core] = own_right_ref[...]
+    other = 1 - core
+    project_block(
+        width, x_ref, flag_ref, weight_ref[...], vector_ref[...], block + other - core,
+        left_ref.at[other], right_ref.at[other], proj_ref,
+    )
+
+
 def whole_mask(pieces, rows, data):
-    total = functools.reduce(jnp.add, [p[data:, :] for p in pieces])
+    total = functools.reduce(jnp.add, [p[k, data:, :] for p in pieces for k in range(CORES)])
     return jnp.concatenate([total[k:k + rows] for k in range(0, total.shape[0], rows)], axis=1)
 
 
-def pair_kernel(n, seqs, rows, columns, width, *refs):
+def pair_kernel(steps, seqs, rows, columns, width, *refs):
+    n = len(steps)
     lefts, rights, own_ref = refs[:n], refs[n:2 * n], refs[2 * n]
     w_ref, bias_ref, out_ref, left_ref, right_ref, outer_ref, flat_ref, raw_ref = refs[2 * n + 1:]
     fold = LANES // width
@@ -90,10 +117,13 @@
     me_res, me_seq = lax.axis_index("res"), lax.axis_index("seq")
     rights = [jnp.where(me_res == me_seq, own_ref[...], rights[0][...])] + list(rights[1:])
     for k in range(n):
-        for pieces, me, whole_ref in ((lefts, me_seq, left_ref), (rights, me_res, right_ref)):
-            at = pl.multiple_of((me ^ k) * seqs, seqs)
-            for tile in range(data // seqs):
-                whole_ref[pl.ds(at, seqs), tile * LANES:(tile + 1) * LANES] = pieces[k][tile * seqs:(tile + 1) * seqs, :]
+        for pieces, chip, whole_ref in ((lefts, me_seq // CORES ^ k, left_ref), (rights, (me_res ^ steps[k]) // CORES, right_ref)):
+            for core in range(CORES):
+                at = pl.multiple_of((chip * CORES + core) * seqs, seqs)
+                for tile in range(data // seqs):
+                    whole_ref[pl.ds(at, seqs), tile * LANES:(tile + 1) * LANES] = (
+                        pieces[k][core, tile * seqs:(tile + 1) * seqs, :]
+                    )
 
     outer = dot(left_ref[...], right_ref[...], TN)
     for tile in range(columns // fold):
@@ -139,37 +169,56 @@
     width = wl.shape[1]
     outs = w.shape[1]
     lanes = rows * width
-    data = lanes // LANES * seqs
+    size = lanes // LANES * seqs + rows * pl.cdiv(n * seqs, LANES)
+    axes = ("res", "seq")
+    flags = flags.T
+
+    swap = [(p, p ^ 1) for p in range(n)]
+    other_x, other_flags = lax.ppermute(x, "seq", swap), lax.ppermute(flags, "seq", swap)
+
     operands = [
-        pltpu.with_memory_space_constraint(o, pltpu.HBM)
-        for o in (x, flags.T, scale, shift, wl.T, bl, wr.T, br)
+        pltpu.with_memory_space_constraint(o, pltpu.HBM) for o in (x, flags, scale, shift, wl.T, bl, wr.T, br)
     ]
-    wire = jax.ShapeDtypeStruct((data + rows * pl.cdiv(n * seqs, LANES), LANES), BF16)
-    left, right = pl.pallas_call(
-        project_kernel,
-        out_shape=(wire, wire),
+    wire = jax.ShapeDtypeStruct((size, LANES), BF16)
+    left, right, weight, vectors = pl.pallas_call(
+        own_kernel,
+        out_shape=(
+            wire, wire,
+            jax.ShapeDtypeStruct((2 * LANES, depth), BF16),
+            jax.ShapeDtypeStruct((8, 2 * LANES), F32),
+        ),
         in_specs=[pl.BlockSpec(memory_space=pltpu.HBM)] * len(operands),
         scratch_shapes=[pltpu.VMEM(o.shape, o.dtype) for o in operands] + [
             pltpu.VMEM((2, seqs * rows, LANES), F32),
             pltpu.SemaphoreType.DMA((len(operands),)),
         ],
         compiler_params=pltpu.CompilerParams(vmem_limit_bytes=16 << 20),
-        name="project",
+        cost_estimate=pl.CostEstimate(flops=1 << 25, bytes_accessed=x.size * 8, transcendentals=0),
+        name="project_own",
     )(*operands)
-
-    axes = ("res", "seq")
+    wire = jax.ShapeDtypeStruct((CORES, size, LANES), BF16)
+    left, right = pl.pallas_call(
+        functools.partial(both_kernel, width),
+        out_shape=(wire, wire),
+        scratch_shapes=[pltpu.VMEM((2, seqs * rows, LANES), F32)],
+        compiler_params=pltpu.CompilerParams(vmem_limit_bytes=16 << 20),
+        name="project_other",
+    )(other_x, other_flags, weight, vectors, left, right)
+
+    steps = [m for m in range(n) if bin(m).count("1") % 2 == 0]
+    lefts = [left] + [
+        lax.ppermute(left, "seq", [(p, p ^ k * CORES) for p in range(n)]) for k in range(1, n // CORES)
+    ]
     rights = []
-    for k in range(n):
+    for m in steps:
         pairs = []
         for a in range(n):
             for p in range(n):
-                r = p ^ k
-                to = ((a + 1) % n, (a + 1) % n) if (r, a) == (a, p) else (r, a)
+                to = (a ^ 1, a ^ 1) if (p ^ m, a) == (a, p) else (p ^ m, a)
                 pairs.append((a * n + p, to[0] * n + to[1]))
         rights.append(lax.ppermute(right, axes, pairs))
-    lefts = [left] + [lax.ppermute(left, "seq", [(p, p ^ k) for p in range(n)]) for k in range(1, n)]
     return pl.pallas_call(
-        functools.partial(pair_kernel, n, seqs, rows, rows, width),
+        functools.partial(pair_kernel, steps, seqs, rows, rows, width),
         out_shape=jax.ShapeDtypeStruct((rows, rows, outs), BF16),
         scratch_shapes=[
             pltpu.VMEM((n * seqs, lanes), BF16),
@@ -185,7 +234,7 @@
 
 def solution(mesh):
     n = mesh.shape["res"]
-    assert n == mesh.shape["seq"] and n & (n - 1) == 0
+    assert n == mesh.shape["seq"] and n & (n - 1) == 0 and n % CORES == 0
     in_specs = (P(("group", "seq"), "res", None), P(("group", "seq"), "res")) + (P(),) * 8
     return jax.shard_map(
         functools.partial(local, n), mesh=mesh, in_specs=in_specs,

time: 18.5 us -> 17 us (0.919)
  starting transfers between devices: 9.65 us -> 7.12 us
  Pallas kernels: 3.74 us -> 4.26 us
  waiting for transfers between devices: 4.95 us -> 5.43 us
    ppermute x4 -> x2, starting transfers between devices: 6.53 us -> 3.6 us  [local(): rights.append(lax.ppermute(right, axes, pairs))]
    pallas_call x2 -> x3, Pallas kernels: 3.74 us -> 4.26 us  [the longest x1 2.15 us: local(): pl.pallas_call(functools.partial(pair_kernel, steps, seqs, rows, rows, wi...]
    ppermute x4 -> x2, waiting for transfers between devices: 4.95 us -> 5.42 us  [local(): rights.append(lax.ppermute(right, axes, pairs))]
    ppermute x3, starting transfers between devices: 3.12 us -> 3.51 us  [the longest x1 3 us: local(): lax.ppermute(left, 'seq', [(p, p ^ k * CORES) for p in range(n)])]
  transfers between devices with their start and end apart: 7 -> 5, of which waited for: 2 -> 2; matrix products, arithmetic and copies ran while one was open for 0% -> 0% of each run, Pallas kernels for 0% -> 9%
where the time goes in v5:
time: 17 us; the launch traced here: 16.9 us
  starting transfers between devices  7.12 us (42%)
  waiting for transfers between devices  5.43 us (32%)
  Pallas kernels  4.26 us (25%)
    ppermute x2, waiting for transfers between devices, local(): rights.append(lax.ppermute(right, axes, pairs))  5.42 us
    ppermute x2, starting transfers between devices, local(): rights.append(lax.ppermute(right, axes, pairs))  3.6 us
    ppermute x1, starting transfers between devices, local(): lax.ppermute(left, 'seq', [(p, p ^ k * CORES) for p in range(n)])  3 us
    pallas_call x1, Pallas kernels, local(): pl.pallas_call(functools.partial(pair_kernel, steps, seqs, rows, rows, wi...  2.15 us
    pallas_call x1, Pallas kernels, local(): pl.pallas_call(own_kernel, out_shape=(wire, wire, jax.ShapeDtypeStruct((2...  1.59 us
    pallas_call x1, Pallas kernels, local(): pl.pallas_call(functools.partial(both_kernel, width), out_shape=(wire, wi...  0.53 us
    ppermute x1, starting transfers between devices, local(): lax.ppermute(x, 'seq', swap)  0.45 us
  transfers between devices with their start and end apart: 5, of which 2 were waited for; matrix products, arithmetic and copies ran while one was open for 0% of the time, Pallas kernels for 9%

profile of v5, /device:TPU:0, one launch (start us, length us, event | category | flops | bytes accessed | tf_op | source)
XLA Modules:
  0.0 16.9 jit_solution(17589643172869924213)
XLA Ops:
  0.0 0.5 %collective-permute-start = (bf16[32,16,256]{2,1,0:T(8,128)(2,1)}, bf16[32,16,256]{2,1,0:T(8,128)(2,1)S(1)}, u32[]{:S(2)}, u32[]{:S(2)}) collective-permute-start(bf16[32,16,256]{2,1,0:T(8,128)(2,1)} %x_hbm.1), channel_id=1, source_target_pairs={{0,1},{1,0},{2,3},{3,2},{4,5},{5,4},{6,7},{7,6},{8,9},{9,8},{10,11... | collective-permute-start | bytes 786440 | tf_op jit(solution)/shard_map/ppermute | solution.py:177
  0.5 0.1 collective-permute-start.1
  0.5 1.6 %project_own.1 = (bf16[144,128]{1,0:T(8,128)(2,1)S(1)}, bf16[144,128]{1,0:T(8,128)(2,1)S(1)}, bf16[256,256]{1,0:T(8,128)(2,1)S(1)}, f32[8,256]{1,0:T(8,128)S(1)}) custom-call(bf16[32,16,256]{2,1,0:T(8,128)(2,1)} %x_hbm.1, s32[16,32]{1,0:T(8,128)} %bitcast.6, f32[256]{0:T(256)} %scale_hbm.1, f32[256]{0:T(256)} %shift_hbm.1, bf16[32,256]{1,0:T(8,128)(2,1)} %bitcast.3, ...), custom_call_target="tpu_custom_call" | custom-call | flops 33554432 | bytes 1048576 | tf_op jit(solution)/shard_map/project_own/pallas_call | solution.py:183
  2.1 0.0 copy-start
  2.1 0.0 collective-permute-done.1.flag_ref
  2.1 0.0 collective-permute-done.x_ref
  2.1 0.5 %project_other.1 = (bf16[2,144,128]{2,1,0:T(8,128)(2,1)S(1)}, bf16[2,144,128]{2,1,0:T(8,128)(2,1)S(1)}) custom-call(bf16[32,16,256]{2,1,0:T(8,128)(2,1)S(1)} %collective-permute-done.x_ref, s32[16,32]{1,0:T(8,128)S(1)} %collective-permute-done.1.flag_ref, bf16[256,256]{1,0:T(8,128)(2,1)S(1)} %get-tuple-element.11.weight_ref, ...), custom_call_target="tpu_custom_call" | custom-call | tf_op jit(solution)/shard_map/project_other/pallas_call | solution.py:200
  2.7 0.0 copy-start.1
  2.7 3.0 %collective-permute-start.2 = (bf16[2,144,128]{2,1,0:T(8,128)(2,1)S(1)}, bf16[2,144,128]{2,1,0:T(8,128)(2,1)S(1)}, u32[]{:S(2)}, u32[]{:S(2)}) collective-permute-start(bf16[2,144,128]{2,1,0:T(8,128)(2,1)S(1)} %get-tuple-element.15.refs_0_), channel_id=1, source_target_pairs={{0,2},{1,3},{2,0},{3,1},{4,6},{5,7},{6,4},{7,5},{8,10},{9,11},{10,... | collective-permute-start | bytes 221192 | tf_op jit(solution)/shard_map/ppermute | solution.py:210
  5.7 3.6 %collective-permute-start.4 = (bf16[2,144,128]{2,1,0:T(8,128)(2,1)S(1)}, bf16[2,144,128]{2,1,0:T(8,128)(2,1)S(1)}, u32[]{:S(2)}, u32[]{:S(2)}) collective-permute-start(bf16[2,144,128]{2,1,0:T(8,128)(2,1)S(1)} %get-tuple-element.16.refs_4_), channel_id=1, source_target_pairs={{0,12},{1,8},{2,4},{3,0},{4,13},{5,9},{6,5},{7,1},{8,14},{9,10},{1... | collective-permute-start | bytes 221192 | tf_op jit(solution)/shard_map/ppermute | solution.py:219
  9.3 0.0 collective-permute-start.3
  9.3 0.0 collective-permute-done.2.refs_1_
  9.3 2.0 %collective-permute-done.4.refs_3_ = bf16[2,144,128]{2,1,0:T(8,128)(2,1)S(1)} collective-permute-done((bf16[2,144,128]{2,1,0:T(8,128)(2,1)S(1)}, bf16[2,144,128]{2,1,0:T(8,128)(2,1)S(1)}, u32[]{:S(2)}, u32[]{:S(2)}) %collective-permute-start.4) | collective-permute-done | bytes 73760 | tf_op jit(solution)/shard_map/ppermute | solution.py:219
  11.3 3.4 %collective-permute-done.3.refs_2_ = bf16[2,144,128]{2,1,0:T(8,128)(2,1)S(1)} collective-permute-done((bf16[2,144,128]{2,1,0:T(8,128)(2,1)S(1)}, bf16[2,144,128]{2,1,0:T(8,128)(2,1)S(1)}, u32[]{:S(2)}, u32[]{:S(2)}) %collective-permute-start.3) | collective-permute-done | bytes 73760 | tf_op jit(solution)/shard_map/ppermute | solution.py:219
  14.7 0.0 copy-done
  14.7 0.0 copy-done.1
  14.7 2.2 %pair.1 = bf16[16,16,128]{2,1,0:T(8,128)(2,1)} custom-call(bf16[2,144,128]{2,1,0:T(8,128)(2,1)S(1)} %get-tuple-element.15.refs_0_, bf16[2,144,128]{2,1,0:T(8,128)(2,1)S(1)} %collective-permute-done.2.refs_1_, bf16[2,144,128]{2,1,0:T(8,128)(2,1)S(1)} %collective-permute-done.3.refs_2_, bf16[2,144,128]{2,1,0:T(8,128)(2,1)S(1)} %collective-permute-done.4.refs_3_, ...), custom_call_target="tpu_custom_call" | custom-call | tf_op jit(solution)/shard_map/pair/pallas_call | solution.py:220
Async XLA Ops:
  0.0 2.1 %collective-permute-start = (bf16[32,16,256]{2,1,0:T(8,128)(2,1)}, bf16[32,16,256]{2,1,0:T(8,128)(2,1)S(1)}, u32[]{:S(2)}, u32[]{:S(2)}) collective-permute-start(bf16[32,16,256]{2,1,0:T(8,128)(2,1)} %x_hbm.1), channel_id=1, source_target_pairs={{0,1},{1,0},{2,3},{3,2},{4,5},{5,4},{6,7},{7,6},{8,9},{9,8},{10,11... | collective-permute-start | bytes 786440 | tf_op jit(solution)/shard_map/ppermute | solution.py:177
  0.5 1.7 %collective-permute-start.1 = (s32[16,32]{1,0:T(8,128)}, s32[16,32]{1,0:T(8,128)S(1)}, u32[]{:S(2)}, u32[]{:S(2)}) collective-permute-start(s32[16,32]{1,0:T(8,128)} %bitcast.5), channel_id=1, source_target_pairs={{0,1},{1,0},{2,3},{3,2},{4,5},{5,4},{6,7},{7,6},{8,9},{9,8},{10,11... | collective-permute-start | bytes 6152 | tf_op jit(solution)/shard_map/ppermute | solution.py:177
  2.1 12.6 %copy-start = (bf16[1024,128]{1,0:T(8,128)(2,1)S(1)}, bf16[1024,128]{1,0:T(8,128)(2,1)}, u32[]{:S(2)}) copy-start(bf16[1024,128]{1,0:T(8,128)(2,1)} %refs_5_.1) | copy-start | bytes 786436
  2.7 12.1 %copy-start.1 = (f32[128]{0:T(128)S(1)}, f32[128]{0:T(128)}, u32[]{:S(2)}) copy-start(f32[128]{0:T(128)} %refs_6_.1) | copy-start | bytes 1540
  2.7 6.6 %collective-permute-start.2 = (bf16[2,144,128]{2,1,0:T(8,128)(2,1)S(1)}, bf16[2,144,128]{2,1,0:T(8,128)(2,1)S(1)}, u32[]{:S(2)}, u32[]{:S(2)}) collective-permute-start(bf16[2,144,128]{2,1,0:T(8,128)(2,1)S(1)} %get-tuple-element.15.refs_0_), channel_id=1, source_target_pairs={{0,2},{1,3},{2,0},{3,1},{4,6},{5,7},{6,4},{7,5},{8,10},{9,11},{10,... | collective-permute-start | bytes 221192 | tf_op jit(solution)/shard_map/ppermute | solution.py:210
  5.7 5.6 %collective-permute-start.4 = (bf16[2,144,128]{2,1,0:T(8,128)(2,1)S(1)}, bf16[2,144,128]{2,1,0:T(8,128)(2,1)S(1)}, u32[]{:S(2)}, u32[]{:S(2)}) collective-permute-start(bf16[2,144,128]{2,1,0:T(8,128)(2,1)S(1)} %get-tuple-element.16.refs_4_), channel_id=1, source_target_pairs={{0,12},{1,8},{2,4},{3,0},{4,13},{5,9},{6,5},{7,1},{8,14},{9,10},{1... | collective-permute-start | bytes 221192 | tf_op jit(solution)/shard_map/ppermute | solution.py:219
  9.3 5.4 %collective-permute-start.3 = (bf16[2,144,128]{2,1,0:T(8,128)(2,1)S(1)}, bf16[2,144,128]{2,1,0:T(8,128)(2,1)S(1)}, u32[]{:S(2)}, u32[]{:S(2)}) collective-permute-start(bf16[2,144,128]{2,1,0:T(8,128)(2,1)S(1)} %get-tuple-element.16.refs_4_), channel_id=1, source_target_pairs={{0,5},{1,4},{2,8},{3,12},{4,1},{5,0},{6,9},{7,13},{8,2},{9,6},{10,... | collective-permute-start | bytes 221192 | tf_op jit(solution)/shard_map/ppermute | solution.py:219

commit v6 on v5

--- a/solution.py
+++ b/solution.py
@@ -109,13 +109,12 @@
 
 def pair_kernel(steps, seqs, rows, columns, width, *refs):
     n = len(steps)
-    lefts, rights, own_ref = refs[:n], refs[n:2 * n], refs[2 * n]
-    w_ref, bias_ref, out_ref, left_ref, right_ref, outer_ref, flat_ref, raw_ref = refs[2 * n + 1:]
+    lefts, rights = refs[:n], refs[n:2 * n]
+    w_ref, bias_ref, out_ref, left_ref, right_ref, outer_ref, flat_ref, raw_ref = refs[2 * n:]
     fold = LANES // width
     data = rows * width // LANES * seqs
 
     me_res, me_seq = lax.axis_index("res"), lax.axis_index("seq")
-    rights = [jnp.where(me_res == me_seq, own_ref[...], rights[0][...])] + list(rights[1:])
     for k in range(n):
         for pieces, chip, whole_ref in ((lefts, me_seq // CORES ^ k, left_ref), (rights, (me_res ^ steps[k]) // CORES, right_ref)):
             for core in range(CORES):
@@ -205,17 +204,13 @@
         name="project_other",
     )(other_x, other_flags, weight, vectors, left, right)
 
-    steps = [m for m in range(n) if bin(m).count("1") % 2 == 0]
+    steps = [m for m in reversed(range(n)) if bin(m).count("1") % 2 == 1]
     lefts = [left] + [
         lax.ppermute(left, "seq", [(p, p ^ k * CORES) for p in range(n)]) for k in range(1, n // CORES)
     ]
     rights = []
     for m in steps:
-        pairs = []
-        for a in range(n):
-            for p in range(n):
-                to = (a ^ 1, a ^ 1) if (p ^ m, a) == (a, p) else (p ^ m, a)
-                pairs.append((a * n + p, to[0] * n + to[1]))
+        pairs = [(a * n + p, (p ^ m) * n + a) for a in range(n) for p in range(n)]
         rights.append(lax.ppermute(right, axes, pairs))
     return pl.pallas_call(
         functools.partial(pair_kernel, steps, seqs, rows, rows, width),
@@ -229,7 +224,7 @@
         ],
         compiler_params=pltpu.CompilerParams(vmem_limit_bytes=24 << 20),
         name="pair",
-    )(*lefts, *rights, right, w, bias)
+    )(*lefts, *rights, w, bias)
 
 
 def solution(mesh):

time: 17 us -> 15.7 us (0.924)
  the two profiles are of different devices: /device:TPU:0 before, /device:TPU:2 now
where the time goes in v6:
time: 15.7 us; the launch traced here: 15.6 us
  waiting for transfers between devices  5.65 us (36%)
  starting transfers between devices  5.63 us (36%)
  Pallas kernels  4.25 us (27%)
    ppermute x2, waiting for transfers between devices, local(): rights.append(lax.ppermute(right, axes, pairs))  5.64 us
    ppermute x2, starting transfers between devices, local(): rights.append(lax.ppermute(right, axes, pairs))  5.05 us
    pallas_call x1, Pallas kernels, local(): pl.pallas_call(functools.partial(pair_kernel, steps, seqs, rows, rows, wi...  2.14 us
    pallas_call x1, Pallas kernels, local(): pl.pallas_call(own_kernel, out_shape=(wire, wire, jax.ShapeDtypeStruct((2...  1.59 us
    pallas_call x1, Pallas kernels, local(): pl.pallas_call(functools.partial(both_kernel, width), out_shape=(wire, wi...  0.53 us
    ppermute x1, starting transfers between devices, local(): lax.ppermute(flags, 'seq', swap)  0.51 us
  transfers between devices with their start and end apart: 5, of which 2 were waited for; matrix products, arithmetic and copies ran while one was open for 0% of the time, Pallas kernels for 10%

profile of v6, /device:TPU:2, one launch (start us, length us, event | category | flops | bytes accessed | tf_op | source)
XLA Modules:
  0.0 15.6 jit_solution(6235642142765266545)
XLA Ops:
  0.0 0.0 collective-permute-start
  0.0 0.5 %collective-permute-start.1 = (s32[16,32]{1,0:T(8,128)}, s32[16,32]{1,0:T(8,128)S(1)}, u32[]{:S(2)}, u32[]{:S(2)}) collective-permute-start(s32[16,32]{1,0:T(8,128)} %bitcast.5), channel_id=1, source_target_pairs={{0,1},{1,0},{2,3},{3,2},{4,5},{5,4},{6,7},{7,6},{8,9},{9,8},{10,11... | collective-permute-start | bytes 6152 | tf_op jit(solution)/shard_map/ppermute | solution.py:176
  0.5 1.6 %project_own.1 = (bf16[144,128]{1,0:T(8,128)(2,1)S(1)}, bf16[144,128]{1,0:T(8,128)(2,1)S(1)}, bf16[256,256]{1,0:T(8,128)(2,1)S(1)}, f32[8,256]{1,0:T(8,128)S(1)}) custom-call(bf16[32,16,256]{2,1,0:T(8,128)(2,1)} %x_hbm.1, s32[16,32]{1,0:T(8,128)} %bitcast.6, f32[256]{0:T(256)} %scale_hbm.1, f32[256]{0:T(256)} %shift_hbm.1, bf16[32,256]{1,0:T(8,128)(2,1)} %bitcast.3, ...), custom_call_target="tpu_custom_call" | custom-call | flops 33554432 | bytes 1048576 | tf_op jit(solution)/shard_map/project_own/pallas_call | solution.py:182
  2.1 0.0 copy-start
  2.1 0.0 collective-permute-done.1.flag_ref
  2.1 0.0 collective-permute-done.x_ref
  2.1 0.5 %project_other.1 = (bf16[2,144,128]{2,1,0:T(8,128)(2,1)S(1)}, bf16[2,144,128]{2,1,0:T(8,128)(2,1)S(1)}) custom-call(bf16[32,16,256]{2,1,0:T(8,128)(2,1)S(1)} %collective-permute-done.x_ref, s32[16,32]{1,0:T(8,128)S(1)} %collective-permute-done.1.flag_ref, bf16[256,256]{1,0:T(8,128)(2,1)S(1)} %get-tuple-element.11.weight_ref, ...), custom_call_target="tpu_custom_call" | custom-call | tf_op jit(solution)/shard_map/project_other/pallas_call | solution.py:199
  2.7 0.0 copy-start.1
  2.7 0.1 collective-permute-start.2
  2.8 5.1 %collective-permute-start.4 = (bf16[2,144,128]{2,1,0:T(8,128)(2,1)S(1)}, bf16[2,144,128]{2,1,0:T(8,128)(2,1)S(1)}, u32[]{:S(2)}, u32[]{:S(2)}) collective-permute-start(bf16[2,144,128]{2,1,0:T(8,128)(2,1)S(1)} %get-tuple-element.16), channel_id=1, source_target_pairs={{0,4},{1,0},{2,12},{3,8},{4,5},{5,1},{6,13},{7,9},{8,6},{9,2},{10,... | collective-permute-start | bytes 221192 | tf_op jit(solution)/shard_map/ppermute | solution.py:214
  7.8 0.0 collective-permute-start.3
  7.8 0.0 collective-permute-done.2.refs_1_
  7.8 2.0 %collective-permute-done.4.refs_3_ = bf16[2,144,128]{2,1,0:T(8,128)(2,1)S(1)} collective-permute-done((bf16[2,144,128]{2,1,0:T(8,128)(2,1)S(1)}, bf16[2,144,128]{2,1,0:T(8,128)(2,1)S(1)}, u32[]{:S(2)}, u32[]{:S(2)}) %collective-permute-start.4) | collective-permute-done | bytes 73760 | tf_op jit(solution)/shard_map/ppermute | solution.py:214
  9.8 3.7 %collective-permute-done.3.refs_2_ = bf16[2,144,128]{2,1,0:T(8,128)(2,1)S(1)} collective-permute-done((bf16[2,144,128]{2,1,0:T(8,128)(2,1)S(1)}, bf16[2,144,128]{2,1,0:T(8,128)(2,1)S(1)}, u32[]{:S(2)}, u32[]{:S(2)}) %collective-permute-start.3) | collective-permute-done | bytes 73760 | tf_op jit(solution)/shard_map/ppermute | solution.py:214
  13.5 0.0 copy-done
  13.5 0.0 copy-done.1
  13.5 2.1 %pair.1 = bf16[16,16,128]{2,1,0:T(8,128)(2,1)} custom-call(bf16[2,144,128]{2,1,0:T(8,128)(2,1)S(1)} %get-tuple-element.15.refs_0_, bf16[2,144,128]{2,1,0:T(8,128)(2,1)S(1)} %collective-permute-done.2.refs_1_, bf16[2,144,128]{2,1,0:T(8,128)(2,1)S(1)} %collective-permute-done.3.refs_2_, bf16[2,144,128]{2,1,0:T(8,128)(2,1)S(1)} %collective-permute-done.4.refs_3_, ...), custom_call_target="tpu_custom_call" | custom-call | tf_op jit(solution)/shard_map/pair/pallas_call | solution.py:215
Async XLA Ops:
  0.0 2.1 %collective-permute-start = (bf16[32,16,256]{2,1,0:T(8,128)(2,1)}, bf16[32,16,256]{2,1,0:T(8,128)(2,1)S(1)}, u32[]{:S(2)}, u32[]{:S(2)}) collective-permute-start(bf16[32,16,256]{2,1,0:T(8,128)(2,1)} %x_hbm.1), channel_id=1, source_target_pairs={{0,1},{1,0},{2,3},{3,2},{4,5},{5,4},{6,7},{7,6},{8,9},{9,8},{10,11... | collective-permute-start | bytes 786440 | tf_op jit(solution)/shard_map/ppermute | solution.py:176
  0.0 2.1 %collective-permute-start.1 = (s32[16,32]{1,0:T(8,128)}, s32[16,32]{1,0:T(8,128)S(1)}, u32[]{:S(2)}, u32[]{:S(2)}) collective-permute-start(s32[16,32]{1,0:T(8,128)} %bitcast.5), channel_id=1, source_target_pairs={{0,1},{1,0},{2,3},{3,2},{4,5},{5,4},{6,7},{7,6},{8,9},{9,8},{10,11... | collective-permute-start | bytes 6152 | tf_op jit(solution)/shard_map/ppermute | solution.py:176
  2.1 11.4 %copy-start = (bf16[1024,128]{1,0:T(8,128)(2,1)S(1)}, bf16[1024,128]{1,0:T(8,128)(2,1)}, u32[]{:S(2)}) copy-start(bf16[1024,128]{1,0:T(8,128)(2,1)} %refs_4_.1) | copy-start | bytes 786436
  2.7 10.8 %copy-start.1 = (f32[128]{0:T(128)S(1)}, f32[128]{0:T(128)}, u32[]{:S(2)}) copy-start(f32[128]{0:T(128)} %refs_5_.1) | copy-start | bytes 1540
  2.7 5.1 %collective-permute-start.2 = (bf16[2,144,128]{2,1,0:T(8,128)(2,1)S(1)}, bf16[2,144,128]{2,1,0:T(8,128)(2,1)S(1)}, u32[]{:S(2)}, u32[]{:S(2)}) collective-permute-start(bf16[2,144,128]{2,1,0:T(8,128)(2,1)S(1)} %get-tuple-element.15.refs_0_), channel_id=1, source_target_pairs={{0,2},{1,3},{2,0},{3,1},{4,6},{5,7},{6,4},{7,5},{8,10},{9,11},{10,... | collective-permute-start | bytes 221192 | tf_op jit(solution)/shard_map/ppermute | solution.py:209
  2.8 7.0 %collective-permute-start.4 = (bf16[2,144,128]{2,1,0:T(8,128)(2,1)S(1)}, bf16[2,144,128]{2,1,0:T(8,128)(2,1)S(1)}, u32[]{:S(2)}, u32[]{:S(2)}) collective-permute-start(bf16[2,144,128]{2,1,0:T(8,128)(2,1)S(1)} %get-tuple-element.16), channel_id=1, source_target_pairs={{0,4},{1,0},{2,12},{3,8},{4,5},{5,1},{6,13},{7,9},{8,6},{9,2},{10,... | collective-permute-start | bytes 221192 | tf_op jit(solution)/shard_map/ppermute | solution.py:214
  7.8 5.6 %collective-permute-start.3 = (bf16[2,144,128]{2,1,0:T(8,128)(2,1)S(1)}, bf16[2,144,128]{2,1,0:T(8,128)(2,1)S(1)}, u32[]{:S(2)}, u32[]{:S(2)}) collective-permute-start(bf16[2,144,128]{2,1,0:T(8,128)(2,1)S(1)} %get-tuple-element.16), channel_id=1, source_target_pairs={{0,8},{1,12},{2,0},{3,4},{4,9},{5,13},{6,1},{7,5},{8,10},{9,14},{1... | collective-permute-start | bytes 221192 | tf_op jit(solution)/shard_map/ppermute | solution.py:214

commit v7 on v6

--- a/solution.py
+++ b/solution.py
@@ -22,6 +22,29 @@
 
 def iota(shape, dim):
     return lax.broadcasted_iota(jnp.int32, shape, dim)
+
+
+ROUTES = (
+    ((2, 0, 3, 1), (1, 0, 2, 3), (1, 3, 0, 2), (1, 3, 0, 2)),
+    ((3, 1, 2, 0), (2, 3, 1, 0), (2, 0, 3, 1), (2, 0, 3, 1)),
+)
+
+
+def routes(n):
+    if n == 4:
+        return ROUTES
+    steps = [m for m in range(n) if bin(m).count("1") % 2 == 1]
+    return tuple(tuple(tuple(p ^ m for p in range(n)) for a in range(n)) for m in steps)
+
+
+def sending_chip(step, r, q):
+    n = len(step)
+    chip = 0
+    for bit in range((n // CORES - 1).bit_length()):
+        for a in range(n):
+            word = sum((step[a].index(to) // CORES >> bit & 1) << to for to in range(n))
+            chip = chip | jnp.where(q == a, (jnp.int32(word) >> r & 1) << bit, 0)
+    return chip
 
 
 def project_block(width, x_ref, flag_ref, weight, vectors, block, left_ref, right_ref, proj_ref):
@@ -116,7 +139,7 @@
 
     me_res, me_seq = lax.axis_index("res"), lax.axis_index("seq")
     for k in range(n):
-        for pieces, chip, whole_ref in ((lefts, me_seq // CORES ^ k, left_ref), (rights, (me_res ^ steps[k]) // CORES, right_ref)):
+        for pieces, chip, whole_ref in ((lefts, me_seq // CORES ^ k, left_ref), (rights, sending_chip(steps[k], me_res, me_seq), right_ref)):
             for core in range(CORES):
                 at = pl.multiple_of((chip * CORES + core) * seqs, seqs)
                 for tile in range(data // seqs):
@@ -204,14 +227,14 @@
         name="project_other",
     )(other_x, other_flags, weight, vectors, left, right)
 
-    steps = [m for m in reversed(range(n)) if bin(m).count("1") % 2 == 1]
+    steps = routes(n)
     lefts = [left] + [
         lax.ppermute(left, "seq", [(p, p ^ k * CORES) for p in range(n)]) for k in range(1, n // CORES)
     ]
-    rights = []
-    for m in steps:
-        pairs = [(a * n + p, (p ^ m) * n + a) for a in range(n) for p in range(n)]
-        rights.append(lax.ppermute(right, axes, pairs))
+    rights = [
+        lax.ppermute(right, axes, [(a * n + p, step[a][p] * n + a) for a in range(n) for p in range(n)])
+        for step in steps
+    ]
     return pl.pallas_call(
         functools.partial(pair_kernel, steps, seqs, rows, rows, width),
         out_shape=jax.ShapeDtypeStruct((rows, rows, outs), BF16),

time: 15.7 us -> 14.3 us (0.911)
  the two profiles are of different devices: /device:TPU:2 before, /device:TPU:0 now
where the time goes in v7:
time: 14.3 us; the launch traced here: 14.1 us
  starting transfers between devices  7.12 us (50%)
  Pallas kernels  4.25 us (30%)
  waiting for transfers between devices  2.68 us (19%)
    ppermute x2, starting transfers between devices, local(): lax.ppermute(right, axes, [(a * n + p, step[a][p] * n + a) for a in range...  3.6 us
    ppermute x1, starting transfers between devices, local(): lax.ppermute(left, 'seq', [(p, p ^ k * CORES) for p in range(n)])  3 us
    ppermute x2, waiting for transfers between devices, local(): lax.ppermute(right, axes, [(a * n + p, step[a][p] * n + a) for a in range...  2.67 us
    pallas_call x1, Pallas kernels, local(): pl.pallas_call(functools.partial(pair_kernel, steps, seqs, rows, rows, wi...  2.14 us
    pallas_call x1, Pallas kernels, local(): pl.pallas_call(own_kernel, out_shape=(wire, wire, jax.ShapeDtypeStruct((2...  1.59 us
    pallas_call x1, Pallas kernels, local(): pl.pallas_call(functools.partial(both_kernel, width), out_shape=(wire, wi...  0.53 us
    ppermute x1, starting transfers between devices, local(): lax.ppermute(x, 'seq', swap)  0.45 us
  transfers between devices with their start and end apart: 5, of which 2 were waited for; matrix products, arithmetic and copies ran while one was open for 0% of the time, Pallas kernels for 11%

profile of v7, /device:TPU:0, one launch (start us, length us, event | category | flops | bytes accessed | tf_op | source)
XLA Modules:
  0.0 14.1 jit_solution(16095206575838455426)
XLA Ops:
  0.0 0.5 %collective-permute-start = (bf16[32,16,256]{2,1,0:T(8,128)(2,1)}, bf16[32,16,256]{2,1,0:T(8,128)(2,1)S(1)}, u32[]{:S(2)}, u32[]{:S(2)}) collective-permute-start(bf16[32,16,256]{2,1,0:T(8,128)(2,1)} %x_hbm.1), channel_id=1, source_target_pairs={{0,1},{1,0},{2,3},{3,2},{4,5},{5,4},{6,7},{7,6},{8,9},{9,8},{10,11... | collective-permute-start | bytes 786440 | tf_op jit(solution)/shard_map/ppermute | solution.py:199
  0.5 0.1 collective-permute-start.1
  0.5 1.6 %project_own.1 = (bf16[144,128]{1,0:T(8,128)(2,1)S(1)}, bf16[144,128]{1,0:T(8,128)(2,1)S(1)}, bf16[256,256]{1,0:T(8,128)(2,1)S(1)}, f32[8,256]{1,0:T(8,128)S(1)}) custom-call(bf16[32,16,256]{2,1,0:T(8,128)(2,1)} %x_hbm.1, s32[16,32]{1,0:T(8,128)} %bitcast.6, f32[256]{0:T(256)} %scale_hbm.1, f32[256]{0:T(256)} %shift_hbm.1, bf16[32,256]{1,0:T(8,128)(2,1)} %bitcast.3, ...), custom_call_target="tpu_custom_call" | custom-call | flops 33554432 | bytes 1048576 | tf_op jit(solution)/shard_map/project_own/pallas_call | solution.py:205
  2.1 0.0 copy-start
  2.1 0.0 collective-permute-done.1.flag_ref
  2.1 0.0 collective-permute-done.x_ref
  2.1 0.5 %project_other.1 = (bf16[2,144,128]{2,1,0:T(8,128)(2,1)S(1)}, bf16[2,144,128]{2,1,0:T(8,128)(2,1)S(1)}) custom-call(bf16[32,16,256]{2,1,0:T(8,128)(2,1)S(1)} %collective-permute-done.x_ref, s32[16,32]{1,0:T(8,128)S(1)} %collective-permute-done.1.flag_ref, bf16[256,256]{1,0:T(8,128)(2,1)S(1)} %get-tuple-element.11.weight_ref, ...), custom_call_target="tpu_custom_call" | custom-call | tf_op jit(solution)/shard_map/project_other/pallas_call | solution.py:222
  2.7 0.0 copy-start.1
  2.7 3.0 %collective-permute-start.2 = (bf16[2,144,128]{2,1,0:T(8,128)(2,1)S(1)}, bf16[2,144,128]{2,1,0:T(8,128)(2,1)S(1)}, u32[]{:S(2)}, u32[]{:S(2)}) collective-permute-start(bf16[2,144,128]{2,1,0:T(8,128)(2,1)S(1)} %get-tuple-element.15.refs_0_), channel_id=1, source_target_pairs={{0,2},{1,3},{2,0},{3,1},{4,6},{5,7},{6,4},{7,5},{8,10},{9,11},{10,... | collective-permute-start | bytes 221192 | tf_op jit(solution)/shard_map/ppermute | solution.py:232
  5.7 3.6 %collective-permute-start.4 = (bf16[2,144,128]{2,1,0:T(8,128)(2,1)S(1)}, bf16[2,144,128]{2,1,0:T(8,128)(2,1)S(1)}, u32[]{:S(2)}, u32[]{:S(2)}) collective-permute-start(bf16[2,144,128]{2,1,0:T(8,128)(2,1)S(1)} %get-tuple-element.16), channel_id=1, source_target_pairs={{0,12},{1,4},{2,8},{3,0},{4,9},{5,13},{6,5},{7,1},{8,10},{9,2},{10... | collective-permute-start | bytes 221192 | tf_op jit(solution)/shard_map/ppermute | solution.py:235
  9.3 0.0 collective-permute-start.3
  9.3 0.0 collective-permute-done.2.refs_1_
  9.3 2.0 %collective-permute-done.4.refs_3_ = bf16[2,144,128]{2,1,0:T(8,128)(2,1)S(1)} collective-permute-done((bf16[2,144,128]{2,1,0:T(8,128)(2,1)S(1)}, bf16[2,144,128]{2,1,0:T(8,128)(2,1)S(1)}, u32[]{:S(2)}, u32[]{:S(2)}) %collective-permute-start.4) | collective-permute-done | bytes 73760 | tf_op jit(solution)/shard_map/ppermute | solution.py:235
  11.3 0.7 %collective-permute-done.3.refs_2_ = bf16[2,144,128]{2,1,0:T(8,128)(2,1)S(1)} collective-permute-done((bf16[2,144,128]{2,1,0:T(8,128)(2,1)S(1)}, bf16[2,144,128]{2,1,0:T(8,128)(2,1)S(1)}, u32[]{:S(2)}, u32[]{:S(2)}) %collective-permute-start.3) | collective-permute-done | bytes 73760 | tf_op jit(solution)/shard_map/ppermute | solution.py:235
  12.0 0.0 copy-done
  12.0 0.0 copy-done.1
  12.0 2.1 %pair.1 = bf16[16,16,128]{2,1,0:T(8,128)(2,1)} custom-call(bf16[2,144,128]{2,1,0:T(8,128)(2,1)S(1)} %get-tuple-element.15.refs_0_, bf16[2,144,128]{2,1,0:T(8,128)(2,1)S(1)} %collective-permute-done.2.refs_1_, bf16[2,144,128]{2,1,0:T(8,128)(2,1)S(1)} %collective-permute-done.3.refs_2_, bf16[2,144,128]{2,1,0:T(8,128)(2,1)S(1)} %collective-permute-done.4.refs_3_, ...), custom_call_target="tpu_custom_call" | custom-call | tf_op jit(solution)/shard_map/pair/pallas_call | solution.py:238
Async XLA Ops:
  0.0 2.1 %collective-permute-start = (bf16[32,16,256]{2,1,0:T(8,128)(2,1)}, bf16[32,16,256]{2,1,0:T(8,128)(2,1)S(1)}, u32[]{:S(2)}, u32[]{:S(2)}) collective-permute-start(bf16[32,16,256]{2,1,0:T(8,128)(2,1)} %x_hbm.1), channel_id=1, source_target_pairs={{0,1},{1,0},{2,3},{3,2},{4,5},{5,4},{6,7},{7,6},{8,9},{9,8},{10,11... | collective-permute-start | bytes 786440 | tf_op jit(solution)/shard_map/ppermute | solution.py:199
  0.5 1.7 %collective-permute-start.1 = (s32[16,32]{1,0:T(8,128)}, s32[16,32]{1,0:T(8,128)S(1)}, u32[]{:S(2)}, u32[]{:S(2)}) collective-permute-start(s32[16,32]{1,0:T(8,128)} %bitcast.5), channel_id=1, source_target_pairs={{0,1},{1,0},{2,3},{3,2},{4,5},{5,4},{6,7},{7,6},{8,9},{9,8},{10,11... | collective-permute-start | bytes 6152 | tf_op jit(solution)/shard_map/ppermute | solution.py:199
  2.1 9.9 %copy-start = (bf16[1024,128]{1,0:T(8,128)(2,1)S(1)}, bf16[1024,128]{1,0:T(8,128)(2,1)}, u32[]{:S(2)}) copy-start(bf16[1024,128]{1,0:T(8,128)(2,1)} %refs_4_.1) | copy-start | bytes 786436
  2.7 9.3 %copy-start.1 = (f32[128]{0:T(128)S(1)}, f32[128]{0:T(128)}, u32[]{:S(2)}) copy-start(f32[128]{0:T(128)} %refs_5_.1) | copy-start | bytes 1540
  2.7 6.6 %collective-permute-start.2 = (bf16[2,144,128]{2,1,0:T(8,128)(2,1)S(1)}, bf16[2,144,128]{2,1,0:T(8,128)(2,1)S(1)}, u32[]{:S(2)}, u32[]{:S(2)}) collective-permute-start(bf16[2,144,128]{2,1,0:T(8,128)(2,1)S(1)} %get-tuple-element.15.refs_0_), channel_id=1, source_target_pairs={{0,2},{1,3},{2,0},{3,1},{4,6},{5,7},{6,4},{7,5},{8,10},{9,11},{10,... | collective-permute-start | bytes 221192 | tf_op jit(solution)/shard_map/ppermute | solution.py:232
  5.7 5.6 %collective-permute-start.4 = (bf16[2,144,128]{2,1,0:T(8,128)(2,1)S(1)}, bf16[2,144,128]{2,1,0:T(8,128)(2,1)S(1)}, u32[]{:S(2)}, u32[]{:S(2)}) collective-permute-start(bf16[2,144,128]{2,1,0:T(8,128)(2,1)S(1)} %get-tuple-element.16), channel_id=1, source_target_pairs={{0,12},{1,4},{2,8},{3,0},{4,9},{5,13},{6,5},{7,1},{8,10},{9,2},{10... | collective-permute-start | bytes 221192 | tf_op jit(solution)/shard_map/ppermute | solution.py:235
  9.3 2.7 %collective-permute-start.3 = (bf16[2,144,128]{2,1,0:T(8,128)(2,1)S(1)}, bf16[2,144,128]{2,1,0:T(8,128)(2,1)S(1)}, u32[]{:S(2)}, u32[]{:S(2)}) collective-permute-start(bf16[2,144,128]{2,1,0:T(8,128)(2,1)S(1)} %get-tuple-element.16), channel_id=1, source_target_pairs={{0,8},{1,0},{2,12},{3,4},{4,5},{5,1},{6,9},{7,13},{8,6},{9,14},{10... | collective-permute-start | bytes 221192 | tf_op jit(solution)/shard_map/ppermute | solution.py:235

commit v8 on v7

--- a/solution.py
+++ b/solution.py
@@ -133,8 +133,9 @@
 def pair_kernel(steps, seqs, rows, columns, width, *refs):
     n = len(steps)
     lefts, rights = refs[:n], refs[n:2 * n]
-    w_ref, bias_ref, out_ref, left_ref, right_ref, outer_ref, flat_ref, raw_ref = refs[2 * n:]
+    w_ref, bias_ref, out_ref, left_ref, right_ref, turned_ref, flat_ref, raw_ref = refs[2 * n:]
     fold = LANES // width
+    assert fold == 4
     data = rows * width // LANES * seqs
 
     me_res, me_seq = lax.axis_index("res"), lax.axis_index("seq")
@@ -147,41 +148,46 @@
                         pieces[k][core, tile * seqs:(tile + 1) * seqs, :]
                     )
 
-    outer = dot(left_ref[...], right_ref[...], TN)
-    for tile in range(columns // fold):
-        outer_ref[tile] = outer[:, tile * LANES:(tile + 1) * LANES]
-
-    place = iota((rows, LANES), 1) // width
+    for tile in range(turned_ref.shape[0]):
+        turned_ref[tile] = left_ref[tile * LANES:(tile + 1) * LANES, :].astype(F32).T
+    turned = jnp.concatenate(
+        [
+            jnp.concatenate(
+                [turned_ref[tile, pl.ds(c, rows, stride=width), :].astype(BF16) for c in range(width)], axis=0
+            )
+            for tile in range(turned_ref.shape[0])
+        ],
+        axis=1,
+    )
+    outer = dot(turned, right_ref[...]).astype(BF16)
+
+    place = (iota((rows, LANES), 1) // width).astype(BF16)
+    even = [None] * fold
+    even[1] = (place == 0.0) | (place == 2.0)
+    even[2] = (place == 0.0) | (place == 1.0)
     for tile in range(columns // fold):
         for quad in range(width // fold):
             part = [
-                outer_ref[tile, pl.ds(quad * fold + k, rows, stride=width), :]
+                outer[(quad * fold + k) * rows:(quad * fold + k + 1) * rows, tile * LANES:(tile + 1) * LANES]
                 for k in range(fold)
             ]
-            step = fold // 2
-            while step:
-                keep = (place // step) % 2 == 0
+            for step in (2, 1):
                 new = list(part)
                 for k in range(fold):
-                    if (k // step) % 2 == 0:
-                        a, b = part[k], part[k + step]
-                        new[k] = jnp.where(keep, a, pltpu.roll(b, step * width, 1))
-                        new[k + step] = jnp.where(keep, pltpu.roll(a, LANES - step * width, 1), b)
+                    if k & step == 0:
+                        x, y = part[k], part[k + step]
+                        new[k] = jnp.where(even[step], x, pltpu.roll(y, step * width, 1))
+                        new[k + step] = jnp.where(even[step], pltpu.roll(x, LANES - step * width, 1), y)
                 part = new
-                step //= 2
             for k in range(fold):
                 j = tile * fold + k
-                flat_ref[j * rows:(j + 1) * rows, quad * LANES:(quad + 1) * LANES] = part[k].astype(BF16)
+                flat_ref[j * rows:(j + 1) * rows, quad * LANES:(quad + 1) * LANES] = part[k]
 
     raw = dot(flat_ref[...], w_ref[...]) + bias_ref[...].reshape(1, -1)
-
-    pair = rows * columns
-    row = iota((pair, rows), 0)
-    live_left = dot((row % rows == iota((pair, rows), 1)).astype(BF16), whole_mask(lefts, rows, data))
-    row = iota((pair, columns), 0)
-    live_right = dot((row // rows == iota((pair, columns), 1)).astype(BF16), whole_mask(rights, rows, data))
-    count = jnp.sum(live_left * live_right, axis=1, keepdims=True)
-    raw_ref[...] = raw / (1.0 + count)
+    count = dot(whole_mask(lefts, rows, data), whole_mask(rights, rows, data), NT)
+    scale = 1.0 / (1.0 + count)
+    for j in range(columns):
+        raw_ref[j * rows:(j + 1) * rows, :] = raw[j * rows:(j + 1) * rows, :] * scale[:, j:j + 1]
     for i in range(rows):
         out_ref[i] = raw_ref[pl.ds(i, columns, stride=rows), :].astype(BF16)
 
@@ -241,7 +247,7 @@
         scratch_shapes=[
             pltpu.VMEM((n * seqs, lanes), BF16),
             pltpu.VMEM((n * seqs, lanes), BF16),
-            pltpu.VMEM((lanes // LANES, lanes, LANES), F32),
+            pltpu.VMEM((n * seqs // LANES, lanes, LANES), F32),
             pltpu.VMEM((rows * rows, width * width), BF16),
             pltpu.VMEM((rows * rows, outs), F32),
         ],

time: 14.3 us -> 13.8 us (0.965)
  Pallas kernels: 4.25 us -> 3.7 us
    pallas_call x1, Pallas kernels: 2.14 us -> 1.59 us  [local(): pl.pallas_call(functools.partial(pair_kernel, steps, seqs, rows, rows, wi...]
  transfers between devices with their start and end apart: 5 -> 5, of which waited for: 2 -> 2; matrix products, arithmetic and copies ran while one was open for 0% -> 0% of each run, Pallas kernels for 11% -> 12%
where the time goes in v8:
time: 13.8 us; the launch traced here: 13.6 us
  starting transfers between devices  7.12 us (52%)
  Pallas kernels  3.7 us (27%)
  waiting for transfers between devices  2.68 us (19%)
    ppermute x2, starting transfers between devices, local(): lax.ppermute(right, axes, [(a * n + p, step[a][p] * n + a) for a in range...  3.6 us
    ppermute x1, starting transfers between devices, local(): lax.ppermute(left, 'seq', [(p, p ^ k * CORES) for p in range(n)])  3 us
    ppermute x2, waiting for transfers between devices, local(): lax.ppermute(right, axes, [(a * n + p, step[a][p] * n + a) for a in range...  2.67 us
    pallas_call x1, Pallas kernels, local(): pl.pallas_call(functools.partial(pair_kernel, steps, seqs, rows, rows, wi...  1.59 us
    pallas_call x1, Pallas kernels, local(): pl.pallas_call(own_kernel, out_shape=(wire, wire, jax.ShapeDtypeStruct((2...  1.59 us
    pallas_call x1, Pallas kernels, local(): pl.pallas_call(functools.partial(both_kernel, width), out_shape=(wire, wi...  0.53 us
    ppermute x1, starting transfers between devices, local(): lax.ppermute(x, 'seq', swap)  0.45 us
  transfers between devices with their start and end apart: 5, of which 2 were waited for; matrix products, arithmetic and copies ran while one was open for 0% of the time, Pallas kernels for 12%

profile of v8, /device:TPU:0, one launch (start us, length us, event | category | flops | bytes accessed | tf_op | source)
XLA Modules:
  0.0 13.6 jit_solution(453204515700414744)
XLA Ops:
  0.0 0.5 %collective-permute-start = (bf16[32,16,256]{2,1,0:T(8,128)(2,1)}, bf16[32,16,256]{2,1,0:T(8,128)(2,1)S(1)}, u32[]{:S(2)}, u32[]{:S(2)}) collective-permute-start(bf16[32,16,256]{2,1,0:T(8,128)(2,1)} %x_hbm.1), channel_id=1, source_target_pairs={{0,1},{1,0},{2,3},{3,2},{4,5},{5,4},{6,7},{7,6},{8,9},{9,8},{10,11... | collective-permute-start | bytes 786440 | tf_op jit(solution)/shard_map/ppermute | solution.py:205
  0.5 0.1 collective-permute-start.1
  0.5 1.6 %project_own.1 = (bf16[144,128]{1,0:T(8,128)(2,1)S(1)}, bf16[144,128]{1,0:T(8,128)(2,1)S(1)}, bf16[256,256]{1,0:T(8,128)(2,1)S(1)}, f32[8,256]{1,0:T(8,128)S(1)}) custom-call(bf16[32,16,256]{2,1,0:T(8,128)(2,1)} %x_hbm.1, s32[16,32]{1,0:T(8,128)} %bitcast.6, f32[256]{0:T(256)} %scale_hbm.1, f32[256]{0:T(256)} %shift_hbm.1, bf16[32,256]{1,0:T(8,128)(2,1)} %bitcast.3, ...), custom_call_target="tpu_custom_call" | custom-call | flops 33554432 | bytes 1048576 | tf_op jit(solution)/shard_map/project_own/pallas_call | solution.py:211
  2.1 0.0 copy-start
  2.1 0.0 collective-permute-done.1.flag_ref
  2.1 0.0 collective-permute-done.x_ref
  2.1 0.5 %project_other.1 = (bf16[2,144,128]{2,1,0:T(8,128)(2,1)S(1)}, bf16[2,144,128]{2,1,0:T(8,128)(2,1)S(1)}) custom-call(bf16[32,16,256]{2,1,0:T(8,128)(2,1)S(1)} %collective-permute-done.x_ref, s32[16,32]{1,0:T(8,128)S(1)} %collective-permute-done.1.flag_ref, bf16[256,256]{1,0:T(8,128)(2,1)S(1)} %get-tuple-element.11.weight_ref, ...), custom_call_target="tpu_custom_call" | custom-call | tf_op jit(solution)/shard_map/project_other/pallas_call | solution.py:228
  2.7 0.0 copy-start.1
  2.7 3.0 %collective-permute-start.2 = (bf16[2,144,128]{2,1,0:T(8,128)(2,1)S(1)}, bf16[2,144,128]{2,1,0:T(8,128)(2,1)S(1)}, u32[]{:S(2)}, u32[]{:S(2)}) collective-permute-start(bf16[2,144,128]{2,1,0:T(8,128)(2,1)S(1)} %get-tuple-element.15.refs_0_), channel_id=1, source_target_pairs={{0,2},{1,3},{2,0},{3,1},{4,6},{5,7},{6,4},{7,5},{8,10},{9,11},{10,... | collective-permute-start | bytes 221192 | tf_op jit(solution)/shard_map/ppermute | solution.py:238
  5.7 3.6 %collective-permute-start.4 = (bf16[2,144,128]{2,1,0:T(8,128)(2,1)S(1)}, bf16[2,144,128]{2,1,0:T(8,128)(2,1)S(1)}, u32[]{:S(2)}, u32[]{:S(2)}) collective-permute-start(bf16[2,144,128]{2,1,0:T(8,128)(2,1)S(1)} %get-tuple-element.16), channel_id=1, source_target_pairs={{0,12},{1,4},{2,8},{3,0},{4,9},{5,13},{6,5},{7,1},{8,10},{9,2},{10... | collective-permute-start | bytes 221192 | tf_op jit(solution)/shard_map/ppermute | solution.py:241
  9.3 0.0 collective-permute-start.3
  9.3 0.0 collective-permute-done.2.refs_1_
  9.3 2.0 %collective-permute-done.4.refs_3_ = bf16[2,144,128]{2,1,0:T(8,128)(2,1)S(1)} collective-permute-done((bf16[2,144,128]{2,1,0:T(8,128)(2,1)S(1)}, bf16[2,144,128]{2,1,0:T(8,128)(2,1)S(1)}, u32[]{:S(2)}, u32[]{:S(2)}) %collective-permute-start.4) | collective-permute-done | bytes 73760 | tf_op jit(solution)/shard_map/ppermute | solution.py:241
  11.3 0.7 %collective-permute-done.3.refs_2_ = bf16[2,144,128]{2,1,0:T(8,128)(2,1)S(1)} collective-permute-done((bf16[2,144,128]{2,1,0:T(8,128)(2,1)S(1)}, bf16[2,144,128]{2,1,0:T(8,128)(2,1)S(1)}, u32[]{:S(2)}, u32[]{:S(2)}) %collective-permute-start.3) | collective-permute-done | bytes 73760 | tf_op jit(solution)/shard_map/ppermute | solution.py:241
  12.0 0.0 copy-done
  12.0 0.0 copy-done.1
  12.0 1.6 %pair.1 = bf16[16,16,128]{2,1,0:T(8,128)(2,1)} custom-call(bf16[2,144,128]{2,1,0:T(8,128)(2,1)S(1)} %get-tuple-element.15.refs_0_, bf16[2,144,128]{2,1,0:T(8,128)(2,1)S(1)} %collective-permute-done.2.refs_1_, bf16[2,144,128]{2,1,0:T(8,128)(2,1)S(1)} %collective-permute-done.3.refs_2_, bf16[2,144,128]{2,1,0:T(8,128)(2,1)S(1)} %collective-permute-done.4.refs_3_, ...), custom_call_target="tpu_custom_call" | custom-call | tf_op jit(solution)/shard_map/pair/pallas_call | solution.py:244
Async XLA Ops:
  0.0 2.1 %collective-permute-start = (bf16[32,16,256]{2,1,0:T(8,128)(2,1)}, bf16[32,16,256]{2,1,0:T(8,128)(2,1)S(1)}, u32[]{:S(2)}, u32[]{:S(2)}) collective-permute-start(bf16[32,16,256]{2,1,0:T(8,128)(2,1)} %x_hbm.1), channel_id=1, source_target_pairs={{0,1},{1,0},{2,3},{3,2},{4,5},{5,4},{6,7},{7,6},{8,9},{9,8},{10,11... | collective-permute-start | bytes 786440 | tf_op jit(solution)/shard_map/ppermute | solution.py:205
  0.5 1.7 %collective-permute-start.1 = (s32[16,32]{1,0:T(8,128)}, s32[16,32]{1,0:T(8,128)S(1)}, u32[]{:S(2)}, u32[]{:S(2)}) collective-permute-start(s32[16,32]{1,0:T(8,128)} %bitcast.5), channel_id=1, source_target_pairs={{0,1},{1,0},{2,3},{3,2},{4,5},{5,4},{6,7},{7,6},{8,9},{9,8},{10,11... | collective-permute-start | bytes 6152 | tf_op jit(solution)/shard_map/ppermute | solution.py:205
  2.1 9.9 %copy-start = (bf16[1024,128]{1,0:T(8,128)(2,1)S(1)}, bf16[1024,128]{1,0:T(8,128)(2,1)}, u32[]{:S(2)}) copy-start(bf16[1024,128]{1,0:T(8,128)(2,1)} %refs_4_.1) | copy-start | bytes 786436
  2.7 9.3 %copy-start.1 = (f32[128]{0:T(128)S(1)}, f32[128]{0:T(128)}, u32[]{:S(2)}) copy-start(f32[128]{0:T(128)} %refs_5_.1) | copy-start | bytes 1540
  2.7 6.6 %collective-permute-start.2 = (bf16[2,144,128]{2,1,0:T(8,128)(2,1)S(1)}, bf16[2,144,128]{2,1,0:T(8,128)(2,1)S(1)}, u32[]{:S(2)}, u32[]{:S(2)}) collective-permute-start(bf16[2,144,128]{2,1,0:T(8,128)(2,1)S(1)} %get-tuple-element.15.refs_0_), channel_id=1, source_target_pairs={{0,2},{1,3},{2,0},{3,1},{4,6},{5,7},{6,4},{7,5},{8,10},{9,11},{10,... | collective-permute-start | bytes 221192 | tf_op jit(solution)/shard_map/ppermute | solution.py:238
  5.7 5.6 %collective-permute-start.4 = (bf16[2,144,128]{2,1,0:T(8,128)(2,1)S(1)}, bf16[2,144,128]{2,1,0:T(8,128)(2,1)S(1)}, u32[]{:S(2)}, u32[]{:S(2)}) collective-permute-start(bf16[2,144,128]{2,1,0:T(8,128)(2,1)S(1)} %get-tuple-element.16), channel_id=1, source_target_pairs={{0,12},{1,4},{2,8},{3,0},{4,9},{5,13},{6,5},{7,1},{8,10},{9,2},{10... | collective-permute-start | bytes 221192 | tf_op jit(solution)/shard_map/ppermute | solution.py:241
  9.3 2.7 %collective-permute-start.3 = (bf16[2,144,128]{2,1,0:T(8,128)(2,1)S(1)}, bf16[2,144,128]{2,1,0:T(8,128)(2,1)S(1)}, u32[]{:S(2)}, u32[]{:S(2)}) collective-permute-start(bf16[2,144,128]{2,1,0:T(8,128)(2,1)S(1)} %get-tuple-element.16), channel_id=1, source_target_pairs={{0,8},{1,0},{2,12},{3,4},{4,5},{5,1},{6,9},{7,13},{8,6},{9,14},{10... | collective-permute-start | bytes 221192 | tf_op jit(solution)/shard_map/ppermute | solution.py:241

commit v9 on v8

--- a/solution.py
+++ b/solution.py
@@ -81,14 +81,14 @@
             out_ref[data + tile * rows:data + (tile + 1) * rows, :] = mine.astype(BF16)
 
 
-def own_kernel(x_hbm, flag_hbm, scale_hbm, shift_hbm, wl_hbm, bl_hbm, wr_hbm, br_hbm,
+def own_kernel(x_hbm, flag_hbm, scale_hbm, shift_hbm, wl_hbm, bl_hbm, wr_hbm, br_hbm, last_hbm,
                left_ref, right_ref, weight_ref, vector_ref,
-               x_ref, flag_ref, scale_ref, shift_ref, wl_ref, bl_ref, wr_ref, br_ref, proj_ref, sems):
+               x_ref, flag_ref, scale_ref, shift_ref, wl_ref, bl_ref, wr_ref, br_ref, last_ref, proj_ref, sems):
     copies = [
         pltpu.make_async_copy(src, dst, sems.at[k])
         for k, (src, dst) in enumerate((
             (x_hbm, x_ref), (flag_hbm, flag_ref), (scale_hbm, scale_ref), (shift_hbm, shift_ref),
-            (wl_hbm, wl_ref), (bl_hbm, bl_ref), (wr_hbm, wr_ref), (br_hbm, br_ref),
+            (wl_hbm, wl_ref), (bl_hbm, bl_ref), (wr_hbm, wr_ref), (br_hbm, br_ref), (last_hbm, last_ref),
         ))
     ]
     for copy in copies:
@@ -104,7 +104,8 @@
             scale_ref[...].reshape(1, depth),
             shift_ref[...].reshape(1, depth),
             jnp.concatenate(bias, axis=1),
-            jnp.zeros((5, depth), F32),
+            jnp.concatenate([last_ref[...].reshape(1, LANES)] * (depth // LANES), axis=1),
+            jnp.zeros((4, depth), F32),
         ],
         axis=0,
     )
@@ -130,36 +131,41 @@
     return jnp.concatenate([total[k:k + rows] for k in range(0, total.shape[0], rows)], axis=1)
 
 
+def gather_factor(pieces, chips, seqs, data, whole_ref):
+    for piece, chip in zip(pieces, chips):
+        for core in range(CORES):
+            at = pl.multiple_of((chip * CORES + core) * seqs, seqs)
+            for tile in range(data // seqs):
+                whole_ref[pl.ds(at, seqs), tile * LANES:(tile + 1) * LANES] = (
+                    piece[core, tile * seqs:(tile + 1) * seqs, :]
+                )
+
+
+def left_kernel(seqs, rows, width, *refs):
+    lefts, (out_ref, mask_ref, left_ref, turned_ref) = refs[:-4], refs[-4:]
+    data = rows * width // LANES * seqs
+    me = lax.axis_index("seq") // CORES
+    gather_factor(lefts, [me ^ k for k in range(len(lefts))], seqs, data, left_ref)
+    mask_ref[...] = whole_mask(lefts, rows, data)
+    for tile in range(turned_ref.shape[0]):
+        turned_ref[tile] = left_ref[tile * LANES:(tile + 1) * LANES, :].astype(F32).T
+        for c in range(width):
+            out_ref[c * rows:(c + 1) * rows, tile * LANES:(tile + 1) * LANES] = (
+                turned_ref[tile, pl.ds(c, rows, stride=width), :].astype(BF16)
+            )
+
+
 def pair_kernel(steps, seqs, rows, columns, width, *refs):
     n = len(steps)
-    lefts, rights = refs[:n], refs[n:2 * n]
-    w_ref, bias_ref, out_ref, left_ref, right_ref, turned_ref, flat_ref, raw_ref = refs[2 * n:]
+    rights = refs[:n]
+    turned_ref, live_ref, w_ref, vector_ref, out_ref, right_ref, flat_ref, raw_ref = refs[n:]
     fold = LANES // width
     assert fold == 4
     data = rows * width // LANES * seqs
 
     me_res, me_seq = lax.axis_index("res"), lax.axis_index("seq")
-    for k in range(n):
-        for pieces, chip, whole_ref in ((lefts, me_seq // CORES ^ k, left_ref), (rights, sending_chip(steps[k], me_res, me_seq), right_ref)):
-            for core in range(CORES):
-                at = pl.multiple_of((chip * CORES + core) * seqs, seqs)
-                for tile in range(data // seqs):
-                    whole_ref[pl.ds(at, seqs), tile * LANES:(tile + 1) * LANES] = (
-                        pieces[k][core, tile * seqs:(tile + 1) * seqs, :]
-                    )
-
-    for tile in range(turned_ref.shape[0]):
-        turned_ref[tile] = left_ref[tile * LANES:(tile + 1) * LANES, :].astype(F32).T
-    turned = jnp.concatenate(
-        [
-            jnp.concatenate(
-                [turned_ref[tile, pl.ds(c, rows, stride=width), :].astype(BF16) for c in range(width)], axis=0
-            )
-            for tile in range(turned_ref.shape[0])
-        ],
-        axis=1,
-    )
-    outer = dot(turned, right_ref[...]).astype(BF16)
+    gather_factor(rights, [sending_chip(step, me_res, me_seq) for step in steps], seqs, data, right_ref)
+    outer = dot(turned_ref[...], right_ref[...]).astype(BF16)
 
     place = (iota((rows, LANES), 1) // width).astype(BF16)
     even = [None] * fold
@@ -183,8 +189,8 @@
                 j = tile * fold + k
                 flat_ref[j * rows:(j + 1) * rows, quad * LANES:(quad + 1) * LANES] = part[k]
 
-    raw = dot(flat_ref[...], w_ref[...]) + bias_ref[...].reshape(1, -1)
-    count = dot(whole_mask(lefts, rows, data), whole_mask(rights, rows, data), NT)
+    raw = dot(flat_ref[...], w_ref[...]) + vector_ref[3:4, :LANES]
+    count = dot(live_ref[...], whole_mask(rights, rows, data), NT)
     scale = 1.0 / (1.0 + count)
     for j in range(columns):
         raw_ref[j * rows:(j + 1) * rows, :] = raw[j * rows:(j + 1) * rows, :] * scale[:, j:j + 1]
@@ -205,7 +211,7 @@
     other_x, other_flags = lax.ppermute(x, "seq", swap), lax.ppermute(flags, "seq", swap)
 
     operands = [
-        pltpu.with_memory_space_constraint(o, pltpu.HBM) for o in (x, flags, scale, shift, wl.T, bl, wr.T, br)
+        pltpu.with_memory_space_constraint(o, pltpu.HBM) for o in (x, flags, scale, shift, wl.T, bl, wr.T, br, bias)
     ]
     wire = jax.ShapeDtypeStruct((size, LANES), BF16)
     left, right, weight, vectors = pl.pallas_call(
@@ -241,19 +247,27 @@
         lax.ppermute(right, axes, [(a * n + p, step[a][p] * n + a) for a in range(n) for p in range(n)])
         for step in steps
     ]
+    turned, live = pl.pallas_call(
+        functools.partial(left_kernel, seqs, rows, width),
+        out_shape=(jax.ShapeDtypeStruct((lanes, n * seqs), BF16), jax.ShapeDtypeStruct((rows, n * seqs), BF16)),
+        scratch_shapes=[
+            pltpu.VMEM((n * seqs, lanes), BF16),
+            pltpu.VMEM((n * seqs // LANES, lanes, LANES), F32),
+        ],
+        compiler_params=pltpu.CompilerParams(vmem_limit_bytes=16 << 20),
+        name="turn_left",
+    )(*lefts)
     return pl.pallas_call(
         functools.partial(pair_kernel, steps, seqs, rows, rows, width),
         out_shape=jax.ShapeDtypeStruct((rows, rows, outs), BF16),
         scratch_shapes=[
             pltpu.VMEM((n * seqs, lanes), BF16),
-            pltpu.VMEM((n * seqs, lanes), BF16),
-            pltpu.VMEM((n * seqs // LANES, lanes, LANES), F32),
             pltpu.VMEM((rows * rows, width * width), BF16),
             pltpu.VMEM((rows * rows, outs), F32),
         ],
-        compiler_params=pltpu.CompilerParams(vmem_limit_bytes=24 << 20),
+        compiler_params=pltpu.CompilerParams(vmem_limit_bytes=16 << 20),
         name="pair",
-    )(*lefts, *rights, w, bias)
+    )(*rights, turned, live, w, vectors)
 
 
 def solution(mesh):

time: 13.8 us -> 13.7 us (level)
  waiting for transfers between devices: 2.68 us -> 2.39 us
  Pallas kernels: 3.7 us -> 3.86 us
    ppermute x2, waiting for transfers between devices: 2.67 us -> 2.38 us  [local(): lax.ppermute(right, axes, [(a * n + p, step[a][p] * n + a) for a in range...]
    pallas_call x0 -> x1, Pallas kernels: none -> 0.28 us  [local(): pl.pallas_call(functools.partial(left_kernel, seqs, rows, width), out_sha...]
  transfers between devices with their start and end apart: 5 -> 5, of which waited for: 2 -> 2; matrix products, arithmetic and copies ran while one was open for 0% -> 0% of each run, Pallas kernels for 12% -> 14%
where the time goes in v9:
time: 13.7 us; the launch traced here: 13.4 us
  starting transfers between devices  7.12 us (52%)
  Pallas kernels  3.86 us (28%)
  waiting for transfers between devices  2.39 us (17%)
    ppermute x2, starting transfers between devices, local(): lax.ppermute(right, axes, [(a * n + p, step[a][p] * n + a) for a in range...  3.6 us
    ppermute x1, starting transfers between devices, local(): lax.ppermute(left, 'seq', [(p, p ^ k * CORES) for p in range(n)])  3 us
    ppermute x2, waiting for transfers between devices, local(): lax.ppermute(right, axes, [(a * n + p, step[a][p] * n + a) for a in range...  2.38 us
    pallas_call x1, Pallas kernels, local(): pl.pallas_call(own_kernel, out_shape=(wire, wire, jax.ShapeDtypeStruct((2...  1.58 us
    pallas_call x1, Pallas kernels, local(): pl.pallas_call(functools.partial(pair_kernel, steps, seqs, rows, rows, wi...  1.47 us
    pallas_call x1, Pallas kernels, local(): pl.pallas_call(functools.partial(both_kernel, width), out_shape=(wire, wi...  0.53 us
    ppermute x1, starting transfers between devices, local(): lax.ppermute(x, 'seq', swap)  0.45 us
    pallas_call x1, Pallas kernels, local(): pl.pallas_call(functools.partial(left_kernel, seqs, rows, width), out_sha...  0.28 us
  transfers between devices with their start and end apart: 5, of which 2 were waited for; matrix products, arithmetic and copies ran while one was open for 0% of the time, Pallas kernels for 14%

profile of v9, /device:TPU:0, one launch (start us, length us, event | category | flops | bytes accessed | tf_op | source)
XLA Modules:
  0.0 13.4 jit_solution(5799463997031380516)
XLA Ops:
  0.0 0.5 %collective-permute-start = (bf16[32,16,256]{2,1,0:T(8,128)(2,1)}, bf16[32,16,256]{2,1,0:T(8,128)(2,1)S(1)}, u32[]{:S(2)}, u32[]{:S(2)}) collective-permute-start(bf16[32,16,256]{2,1,0:T(8,128)(2,1)} %x_hbm.1), channel_id=1, source_target_pairs={{0,1},{1,0},{2,3},{3,2},{4,5},{5,4},{6,7},{7,6},{8,9},{9,8},{10,11... | collective-permute-start | bytes 786440 | tf_op jit(solution)/shard_map/ppermute | solution.py:211
  0.5 0.1 collective-permute-start.1
  0.5 1.6 %project_own.1 = (bf16[144,128]{1,0:T(8,128)(2,1)S(1)}, bf16[144,128]{1,0:T(8,128)(2,1)S(1)}, bf16[256,256]{1,0:T(8,128)(2,1)S(1)}, f32[8,256]{1,0:T(8,128)S(1)}) custom-call(bf16[32,16,256]{2,1,0:T(8,128)(2,1)} %x_hbm.1, s32[16,32]{1,0:T(8,128)} %bitcast.6, f32[256]{0:T(256)} %scale_hbm.1, f32[256]{0:T(256)} %shift_hbm.1, bf16[32,256]{1,0:T(8,128)(2,1)} %bitcast.3, ...), custom_call_target="tpu_custom_call" | custom-call | flops 33554432 | bytes 1048576 | tf_op jit(solution)/shard_map/project_own/pallas_call | solution.py:217
  2.1 0.0 collective-permute-done.1.flag_ref
  2.1 0.0 collective-permute-done.x_ref
  2.1 0.0 copy-start
  2.1 0.5 %project_other.1 = (bf16[2,144,128]{2,1,0:T(8,128)(2,1)S(1)}, bf16[2,144,128]{2,1,0:T(8,128)(2,1)S(1)}) custom-call(bf16[32,16,256]{2,1,0:T(8,128)(2,1)S(1)} %collective-permute-done.x_ref, s32[16,32]{1,0:T(8,128)S(1)} %collective-permute-done.1.flag_ref, bf16[256,256]{1,0:T(8,128)(2,1)S(1)} %get-tuple-element.13.weight_ref, ...), custom_call_target="tpu_custom_call" | custom-call | tf_op jit(solution)/shard_map/project_other/pallas_call | solution.py:234
  2.7 3.0 %collective-permute-start.4 = (bf16[2,144,128]{2,1,0:T(8,128)(2,1)S(1)}, bf16[2,144,128]{2,1,0:T(8,128)(2,1)S(1)}, u32[]{:S(2)}, u32[]{:S(2)}) collective-permute-start(bf16[2,144,128]{2,1,0:T(8,128)(2,1)S(1)} %get-tuple-element.18.refs_0_), channel_id=1, source_target_pairs={{0,2},{1,3},{2,0},{3,1},{4,6},{5,7},{6,4},{7,5},{8,10},{9,11},{10,... | collective-permute-start | bytes 221192 | tf_op jit(solution)/shard_map/ppermute | solution.py:244
  5.7 3.6 %collective-permute-start.3 = (bf16[2,144,128]{2,1,0:T(8,128)(2,1)S(1)}, bf16[2,144,128]{2,1,0:T(8,128)(2,1)S(1)}, u32[]{:S(2)}, u32[]{:S(2)}) collective-permute-start(bf16[2,144,128]{2,1,0:T(8,128)(2,1)S(1)} %get-tuple-element.17), channel_id=1, source_target_pairs={{0,12},{1,4},{2,8},{3,0},{4,9},{5,13},{6,5},{7,1},{8,10},{9,2},{10... | collective-permute-start | bytes 221192 | tf_op jit(solution)/shard_map/ppermute | solution.py:247
  9.3 0.0 collective-permute-start.2
  9.3 0.0 collective-permute-done.4.refs_1_
  9.3 0.3 %turn_left.1 = (bf16[512,128]{1,0:T(8,128)(2,1)S(1)}, bf16[16,128]{1,0:T(8,128)(2,1)S(1)}) custom-call(bf16[2,144,128]{2,1,0:T(8,128)(2,1)S(1)} %get-tuple-element.18.refs_0_, bf16[2,144,128]{2,1,0:T(8,128)(2,1)S(1)} %collective-permute-done.4.refs_1_), custom_call_target="tpu_custom_call" | custom-call | tf_op jit(solution)/shard_map/turn_left/pallas_call | solution.py:250
  9.6 1.7 %collective-permute-done.3.refs_1_ = bf16[2,144,128]{2,1,0:T(8,128)(2,1)S(1)} collective-permute-done((bf16[2,144,128]{2,1,0:T(8,128)(2,1)S(1)}, bf16[2,144,128]{2,1,0:T(8,128)(2,1)S(1)}, u32[]{:S(2)}, u32[]{:S(2)}) %collective-permute-start.3) | collective-permute-done | bytes 73760 | tf_op jit(solution)/shard_map/ppermute | solution.py:247
  11.3 0.7 %collective-permute-done.2.refs_0_ = bf16[2,144,128]{2,1,0:T(8,128)(2,1)S(1)} collective-permute-done((bf16[2,144,128]{2,1,0:T(8,128)(2,1)S(1)}, bf16[2,144,128]{2,1,0:T(8,128)(2,1)S(1)}, u32[]{:S(2)}, u32[]{:S(2)}) %collective-permute-start.2) | collective-permute-done | bytes 73760 | tf_op jit(solution)/shard_map/ppermute | solution.py:247
  12.0 0.0 copy-done
  12.0 1.5 %pair.1 = bf16[16,16,128]{2,1,0:T(8,128)(2,1)} custom-call(bf16[2,144,128]{2,1,0:T(8,128)(2,1)S(1)} %collective-permute-done.2.refs_0_, bf16[2,144,128]{2,1,0:T(8,128)(2,1)S(1)} %collective-permute-done.3.refs_1_, bf16[512,128]{1,0:T(8,128)(2,1)S(1)} %get-tuple-element.19.refs_2_, bf16[16,128]{1,0:T(8,128)(2,1)S(1)} %get-tuple-element.20.refs_3_, ...), custom_call_target="tpu_custom_call" | custom-call | tf_op jit(solution)/shard_map/pair/pallas_call | solution.py:260
Async XLA Ops:
  0.0 2.1 %collective-permute-start = (bf16[32,16,256]{2,1,0:T(8,128)(2,1)}, bf16[32,16,256]{2,1,0:T(8,128)(2,1)S(1)}, u32[]{:S(2)}, u32[]{:S(2)}) collective-permute-start(bf16[32,16,256]{2,1,0:T(8,128)(2,1)} %x_hbm.1), channel_id=1, source_target_pairs={{0,1},{1,0},{2,3},{3,2},{4,5},{5,4},{6,7},{7,6},{8,9},{9,8},{10,11... | collective-permute-start | bytes 786440 | tf_op jit(solution)/shard_map/ppermute | solution.py:211
  0.5 1.7 %collective-permute-start.1 = (s32[16,32]{1,0:T(8,128)}, s32[16,32]{1,0:T(8,128)S(1)}, u32[]{:S(2)}, u32[]{:S(2)}) collective-permute-start(s32[16,32]{1,0:T(8,128)} %bitcast.5), channel_id=1, source_target_pairs={{0,1},{1,0},{2,3},{3,2},{4,5},{5,4},{6,7},{7,6},{8,9},{9,8},{10,11... | collective-permute-start | bytes 6152 | tf_op jit(solution)/shard_map/ppermute | solution.py:211
  2.1 9.8 %copy-start = (bf16[1024,128]{1,0:T(8,128)(2,1)S(1)}, bf16[1024,128]{1,0:T(8,128)(2,1)}, u32[]{:S(2)}) copy-start(bf16[1024,128]{1,0:T(8,128)(2,1)} %refs_4_.1) | copy-start | bytes 786436
  2.7 6.6 %collective-permute-start.4 = (bf16[2,144,128]{2,1,0:T(8,128)(2,1)S(1)}, bf16[2,144,128]{2,1,0:T(8,128)(2,1)S(1)}, u32[]{:S(2)}, u32[]{:S(2)}) collective-permute-start(bf16[2,144,128]{2,1,0:T(8,128)(2,1)S(1)} %get-tuple-element.18.refs_0_), channel_id=1, source_target_pairs={{0,2},{1,3},{2,0},{3,1},{4,6},{5,7},{6,4},{7,5},{8,10},{9,11},{10,... | collective-permute-start | bytes 221192 | tf_op jit(solution)/shard_map/ppermute | solution.py:244
  5.7 5.6 %collective-permute-start.3 = (bf16[2,144,128]{2,1,0:T(8,128)(2,1)S(1)}, bf16[2,144,128]{2,1,0:T(8,128)(2,1)S(1)}, u32[]{:S(2)}, u32[]{:S(2)}) collective-permute-start(bf16[2,144,128]{2,1,0:T(8,128)(2,1)S(1)} %get-tuple-element.17), channel_id=1, source_target_pairs={{0,12},{1,4},{2,8},{3,0},{4,9},{5,13},{6,5},{7,1},{8,10},{9,2},{10... | collective-permute-start | bytes 221192 | tf_op jit(solution)/shard_map/ppermute | solution.py:247
  9.3 2.7 %collective-permute-start.2 = (bf16[2,144,128]{2,1,0:T(8,128)(2,1)S(1)}, bf16[2,144,128]{2,1,0:T(8,128)(2,1)S(1)}, u32[]{:S(2)}, u32[]{:S(2)}) collective-permute-start(bf16[2,144,128]{2,1,0:T(8,128)(2,1)S(1)} %get-tuple-element.17), channel_id=1, source_target_pairs={{0,8},{1,0},{2,12},{3,4},{4,5},{5,1},{6,9},{7,13},{8,6},{9,14},{10... | collective-permute-start | bytes 221192 | tf_op jit(solution)/shard_map/ppermute | solution.py:247

commit v10 on v9

--- a/solution.py
+++ b/solution.py
@@ -47,81 +47,99 @@
     return chip
 
 
-def project_block(width, x_ref, flag_ref, weight, vectors, block, left_ref, right_ref, proj_ref):
+def project_constants(seqs, rows, width, block, copies):
+    lanes = rows * width
+    spreader = (iota((rows, lanes), 1) // width == iota((rows, lanes), 0)).astype(BF16)
+    place = iota((seqs, LANES), 1) // width
+    mine = [iota((rows, LANES), 1) // seqs + tile * (LANES // seqs) == block for tile in range(copies)]
+    return spreader, place, mine
+
+
+def project_block(width, x_ref, flag_ref, weight, vectors, constants, chunks, left_ref, right_ref, proj_ref):
     seqs, rows, depth = x_ref.shape
     fold = LANES // width
+    assert fold == 4
     lanes = rows * width
     data = lanes // LANES * seqs
-    x = x_ref[...].astype(F32).reshape(seqs * rows, depth)
-    center = jnp.mean(x, axis=-1, keepdims=True)
-    x = x - center
-    spread = jnp.mean(x * x, axis=-1, keepdims=True)
-    normed = x * lax.rsqrt(spread + 1e-05) * vectors[0:1] + vectors[1:2]
-    both = dot(normed.astype(BF16), weight, NT) + vectors[2:3]
-    proj_ref[0] = both[:, :LANES]
-    proj_ref[1] = both[:, LANES:]
+    spreader, place, mine = constants
+    part = seqs // len(chunks)
+    for k, wait in enumerate(chunks):
+        wait()
+        x = x_ref[k * part:(k + 1) * part].astype(F32).reshape(part * rows, depth)
+        center = jnp.mean(x, axis=-1, keepdims=True)
+        x = x - center
+        spread = jnp.mean(x * x, axis=-1, keepdims=True)
+        normed = x * lax.rsqrt(spread + 1e-05) * vectors[0:1] + vectors[1:2]
+        proj_ref[k * part * rows:(k + 1) * part * rows, :] = dot(normed.astype(BF16), weight, NT) + vectors[2:3, :LANES]
 
     flags = flag_ref[...].astype(F32)
-    spreader = (iota((rows, lanes), 1) // width == iota((rows, lanes), 0)).astype(BF16)
     mask = dot(flags.astype(BF16), spreader, TN)
     flags = jnp.concatenate([flags] * (LANES // seqs), axis=1)
-    lane_block = iota((rows, LANES), 1) // seqs
-
-    place = iota((seqs, LANES), 1) // width
-    for half, out_ref in ((0, left_ref), (1, right_ref)):
-        for tile in range(rows // fold):
-            merged = proj_ref[half, pl.ds(tile * fold, seqs, stride=rows), :]
-            for k in range(1, fold):
-                part = proj_ref[half, pl.ds(tile * fold + k, seqs, stride=rows), :]
-                merged = jnp.where(place == k, part, merged)
-            merged = merged * mask[:, tile * LANES:(tile + 1) * LANES]
-            out_ref[tile * seqs:(tile + 1) * seqs, :] = merged.astype(BF16)
-        for tile in range((out_ref.shape[0] - data) // rows):
-            mine = jnp.where(lane_block + tile * (LANES // seqs) == block, flags, 0.0)
-            out_ref[data + tile * rows:data + (tile + 1) * rows, :] = mine.astype(BF16)
-
-
-def own_kernel(x_hbm, flag_hbm, scale_hbm, shift_hbm, wl_hbm, bl_hbm, wr_hbm, br_hbm, last_hbm,
+    for tile in range(rows // fold):
+        own = [proj_ref[pl.ds(tile * fold + k, seqs, stride=rows), :] for k in range(fold)]
+        moved = [pltpu.roll(p, width, 1) for p in own]
+        where = slice(tile * LANES, (tile + 1) * LANES)
+        for out_ref, (g0, g1, g2, g3) in (
+            (left_ref, (own[0], moved[1], own[2], moved[3])),
+            (right_ref, (moved[0], own[1], moved[2], own[3])),
+        ):
+            merged = jnp.where(place < 2, jnp.where(place == 0, g0, g1), jnp.where(place == 2, g2, g3))
+            out_ref[tile * seqs:(tile + 1) * seqs, :] = (merged * mask[:, where]).astype(BF16)
+    for tile, here in enumerate(mine):
+        placed = jnp.where(here, flags, 0.0).astype(BF16)
+        for out_ref in (left_ref, right_ref):
+            out_ref[data + tile * rows:data + (tile + 1) * rows, :] = placed
+
+
+def own_kernel(chunks, x_hbm, flag_hbm, scale_hbm, shift_hbm, wl_hbm, bl_hbm, wr_hbm, br_hbm, last_hbm,
                left_ref, right_ref, weight_ref, vector_ref,
                x_ref, flag_ref, scale_ref, shift_ref, wl_ref, bl_ref, wr_ref, br_ref, last_ref, proj_ref, sems):
+    seqs, rows, depth = x_ref.shape
+    part = seqs // chunks
     copies = [
         pltpu.make_async_copy(src, dst, sems.at[k])
         for k, (src, dst) in enumerate((
-            (x_hbm, x_ref), (flag_hbm, flag_ref), (scale_hbm, scale_ref), (shift_hbm, shift_ref),
-            (wl_hbm, wl_ref), (bl_hbm, bl_ref), (wr_hbm, wr_ref), (br_hbm, br_ref), (last_hbm, last_ref),
+            (wl_hbm, wl_ref), (wr_hbm, wr_ref), (scale_hbm, scale_ref), (shift_hbm, shift_ref),
+            (bl_hbm, bl_ref), (br_hbm, br_ref),
+            *((x_hbm.at[k * part:(k + 1) * part], x_ref.at[k * part:(k + 1) * part]) for k in range(chunks)),
+            (flag_hbm, flag_ref), (last_hbm, last_ref),
         ))
     ]
     for copy in copies:
         copy.start()
-    for copy in copies:
+    width = wl_ref.shape[0]
+    fold = LANES // width
+    data = rows * width // LANES * seqs
+    constants = project_constants(seqs, rows, width, lax.axis_index("seq"), (left_ref.shape[0] - data) // rows)
+    for copy in copies[:6]:
         copy.wait()
-    width, depth = wl_ref.shape
-    fold = LANES // width
-    weight = jnp.concatenate([wl_ref[...]] * fold + [wr_ref[...]] * fold, axis=0)
-    bias = [bl_ref[...].reshape(1, width)] * fold + [br_ref[...].reshape(1, width)] * fold
-    vectors = jnp.concatenate(
-        [
-            scale_ref[...].reshape(1, depth),
-            shift_ref[...].reshape(1, depth),
-            jnp.concatenate(bias, axis=1),
-            jnp.concatenate([last_ref[...].reshape(1, LANES)] * (depth // LANES), axis=1),
-            jnp.zeros((4, depth), F32),
-        ],
-        axis=0,
-    )
+    weight = jnp.concatenate([wl_ref[...], wr_ref[...]] * (fold // 2), axis=0)
+    bias = [bl_ref[...].reshape(1, width), br_ref[...].reshape(1, width)] * (fold // 2)
+    bias = jnp.concatenate(bias + [jnp.zeros((1, depth - LANES), F32)], axis=1)
+    vectors = jnp.concatenate([scale_ref[...].reshape(1, depth), shift_ref[...].reshape(1, depth), bias], axis=0)
+
+    def last_chunk():
+        for copy in copies[5 + chunks:]:
+            copy.wait()
+
+    waits = [copy.wait for copy in copies[6:5 + chunks]] + [last_chunk]
+    project_block(width, x_ref, flag_ref, weight, vectors, constants, waits, left_ref, right_ref, proj_ref)
     weight_ref[...] = weight
-    vector_ref[...] = vectors
-    project_block(width, x_ref, flag_ref, weight, vectors, lax.axis_index("seq"), left_ref, right_ref, proj_ref)
+    last = jnp.concatenate([last_ref[...].reshape(1, LANES)] * (depth // LANES), axis=1)
+    vector_ref[...] = jnp.concatenate([vectors, last, jnp.zeros((4, depth), F32)], axis=0)
 
 
 def both_kernel(width, x_ref, flag_ref, weight_ref, vector_ref, own_left_ref, own_right_ref, left_ref, right_ref, proj_ref):
+    seqs, rows, _ = x_ref.shape
     block = lax.axis_index("seq")
     core = block % CORES
     left_ref[core] = own_left_ref[...]
     right_ref[core] = own_right_ref[...]
     other = 1 - core
+    data = rows * width // LANES * seqs
+    constants = project_constants(seqs, rows, width, block + other - core, (left_ref.shape[1] - data) // rows)
     project_block(
-        width, x_ref, flag_ref, weight_ref[...], vector_ref[...], block + other - core,
+        width, x_ref, flag_ref, weight_ref[...], vector_ref[...], constants, [lambda: None],
         left_ref.at[other], right_ref.at[other], proj_ref,
     )
 
@@ -210,21 +228,22 @@
     swap = [(p, p ^ 1) for p in range(n)]
     other_x, other_flags = lax.ppermute(x, "seq", swap), lax.ppermute(flags, "seq", swap)
 
+    chunks = 4
     operands = [
         pltpu.with_memory_space_constraint(o, pltpu.HBM) for o in (x, flags, scale, shift, wl.T, bl, wr.T, br, bias)
     ]
     wire = jax.ShapeDtypeStruct((size, LANES), BF16)
     left, right, weight, vectors = pl.pallas_call(
-        own_kernel,
+        functools.partial(own_kernel, chunks),
         out_shape=(
             wire, wire,
-            jax.ShapeDtypeStruct((2 * LANES, depth), BF16),
-            jax.ShapeDtypeStruct((8, 2 * LANES), F32),
+            jax.ShapeDtypeStruct((LANES, depth), BF16),
+            jax.ShapeDtypeStruct((8, depth), F32),
         ),
         in_specs=[pl.BlockSpec(memory_space=pltpu.HBM)] * len(operands),
         scratch_shapes=[pltpu.VMEM(o.shape, o.dtype) for o in operands] + [
-            pltpu.VMEM((2, seqs * rows, LANES), F32),
-            pltpu.SemaphoreType.DMA((len(operands),)),
+            pltpu.VMEM((seqs * rows, LANES), F32),
+            pltpu.SemaphoreType.DMA((len(operands) - 1 + chunks,)),
         ],
         compiler_params=pltpu.CompilerParams(vmem_limit_bytes=16 << 20),
         cost_estimate=pl.CostEstimate(flops=1 << 25, bytes_accessed=x.size * 8, transcendentals=0),
@@ -234,7 +253,7 @@
     left, right = pl.pallas_call(
         functools.partial(both_kernel, width),
         out_shape=(wire, wire),
-        scratch_shapes=[pltpu.VMEM((2, seqs * rows, LANES), F32)],
+        scratch_shapes=[pltpu.VMEM((seqs * rows, LANES), F32)],
         compiler_params=pltpu.CompilerParams(vmem_limit_bytes=16 << 20),
         name="project_other",
     )(other_x, other_flags, weight, vectors, left, right)

time: 13.7 us -> 14.7 us (1.073)
  the two profiles are of different devices: /device:TPU:0 before, /device:TPU:6 now
where the time goes in v10:
time: 14.7 us; the launch traced here: 14.4 us
  starting transfers between devices  5.64 us (38%)
  Pallas kernels  4.76 us (32%)
  waiting for transfers between devices  3.95 us (27%)
    ppermute x2, starting transfers between devices, local(): lax.ppermute(right, axes, [(a * n + p, step[a][p] * n + a) for a in range...  4.53 us
    ppermute x2, waiting for transfers between devices, local(): lax.ppermute(right, axes, [(a * n + p, step[a][p] * n + a) for a in range...  3.94 us
    pallas_call x1, Pallas kernels, local(): pl.pallas_call(functools.partial(own_kernel, chunks), out_shape=(wire, wi...  2.45 us
    pallas_call x1, Pallas kernels, local(): pl.pallas_call(functools.partial(pair_kernel, steps, seqs, rows, rows, wi...  1.48 us
    ppermute x1, starting transfers between devices, local(): lax.ppermute(left, 'seq', [(p, p ^ k * CORES) for p in range(n)])  0.6 us
    pallas_call x1, Pallas kernels, local(): pl.pallas_call(functools.partial(both_kernel, width), out_shape=(wire, wi...  0.56 us
    ppermute x1, starting transfers between devices, local(): lax.ppermute(flags, 'seq', swap)  0.51 us
  transfers between devices with their start and end apart: 5, of which 2 were waited for; matrix products, arithmetic and copies ran while one was open for 0% of the time, Pallas kernels for 19%

profile of v10, /device:TPU:6, one launch (start us, length us, event | category | flops | bytes accessed | tf_op | source)
XLA Modules:
  0.0 14.4 jit_solution(1415069763414474771)
XLA Ops:
  0.0 0.0 collective-permute-start
  0.0 0.5 %collective-permute-start.1 = (s32[16,32]{1,0:T(8,128)}, s32[16,32]{1,0:T(8,128)S(1)}, u32[]{:S(2)}, u32[]{:S(2)}) collective-permute-start(s32[16,32]{1,0:T(8,128)} %bitcast.5), channel_id=1, source_target_pairs={{0,1},{1,0},{2,3},{3,2},{4,5},{5,4},{6,7},{7,6},{8,9},{9,8},{10,11... | collective-permute-start | bytes 6152 | tf_op jit(solution)/shard_map/ppermute | solution.py:229
  0.5 2.4 %project_own.1 = (bf16[144,128]{1,0:T(8,128)(2,1)S(1)}, bf16[144,128]{1,0:T(8,128)(2,1)S(1)}, bf16[128,256]{1,0:T(8,128)(2,1)S(1)}, f32[8,256]{1,0:T(8,128)S(1)}) custom-call(bf16[32,16,256]{2,1,0:T(8,128)(2,1)} %x_hbm.1, s32[16,32]{1,0:T(8,128)} %bitcast.6, f32[256]{0:T(256)} %scale_hbm.1, f32[256]{0:T(256)} %shift_hbm.1, bf16[32,256]{1,0:T(8,128)(2,1)} %bitcast.3, ...), custom_call_target="tpu_custom_call" | custom-call | flops 33554432 | bytes 1048576 | tf_op jit(solution)/shard_map/project_own/pallas_call | solution.py:236
  3.0 0.0 collective-permute-done.1.flag_ref
  3.0 0.0 collective-permute-done.x_ref
  3.0 0.0 copy-start
  3.0 0.6 %project_other.1 = (bf16[2,144,128]{2,1,0:T(8,128)(2,1)S(1)}, bf16[2,144,128]{2,1,0:T(8,128)(2,1)S(1)}) custom-call(bf16[32,16,256]{2,1,0:T(8,128)(2,1)S(1)} %collective-permute-done.x_ref, s32[16,32]{1,0:T(8,128)S(1)} %collective-permute-done.1.flag_ref, bf16[128,256]{1,0:T(8,128)(2,1)S(1)} %get-tuple-element.13.weight_ref, ...), custom_call_target="tpu_custom_call" | custom-call | tf_op jit(solution)/shard_map/project_other/pallas_call | solution.py:253
  3.6 0.6 %collective-permute-start.4 = (bf16[2,144,128]{2,1,0:T(8,128)(2,1)S(1)}, bf16[2,144,128]{2,1,0:T(8,128)(2,1)S(1)}, u32[]{:S(2)}, u32[]{:S(2)}) collective-permute-start(bf16[2,144,128]{2,1,0:T(8,128)(2,1)S(1)} %get-tuple-element.18.refs_0_), channel_id=1, source_target_pairs={{0,2},{1,3},{2,0},{3,1},{4,6},{5,7},{6,4},{7,5},{8,10},{9,11},{10,... | collective-permute-start | bytes 221192 | tf_op jit(solution)/shard_map/ppermute | solution.py:263
  4.2 3.5 %collective-permute-start.3 = (bf16[2,144,128]{2,1,0:T(8,128)(2,1)S(1)}, bf16[2,144,128]{2,1,0:T(8,128)(2,1)S(1)}, u32[]{:S(2)}, u32[]{:S(2)}) collective-permute-start(bf16[2,144,128]{2,1,0:T(8,128)(2,1)S(1)} %get-tuple-element.17), channel_id=1, source_target_pairs={{0,12},{1,4},{2,8},{3,0},{4,9},{5,13},{6,5},{7,1},{8,10},{9,2},{10... | collective-permute-start | bytes 221192 | tf_op jit(solution)/shard_map/ppermute | solution.py:266
  7.7 1.0 %collective-permute-start.2 = (bf16[2,144,128]{2,1,0:T(8,128)(2,1)S(1)}, bf16[2,144,128]{2,1,0:T(8,128)(2,1)S(1)}, u32[]{:S(2)}, u32[]{:S(2)}) collective-permute-start(bf16[2,144,128]{2,1,0:T(8,128)(2,1)S(1)} %get-tuple-element.17), channel_id=1, source_target_pairs={{0,8},{1,0},{2,12},{3,4},{4,5},{5,1},{6,9},{7,13},{8,6},{9,14},{10... | collective-permute-start | bytes 221192 | tf_op jit(solution)/shard_map/ppermute | solution.py:266
  8.7 0.0 collective-permute-done.4.refs_1_
  8.7 0.3 %turn_left.1 = (bf16[512,128]{1,0:T(8,128)(2,1)S(1)}, bf16[16,128]{1,0:T(8,128)(2,1)S(1)}) custom-call(bf16[2,144,128]{2,1,0:T(8,128)(2,1)S(1)} %get-tuple-element.18.refs_0_, bf16[2,144,128]{2,1,0:T(8,128)(2,1)S(1)} %collective-permute-done.4.refs_1_), custom_call_target="tpu_custom_call" | custom-call | tf_op jit(solution)/shard_map/turn_left/pallas_call | solution.py:269
  9.0 1.6 %collective-permute-done.3.refs_1_ = bf16[2,144,128]{2,1,0:T(8,128)(2,1)S(1)} collective-permute-done((bf16[2,144,128]{2,1,0:T(8,128)(2,1)S(1)}, bf16[2,144,128]{2,1,0:T(8,128)(2,1)S(1)}, u32[]{:S(2)}, u32[]{:S(2)}) %collective-permute-start.3) | collective-permute-done | bytes 73760 | tf_op jit(solution)/shard_map/ppermute | solution.py:266
  10.6 2.3 %collective-permute-done.2.refs_0_ = bf16[2,144,128]{2,1,0:T(8,128)(2,1)S(1)} collective-permute-done((bf16[2,144,128]{2,1,0:T(8,128)(2,1)S(1)}, bf16[2,144,128]{2,1,0:T(8,128)(2,1)S(1)}, u32[]{:S(2)}, u32[]{:S(2)}) %collective-permute-start.2) | collective-permute-done | bytes 73760 | tf_op jit(solution)/shard_map/ppermute | solution.py:266
  12.9 0.0 copy-done
  12.9 1.5 %pair.1 = bf16[16,16,128]{2,1,0:T(8,128)(2,1)} custom-call(bf16[2,144,128]{2,1,0:T(8,128)(2,1)S(1)} %collective-permute-done.2.refs_0_, bf16[2,144,128]{2,1,0:T(8,128)(2,1)S(1)} %collective-permute-done.3.refs_1_, bf16[512,128]{1,0:T(8,128)(2,1)S(1)} %get-tuple-element.19.refs_2_, bf16[16,128]{1,0:T(8,128)(2,1)S(1)} %get-tuple-element.20.refs_3_, ...), custom_call_target="tpu_custom_call" | custom-call | tf_op jit(solution)/shard_map/pair/pallas_call | solution.py:279
Async XLA Ops:
  0.0 3.0 %collective-permute-start = (bf16[32,16,256]{2,1,0:T(8,128)(2,1)}, bf16[32,16,256]{2,1,0:T(8,128)(2,1)S(1)}, u32[]{:S(2)}, u32[]{:S(2)}) collective-permute-start(bf16[32,16,256]{2,1,0:T(8,128)(2,1)} %x_hbm.1), channel_id=1, source_target_pairs={{0,1},{1,0},{2,3},{3,2},{4,5},{5,4},{6,7},{7,6},{8,9},{9,8},{10,11... | collective-permute-start | bytes 786440 | tf_op jit(solution)/shard_map/ppermute | solution.py:229
  0.0 3.0 %collective-permute-start.1 = (s32[16,32]{1,0:T(8,128)}, s32[16,32]{1,0:T(8,128)S(1)}, u32[]{:S(2)}, u32[]{:S(2)}) collective-permute-start(s32[16,32]{1,0:T(8,128)} %bitcast.5), channel_id=1, source_target_pairs={{0,1},{1,0},{2,3},{3,2},{4,5},{5,4},{6,7},{7,6},{8,9},{9,8},{10,11... | collective-permute-start | bytes 6152 | tf_op jit(solution)/shard_map/ppermute | solution.py:229
  3.0 9.9 %copy-start = (bf16[1024,128]{1,0:T(8,128)(2,1)S(1)}, bf16[1024,128]{1,0:T(8,128)(2,1)}, u32[]{:S(2)}) copy-start(bf16[1024,128]{1,0:T(8,128)(2,1)} %refs_4_.1) | copy-start | bytes 786436
  3.6 5.1 %collective-permute-start.4 = (bf16[2,144,128]{2,1,0:T(8,128)(2,1)S(1)}, bf16[2,144,128]{2,1,0:T(8,128)(2,1)S(1)}, u32[]{:S(2)}, u32[]{:S(2)}) collective-permute-start(bf16[2,144,128]{2,1,0:T(8,128)(2,1)S(1)} %get-tuple-element.18.refs_0_), channel_id=1, source_target_pairs={{0,2},{1,3},{2,0},{3,1},{4,6},{5,7},{6,4},{7,5},{8,10},{9,11},{10,... | collective-permute-start | bytes 221192 | tf_op jit(solution)/shard_map/ppermute | solution.py:263
  4.2 6.5 %collective-permute-start.3 = (bf16[2,144,128]{2,1,0:T(8,128)(2,1)S(1)}, bf16[2,144,128]{2,1,0:T(8,128)(2,1)S(1)}, u32[]{:S(2)}, u32[]{:S(2)}) collective-permute-start(bf16[2,144,128]{2,1,0:T(8,128)(2,1)S(1)} %get-tuple-element.17), channel_id=1, source_target_pairs={{0,12},{1,4},{2,8},{3,0},{4,9},{5,13},{6,5},{7,1},{8,10},{9,2},{10... | collective-permute-start | bytes 221192 | tf_op jit(solution)/shard_map/ppermute | solution.py:266
  7.7 5.3 %collective-permute-start.2 = (bf16[2,144,128]{2,1,0:T(8,128)(2,1)S(1)}, bf16[2,144,128]{2,1,0:T(8,128)(2,1)S(1)}, u32[]{:S(2)}, u32[]{:S(2)}) collective-permute-start(bf16[2,144,128]{2,1,0:T(8,128)(2,1)S(1)} %get-tuple-element.17), channel_id=1, source_target_pairs={{0,8},{1,0},{2,12},{3,4},{4,5},{5,1},{6,9},{7,13},{8,6},{9,14},{10... | collective-permute-start | bytes 221192 | tf_op jit(solution)/shard_map/ppermute | solution.py:266

commit v11 on v9

--- a/solution.py
+++ b/solution.py
@@ -47,11 +47,20 @@
     return chip
 
 
-def project_block(width, x_ref, flag_ref, weight, vectors, block, left_ref, right_ref, proj_ref):
+def project_constants(seqs, rows, width, block, tiles):
+    lanes = rows * width
+    spreader = (iota((rows, lanes), 1) // width == iota((rows, lanes), 0)).astype(BF16)
+    place = iota((seqs, LANES), 1) // width
+    mine = [iota((rows, LANES), 1) // seqs + tile * (LANES // seqs) == block for tile in range(tiles)]
+    return spreader, place, mine
+
+
+def project_block(width, x_ref, flag_ref, weight, vectors, constants, left_ref, right_ref, proj_ref):
     seqs, rows, depth = x_ref.shape
     fold = LANES // width
     lanes = rows * width
     data = lanes // LANES * seqs
+    spreader, place, mine = constants
     x = x_ref[...].astype(F32).reshape(seqs * rows, depth)
     center = jnp.mean(x, axis=-1, keepdims=True)
     x = x - center
@@ -62,12 +71,9 @@
     proj_ref[1] = both[:, LANES:]
 
     flags = flag_ref[...].astype(F32)
-    spreader = (iota((rows, lanes), 1) // width == iota((rows, lanes), 0)).astype(BF16)
     mask = dot(flags.astype(BF16), spreader, TN)
     flags = jnp.concatenate([flags] * (LANES // seqs), axis=1)
-    lane_block = iota((rows, LANES), 1) // seqs
-
-    place = iota((seqs, LANES), 1) // width
+
     for half, out_ref in ((0, left_ref), (1, right_ref)):
         for tile in range(rows // fold):
             merged = proj_ref[half, pl.ds(tile * fold, seqs, stride=rows), :]
@@ -76,26 +82,30 @@
                 merged = jnp.where(place == k, part, merged)
             merged = merged * mask[:, tile * LANES:(tile + 1) * LANES]
             out_ref[tile * seqs:(tile + 1) * seqs, :] = merged.astype(BF16)
-        for tile in range((out_ref.shape[0] - data) // rows):
-            mine = jnp.where(lane_block + tile * (LANES // seqs) == block, flags, 0.0)
-            out_ref[data + tile * rows:data + (tile + 1) * rows, :] = mine.astype(BF16)
-
-
-def own_kernel(x_hbm, flag_hbm, scale_hbm, shift_hbm, wl_hbm, bl_hbm, wr_hbm, br_hbm, last_hbm,
+        for tile, here in enumerate(mine):
+            out_ref[data + tile * rows:data + (tile + 1) * rows, :] = jnp.where(here, flags, 0.0).astype(BF16)
+
+
+def own_kernel(chunks, x_hbm, flag_hbm, scale_hbm, shift_hbm, wl_hbm, bl_hbm, wr_hbm, br_hbm, last_hbm,
                left_ref, right_ref, weight_ref, vector_ref,
                x_ref, flag_ref, scale_ref, shift_ref, wl_ref, bl_ref, wr_ref, br_ref, last_ref, proj_ref, sems):
+    seqs, rows, depth = x_ref.shape
+    part = seqs // chunks
     copies = [
         pltpu.make_async_copy(src, dst, sems.at[k])
         for k, (src, dst) in enumerate((
-            (x_hbm, x_ref), (flag_hbm, flag_ref), (scale_hbm, scale_ref), (shift_hbm, shift_ref),
+            *((x_hbm.at[k * part:(k + 1) * part], x_ref.at[k * part:(k + 1) * part]) for k in range(chunks)),
+            (flag_hbm, flag_ref), (scale_hbm, scale_ref), (shift_hbm, shift_ref),
             (wl_hbm, wl_ref), (bl_hbm, bl_ref), (wr_hbm, wr_ref), (br_hbm, br_ref), (last_hbm, last_ref),
         ))
     ]
     for copy in copies:
         copy.start()
+    width = wl_ref.shape[0]
+    data = rows * width // LANES * seqs
+    constants = project_constants(seqs, rows, width, lax.axis_index("seq"), (left_ref.shape[0] - data) // rows)
     for copy in copies:
         copy.wait()
-    width, depth = wl_ref.shape
     fold = LANES // width
     weight = jnp.concatenate([wl_ref[...]] * fold + [wr_ref[...]] * fold, axis=0)
     bias = [bl_ref[...].reshape(1, width)] * fold + [br_ref[...].reshape(1, width)] * fold
@@ -111,7 +121,7 @@
     )
     weight_ref[...] = weight
     vector_ref[...] = vectors
-    project_block(width, x_ref, flag_ref, weight, vectors, lax.axis_index("seq"), left_ref, right_ref, proj_ref)
+    project_block(width, x_ref, flag_ref, weight, vectors, constants, left_ref, right_ref, proj_ref)
 
 
 def both_kernel(width, x_ref, flag_ref, weight_ref, vector_ref, own_left_ref, own_right_ref, left_ref, right_ref, proj_ref):
@@ -120,8 +130,11 @@
     left_ref[core] = own_left_ref[...]
     right_ref[core] = own_right_ref[...]
     other = 1 - core
+    seqs, rows, _ = x_ref.shape
+    data = rows * width // LANES * seqs
+    constants = project_constants(seqs, rows, width, block + other - core, (left_ref.shape[1] - data) // rows)
     project_block(
-        width, x_ref, flag_ref, weight_ref[...], vector_ref[...], block + other - core,
+        width, x_ref, flag_ref, weight_ref[...], vector_ref[...], constants,
         left_ref.at[other], right_ref.at[other], proj_ref,
     )
 
@@ -210,12 +223,13 @@
     swap = [(p, p ^ 1) for p in range(n)]
     other_x, other_flags = lax.ppermute(x, "seq", swap), lax.ppermute(flags, "seq", swap)
 
+    chunks = 4
     operands = [
         pltpu.with_memory_space_constraint(o, pltpu.HBM) for o in (x, flags, scale, shift, wl.T, bl, wr.T, br, bias)
     ]
     wire = jax.ShapeDtypeStruct((size, LANES), BF16)
     left, right, weight, vectors = pl.pallas_call(
-        own_kernel,
+        functools.partial(own_kernel, chunks),
         out_shape=(
             wire, wire,
             jax.ShapeDtypeStruct((2 * LANES, depth), BF16),
@@ -224,7 +238,7 @@
         in_specs=[pl.BlockSpec(memory_space=pltpu.HBM)] * len(operands),
         scratch_shapes=[pltpu.VMEM(o.shape, o.dtype) for o in operands] + [
             pltpu.VMEM((2, seqs * rows, LANES), F32),
-            pltpu.SemaphoreType.DMA((len(operands),)),
+            pltpu.SemaphoreType.DMA((len(operands) - 1 + chunks,)),
         ],
         compiler_params=pltpu.CompilerParams(vmem_limit_bytes=16 << 20),
         cost_estimate=pl.CostEstimate(flops=1 << 25, bytes_accessed=x.size * 8, transcendentals=0),

time: 13.7 us -> 13.7 us (level)
  no operation moved by 1% of the time
where the time goes in v11:
time: 13.7 us; the launch traced here: 13.4 us
  starting transfers between devices  7.12 us (52%)
  Pallas kernels  3.86 us (28%)
  waiting for transfers between devices  2.39 us (17%)
    ppermute x2, starting transfers between devices, local(): lax.ppermute(right, axes, [(a * n + p, step[a][p] * n + a) for a in range...  3.6 us
    ppermute x1, starting transfers between devices, local(): lax.ppermute(left, 'seq', [(p, p ^ k * CORES) for p in range(n)])  3 us
    ppermute x2, waiting for transfers between devices, local(): lax.ppermute(right, axes, [(a * n + p, step[a][p] * n + a) for a in range...  2.38 us
    pallas_call x1, Pallas kernels, local(): pl.pallas_call(functools.partial(own_kernel, chunks), out_shape=(wire, wi...  1.6 us
    pallas_call x1, Pallas kernels, local(): pl.pallas_call(functools.partial(pair_kernel, steps, seqs, rows, rows, wi...  1.46 us
    pallas_call x1, Pallas kernels, local(): pl.pallas_call(functools.partial(both_kernel, width), out_shape=(wire, wi...  0.53 us
    ppermute x1, starting transfers between devices, local(): lax.ppermute(x, 'seq', swap)  0.45 us
    pallas_call x1, Pallas kernels, local(): pl.pallas_call(functools.partial(left_kernel, seqs, rows, width), out_sha...  0.28 us
  transfers between devices with their start and end apart: 5, of which 2 were waited for; matrix products, arithmetic and copies ran while one was open for 0% of the time, Pallas kernels for 14%

profile of v11, /device:TPU:0, one launch (start us, length us, event | category | flops | bytes accessed | tf_op | source)
XLA Modules:
  0.0 13.4 jit_solution(13958739300150536718)
XLA Ops:
  0.0 0.5 %collective-permute-start = (bf16[32,16,256]{2,1,0:T(8,128)(2,1)}, bf16[32,16,256]{2,1,0:T(8,128)(2,1)S(1)}, u32[]{:S(2)}, u32[]{:S(2)}) collective-permute-start(bf16[32,16,256]{2,1,0:T(8,128)(2,1)} %x_hbm.1), channel_id=1, source_target_pairs={{0,1},{1,0},{2,3},{3,2},{4,5},{5,4},{6,7},{7,6},{8,9},{9,8},{10,11... | collective-permute-start | bytes 786440 | tf_op jit(solution)/shard_map/ppermute | solution.py:224
  0.5 0.1 collective-permute-start.1
  0.5 1.6 %project_own.1 = (bf16[144,128]{1,0:T(8,128)(2,1)S(1)}, bf16[144,128]{1,0:T(8,128)(2,1)S(1)}, bf16[256,256]{1,0:T(8,128)(2,1)S(1)}, f32[8,256]{1,0:T(8,128)S(1)}) custom-call(bf16[32,16,256]{2,1,0:T(8,128)(2,1)} %x_hbm.1, s32[16,32]{1,0:T(8,128)} %bitcast.6, f32[256]{0:T(256)} %scale_hbm.1, f32[256]{0:T(256)} %shift_hbm.1, bf16[32,256]{1,0:T(8,128)(2,1)} %bitcast.3, ...), custom_call_target="tpu_custom_call" | custom-call | flops 33554432 | bytes 1048576 | tf_op jit(solution)/shard_map/project_own/pallas_call | solution.py:231
  2.1 0.0 collective-permute-done.1.flag_ref
  2.1 0.0 collective-permute-done.x_ref
  2.1 0.0 copy-start
  2.1 0.5 %project_other.1 = (bf16[2,144,128]{2,1,0:T(8,128)(2,1)S(1)}, bf16[2,144,128]{2,1,0:T(8,128)(2,1)S(1)}) custom-call(bf16[32,16,256]{2,1,0:T(8,128)(2,1)S(1)} %collective-permute-done.x_ref, s32[16,32]{1,0:T(8,128)S(1)} %collective-permute-done.1.flag_ref, bf16[256,256]{1,0:T(8,128)(2,1)S(1)} %get-tuple-element.13.weight_ref, ...), custom_call_target="tpu_custom_call" | custom-call | tf_op jit(solution)/shard_map/project_other/pallas_call | solution.py:248
  2.7 3.0 %collective-permute-start.4 = (bf16[2,144,128]{2,1,0:T(8,128)(2,1)S(1)}, bf16[2,144,128]{2,1,0:T(8,128)(2,1)S(1)}, u32[]{:S(2)}, u32[]{:S(2)}) collective-permute-start(bf16[2,144,128]{2,1,0:T(8,128)(2,1)S(1)} %get-tuple-element.18.refs_0_), channel_id=1, source_target_pairs={{0,2},{1,3},{2,0},{3,1},{4,6},{5,7},{6,4},{7,5},{8,10},{9,11},{10,... | collective-permute-start | bytes 221192 | tf_op jit(solution)/shard_map/ppermute | solution.py:258
  5.7 3.6 %collective-permute-start.3 = (bf16[2,144,128]{2,1,0:T(8,128)(2,1)S(1)}, bf16[2,144,128]{2,1,0:T(8,128)(2,1)S(1)}, u32[]{:S(2)}, u32[]{:S(2)}) collective-permute-start(bf16[2,144,128]{2,1,0:T(8,128)(2,1)S(1)} %get-tuple-element.17), channel_id=1, source_target_pairs={{0,12},{1,4},{2,8},{3,0},{4,9},{5,13},{6,5},{7,1},{8,10},{9,2},{10... | collective-permute-start | bytes 221192 | tf_op jit(solution)/shard_map/ppermute | solution.py:261
  9.3 0.0 collective-permute-start.2
  9.3 0.0 collective-permute-done.4.refs_1_
  9.3 0.3 %turn_left.1 = (bf16[512,128]{1,0:T(8,128)(2,1)S(1)}, bf16[16,128]{1,0:T(8,128)(2,1)S(1)}) custom-call(bf16[2,144,128]{2,1,0:T(8,128)(2,1)S(1)} %get-tuple-element.18.refs_0_, bf16[2,144,128]{2,1,0:T(8,128)(2,1)S(1)} %collective-permute-done.4.refs_1_), custom_call_target="tpu_custom_call" | custom-call | tf_op jit(solution)/shard_map/turn_left/pallas_call | solution.py:264
  9.6 1.7 %collective-permute-done.3.refs_1_ = bf16[2,144,128]{2,1,0:T(8,128)(2,1)S(1)} collective-permute-done((bf16[2,144,128]{2,1,0:T(8,128)(2,1)S(1)}, bf16[2,144,128]{2,1,0:T(8,128)(2,1)S(1)}, u32[]{:S(2)}, u32[]{:S(2)}) %collective-permute-start.3) | collective-permute-done | bytes 73760 | tf_op jit(solution)/shard_map/ppermute | solution.py:261
  11.3 0.7 %collective-permute-done.2.refs_0_ = bf16[2,144,128]{2,1,0:T(8,128)(2,1)S(1)} collective-permute-done((bf16[2,144,128]{2,1,0:T(8,128)(2,1)S(1)}, bf16[2,144,128]{2,1,0:T(8,128)(2,1)S(1)}, u32[]{:S(2)}, u32[]{:S(2)}) %collective-permute-start.2) | collective-permute-done | bytes 73760 | tf_op jit(solution)/shard_map/ppermute | solution.py:261
  12.0 0.0 copy-done
  12.0 1.5 %pair.1 = bf16[16,16,128]{2,1,0:T(8,128)(2,1)} custom-call(bf16[2,144,128]{2,1,0:T(8,128)(2,1)S(1)} %collective-permute-done.2.refs_0_, bf16[2,144,128]{2,1,0:T(8,128)(2,1)S(1)} %collective-permute-done.3.refs_1_, bf16[512,128]{1,0:T(8,128)(2,1)S(1)} %get-tuple-element.19.refs_2_, bf16[16,128]{1,0:T(8,128)(2,1)S(1)} %get-tuple-element.20.refs_3_, ...), custom_call_target="tpu_custom_call" | custom-call | tf_op jit(solution)/shard_map/pair/pallas_call | solution.py:274
Async XLA Ops:
  0.0 2.1 %collective-permute-start = (bf16[32,16,256]{2,1,0:T(8,128)(2,1)}, bf16[32,16,256]{2,1,0:T(8,128)(2,1)S(1)}, u32[]{:S(2)}, u32[]{:S(2)}) collective-permute-start(bf16[32,16,256]{2,1,0:T(8,128)(2,1)} %x_hbm.1), channel_id=1, source_target_pairs={{0,1},{1,0},{2,3},{3,2},{4,5},{5,4},{6,7},{7,6},{8,9},{9,8},{10,11... | collective-permute-start | bytes 786440 | tf_op jit(solution)/shard_map/ppermute | solution.py:224
  0.5 1.7 %collective-permute-start.1 = (s32[16,32]{1,0:T(8,128)}, s32[16,32]{1,0:T(8,128)S(1)}, u32[]{:S(2)}, u32[]{:S(2)}) collective-permute-start(s32[16,32]{1,0:T(8,128)} %bitcast.5), channel_id=1, source_target_pairs={{0,1},{1,0},{2,3},{3,2},{4,5},{5,4},{6,7},{7,6},{8,9},{9,8},{10,11... | collective-permute-start | bytes 6152 | tf_op jit(solution)/shard_map/ppermute | solution.py:224
  2.1 9.8 %copy-start = (bf16[1024,128]{1,0:T(8,128)(2,1)S(1)}, bf16[1024,128]{1,0:T(8,128)(2,1)}, u32[]{:S(2)}) copy-start(bf16[1024,128]{1,0:T(8,128)(2,1)} %refs_4_.1) | copy-start | bytes 786436
  2.7 6.6 %collective-permute-start.4 = (bf16[2,144,128]{2,1,0:T(8,128)(2,1)S(1)}, bf16[2,144,128]{2,1,0:T(8,128)(2,1)S(1)}, u32[]{:S(2)}, u32[]{:S(2)}) collective-permute-start(bf16[2,144,128]{2,1,0:T(8,128)(2,1)S(1)} %get-tuple-element.18.refs_0_), channel_id=1, source_target_pairs={{0,2},{1,3},{2,0},{3,1},{4,6},{5,7},{6,4},{7,5},{8,10},{9,11},{10,... | collective-permute-start | bytes 221192 | tf_op jit(solution)/shard_map/ppermute | solution.py:258
  5.7 5.6 %collective-permute-start.3 = (bf16[2,144,128]{2,1,0:T(8,128)(2,1)S(1)}, bf16[2,144,128]{2,1,0:T(8,128)(2,1)S(1)}, u32[]{:S(2)}, u32[]{:S(2)}) collective-permute-start(bf16[2,144,128]{2,1,0:T(8,128)(2,1)S(1)} %get-tuple-element.17), channel_id=1, source_target_pairs={{0,12},{1,4},{2,8},{3,0},{4,9},{5,13},{6,5},{7,1},{8,10},{9,2},{10... | collective-permute-start | bytes 221192 | tf_op jit(solution)/shard_map/ppermute | solution.py:261
  9.3 2.7 %collective-permute-start.2 = (bf16[2,144,128]{2,1,0:T(8,128)(2,1)S(1)}, bf16[2,144,128]{2,1,0:T(8,128)(2,1)S(1)}, u32[]{:S(2)}, u32[]{:S(2)}) collective-permute-start(bf16[2,144,128]{2,1,0:T(8,128)(2,1)S(1)} %get-tuple-element.17), channel_id=1, source_target_pairs={{0,8},{1,0},{2,12},{3,4},{4,5},{5,1},{6,9},{7,13},{8,6},{9,14},{10... | collective-permute-start | bytes 221192 | tf_op jit(solution)/shard_map/ppermute | solution.py:261

commit v12 on v11

--- a/solution.py
+++ b/solution.py
@@ -86,30 +86,25 @@
             out_ref[data + tile * rows:data + (tile + 1) * rows, :] = jnp.where(here, flags, 0.0).astype(BF16)
 
 
-def own_kernel(chunks, x_hbm, flag_hbm, scale_hbm, shift_hbm, wl_hbm, bl_hbm, wr_hbm, br_hbm, last_hbm,
-               left_ref, right_ref, weight_ref, vector_ref,
-               x_ref, flag_ref, scale_ref, shift_ref, wl_ref, bl_ref, wr_ref, br_ref, last_ref, proj_ref, sems):
-    seqs, rows, depth = x_ref.shape
-    part = seqs // chunks
+def load_kernel(x_hbm, flag_hbm, scale_hbm, shift_hbm, wl_hbm, bl_hbm, wr_hbm, br_hbm, last_hbm,
+                x_ref, flag_ref, weight_ref, vector_ref,
+                scale_ref, shift_ref, wl_ref, bl_ref, wr_ref, br_ref, last_ref, sems):
     copies = [
         pltpu.make_async_copy(src, dst, sems.at[k])
         for k, (src, dst) in enumerate((
-            *((x_hbm.at[k * part:(k + 1) * part], x_ref.at[k * part:(k + 1) * part]) for k in range(chunks)),
-            (flag_hbm, flag_ref), (scale_hbm, scale_ref), (shift_hbm, shift_ref),
+            (x_hbm, x_ref), (flag_hbm, flag_ref), (scale_hbm, scale_ref), (shift_hbm, shift_ref),
             (wl_hbm, wl_ref), (bl_hbm, bl_ref), (wr_hbm, wr_ref), (br_hbm, br_ref), (last_hbm, last_ref),
         ))
     ]
     for copy in copies:
         copy.start()
-    width = wl_ref.shape[0]
-    data = rows * width // LANES * seqs
-    constants = project_constants(seqs, rows, width, lax.axis_index("seq"), (left_ref.shape[0] - data) // rows)
-    for copy in copies:
+    for copy in copies[1:]:
         copy.wait()
+    width, depth = wl_ref.shape
     fold = LANES // width
-    weight = jnp.concatenate([wl_ref[...]] * fold + [wr_ref[...]] * fold, axis=0)
+    weight_ref[...] = jnp.concatenate([wl_ref[...]] * fold + [wr_ref[...]] * fold, axis=0)
     bias = [bl_ref[...].reshape(1, width)] * fold + [br_ref[...].reshape(1, width)] * fold
-    vectors = jnp.concatenate(
+    vector_ref[...] = jnp.concatenate(
         [
             scale_ref[...].reshape(1, depth),
             shift_ref[...].reshape(1, depth),
@@ -119,24 +114,25 @@
         ],
         axis=0,
     )
-    weight_ref[...] = weight
-    vector_ref[...] = vectors
-    project_block(width, x_ref, flag_ref, weight, vectors, constants, left_ref, right_ref, proj_ref)
-
-
-def both_kernel(width, x_ref, flag_ref, weight_ref, vector_ref, own_left_ref, own_right_ref, left_ref, right_ref, proj_ref):
+    copies[0].wait()
+
+
+def project_kernel(width, own_x_ref, own_flag_ref, other_x_ref, other_flag_ref, weight_ref, vector_ref,
+                   left_ref, right_ref, own_proj_ref, other_proj_ref):
+    seqs, rows, _ = own_x_ref.shape
     block = lax.axis_index("seq")
     core = block % CORES
-    left_ref[core] = own_left_ref[...]
-    right_ref[core] = own_right_ref[...]
     other = 1 - core
-    seqs, rows, _ = x_ref.shape
-    data = rows * width // LANES * seqs
-    constants = project_constants(seqs, rows, width, block + other - core, (left_ref.shape[1] - data) // rows)
-    project_block(
-        width, x_ref, flag_ref, weight_ref[...], vector_ref[...], constants,
-        left_ref.at[other], right_ref.at[other], proj_ref,
-    )
+    tiles = (left_ref.shape[1] - rows * width // LANES * seqs) // rows
+    for x_ref, flag_ref, proj_ref, at in (
+        (own_x_ref, own_flag_ref, own_proj_ref, core),
+        (other_x_ref, other_flag_ref, other_proj_ref, other),
+    ):
+        project_block(
+            width, x_ref, flag_ref, weight_ref[...], vector_ref[...],
+            project_constants(seqs, rows, width, block - core + at, tiles),
+            left_ref.at[at], right_ref.at[at], proj_ref,
+        )
 
 
 def whole_mask(pieces, rows, data):
@@ -144,21 +140,20 @@
     return jnp.concatenate([total[k:k + rows] for k in range(0, total.shape[0], rows)], axis=1)
 
 
-def gather_factor(pieces, chips, seqs, data, whole_ref):
-    for piece, chip in zip(pieces, chips):
+def left_kernel(steps, seqs, rows, width, *refs):
+    lefts, (out_ref, mask_ref, left_ref, turned_ref) = refs[:-4], refs[-4:]
+    data = rows * width // LANES * seqs
+    me_res, me_seq = lax.axis_index("res"), lax.axis_index("seq")
+    order = [sending_chip(step, me_res, me_seq) for step in steps]
+    for k, piece in enumerate(lefts):
+        chip = me_seq // CORES ^ k
+        slot = sum(jnp.where(there == chip, place, 0) for place, there in enumerate(order))
         for core in range(CORES):
-            at = pl.multiple_of((chip * CORES + core) * seqs, seqs)
+            at = pl.multiple_of((slot * CORES + core) * seqs, seqs)
             for tile in range(data // seqs):
-                whole_ref[pl.ds(at, seqs), tile * LANES:(tile + 1) * LANES] = (
+                left_ref[pl.ds(at, seqs), tile * LANES:(tile + 1) * LANES] = (
                     piece[core, tile * seqs:(tile + 1) * seqs, :]
                 )
-
-
-def left_kernel(seqs, rows, width, *refs):
-    lefts, (out_ref, mask_ref, left_ref, turned_ref) = refs[:-4], refs[-4:]
-    data = rows * width // LANES * seqs
-    me = lax.axis_index("seq") // CORES
-    gather_factor(lefts, [me ^ k for k in range(len(lefts))], seqs, data, left_ref)
     mask_ref[...] = whole_mask(lefts, rows, data)
     for tile in range(turned_ref.shape[0]):
         turned_ref[tile] = left_ref[tile * LANES:(tile + 1) * LANES, :].astype(F32).T
@@ -168,17 +163,22 @@
             )
 
 
-def pair_kernel(steps, seqs, rows, columns, width, *refs):
-    n = len(steps)
-    rights = refs[:n]
-    turned_ref, live_ref, w_ref, vector_ref, out_ref, right_ref, flat_ref, raw_ref = refs[n:]
+def pair_kernel(seqs, rows, columns, width, *refs):
+    rights = refs[:-7]
+    turned_ref, live_ref, w_ref, vector_ref, out_ref, flat_ref, raw_ref = refs[-7:]
     fold = LANES // width
     assert fold == 4
     data = rows * width // LANES * seqs
 
-    me_res, me_seq = lax.axis_index("res"), lax.axis_index("seq")
-    gather_factor(rights, [sending_chip(step, me_res, me_seq) for step in steps], seqs, data, right_ref)
-    outer = dot(turned_ref[...], right_ref[...]).astype(BF16)
+    right = jnp.concatenate(
+        [
+            jnp.concatenate([p[core, t * seqs:(t + 1) * seqs, :] for t in range(data // seqs)], axis=1)
+            for p in rights
+            for core in range(CORES)
+        ],
+        axis=0,
+    )
+    outer = dot(turned_ref[...], right).astype(BF16)
 
     place = (iota((rows, LANES), 1) // width).astype(BF16)
     even = [None] * fold
@@ -223,35 +223,32 @@
     swap = [(p, p ^ 1) for p in range(n)]
     other_x, other_flags = lax.ppermute(x, "seq", swap), lax.ppermute(flags, "seq", swap)
 
-    chunks = 4
     operands = [
         pltpu.with_memory_space_constraint(o, pltpu.HBM) for o in (x, flags, scale, shift, wl.T, bl, wr.T, br, bias)
     ]
-    wire = jax.ShapeDtypeStruct((size, LANES), BF16)
-    left, right, weight, vectors = pl.pallas_call(
-        functools.partial(own_kernel, chunks),
+    own_x, own_flags, weight, vectors = pl.pallas_call(
+        load_kernel,
         out_shape=(
-            wire, wire,
+            jax.ShapeDtypeStruct(x.shape, x.dtype),
+            jax.ShapeDtypeStruct(flags.shape, flags.dtype),
             jax.ShapeDtypeStruct((2 * LANES, depth), BF16),
             jax.ShapeDtypeStruct((8, 2 * LANES), F32),
         ),
         in_specs=[pl.BlockSpec(memory_space=pltpu.HBM)] * len(operands),
-        scratch_shapes=[pltpu.VMEM(o.shape, o.dtype) for o in operands] + [
-            pltpu.VMEM((2, seqs * rows, LANES), F32),
-            pltpu.SemaphoreType.DMA((len(operands) - 1 + chunks,)),
-        ],
+        scratch_shapes=[pltpu.VMEM(o.shape, o.dtype) for o in operands[2:]]
+        + [pltpu.SemaphoreType.DMA((len(operands),))],
         compiler_params=pltpu.CompilerParams(vmem_limit_bytes=16 << 20),
         cost_estimate=pl.CostEstimate(flops=1 << 25, bytes_accessed=x.size * 8, transcendentals=0),
-        name="project_own",
+        name="load",
     )(*operands)
     wire = jax.ShapeDtypeStruct((CORES, size, LANES), BF16)
     left, right = pl.pallas_call(
-        functools.partial(both_kernel, width),
+        functools.partial(project_kernel, width),
         out_shape=(wire, wire),
-        scratch_shapes=[pltpu.VMEM((2, seqs * rows, LANES), F32)],
-        compiler_params=pltpu.CompilerParams(vmem_limit_bytes=16 << 20),
-        name="project_other",
-    )(other_x, other_flags, weight, vectors, left, right)
+        scratch_shapes=[pltpu.VMEM((2, seqs * rows, LANES), F32)] * 2,
+        compiler_params=pltpu.CompilerParams(vmem_limit_bytes=16 << 20),
+        name="project",
+    )(own_x, own_flags, other_x, other_flags, weight, vectors)
 
     steps = routes(n)
     lefts = [left] + [
@@ -262,7 +259,7 @@
         for step in steps
     ]
     turned, live = pl.pallas_call(
-        functools.partial(left_kernel, seqs, rows, width),
+        functools.partial(left_kernel, steps, seqs, rows, width),
         out_shape=(jax.ShapeDtypeStruct((lanes, n * seqs), BF16), jax.ShapeDtypeStruct((rows, n * seqs), BF16)),
         scratch_shapes=[
             pltpu.VMEM((n * seqs, lanes), BF16),
@@ -272,10 +269,9 @@
         name="turn_left",
     )(*lefts)
     return pl.pallas_call(
-        functools.partial(pair_kernel, steps, seqs, rows, rows, width),
+        functools.partial(pair_kernel, seqs, rows, rows, width),
         out_shape=jax.ShapeDtypeStruct((rows, rows, outs), BF16),
         scratch_shapes=[
-            pltpu.VMEM((n * seqs, lanes), BF16),
             pltpu.VMEM((rows * rows, width * width), BF16),
             pltpu.VMEM((rows * rows, outs), F32),
         ],

time: 13.7 us -> 13.5 us (0.985)
  Pallas kernels: 3.86 us -> 3.53 us
  waiting for transfers between devices: 2.39 us -> 2.66 us
    pallas_call x4, Pallas kernels: 3.86 us -> 3.53 us  [the longest x1 1.43 us: local(): pl.pallas_call(functools.partial(pair_kernel, seqs, rows, rows, width), o...]
    ppermute x1, waiting for transfers between devices: 0.01 us -> 0.28 us  [local(): lax.ppermute(flags, 'seq', swap)]
  transfers between devices with their start and end apart: 5 -> 5, of which waited for: 2 -> 3; matrix products, arithmetic and copies ran while one was open for 0% -> 0% of each run, Pallas kernels for 14% -> 10%
where the time goes in v12:
time: 13.5 us; the launch traced here: 13.3 us
  starting transfers between devices  7.04 us (52%)
  Pallas kernels  3.53 us (26%)
  waiting for transfers between devices  2.66 us (20%)
    ppermute x2, starting transfers between devices, local(): lax.ppermute(right, axes, [(a * n + p, step[a][p] * n + a) for a in range...  3.6 us
    ppermute x1, starting transfers between devices, local(): lax.ppermute(left, 'seq', [(p, p ^ k * CORES) for p in range(n)])  2.93 us
    ppermute x2, waiting for transfers between devices, local(): lax.ppermute(right, axes, [(a * n + p, step[a][p] * n + a) for a in range...  2.38 us
    pallas_call x1, Pallas kernels, local(): pl.pallas_call(functools.partial(pair_kernel, seqs, rows, rows, width), o...  1.43 us
    pallas_call x1, Pallas kernels, local(): pl.pallas_call(load_kernel, out_shape=(jax.ShapeDtypeStruct(x.shape, x.dt...  1.04 us
    pallas_call x1, Pallas kernels, local(): pl.pallas_call(functools.partial(project_kernel, width), out_shape=(wire,...  0.78 us
    ppermute x1, starting transfers between devices, local(): lax.ppermute(x, 'seq', swap)  0.45 us
    pallas_call x1, Pallas kernels, local(): pl.pallas_call(functools.partial(left_kernel, steps, seqs, rows, width),...  0.28 us
  transfers between devices with their start and end apart: 5, of which 3 were waited for; matrix products, arithmetic and copies ran while one was open for 0% of the time, Pallas kernels for 10%

profile of v12, /device:TPU:0, one launch (start us, length us, event | category | flops | bytes accessed | tf_op | source)
XLA Modules:
  0.0 13.3 jit_solution(4748091400951151964)
XLA Ops:
  0.0 0.5 %collective-permute-start = (bf16[32,16,256]{2,1,0:T(8,128)(2,1)}, bf16[32,16,256]{2,1,0:T(8,128)(2,1)S(1)}, u32[]{:S(2)}, u32[]{:S(2)}) collective-permute-start(bf16[32,16,256]{2,1,0:T(8,128)(2,1)} %x_hbm.1), channel_id=1, source_target_pairs={{0,1},{1,0},{2,3},{3,2},{4,5},{5,4},{6,7},{7,6},{8,9},{9,8},{10,11... | collective-permute-start | bytes 786440 | tf_op jit(solution)/shard_map/ppermute | solution.py:224
  0.5 0.1 collective-permute-start.1
  0.5 1.0 %load.1 = (bf16[32,16,256]{2,1,0:T(8,128)(2,1)S(1)}, s32[16,32]{1,0:T(8,128)S(1)}, bf16[256,256]{1,0:T(8,128)(2,1)S(1)}, f32[8,256]{1,0:T(8,128)S(1)}) custom-call(bf16[32,16,256]{2,1,0:T(8,128)(2,1)} %x_hbm.1, s32[16,32]{1,0:T(8,128)} %bitcast.6, f32[256]{0:T(256)} %scale_hbm.1, f32[256]{0:T(256)} %shift_hbm.1, bf16[32,256]{1,0:T(8,128)(2,1)} %bitcast.3, ...), custom_call_target="tpu_custom_call" | custom-call | flops 33554432 | bytes 1048576 | tf_op jit(solution)/shard_map/load/pallas_call | solution.py:229
  1.6 0.3 %collective-permute-done.1.other_flag_ref = s32[16,32]{1,0:T(8,128)S(1)} collective-permute-done((s32[16,32]{1,0:T(8,128)}, s32[16,32]{1,0:T(8,128)S(1)}, u32[]{:S(2)}, u32[]{:S(2)}) %collective-permute-start.1) | collective-permute-done | bytes 2080 | tf_op jit(solution)/shard_map/ppermute | solution.py:224
  1.8 0.0 collective-permute-done.other_x_ref
  1.8 0.0 copy-start
  1.8 0.8 %project.1 = (bf16[2,144,128]{2,1,0:T(8,128)(2,1)S(1)}, bf16[2,144,128]{2,1,0:T(8,128)(2,1)S(1)}) custom-call(bf16[32,16,256]{2,1,0:T(8,128)(2,1)S(1)} %get-tuple-element.13.own_x_ref, s32[16,32]{1,0:T(8,128)S(1)} %get-tuple-element.14.own_flag_ref, bf16[32,16,256]{2,1,0:T(8,128)(2,1)S(1)} %collective-permute-done.other_x_ref, ...), custom_call_target="tpu_custom_call" | custom-call | tf_op jit(solution)/shard_map/project/pallas_call | solution.py:245
  2.6 2.9 %collective-permute-start.4 = (bf16[2,144,128]{2,1,0:T(8,128)(2,1)S(1)}, bf16[2,144,128]{2,1,0:T(8,128)(2,1)S(1)}, u32[]{:S(2)}, u32[]{:S(2)}) collective-permute-start(bf16[2,144,128]{2,1,0:T(8,128)(2,1)S(1)} %get-tuple-element.18.refs_0_), channel_id=1, source_target_pairs={{0,2},{1,3},{2,0},{3,1},{4,6},{5,7},{6,4},{7,5},{8,10},{9,11},{10,... | collective-permute-start | bytes 221192 | tf_op jit(solution)/shard_map/ppermute | solution.py:255
  5.6 3.6 %collective-permute-start.3 = (bf16[2,144,128]{2,1,0:T(8,128)(2,1)S(1)}, bf16[2,144,128]{2,1,0:T(8,128)(2,1)S(1)}, u32[]{:S(2)}, u32[]{:S(2)}) collective-permute-start(bf16[2,144,128]{2,1,0:T(8,128)(2,1)S(1)} %get-tuple-element.17), channel_id=1, source_target_pairs={{0,12},{1,4},{2,8},{3,0},{4,9},{5,13},{6,5},{7,1},{8,10},{9,2},{10... | collective-permute-start | bytes 221192 | tf_op jit(solution)/shard_map/ppermute | solution.py:258
  9.2 0.0 collective-permute-start.2
  9.2 0.0 collective-permute-done.4.refs_1_
  9.2 0.3 %turn_left.1 = (bf16[512,128]{1,0:T(8,128)(2,1)S(1)}, bf16[16,128]{1,0:T(8,128)(2,1)S(1)}) custom-call(bf16[2,144,128]{2,1,0:T(8,128)(2,1)S(1)} %get-tuple-element.18.refs_0_, bf16[2,144,128]{2,1,0:T(8,128)(2,1)S(1)} %collective-permute-done.4.refs_1_), custom_call_target="tpu_custom_call" | custom-call | tf_op jit(solution)/shard_map/turn_left/pallas_call | solution.py:261
  9.5 1.7 %collective-permute-done.3.refs_1_ = bf16[2,144,128]{2,1,0:T(8,128)(2,1)S(1)} collective-permute-done((bf16[2,144,128]{2,1,0:T(8,128)(2,1)S(1)}, bf16[2,144,128]{2,1,0:T(8,128)(2,1)S(1)}, u32[]{:S(2)}, u32[]{:S(2)}) %collective-permute-start.3) | collective-permute-done | bytes 73760 | tf_op jit(solution)/shard_map/ppermute | solution.py:258
  11.1 0.7 %collective-permute-done.2.refs_0_ = bf16[2,144,128]{2,1,0:T(8,128)(2,1)S(1)} collective-permute-done((bf16[2,144,128]{2,1,0:T(8,128)(2,1)S(1)}, bf16[2,144,128]{2,1,0:T(8,128)(2,1)S(1)}, u32[]{:S(2)}, u32[]{:S(2)}) %collective-permute-start.2) | collective-permute-done | bytes 73760 | tf_op jit(solution)/shard_map/ppermute | solution.py:258
  11.8 0.0 copy-done
  11.8 1.4 %pair.1 = bf16[16,16,128]{2,1,0:T(8,128)(2,1)} custom-call(bf16[2,144,128]{2,1,0:T(8,128)(2,1)S(1)} %collective-permute-done.2.refs_0_, bf16[2,144,128]{2,1,0:T(8,128)(2,1)S(1)} %collective-permute-done.3.refs_1_, bf16[512,128]{1,0:T(8,128)(2,1)S(1)} %get-tuple-element.19.refs_2_, bf16[16,128]{1,0:T(8,128)(2,1)S(1)} %get-tuple-element.20.refs_3_, ...), custom_call_target="tpu_custom_call" | custom-call | tf_op jit(solution)/shard_map/pair/pallas_call | solution.py:271
Async XLA Ops:
  0.0 1.8 %collective-permute-start = (bf16[32,16,256]{2,1,0:T(8,128)(2,1)}, bf16[32,16,256]{2,1,0:T(8,128)(2,1)S(1)}, u32[]{:S(2)}, u32[]{:S(2)}) collective-permute-start(bf16[32,16,256]{2,1,0:T(8,128)(2,1)} %x_hbm.1), channel_id=1, source_target_pairs={{0,1},{1,0},{2,3},{3,2},{4,5},{5,4},{6,7},{7,6},{8,9},{9,8},{10,11... | collective-permute-start | bytes 786440 | tf_op jit(solution)/shard_map/ppermute | solution.py:224
  0.5 1.4 %collective-permute-start.1 = (s32[16,32]{1,0:T(8,128)}, s32[16,32]{1,0:T(8,128)S(1)}, u32[]{:S(2)}, u32[]{:S(2)}) collective-permute-start(s32[16,32]{1,0:T(8,128)} %bitcast.5), channel_id=1, source_target_pairs={{0,1},{1,0},{2,3},{3,2},{4,5},{5,4},{6,7},{7,6},{8,9},{9,8},{10,11... | collective-permute-start | bytes 6152 | tf_op jit(solution)/shard_map/ppermute | solution.py:224
  1.8 10.0 %copy-start = (bf16[1024,128]{1,0:T(8,128)(2,1)S(1)}, bf16[1024,128]{1,0:T(8,128)(2,1)}, u32[]{:S(2)}) copy-start(bf16[1024,128]{1,0:T(8,128)(2,1)} %refs_4_.1) | copy-start | bytes 786436
  2.6 6.5 %collective-permute-start.4 = (bf16[2,144,128]{2,1,0:T(8,128)(2,1)S(1)}, bf16[2,144,128]{2,1,0:T(8,128)(2,1)S(1)}, u32[]{:S(2)}, u32[]{:S(2)}) collective-permute-start(bf16[2,144,128]{2,1,0:T(8,128)(2,1)S(1)} %get-tuple-element.18.refs_0_), channel_id=1, source_target_pairs={{0,2},{1,3},{2,0},{3,1},{4,6},{5,7},{6,4},{7,5},{8,10},{9,11},{10,... | collective-permute-start | bytes 221192 | tf_op jit(solution)/shard_map/ppermute | solution.py:255
  5.6 5.6 %collective-permute-start.3 = (bf16[2,144,128]{2,1,0:T(8,128)(2,1)S(1)}, bf16[2,144,128]{2,1,0:T(8,128)(2,1)S(1)}, u32[]{:S(2)}, u32[]{:S(2)}) collective-permute-start(bf16[2,144,128]{2,1,0:T(8,128)(2,1)S(1)} %get-tuple-element.17), channel_id=1, source_target_pairs={{0,12},{1,4},{2,8},{3,0},{4,9},{5,13},{6,5},{7,1},{8,10},{9,2},{10... | collective-permute-start | bytes 221192 | tf_op jit(solution)/shard_map/ppermute | solution.py:258
  9.2 2.7 %collective-permute-start.2 = (bf16[2,144,128]{2,1,0:T(8,128)(2,1)S(1)}, bf16[2,144,128]{2,1,0:T(8,128)(2,1)S(1)}, u32[]{:S(2)}, u32[]{:S(2)}) collective-permute-start(bf16[2,144,128]{2,1,0:T(8,128)(2,1)S(1)} %get-tuple-element.17), channel_id=1, source_target_pairs={{0,8},{1,0},{2,12},{3,4},{4,5},{5,1},{6,9},{7,13},{8,6},{9,14},{10... | collective-permute-start | bytes 221192 | tf_op jit(solution)/shard_map/ppermute | solution.py:258

commit v13 on v12

--- a/solution.py
+++ b/solution.py
@@ -58,32 +58,33 @@
 def project_block(width, x_ref, flag_ref, weight, vectors, constants, left_ref, right_ref, proj_ref):
     seqs, rows, depth = x_ref.shape
     fold = LANES // width
-    lanes = rows * width
-    data = lanes // LANES * seqs
+    assert fold == 4
+    data = rows * width // LANES * seqs
     spreader, place, mine = constants
     x = x_ref[...].astype(F32).reshape(seqs * rows, depth)
     center = jnp.mean(x, axis=-1, keepdims=True)
     x = x - center
     spread = jnp.mean(x * x, axis=-1, keepdims=True)
     normed = x * lax.rsqrt(spread + 1e-05) * vectors[0:1] + vectors[1:2]
-    both = dot(normed.astype(BF16), weight, NT) + vectors[2:3]
-    proj_ref[0] = both[:, :LANES]
-    proj_ref[1] = both[:, LANES:]
+    proj_ref[...] = dot(normed.astype(BF16), weight, NT) + vectors[2:3, :LANES]
 
     flags = flag_ref[...].astype(F32)
     mask = dot(flags.astype(BF16), spreader, TN)
     flags = jnp.concatenate([flags] * (LANES // seqs), axis=1)
-
-    for half, out_ref in ((0, left_ref), (1, right_ref)):
-        for tile in range(rows // fold):
-            merged = proj_ref[half, pl.ds(tile * fold, seqs, stride=rows), :]
-            for k in range(1, fold):
-                part = proj_ref[half, pl.ds(tile * fold + k, seqs, stride=rows), :]
-                merged = jnp.where(place == k, part, merged)
+    for tile in range(rows // fold):
+        own = [proj_ref[pl.ds(tile * fold + k, seqs, stride=rows), :] for k in range(fold)]
+        moved = [pltpu.roll(p, width, 1) for p in own]
+        for out_ref, (g0, g1, g2, g3) in (
+            (left_ref, (own[0], moved[1], own[2], moved[3])),
+            (right_ref, (moved[0], own[1], moved[2], own[3])),
+        ):
+            merged = jnp.where(place < 2, jnp.where(place == 0, g0, g1), jnp.where(place == 2, g2, g3))
             merged = merged * mask[:, tile * LANES:(tile + 1) * LANES]
             out_ref[tile * seqs:(tile + 1) * seqs, :] = merged.astype(BF16)
-        for tile, here in enumerate(mine):
-            out_ref[data + tile * rows:data + (tile + 1) * rows, :] = jnp.where(here, flags, 0.0).astype(BF16)
+    for tile, here in enumerate(mine):
+        placed = jnp.where(here, flags, 0.0).astype(BF16)
+        for out_ref in (left_ref, right_ref):
+            out_ref[data + tile * rows:data + (tile + 1) * rows, :] = placed
 
 
 def load_kernel(x_hbm, flag_hbm, scale_hbm, shift_hbm, wl_hbm, bl_hbm, wr_hbm, br_hbm, last_hbm,
@@ -102,8 +103,8 @@
         copy.wait()
     width, depth = wl_ref.shape
     fold = LANES // width
-    weight_ref[...] = jnp.concatenate([wl_ref[...]] * fold + [wr_ref[...]] * fold, axis=0)
-    bias = [bl_ref[...].reshape(1, width)] * fold + [br_ref[...].reshape(1, width)] * fold
+    weight_ref[...] = jnp.concatenate([wl_ref[...], wr_ref[...]] * (fold // 2), axis=0)
+    bias = [bl_ref[...].reshape(1, width), br_ref[...].reshape(1, width)] * (depth // width // 2)
     vector_ref[...] = jnp.concatenate(
         [
             scale_ref[...].reshape(1, depth),
@@ -231,8 +232,8 @@
         out_shape=(
             jax.ShapeDtypeStruct(x.shape, x.dtype),
             jax.ShapeDtypeStruct(flags.shape, flags.dtype),
-            jax.ShapeDtypeStruct((2 * LANES, depth), BF16),
-            jax.ShapeDtypeStruct((8, 2 * LANES), F32),
+            jax.ShapeDtypeStruct((LANES, depth), BF16),
+            jax.ShapeDtypeStruct((8, depth), F32),
         ),
         in_specs=[pl.BlockSpec(memory_space=pltpu.HBM)] * len(operands),
         scratch_shapes=[pltpu.VMEM(o.shape, o.dtype) for o in operands[2:]]
@@ -245,7 +246,7 @@
     left, right = pl.pallas_call(
         functools.partial(project_kernel, width),
         out_shape=(wire, wire),
-        scratch_shapes=[pltpu.VMEM((2, seqs * rows, LANES), F32)] * 2,
+        scratch_shapes=[pltpu.VMEM((seqs * rows, LANES), F32)] * 2,
         compiler_params=pltpu.CompilerParams(vmem_limit_bytes=16 << 20),
         name="project",
     )(own_x, own_flags, other_x, other_flags, weight, vectors)

time: 13.5 us -> 13.5 us (level)
  no operation moved by 1% of the time
where the time goes in v13:
time: 13.5 us; the launch traced here: 13.3 us
  starting transfers between devices  7.04 us (52%)
  Pallas kernels  3.56 us (26%)
  waiting for transfers between devices  2.67 us (20%)
    ppermute x2, starting transfers between devices, local(): lax.ppermute(right, axes, [(a * n + p, step[a][p] * n + a) for a in range...  3.6 us
    ppermute x1, starting transfers between devices, local(): lax.ppermute(left, 'seq', [(p, p ^ k * CORES) for p in range(n)])  2.92 us
    ppermute x2, waiting for transfers between devices, local(): lax.ppermute(right, axes, [(a * n + p, step[a][p] * n + a) for a in range...  2.38 us
    pallas_call x1, Pallas kernels, local(): pl.pallas_call(functools.partial(pair_kernel, seqs, rows, rows, width), o...  1.44 us
    pallas_call x1, Pallas kernels, local(): pl.pallas_call(load_kernel, out_shape=(jax.ShapeDtypeStruct(x.shape, x.dt...  1.04 us
    pallas_call x1, Pallas kernels, local(): pl.pallas_call(functools.partial(project_kernel, width), out_shape=(wire,...  0.8 us
    ppermute x1, starting transfers between devices, local(): lax.ppermute(x, 'seq', swap)  0.45 us
    pallas_call x1, Pallas kernels, local(): pl.pallas_call(functools.partial(left_kernel, steps, seqs, rows, width),...  0.28 us
  transfers between devices with their start and end apart: 5, of which 3 were waited for; matrix products, arithmetic and copies ran while one was open for 0% of the time, Pallas kernels for 10%

profile of v13, /device:TPU:0, one launch (start us, length us, event | category | flops | bytes accessed | tf_op | source)
XLA Modules:
  0.0 13.3 jit_solution(11128031073839418745)
XLA Ops:
  0.0 0.5 %collective-permute-start = (bf16[32,16,256]{2,1,0:T(8,128)(2,1)}, bf16[32,16,256]{2,1,0:T(8,128)(2,1)S(1)}, u32[]{:S(2)}, u32[]{:S(2)}) collective-permute-start(bf16[32,16,256]{2,1,0:T(8,128)(2,1)} %x_hbm.1), channel_id=1, source_target_pairs={{0,1},{1,0},{2,3},{3,2},{4,5},{5,4},{6,7},{7,6},{8,9},{9,8},{10,11... | collective-permute-start | bytes 786440 | tf_op jit(solution)/shard_map/ppermute | solution.py:225
  0.5 0.1 collective-permute-start.1
  0.5 1.0 %load.1 = (bf16[32,16,256]{2,1,0:T(8,128)(2,1)S(1)}, s32[16,32]{1,0:T(8,128)S(1)}, bf16[128,256]{1,0:T(8,128)(2,1)S(1)}, f32[8,256]{1,0:T(8,128)S(1)}) custom-call(bf16[32,16,256]{2,1,0:T(8,128)(2,1)} %x_hbm.1, s32[16,32]{1,0:T(8,128)} %bitcast.6, f32[256]{0:T(256)} %scale_hbm.1, f32[256]{0:T(256)} %shift_hbm.1, bf16[32,256]{1,0:T(8,128)(2,1)} %bitcast.3, ...), custom_call_target="tpu_custom_call" | custom-call | flops 33554432 | bytes 1048576 | tf_op jit(solution)/shard_map/load/pallas_call | solution.py:230
  1.6 0.3 %collective-permute-done.1.other_flag_ref = s32[16,32]{1,0:T(8,128)S(1)} collective-permute-done((s32[16,32]{1,0:T(8,128)}, s32[16,32]{1,0:T(8,128)S(1)}, u32[]{:S(2)}, u32[]{:S(2)}) %collective-permute-start.1) | collective-permute-done | bytes 2080 | tf_op jit(solution)/shard_map/ppermute | solution.py:225
  1.8 0.0 collective-permute-done.other_x_ref
  1.8 0.0 copy-start
  1.8 0.8 %project.1 = (bf16[2,144,128]{2,1,0:T(8,128)(2,1)S(1)}, bf16[2,144,128]{2,1,0:T(8,128)(2,1)S(1)}) custom-call(bf16[32,16,256]{2,1,0:T(8,128)(2,1)S(1)} %get-tuple-element.13.own_x_ref, s32[16,32]{1,0:T(8,128)S(1)} %get-tuple-element.14.own_flag_ref, bf16[32,16,256]{2,1,0:T(8,128)(2,1)S(1)} %collective-permute-done.other_x_ref, ...), custom_call_target="tpu_custom_call" | custom-call | tf_op jit(solution)/shard_map/project/pallas_call | solution.py:246
  2.6 2.9 %collective-permute-start.4 = (bf16[2,144,128]{2,1,0:T(8,128)(2,1)S(1)}, bf16[2,144,128]{2,1,0:T(8,128)(2,1)S(1)}, u32[]{:S(2)}, u32[]{:S(2)}) collective-permute-start(bf16[2,144,128]{2,1,0:T(8,128)(2,1)S(1)} %get-tuple-element.18.refs_0_), channel_id=1, source_target_pairs={{0,2},{1,3},{2,0},{3,1},{4,6},{5,7},{6,4},{7,5},{8,10},{9,11},{10,... | collective-permute-start | bytes 221192 | tf_op jit(solution)/shard_map/ppermute | solution.py:256
  5.6 3.6 %collective-permute-start.3 = (bf16[2,144,128]{2,1,0:T(8,128)(2,1)S(1)}, bf16[2,144,128]{2,1,0:T(8,128)(2,1)S(1)}, u32[]{:S(2)}, u32[]{:S(2)}) collective-permute-start(bf16[2,144,128]{2,1,0:T(8,128)(2,1)S(1)} %get-tuple-element.17), channel_id=1, source_target_pairs={{0,12},{1,4},{2,8},{3,0},{4,9},{5,13},{6,5},{7,1},{8,10},{9,2},{10... | collective-permute-start | bytes 221192 | tf_op jit(solution)/shard_map/ppermute | solution.py:259
  9.2 0.0 collective-permute-start.2
  9.2 0.0 collective-permute-done.4.refs_1_
  9.2 0.3 %turn_left.1 = (bf16[512,128]{1,0:T(8,128)(2,1)S(1)}, bf16[16,128]{1,0:T(8,128)(2,1)S(1)}) custom-call(bf16[2,144,128]{2,1,0:T(8,128)(2,1)S(1)} %get-tuple-element.18.refs_0_, bf16[2,144,128]{2,1,0:T(8,128)(2,1)S(1)} %collective-permute-done.4.refs_1_), custom_call_target="tpu_custom_call" | custom-call | tf_op jit(solution)/shard_map/turn_left/pallas_call | solution.py:262
  9.5 1.7 %collective-permute-done.3.refs_1_ = bf16[2,144,128]{2,1,0:T(8,128)(2,1)S(1)} collective-permute-done((bf16[2,144,128]{2,1,0:T(8,128)(2,1)S(1)}, bf16[2,144,128]{2,1,0:T(8,128)(2,1)S(1)}, u32[]{:S(2)}, u32[]{:S(2)}) %collective-permute-start.3) | collective-permute-done | bytes 73760 | tf_op jit(solution)/shard_map/ppermute | solution.py:259
  11.2 0.7 %collective-permute-done.2.refs_0_ = bf16[2,144,128]{2,1,0:T(8,128)(2,1)S(1)} collective-permute-done((bf16[2,144,128]{2,1,0:T(8,128)(2,1)S(1)}, bf16[2,144,128]{2,1,0:T(8,128)(2,1)S(1)}, u32[]{:S(2)}, u32[]{:S(2)}) %collective-permute-start.2) | collective-permute-done | bytes 73760 | tf_op jit(solution)/shard_map/ppermute | solution.py:259
  11.9 0.0 copy-done
  11.9 1.4 %pair.1 = bf16[16,16,128]{2,1,0:T(8,128)(2,1)} custom-call(bf16[2,144,128]{2,1,0:T(8,128)(2,1)S(1)} %collective-permute-done.2.refs_0_, bf16[2,144,128]{2,1,0:T(8,128)(2,1)S(1)} %collective-permute-done.3.refs_1_, bf16[512,128]{1,0:T(8,128)(2,1)S(1)} %get-tuple-element.19.refs_2_, bf16[16,128]{1,0:T(8,128)(2,1)S(1)} %get-tuple-element.20.refs_3_, ...), custom_call_target="tpu_custom_call" | custom-call | tf_op jit(solution)/shard_map/pair/pallas_call | solution.py:272
Async XLA Ops:
  0.0 1.8 %collective-permute-start = (bf16[32,16,256]{2,1,0:T(8,128)(2,1)}, bf16[32,16,256]{2,1,0:T(8,128)(2,1)S(1)}, u32[]{:S(2)}, u32[]{:S(2)}) collective-permute-start(bf16[32,16,256]{2,1,0:T(8,128)(2,1)} %x_hbm.1), channel_id=1, source_target_pairs={{0,1},{1,0},{2,3},{3,2},{4,5},{5,4},{6,7},{7,6},{8,9},{9,8},{10,11... | collective-permute-start | bytes 786440 | tf_op jit(solution)/shard_map/ppermute | solution.py:225
  0.5 1.4 %collective-permute-start.1 = (s32[16,32]{1,0:T(8,128)}, s32[16,32]{1,0:T(8,128)S(1)}, u32[]{:S(2)}, u32[]{:S(2)}) collective-permute-start(s32[16,32]{1,0:T(8,128)} %bitcast.5), channel_id=1, source_target_pairs={{0,1},{1,0},{2,3},{3,2},{4,5},{5,4},{6,7},{7,6},{8,9},{9,8},{10,11... | collective-permute-start | bytes 6152 | tf_op jit(solution)/shard_map/ppermute | solution.py:225
  1.8 10.0 %copy-start = (bf16[1024,128]{1,0:T(8,128)(2,1)S(1)}, bf16[1024,128]{1,0:T(8,128)(2,1)}, u32[]{:S(2)}) copy-start(bf16[1024,128]{1,0:T(8,128)(2,1)} %refs_4_.1) | copy-start | bytes 786436
  2.6 6.5 %collective-permute-start.4 = (bf16[2,144,128]{2,1,0:T(8,128)(2,1)S(1)}, bf16[2,144,128]{2,1,0:T(8,128)(2,1)S(1)}, u32[]{:S(2)}, u32[]{:S(2)}) collective-permute-start(bf16[2,144,128]{2,1,0:T(8,128)(2,1)S(1)} %get-tuple-element.18.refs_0_), channel_id=1, source_target_pairs={{0,2},{1,3},{2,0},{3,1},{4,6},{5,7},{6,4},{7,5},{8,10},{9,11},{10,... | collective-permute-start | bytes 221192 | tf_op jit(solution)/shard_map/ppermute | solution.py:256
  5.6 5.6 %collective-permute-start.3 = (bf16[2,144,128]{2,1,0:T(8,128)(2,1)S(1)}, bf16[2,144,128]{2,1,0:T(8,128)(2,1)S(1)}, u32[]{:S(2)}, u32[]{:S(2)}) collective-permute-start(bf16[2,144,128]{2,1,0:T(8,128)(2,1)S(1)} %get-tuple-element.17), channel_id=1, source_target_pairs={{0,12},{1,4},{2,8},{3,0},{4,9},{5,13},{6,5},{7,1},{8,10},{9,2},{10... | collective-permute-start | bytes 221192 | tf_op jit(solution)/shard_map/ppermute | solution.py:259
  9.2 2.7 %collective-permute-start.2 = (bf16[2,144,128]{2,1,0:T(8,128)(2,1)S(1)}, bf16[2,144,128]{2,1,0:T(8,128)(2,1)S(1)}, u32[]{:S(2)}, u32[]{:S(2)}) collective-permute-start(bf16[2,144,128]{2,1,0:T(8,128)(2,1)S(1)} %get-tuple-element.17), channel_id=1, source_target_pairs={{0,8},{1,0},{2,12},{3,4},{4,5},{5,1},{6,9},{7,13},{8,6},{9,14},{10... | collective-permute-start | bytes 221192 | tf_op jit(solution)/shard_map/ppermute | solution.py:259

commit v14 on v12

--- a/solution.py
+++ b/solution.py
@@ -164,8 +164,8 @@
 
 
 def pair_kernel(seqs, rows, columns, width, *refs):
-    rights = refs[:-7]
-    turned_ref, live_ref, w_ref, vector_ref, out_ref, flat_ref, raw_ref = refs[-7:]
+    rights = refs[:-6]
+    turned_ref, live_ref, w_ref, vector_ref, out_ref, raw_ref = refs[-6:]
     fold = LANES // width
     assert fold == 4
     data = rows * width // LANES * seqs
@@ -178,31 +178,36 @@
         ],
         axis=0,
     )
-    outer = dot(turned_ref[...], right).astype(BF16)
 
     place = (iota((rows, LANES), 1) // width).astype(BF16)
-    even = [None] * fold
-    even[1] = (place == 0.0) | (place == 2.0)
-    even[2] = (place == 0.0) | (place == 1.0)
-    for tile in range(columns // fold):
-        for quad in range(width // fold):
-            part = [
-                outer[(quad * fold + k) * rows:(quad * fold + k + 1) * rows, tile * LANES:(tile + 1) * LANES]
-                for k in range(fold)
-            ]
-            for step in (2, 1):
-                new = list(part)
+    even = {1: (place == 0.0) | (place == 2.0), 2: (place == 0.0) | (place == 1.0)}
+    quads = 2
+    passes = width // (fold * quads)
+    raw = vector_ref[3:4, :LANES]
+    for step_of in range(passes):
+        first = step_of * fold * quads * rows
+        outer = dot(turned_ref[first:first + fold * quads * rows, :], right).astype(BF16)
+        flat = [[] for _ in range(columns)]
+        for quad in range(quads):
+            for tile in range(columns // fold):
+                part = [
+                    outer[(quad * fold + k) * rows:(quad * fold + k + 1) * rows, tile * LANES:(tile + 1) * LANES]
+                    for k in range(fold)
+                ]
+                for step in (2, 1):
+                    new = list(part)
+                    for k in range(fold):
+                        if k & step == 0:
+                            x, y = part[k], part[k + step]
+                            new[k] = jnp.where(even[step], x, pltpu.roll(y, step * width, 1))
+                            new[k + step] = jnp.where(even[step], pltpu.roll(x, LANES - step * width, 1), y)
+                    part = new
                 for k in range(fold):
-                    if k & step == 0:
-                        x, y = part[k], part[k + step]
-                        new[k] = jnp.where(even[step], x, pltpu.roll(y, step * width, 1))
-                        new[k + step] = jnp.where(even[step], pltpu.roll(x, LANES - step * width, 1), y)
-                part = new
-            for k in range(fold):
-                j = tile * fold + k
-                flat_ref[j * rows:(j + 1) * rows, quad * LANES:(quad + 1) * LANES] = part[k]
-
-    raw = dot(flat_ref[...], w_ref[...]) + vector_ref[3:4, :LANES]
+                    flat[tile * fold + k].append(part[k])
+        flat = jnp.concatenate([jnp.concatenate(j, axis=1) for j in flat], axis=0)
+        first = step_of * fold * quads * width
+        raw = raw + dot(flat, w_ref[first:first + fold * quads * width, :])
+
     count = dot(live_ref[...], whole_mask(rights, rows, data), NT)
     scale = 1.0 / (1.0 + count)
     for j in range(columns):
@@ -272,7 +277,6 @@
         functools.partial(pair_kernel, seqs, rows, rows, width),
         out_shape=jax.ShapeDtypeStruct((rows, rows, outs), BF16),
         scratch_shapes=[
-            pltpu.VMEM((rows * rows, width * width), BF16),
             pltpu.VMEM((rows * rows, outs), F32),
         ],
         compiler_params=pltpu.CompilerParams(vmem_limit_bytes=16 << 20),

time: 13.5 us -> 13.7 us (1.015)
  Pallas kernels: 3.53 us -> 3.68 us
    pallas_call x1, Pallas kernels: 1.43 us -> 1.58 us  [local(): pl.pallas_call(functools.partial(pair_kernel, seqs, rows, rows, width), o...]
where the time goes in v14:
time: 13.7 us; the launch traced here: 13.4 us
  starting transfers between devices  7.04 us (51%)
  Pallas kernels  3.68 us (27%)
  waiting for transfers between devices  2.66 us (19%)
    ppermute x2, starting transfers between devices, local(): lax.ppermute(right, axes, [(a * n + p, step[a][p] * n + a) for a in range...  3.6 us
    ppermute x1, starting transfers between devices, local(): lax.ppermute(left, 'seq', [(p, p ^ k * CORES) for p in range(n)])  2.93 us
    ppermute x2, waiting for transfers between devices, local(): lax.ppermute(right, axes, [(a * n + p, step[a][p] * n + a) for a in range...  2.38 us
    pallas_call x1, Pallas kernels, local(): pl.pallas_call(functools.partial(pair_kernel, seqs, rows, rows, width), o...  1.58 us
    pallas_call x1, Pallas kernels, local(): pl.pallas_call(load_kernel, out_shape=(jax.ShapeDtypeStruct(x.shape, x.dt...  1.04 us
    pallas_call x1, Pallas kernels, local(): pl.pallas_call(functools.partial(project_kernel, width), out_shape=(wire,...  0.78 us
    ppermute x1, starting transfers between devices, local(): lax.ppermute(x, 'seq', swap)  0.45 us
    pallas_call x1, Pallas kernels, local(): pl.pallas_call(functools.partial(left_kernel, steps, seqs, rows, width),...  0.28 us
  transfers between devices with their start and end apart: 5, of which 3 were waited for; matrix products, arithmetic and copies ran while one was open for 0% of the time, Pallas kernels for 10%

profile of v14, /device:TPU:0, one launch (start us, length us, event | category | flops | bytes accessed | tf_op | source)
XLA Modules:
  0.0 13.4 jit_solution(13966247582157727319)
XLA Ops:
  0.0 0.5 %collective-permute-start = (bf16[32,16,256]{2,1,0:T(8,128)(2,1)}, bf16[32,16,256]{2,1,0:T(8,128)(2,1)S(1)}, u32[]{:S(2)}, u32[]{:S(2)}) collective-permute-start(bf16[32,16,256]{2,1,0:T(8,128)(2,1)} %x_hbm.1), channel_id=1, source_target_pairs={{0,1},{1,0},{2,3},{3,2},{4,5},{5,4},{6,7},{7,6},{8,9},{9,8},{10,11... | collective-permute-start | bytes 786440 | tf_op jit(solution)/shard_map/ppermute | solution.py:229
  0.5 0.1 collective-permute-start.1
  0.5 1.0 %load.1 = (bf16[32,16,256]{2,1,0:T(8,128)(2,1)S(1)}, s32[16,32]{1,0:T(8,128)S(1)}, bf16[256,256]{1,0:T(8,128)(2,1)S(1)}, f32[8,256]{1,0:T(8,128)S(1)}) custom-call(bf16[32,16,256]{2,1,0:T(8,128)(2,1)} %x_hbm.1, s32[16,32]{1,0:T(8,128)} %bitcast.6, f32[256]{0:T(256)} %scale_hbm.1, f32[256]{0:T(256)} %shift_hbm.1, bf16[32,256]{1,0:T(8,128)(2,1)} %bitcast.3, ...), custom_call_target="tpu_custom_call" | custom-call | flops 33554432 | bytes 1048576 | tf_op jit(solution)/shard_map/load/pallas_call | solution.py:234
  1.6 0.3 %collective-permute-done.1.other_flag_ref = s32[16,32]{1,0:T(8,128)S(1)} collective-permute-done((s32[16,32]{1,0:T(8,128)}, s32[16,32]{1,0:T(8,128)S(1)}, u32[]{:S(2)}, u32[]{:S(2)}) %collective-permute-start.1) | collective-permute-done | bytes 2080 | tf_op jit(solution)/shard_map/ppermute | solution.py:229
  1.8 0.0 collective-permute-done.other_x_ref
  1.8 0.0 copy-start
  1.8 0.8 %project.1 = (bf16[2,144,128]{2,1,0:T(8,128)(2,1)S(1)}, bf16[2,144,128]{2,1,0:T(8,128)(2,1)S(1)}) custom-call(bf16[32,16,256]{2,1,0:T(8,128)(2,1)S(1)} %get-tuple-element.13.own_x_ref, s32[16,32]{1,0:T(8,128)S(1)} %get-tuple-element.14.own_flag_ref, bf16[32,16,256]{2,1,0:T(8,128)(2,1)S(1)} %collective-permute-done.other_x_ref, ...), custom_call_target="tpu_custom_call" | custom-call | tf_op jit(solution)/shard_map/project/pallas_call | solution.py:250
  2.6 2.9 %collective-permute-start.4 = (bf16[2,144,128]{2,1,0:T(8,128)(2,1)S(1)}, bf16[2,144,128]{2,1,0:T(8,128)(2,1)S(1)}, u32[]{:S(2)}, u32[]{:S(2)}) collective-permute-start(bf16[2,144,128]{2,1,0:T(8,128)(2,1)S(1)} %get-tuple-element.18.refs_0_), channel_id=1, source_target_pairs={{0,2},{1,3},{2,0},{3,1},{4,6},{5,7},{6,4},{7,5},{8,10},{9,11},{10,... | collective-permute-start | bytes 221192 | tf_op jit(solution)/shard_map/ppermute | solution.py:260
  5.6 3.6 %collective-permute-start.3 = (bf16[2,144,128]{2,1,0:T(8,128)(2,1)S(1)}, bf16[2,144,128]{2,1,0:T(8,128)(2,1)S(1)}, u32[]{:S(2)}, u32[]{:S(2)}) collective-permute-start(bf16[2,144,128]{2,1,0:T(8,128)(2,1)S(1)} %get-tuple-element.17), channel_id=1, source_target_pairs={{0,12},{1,4},{2,8},{3,0},{4,9},{5,13},{6,5},{7,1},{8,10},{9,2},{10... | collective-permute-start | bytes 221192 | tf_op jit(solution)/shard_map/ppermute | solution.py:263
  9.2 0.0 collective-permute-start.2
  9.2 0.0 collective-permute-done.4.refs_1_
  9.2 0.3 %turn_left.1 = (bf16[512,128]{1,0:T(8,128)(2,1)S(1)}, bf16[16,128]{1,0:T(8,128)(2,1)S(1)}) custom-call(bf16[2,144,128]{2,1,0:T(8,128)(2,1)S(1)} %get-tuple-element.18.refs_0_, bf16[2,144,128]{2,1,0:T(8,128)(2,1)S(1)} %collective-permute-done.4.refs_1_), custom_call_target="tpu_custom_call" | custom-call | tf_op jit(solution)/shard_map/turn_left/pallas_call | solution.py:266
  9.5 1.7 %collective-permute-done.3.refs_1_ = bf16[2,144,128]{2,1,0:T(8,128)(2,1)S(1)} collective-permute-done((bf16[2,144,128]{2,1,0:T(8,128)(2,1)S(1)}, bf16[2,144,128]{2,1,0:T(8,128)(2,1)S(1)}, u32[]{:S(2)}, u32[]{:S(2)}) %collective-permute-start.3) | collective-permute-done | bytes 73760 | tf_op jit(solution)/shard_map/ppermute | solution.py:263
  11.1 0.7 %collective-permute-done.2.refs_0_ = bf16[2,144,128]{2,1,0:T(8,128)(2,1)S(1)} collective-permute-done((bf16[2,144,128]{2,1,0:T(8,128)(2,1)S(1)}, bf16[2,144,128]{2,1,0:T(8,128)(2,1)S(1)}, u32[]{:S(2)}, u32[]{:S(2)}) %collective-permute-start.2) | collective-permute-done | bytes 73760 | tf_op jit(solution)/shard_map/ppermute | solution.py:263
  11.8 0.0 copy-done
  11.8 1.6 %pair.1 = bf16[16,16,128]{2,1,0:T(8,128)(2,1)} custom-call(bf16[2,144,128]{2,1,0:T(8,128)(2,1)S(1)} %collective-permute-done.2.refs_0_, bf16[2,144,128]{2,1,0:T(8,128)(2,1)S(1)} %collective-permute-done.3.refs_1_, bf16[512,128]{1,0:T(8,128)(2,1)S(1)} %get-tuple-element.19.refs_2_, bf16[16,128]{1,0:T(8,128)(2,1)S(1)} %get-tuple-element.20.refs_3_, ...), custom_call_target="tpu_custom_call" | custom-call | tf_op jit(solution)/shard_map/pair/pallas_call | solution.py:276
Async XLA Ops:
  0.0 1.8 %collective-permute-start = (bf16[32,16,256]{2,1,0:T(8,128)(2,1)}, bf16[32,16,256]{2,1,0:T(8,128)(2,1)S(1)}, u32[]{:S(2)}, u32[]{:S(2)}) collective-permute-start(bf16[32,16,256]{2,1,0:T(8,128)(2,1)} %x_hbm.1), channel_id=1, source_target_pairs={{0,1},{1,0},{2,3},{3,2},{4,5},{5,4},{6,7},{7,6},{8,9},{9,8},{10,11... | collective-permute-start | bytes 786440 | tf_op jit(solution)/shard_map/ppermute | solution.py:229
  0.5 1.4 %collective-permute-start.1 = (s32[16,32]{1,0:T(8,128)}, s32[16,32]{1,0:T(8,128)S(1)}, u32[]{:S(2)}, u32[]{:S(2)}) collective-permute-start(s32[16,32]{1,0:T(8,128)} %bitcast.5), channel_id=1, source_target_pairs={{0,1},{1,0},{2,3},{3,2},{4,5},{5,4},{6,7},{7,6},{8,9},{9,8},{10,11... | collective-permute-start | bytes 6152 | tf_op jit(solution)/shard_map/ppermute | solution.py:229
  1.8 10.0 %copy-start = (bf16[1024,128]{1,0:T(8,128)(2,1)S(1)}, bf16[1024,128]{1,0:T(8,128)(2,1)}, u32[]{:S(2)}) copy-start(bf16[1024,128]{1,0:T(8,128)(2,1)} %refs_4_.1) | copy-start | bytes 786436
  2.6 6.5 %collective-permute-start.4 = (bf16[2,144,128]{2,1,0:T(8,128)(2,1)S(1)}, bf16[2,144,128]{2,1,0:T(8,128)(2,1)S(1)}, u32[]{:S(2)}, u32[]{:S(2)}) collective-permute-start(bf16[2,144,128]{2,1,0:T(8,128)(2,1)S(1)} %get-tuple-element.18.refs_0_), channel_id=1, source_target_pairs={{0,2},{1,3},{2,0},{3,1},{4,6},{5,7},{6,4},{7,5},{8,10},{9,11},{10,... | collective-permute-start | bytes 221192 | tf_op jit(solution)/shard_map/ppermute | solution.py:260
  5.6 5.6 %collective-permute-start.3 = (bf16[2,144,128]{2,1,0:T(8,128)(2,1)S(1)}, bf16[2,144,128]{2,1,0:T(8,128)(2,1)S(1)}, u32[]{:S(2)}, u32[]{:S(2)}) collective-permute-start(bf16[2,144,128]{2,1,0:T(8,128)(2,1)S(1)} %get-tuple-element.17), channel_id=1, source_target_pairs={{0,12},{1,4},{2,8},{3,0},{4,9},{5,13},{6,5},{7,1},{8,10},{9,2},{10... | collective-permute-start | bytes 221192 | tf_op jit(solution)/shard_map/ppermute | solution.py:263
  9.2 2.7 %collective-permute-start.2 = (bf16[2,144,128]{2,1,0:T(8,128)(2,1)S(1)}, bf16[2,144,128]{2,1,0:T(8,128)(2,1)S(1)}, u32[]{:S(2)}, u32[]{:S(2)}) collective-permute-start(bf16[2,144,128]{2,1,0:T(8,128)(2,1)S(1)} %get-tuple-element.17), channel_id=1, source_target_pairs={{0,8},{1,0},{2,12},{3,4},{4,5},{5,1},{6,9},{7,13},{8,6},{9,14},{10... | collective-permute-start | bytes 221192 | tf_op jit(solution)/shard_map/ppermute | solution.py:263

commit v15 on v12

--- a/solution.py
+++ b/solution.py
@@ -24,17 +24,24 @@
     return lax.broadcasted_iota(jnp.int32, shape, dim)
 
 
-ROUTES = (
-    ((2, 0, 3, 1), (1, 0, 2, 3), (1, 3, 0, 2), (1, 3, 0, 2)),
-    ((3, 1, 2, 0), (2, 3, 1, 0), (2, 0, 3, 1), (2, 0, 3, 1)),
+RIGHT = (
+    ((1, 0, 2, 3), (0, 2, 1, 3), (3, 1, 0, 2), (2, 1, 3, 0)),
+    ((3, 2, 1, 0), (1, 3, 2, 0), (0, 2, 3, 1), (3, 0, 2, 1)),
 )
-
-
-def routes(n):
+LEFT = ((3, 2, 1, 0), (3, 2, 0, 1), (3, 2, 0, 1), (2, 3, 0, 1))
+
+
+def right_routes(n):
     if n == 4:
-        return ROUTES
+        return RIGHT
     steps = [m for m in range(n) if bin(m).count("1") % 2 == 1]
     return tuple(tuple(tuple(p ^ m for p in range(n)) for a in range(n)) for m in steps)
+
+
+def left_routes(n):
+    if n == 4:
+        return (LEFT,)
+    return tuple(tuple(tuple(p ^ k * CORES for p in range(n)) for a in range(n)) for k in range(1, n // CORES))
 
 
 def sending_chip(step, r, q):
@@ -61,9 +68,9 @@
     lanes = rows * width
     data = lanes // LANES * seqs
     spreader, place, mine = constants
-    x = x_ref[...].astype(F32).reshape(seqs * rows, depth)
-    center = jnp.mean(x, axis=-1, keepdims=True)
-    x = x - center
+    x = x_ref[...].reshape(seqs * rows, depth)
+    center = dot(x, jnp.full((depth, LANES), 1.0 / depth, BF16))
+    x = x.astype(F32) - jnp.concatenate([center] * (depth // LANES), axis=1)
     spread = jnp.mean(x * x, axis=-1, keepdims=True)
     normed = x * lax.rsqrt(spread + 1e-05) * vectors[0:1] + vectors[1:2]
     both = dot(normed.astype(BF16), weight, NT) + vectors[2:3]
@@ -250,9 +257,10 @@
         name="project",
     )(own_x, own_flags, other_x, other_flags, weight, vectors)
 
-    steps = routes(n)
+    steps = right_routes(n)
     lefts = [left] + [
-        lax.ppermute(left, "seq", [(p, p ^ k * CORES) for p in range(n)]) for k in range(1, n // CORES)
+        lax.ppermute(left, axes, [(a * n + p, a * n + step[a][p]) for a in range(n) for p in range(n)])
+        for step in left_routes(n)
     ]
     rights = [
         lax.ppermute(right, axes, [(a * n + p, step[a][p] * n + a) for a in range(n) for p in range(n)])

time: 13.5 us -> 13.7 us (1.015)
  Pallas kernels: 3.53 us -> 3.77 us
    ppermute x2, starting transfers between devices: 3.6 us -> 3.9 us  [local(): lax.ppermute(right, axes, [(a * n + p, step[a][p] * n + a) for a in range...]
    ppermute x1, starting transfers between devices: 2.93 us -> 2.65 us  [local(): lax.ppermute(left, axes, [(a * n + p, a * n + step[a][p]) for a in range(...]
    pallas_call x1, Pallas kernels: 0.78 us -> 1.02 us  [local(): pl.pallas_call(functools.partial(project_kernel, width), out_shape=(wire,...]
where the time goes in v15:
time: 13.7 us; the launch traced here: 13.5 us
  starting transfers between devices  7.05 us (51%)
  Pallas kernels  3.77 us (28%)
  waiting for transfers between devices  2.66 us (19%)
    ppermute x2, starting transfers between devices, local(): lax.ppermute(right, axes, [(a * n + p, step[a][p] * n + a) for a in range...  3.9 us
    ppermute x1, starting transfers between devices, local(): lax.ppermute(left, axes, [(a * n + p, a * n + step[a][p]) for a in range(...  2.65 us
    ppermute x2, waiting for transfers between devices, local(): lax.ppermute(right, axes, [(a * n + p, step[a][p] * n + a) for a in range...  2.38 us
    pallas_call x1, Pallas kernels, local(): pl.pallas_call(functools.partial(pair_kernel, seqs, rows, rows, width), o...  1.43 us
    pallas_call x1, Pallas kernels, local(): pl.pallas_call(load_kernel, out_shape=(jax.ShapeDtypeStruct(x.shape, x.dt...  1.04 us
    pallas_call x1, Pallas kernels, local(): pl.pallas_call(functools.partial(project_kernel, width), out_shape=(wire,...  1.02 us
    ppermute x1, starting transfers between devices, local(): lax.ppermute(x, 'seq', swap)  0.45 us
    pallas_call x1, Pallas kernels, local(): pl.pallas_call(functools.partial(left_kernel, steps, seqs, rows, width),...  0.29 us
  transfers between devices with their start and end apart: 5, of which 3 were waited for; matrix products, arithmetic and copies ran while one was open for 0% of the time, Pallas kernels for 10%

profile of v15, /device:TPU:0, one launch (start us, length us, event | category | flops | bytes accessed | tf_op | source)
XLA Modules:
  0.0 13.5 jit_solution(12424492216477034548)
XLA Ops:
  0.0 0.5 %collective-permute-start = (bf16[32,16,256]{2,1,0:T(8,128)(2,1)}, bf16[32,16,256]{2,1,0:T(8,128)(2,1)S(1)}, u32[]{:S(2)}, u32[]{:S(2)}) collective-permute-start(bf16[32,16,256]{2,1,0:T(8,128)(2,1)} %x_hbm.1), channel_id=1, source_target_pairs={{0,1},{1,0},{2,3},{3,2},{4,5},{5,4},{6,7},{7,6},{8,9},{9,8},{10,11... | collective-permute-start | bytes 786440 | tf_op jit(solution)/shard_map/ppermute | solution.py:231
  0.5 0.1 collective-permute-start.1
  0.5 1.0 %load.1 = (bf16[32,16,256]{2,1,0:T(8,128)(2,1)S(1)}, s32[16,32]{1,0:T(8,128)S(1)}, bf16[256,256]{1,0:T(8,128)(2,1)S(1)}, f32[8,256]{1,0:T(8,128)S(1)}) custom-call(bf16[32,16,256]{2,1,0:T(8,128)(2,1)} %x_hbm.1, s32[16,32]{1,0:T(8,128)} %bitcast.6, f32[256]{0:T(256)} %scale_hbm.1, f32[256]{0:T(256)} %shift_hbm.1, bf16[32,256]{1,0:T(8,128)(2,1)} %bitcast.3, ...), custom_call_target="tpu_custom_call" | custom-call | flops 33554432 | bytes 1048576 | tf_op jit(solution)/shard_map/load/pallas_call | solution.py:236
  1.6 0.3 %collective-permute-done.1.other_flag_ref = s32[16,32]{1,0:T(8,128)S(1)} collective-permute-done((s32[16,32]{1,0:T(8,128)}, s32[16,32]{1,0:T(8,128)S(1)}, u32[]{:S(2)}, u32[]{:S(2)}) %collective-permute-start.1) | collective-permute-done | bytes 2080 | tf_op jit(solution)/shard_map/ppermute | solution.py:231
  1.8 0.0 collective-permute-done.other_x_ref
  1.8 0.0 copy-start
  1.8 1.0 %project.1 = (bf16[2,144,128]{2,1,0:T(8,128)(2,1)S(1)}, bf16[2,144,128]{2,1,0:T(8,128)(2,1)S(1)}) custom-call(bf16[32,16,256]{2,1,0:T(8,128)(2,1)S(1)} %get-tuple-element.13.own_x_ref, s32[16,32]{1,0:T(8,128)S(1)} %get-tuple-element.14.own_flag_ref, bf16[32,16,256]{2,1,0:T(8,128)(2,1)S(1)} %collective-permute-done.other_x_ref, ...), custom_call_target="tpu_custom_call" | custom-call | tf_op jit(solution)/shard_map/project/pallas_call | solution.py:252
  2.9 2.6 %collective-permute-start.4 = (bf16[2,144,128]{2,1,0:T(8,128)(2,1)S(1)}, bf16[2,144,128]{2,1,0:T(8,128)(2,1)S(1)}, u32[]{:S(2)}, u32[]{:S(2)}) collective-permute-start(bf16[2,144,128]{2,1,0:T(8,128)(2,1)S(1)} %get-tuple-element.18.refs_0_), channel_id=1, source_target_pairs={{0,3},{1,2},{2,1},{3,0},{4,7},{5,6},{6,4},{7,5},{8,11},{9,10},{10,... | collective-permute-start | bytes 221192 | tf_op jit(solution)/shard_map/ppermute | solution.py:262
  5.5 3.9 %collective-permute-start.3 = (bf16[2,144,128]{2,1,0:T(8,128)(2,1)S(1)}, bf16[2,144,128]{2,1,0:T(8,128)(2,1)S(1)}, u32[]{:S(2)}, u32[]{:S(2)}) collective-permute-start(bf16[2,144,128]{2,1,0:T(8,128)(2,1)S(1)} %get-tuple-element.17), channel_id=1, source_target_pairs={{0,12},{1,8},{2,4},{3,0},{4,5},{5,13},{6,9},{7,1},{8,2},{9,10},{10... | collective-permute-start | bytes 221192 | tf_op jit(solution)/shard_map/ppermute | solution.py:266
  9.4 0.0 collective-permute-start.2
  9.4 0.0 collective-permute-done.4.refs_1_
  9.4 0.3 %turn_left.1 = (bf16[512,128]{1,0:T(8,128)(2,1)S(1)}, bf16[16,128]{1,0:T(8,128)(2,1)S(1)}) custom-call(bf16[2,144,128]{2,1,0:T(8,128)(2,1)S(1)} %get-tuple-element.18.refs_0_, bf16[2,144,128]{2,1,0:T(8,128)(2,1)S(1)} %collective-permute-done.4.refs_1_), custom_call_target="tpu_custom_call" | custom-call | tf_op jit(solution)/shard_map/turn_left/pallas_call | solution.py:269
  9.7 1.7 %collective-permute-done.3.refs_1_ = bf16[2,144,128]{2,1,0:T(8,128)(2,1)S(1)} collective-permute-done((bf16[2,144,128]{2,1,0:T(8,128)(2,1)S(1)}, bf16[2,144,128]{2,1,0:T(8,128)(2,1)S(1)}, u32[]{:S(2)}, u32[]{:S(2)}) %collective-permute-start.3) | collective-permute-done | bytes 73760 | tf_op jit(solution)/shard_map/ppermute | solution.py:266
  11.4 0.7 %collective-permute-done.2.refs_0_ = bf16[2,144,128]{2,1,0:T(8,128)(2,1)S(1)} collective-permute-done((bf16[2,144,128]{2,1,0:T(8,128)(2,1)S(1)}, bf16[2,144,128]{2,1,0:T(8,128)(2,1)S(1)}, u32[]{:S(2)}, u32[]{:S(2)}) %collective-permute-start.2) | collective-permute-done | bytes 73760 | tf_op jit(solution)/shard_map/ppermute | solution.py:266
  12.1 0.0 copy-done
  12.1 1.4 %pair.1 = bf16[16,16,128]{2,1,0:T(8,128)(2,1)} custom-call(bf16[2,144,128]{2,1,0:T(8,128)(2,1)S(1)} %collective-permute-done.2.refs_0_, bf16[2,144,128]{2,1,0:T(8,128)(2,1)S(1)} %collective-permute-done.3.refs_1_, bf16[512,128]{1,0:T(8,128)(2,1)S(1)} %get-tuple-element.19.refs_2_, bf16[16,128]{1,0:T(8,128)(2,1)S(1)} %get-tuple-element.20.refs_3_, ...), custom_call_target="tpu_custom_call" | custom-call | tf_op jit(solution)/shard_map/pair/pallas_call | solution.py:279
Async XLA Ops:
  0.0 1.8 %collective-permute-start = (bf16[32,16,256]{2,1,0:T(8,128)(2,1)}, bf16[32,16,256]{2,1,0:T(8,128)(2,1)S(1)}, u32[]{:S(2)}, u32[]{:S(2)}) collective-permute-start(bf16[32,16,256]{2,1,0:T(8,128)(2,1)} %x_hbm.1), channel_id=1, source_target_pairs={{0,1},{1,0},{2,3},{3,2},{4,5},{5,4},{6,7},{7,6},{8,9},{9,8},{10,11... | collective-permute-start | bytes 786440 | tf_op jit(solution)/shard_map/ppermute | solution.py:231
  0.5 1.4 %collective-permute-start.1 = (s32[16,32]{1,0:T(8,128)}, s32[16,32]{1,0:T(8,128)S(1)}, u32[]{:S(2)}, u32[]{:S(2)}) collective-permute-start(s32[16,32]{1,0:T(8,128)} %bitcast.5), channel_id=1, source_target_pairs={{0,1},{1,0},{2,3},{3,2},{4,5},{5,4},{6,7},{7,6},{8,9},{9,8},{10,11... | collective-permute-start | bytes 6152 | tf_op jit(solution)/shard_map/ppermute | solution.py:231
  1.8 10.2 %copy-start = (bf16[1024,128]{1,0:T(8,128)(2,1)S(1)}, bf16[1024,128]{1,0:T(8,128)(2,1)}, u32[]{:S(2)}) copy-start(bf16[1024,128]{1,0:T(8,128)(2,1)} %refs_4_.1) | copy-start | bytes 786436
  2.9 6.5 %collective-permute-start.4 = (bf16[2,144,128]{2,1,0:T(8,128)(2,1)S(1)}, bf16[2,144,128]{2,1,0:T(8,128)(2,1)S(1)}, u32[]{:S(2)}, u32[]{:S(2)}) collective-permute-start(bf16[2,144,128]{2,1,0:T(8,128)(2,1)S(1)} %get-tuple-element.18.refs_0_), channel_id=1, source_target_pairs={{0,3},{1,2},{2,1},{3,0},{4,7},{5,6},{6,4},{7,5},{8,11},{9,10},{10,... | collective-permute-start | bytes 221192 | tf_op jit(solution)/shard_map/ppermute | solution.py:262
  5.5 5.9 %collective-permute-start.3 = (bf16[2,144,128]{2,1,0:T(8,128)(2,1)S(1)}, bf16[2,144,128]{2,1,0:T(8,128)(2,1)S(1)}, u32[]{:S(2)}, u32[]{:S(2)}) collective-permute-start(bf16[2,144,128]{2,1,0:T(8,128)(2,1)S(1)} %get-tuple-element.17), channel_id=1, source_target_pairs={{0,12},{1,8},{2,4},{3,0},{4,5},{5,13},{6,9},{7,1},{8,2},{9,10},{10... | collective-permute-start | bytes 221192 | tf_op jit(solution)/shard_map/ppermute | solution.py:266
  9.4 2.7 %collective-permute-start.2 = (bf16[2,144,128]{2,1,0:T(8,128)(2,1)S(1)}, bf16[2,144,128]{2,1,0:T(8,128)(2,1)S(1)}, u32[]{:S(2)}, u32[]{:S(2)}) collective-permute-start(bf16[2,144,128]{2,1,0:T(8,128)(2,1)S(1)} %get-tuple-element.17), channel_id=1, source_target_pairs={{0,4},{1,0},{2,8},{3,12},{4,1},{5,9},{6,5},{7,13},{8,14},{9,6},{10... | collective-permute-start | bytes 221192 | tf_op jit(solution)/shard_map/ppermute | solution.py:266

commit v16 on v15

--- a/solution.py
+++ b/solution.py
@@ -68,9 +68,9 @@
     lanes = rows * width
     data = lanes // LANES * seqs
     spreader, place, mine = constants
-    x = x_ref[...].reshape(seqs * rows, depth)
-    center = dot(x, jnp.full((depth, LANES), 1.0 / depth, BF16))
-    x = x.astype(F32) - jnp.concatenate([center] * (depth // LANES), axis=1)
+    x = x_ref[...].astype(F32).reshape(seqs * rows, depth)
+    center = jnp.mean(x, axis=-1, keepdims=True)
+    x = x - center
     spread = jnp.mean(x * x, axis=-1, keepdims=True)
     normed = x * lax.rsqrt(spread + 1e-05) * vectors[0:1] + vectors[1:2]
     both = dot(normed.astype(BF16), weight, NT) + vectors[2:3]

time: 13.7 us -> 13.4 us (0.978)
  Pallas kernels: 3.77 us -> 3.54 us
    pallas_call x1, Pallas kernels: 1.02 us -> 0.78 us  [local(): pl.pallas_call(functools.partial(project_kernel, width), out_shape=(wire,...]
where the time goes in v16:
time: 13.4 us; the launch traced here: 13.3 us
  starting transfers between devices  7.05 us (53%)
  Pallas kernels  3.54 us (26%)
  waiting for transfers between devices  2.66 us (20%)
    ppermute x2, starting transfers between devices, local(): lax.ppermute(right, axes, [(a * n + p, step[a][p] * n + a) for a in range...  3.9 us
    ppermute x1, starting transfers between devices, local(): lax.ppermute(left, axes, [(a * n + p, a * n + step[a][p]) for a in range(...  2.65 us
    ppermute x2, waiting for transfers between devices, local(): lax.ppermute(right, axes, [(a * n + p, step[a][p] * n + a) for a in range...  2.38 us
    pallas_call x1, Pallas kernels, local(): pl.pallas_call(functools.partial(pair_kernel, seqs, rows, rows, width), o...  1.44 us
    pallas_call x1, Pallas kernels, local(): pl.pallas_call(load_kernel, out_shape=(jax.ShapeDtypeStruct(x.shape, x.dt...  1.04 us
    pallas_call x1, Pallas kernels, local(): pl.pallas_call(functools.partial(project_kernel, width), out_shape=(wire,...  0.78 us
    ppermute x1, starting transfers between devices, local(): lax.ppermute(x, 'seq', swap)  0.45 us
    pallas_call x1, Pallas kernels, local(): pl.pallas_call(functools.partial(left_kernel, steps, seqs, rows, width),...  0.29 us
  transfers between devices with their start and end apart: 5, of which 3 were waited for; matrix products, arithmetic and copies ran while one was open for 0% of the time, Pallas kernels for 10%

profile of v16, /device:TPU:0, one launch (start us, length us, event | category | flops | bytes accessed | tf_op | source)
XLA Modules:
  0.0 13.3 jit_solution(5036159011535095935)
XLA Ops:
  0.0 0.5 %collective-permute-start = (bf16[32,16,256]{2,1,0:T(8,128)(2,1)}, bf16[32,16,256]{2,1,0:T(8,128)(2,1)S(1)}, u32[]{:S(2)}, u32[]{:S(2)}) collective-permute-start(bf16[32,16,256]{2,1,0:T(8,128)(2,1)} %x_hbm.1), channel_id=1, source_target_pairs={{0,1},{1,0},{2,3},{3,2},{4,5},{5,4},{6,7},{7,6},{8,9},{9,8},{10,11... | collective-permute-start | bytes 786440 | tf_op jit(solution)/shard_map/ppermute | solution.py:231
  0.5 0.1 collective-permute-start.1
  0.5 1.0 %load.1 = (bf16[32,16,256]{2,1,0:T(8,128)(2,1)S(1)}, s32[16,32]{1,0:T(8,128)S(1)}, bf16[256,256]{1,0:T(8,128)(2,1)S(1)}, f32[8,256]{1,0:T(8,128)S(1)}) custom-call(bf16[32,16,256]{2,1,0:T(8,128)(2,1)} %x_hbm.1, s32[16,32]{1,0:T(8,128)} %bitcast.6, f32[256]{0:T(256)} %scale_hbm.1, f32[256]{0:T(256)} %shift_hbm.1, bf16[32,256]{1,0:T(8,128)(2,1)} %bitcast.3, ...), custom_call_target="tpu_custom_call" | custom-call | flops 33554432 | bytes 1048576 | tf_op jit(solution)/shard_map/load/pallas_call | solution.py:236
  1.6 0.3 %collective-permute-done.1.other_flag_ref = s32[16,32]{1,0:T(8,128)S(1)} collective-permute-done((s32[16,32]{1,0:T(8,128)}, s32[16,32]{1,0:T(8,128)S(1)}, u32[]{:S(2)}, u32[]{:S(2)}) %collective-permute-start.1) | collective-permute-done | bytes 2080 | tf_op jit(solution)/shard_map/ppermute | solution.py:231
  1.8 0.0 collective-permute-done.other_x_ref
  1.8 0.0 copy-start
  1.8 0.8 %project.1 = (bf16[2,144,128]{2,1,0:T(8,128)(2,1)S(1)}, bf16[2,144,128]{2,1,0:T(8,128)(2,1)S(1)}) custom-call(bf16[32,16,256]{2,1,0:T(8,128)(2,1)S(1)} %get-tuple-element.13.own_x_ref, s32[16,32]{1,0:T(8,128)S(1)} %get-tuple-element.14.own_flag_ref, bf16[32,16,256]{2,1,0:T(8,128)(2,1)S(1)} %collective-permute-done.other_x_ref, ...), custom_call_target="tpu_custom_call" | custom-call | tf_op jit(solution)/shard_map/project/pallas_call | solution.py:252
  2.6 2.6 %collective-permute-start.4 = (bf16[2,144,128]{2,1,0:T(8,128)(2,1)S(1)}, bf16[2,144,128]{2,1,0:T(8,128)(2,1)S(1)}, u32[]{:S(2)}, u32[]{:S(2)}) collective-permute-start(bf16[2,144,128]{2,1,0:T(8,128)(2,1)S(1)} %get-tuple-element.18.refs_0_), channel_id=1, source_target_pairs={{0,3},{1,2},{2,1},{3,0},{4,7},{5,6},{6,4},{7,5},{8,11},{9,10},{10,... | collective-permute-start | bytes 221192 | tf_op jit(solution)/shard_map/ppermute | solution.py:262
  5.3 3.9 %collective-permute-start.3 = (bf16[2,144,128]{2,1,0:T(8,128)(2,1)S(1)}, bf16[2,144,128]{2,1,0:T(8,128)(2,1)S(1)}, u32[]{:S(2)}, u32[]{:S(2)}) collective-permute-start(bf16[2,144,128]{2,1,0:T(8,128)(2,1)S(1)} %get-tuple-element.17), channel_id=1, source_target_pairs={{0,12},{1,8},{2,4},{3,0},{4,5},{5,13},{6,9},{7,1},{8,2},{9,10},{10... | collective-permute-start | bytes 221192 | tf_op jit(solution)/shard_map/ppermute | solution.py:266
  9.2 0.0 collective-permute-start.2
  9.2 0.0 collective-permute-done.4.refs_1_
  9.2 0.3 %turn_left.1 = (bf16[512,128]{1,0:T(8,128)(2,1)S(1)}, bf16[16,128]{1,0:T(8,128)(2,1)S(1)}) custom-call(bf16[2,144,128]{2,1,0:T(8,128)(2,1)S(1)} %get-tuple-element.18.refs_0_, bf16[2,144,128]{2,1,0:T(8,128)(2,1)S(1)} %collective-permute-done.4.refs_1_), custom_call_target="tpu_custom_call" | custom-call | tf_op jit(solution)/shard_map/turn_left/pallas_call | solution.py:269
  9.5 1.7 %collective-permute-done.3.refs_1_ = bf16[2,144,128]{2,1,0:T(8,128)(2,1)S(1)} collective-permute-done((bf16[2,144,128]{2,1,0:T(8,128)(2,1)S(1)}, bf16[2,144,128]{2,1,0:T(8,128)(2,1)S(1)}, u32[]{:S(2)}, u32[]{:S(2)}) %collective-permute-start.3) | collective-permute-done | bytes 73760 | tf_op jit(solution)/shard_map/ppermute | solution.py:266
  11.2 0.7 %collective-permute-done.2.refs_0_ = bf16[2,144,128]{2,1,0:T(8,128)(2,1)S(1)} collective-permute-done((bf16[2,144,128]{2,1,0:T(8,128)(2,1)S(1)}, bf16[2,144,128]{2,1,0:T(8,128)(2,1)S(1)}, u32[]{:S(2)}, u32[]{:S(2)}) %collective-permute-start.2) | collective-permute-done | bytes 73760 | tf_op jit(solution)/shard_map/ppermute | solution.py:266
  11.8 0.0 copy-done
  11.9 1.4 %pair.1 = bf16[16,16,128]{2,1,0:T(8,128)(2,1)} custom-call(bf16[2,144,128]{2,1,0:T(8,128)(2,1)S(1)} %collective-permute-done.2.refs_0_, bf16[2,144,128]{2,1,0:T(8,128)(2,1)S(1)} %collective-permute-done.3.refs_1_, bf16[512,128]{1,0:T(8,128)(2,1)S(1)} %get-tuple-element.19.refs_2_, bf16[16,128]{1,0:T(8,128)(2,1)S(1)} %get-tuple-element.20.refs_3_, ...), custom_call_target="tpu_custom_call" | custom-call | tf_op jit(solution)/shard_map/pair/pallas_call | solution.py:279
Async XLA Ops:
  0.0 1.8 %collective-permute-start = (bf16[32,16,256]{2,1,0:T(8,128)(2,1)}, bf16[32,16,256]{2,1,0:T(8,128)(2,1)S(1)}, u32[]{:S(2)}, u32[]{:S(2)}) collective-permute-start(bf16[32,16,256]{2,1,0:T(8,128)(2,1)} %x_hbm.1), channel_id=1, source_target_pairs={{0,1},{1,0},{2,3},{3,2},{4,5},{5,4},{6,7},{7,6},{8,9},{9,8},{10,11... | collective-permute-start | bytes 786440 | tf_op jit(solution)/shard_map/ppermute | solution.py:231
  0.5 1.4 %collective-permute-start.1 = (s32[16,32]{1,0:T(8,128)}, s32[16,32]{1,0:T(8,128)S(1)}, u32[]{:S(2)}, u32[]{:S(2)}) collective-permute-start(s32[16,32]{1,0:T(8,128)} %bitcast.5), channel_id=1, source_target_pairs={{0,1},{1,0},{2,3},{3,2},{4,5},{5,4},{6,7},{7,6},{8,9},{9,8},{10,11... | collective-permute-start | bytes 6152 | tf_op jit(solution)/shard_map/ppermute | solution.py:231
  1.8 10.0 %copy-start = (bf16[1024,128]{1,0:T(8,128)(2,1)S(1)}, bf16[1024,128]{1,0:T(8,128)(2,1)}, u32[]{:S(2)}) copy-start(bf16[1024,128]{1,0:T(8,128)(2,1)} %refs_4_.1) | copy-start | bytes 786436
  2.6 6.5 %collective-permute-start.4 = (bf16[2,144,128]{2,1,0:T(8,128)(2,1)S(1)}, bf16[2,144,128]{2,1,0:T(8,128)(2,1)S(1)}, u32[]{:S(2)}, u32[]{:S(2)}) collective-permute-start(bf16[2,144,128]{2,1,0:T(8,128)(2,1)S(1)} %get-tuple-element.18.refs_0_), channel_id=1, source_target_pairs={{0,3},{1,2},{2,1},{3,0},{4,7},{5,6},{6,4},{7,5},{8,11},{9,10},{10,... | collective-permute-start | bytes 221192 | tf_op jit(solution)/shard_map/ppermute | solution.py:262
  5.3 5.9 %collective-permute-start.3 = (bf16[2,144,128]{2,1,0:T(8,128)(2,1)S(1)}, bf16[2,144,128]{2,1,0:T(8,128)(2,1)S(1)}, u32[]{:S(2)}, u32[]{:S(2)}) collective-permute-start(bf16[2,144,128]{2,1,0:T(8,128)(2,1)S(1)} %get-tuple-element.17), channel_id=1, source_target_pairs={{0,12},{1,8},{2,4},{3,0},{4,5},{5,13},{6,9},{7,1},{8,2},{9,10},{10... | collective-permute-start | bytes 221192 | tf_op jit(solution)/shard_map/ppermute | solution.py:266
  9.2 2.7 %collective-permute-start.2 = (bf16[2,144,128]{2,1,0:T(8,128)(2,1)S(1)}, bf16[2,144,128]{2,1,0:T(8,128)(2,1)S(1)}, u32[]{:S(2)}, u32[]{:S(2)}) collective-permute-start(bf16[2,144,128]{2,1,0:T(8,128)(2,1)S(1)} %get-tuple-element.17), channel_id=1, source_target_pairs={{0,4},{1,0},{2,8},{3,12},{4,1},{5,9},{6,5},{7,13},{8,14},{9,6},{10... | collective-permute-start | bytes 221192 | tf_op jit(solution)/shard_map/ppermute | solution.py:266

commit v17 on v16

--- a/solution.py
+++ b/solution.py
@@ -25,10 +25,10 @@
 
 
 RIGHT = (
-    ((1, 0, 2, 3), (0, 2, 1, 3), (3, 1, 0, 2), (2, 1, 3, 0)),
-    ((3, 2, 1, 0), (1, 3, 2, 0), (0, 2, 3, 1), (3, 0, 2, 1)),
+    ((1, 0, 2, 3), (1, 0, 2, 3), (2, 3, 1, 0), (3, 1, 0, 2)),
+    ((3, 2, 1, 0), (2, 3, 1, 0), (0, 1, 3, 2), (2, 0, 3, 1)),
 )
-LEFT = ((3, 2, 1, 0), (3, 2, 0, 1), (3, 2, 0, 1), (2, 3, 0, 1))
+LEFT = ((3, 2, 1, 0), (2, 3, 1, 0), (3, 2, 0, 1), (3, 2, 1, 0))
 
 
 def right_routes(n):

time: 13.4 us -> 13.2 us (0.985)
  starting transfers between devices: 7.05 us -> 6.76 us
    ppermute x2, starting transfers between devices: 3.9 us -> 3.61 us  [local(): lax.ppermute(right, axes, [(a * n + p, step[a][p] * n + a) for a in range...]
where the time goes in v17:
time: 13.2 us; the launch traced here: 13 us
  starting transfers between devices  6.76 us (51%)
  Pallas kernels  3.54 us (27%)
  waiting for transfers between devices  2.66 us (20%)
    ppermute x2, starting transfers between devices, local(): lax.ppermute(right, axes, [(a * n + p, step[a][p] * n + a) for a in range...  3.61 us
    ppermute x1, starting transfers between devices, local(): lax.ppermute(left, axes, [(a * n + p, a * n + step[a][p]) for a in range(...  2.65 us
    ppermute x2, waiting for transfers between devices, local(): lax.ppermute(right, axes, [(a * n + p, step[a][p] * n + a) for a in range...  2.38 us
    pallas_call x1, Pallas kernels, local(): pl.pallas_call(functools.partial(pair_kernel, seqs, rows, rows, width), o...  1.44 us
    pallas_call x1, Pallas kernels, local(): pl.pallas_call(load_kernel, out_shape=(jax.ShapeDtypeStruct(x.shape, x.dt...  1.04 us
    pallas_call x1, Pallas kernels, local(): pl.pallas_call(functools.partial(project_kernel, width), out_shape=(wire,...  0.78 us
    ppermute x1, starting transfers between devices, local(): lax.ppermute(x, 'seq', swap)  0.45 us
    pallas_call x1, Pallas kernels, local(): pl.pallas_call(functools.partial(left_kernel, steps, seqs, rows, width),...  0.28 us
  transfers between devices with their start and end apart: 5, of which 3 were waited for; matrix products, arithmetic and copies ran while one was open for 0% of the time, Pallas kernels for 10%

profile of v17, /device:TPU:0, one launch (start us, length us, event | category | flops | bytes accessed | tf_op | source)
XLA Modules:
  0.0 13.0 jit_solution(2581268115441945338)
XLA Ops:
  0.0 0.5 %collective-permute-start = (bf16[32,16,256]{2,1,0:T(8,128)(2,1)}, bf16[32,16,256]{2,1,0:T(8,128)(2,1)S(1)}, u32[]{:S(2)}, u32[]{:S(2)}) collective-permute-start(bf16[32,16,256]{2,1,0:T(8,128)(2,1)} %x_hbm.1), channel_id=1, source_target_pairs={{0,1},{1,0},{2,3},{3,2},{4,5},{5,4},{6,7},{7,6},{8,9},{9,8},{10,11... | collective-permute-start | bytes 786440 | tf_op jit(solution)/shard_map/ppermute | solution.py:231
  0.5 0.1 collective-permute-start.1
  0.5 1.0 %load.1 = (bf16[32,16,256]{2,1,0:T(8,128)(2,1)S(1)}, s32[16,32]{1,0:T(8,128)S(1)}, bf16[256,256]{1,0:T(8,128)(2,1)S(1)}, f32[8,256]{1,0:T(8,128)S(1)}) custom-call(bf16[32,16,256]{2,1,0:T(8,128)(2,1)} %x_hbm.1, s32[16,32]{1,0:T(8,128)} %bitcast.6, f32[256]{0:T(256)} %scale_hbm.1, f32[256]{0:T(256)} %shift_hbm.1, bf16[32,256]{1,0:T(8,128)(2,1)} %bitcast.3, ...), custom_call_target="tpu_custom_call" | custom-call | flops 33554432 | bytes 1048576 | tf_op jit(solution)/shard_map/load/pallas_call | solution.py:236
  1.6 0.3 %collective-permute-done.1.other_flag_ref = s32[16,32]{1,0:T(8,128)S(1)} collective-permute-done((s32[16,32]{1,0:T(8,128)}, s32[16,32]{1,0:T(8,128)S(1)}, u32[]{:S(2)}, u32[]{:S(2)}) %collective-permute-start.1) | collective-permute-done | bytes 2080 | tf_op jit(solution)/shard_map/ppermute | solution.py:231
  1.8 0.0 collective-permute-done.other_x_ref
  1.8 0.0 copy-start
  1.8 0.8 %project.1 = (bf16[2,144,128]{2,1,0:T(8,128)(2,1)S(1)}, bf16[2,144,128]{2,1,0:T(8,128)(2,1)S(1)}) custom-call(bf16[32,16,256]{2,1,0:T(8,128)(2,1)S(1)} %get-tuple-element.13.own_x_ref, s32[16,32]{1,0:T(8,128)S(1)} %get-tuple-element.14.own_flag_ref, bf16[32,16,256]{2,1,0:T(8,128)(2,1)S(1)} %collective-permute-done.other_x_ref, ...), custom_call_target="tpu_custom_call" | custom-call | tf_op jit(solution)/shard_map/project/pallas_call | solution.py:252
  2.6 2.6 %collective-permute-start.4 = (bf16[2,144,128]{2,1,0:T(8,128)(2,1)S(1)}, bf16[2,144,128]{2,1,0:T(8,128)(2,1)S(1)}, u32[]{:S(2)}, u32[]{:S(2)}) collective-permute-start(bf16[2,144,128]{2,1,0:T(8,128)(2,1)S(1)} %get-tuple-element.18.refs_0_), channel_id=1, source_target_pairs={{0,3},{1,2},{2,1},{3,0},{4,6},{5,7},{6,5},{7,4},{8,11},{9,10},{10,... | collective-permute-start | bytes 221192 | tf_op jit(solution)/shard_map/ppermute | solution.py:262
  5.3 3.6 %collective-permute-start.3 = (bf16[2,144,128]{2,1,0:T(8,128)(2,1)S(1)}, bf16[2,144,128]{2,1,0:T(8,128)(2,1)S(1)}, u32[]{:S(2)}, u32[]{:S(2)}) collective-permute-start(bf16[2,144,128]{2,1,0:T(8,128)(2,1)S(1)} %get-tuple-element.17), channel_id=1, source_target_pairs={{0,12},{1,8},{2,4},{3,0},{4,9},{5,13},{6,5},{7,1},{8,2},{9,6},{10,... | collective-permute-start | bytes 221192 | tf_op jit(solution)/shard_map/ppermute | solution.py:266
  8.9 0.0 collective-permute-start.2
  8.9 0.0 collective-permute-done.4.refs_1_
  8.9 0.3 %turn_left.1 = (bf16[512,128]{1,0:T(8,128)(2,1)S(1)}, bf16[16,128]{1,0:T(8,128)(2,1)S(1)}) custom-call(bf16[2,144,128]{2,1,0:T(8,128)(2,1)S(1)} %get-tuple-element.18.refs_0_, bf16[2,144,128]{2,1,0:T(8,128)(2,1)S(1)} %collective-permute-done.4.refs_1_), custom_call_target="tpu_custom_call" | custom-call | tf_op jit(solution)/shard_map/turn_left/pallas_call | solution.py:269
  9.2 1.7 %collective-permute-done.3.refs_1_ = bf16[2,144,128]{2,1,0:T(8,128)(2,1)S(1)} collective-permute-done((bf16[2,144,128]{2,1,0:T(8,128)(2,1)S(1)}, bf16[2,144,128]{2,1,0:T(8,128)(2,1)S(1)}, u32[]{:S(2)}, u32[]{:S(2)}) %collective-permute-start.3) | collective-permute-done | bytes 73760 | tf_op jit(solution)/shard_map/ppermute | solution.py:266
  10.9 0.7 %collective-permute-done.2.refs_0_ = bf16[2,144,128]{2,1,0:T(8,128)(2,1)S(1)} collective-permute-done((bf16[2,144,128]{2,1,0:T(8,128)(2,1)S(1)}, bf16[2,144,128]{2,1,0:T(8,128)(2,1)S(1)}, u32[]{:S(2)}, u32[]{:S(2)}) %collective-permute-start.2) | collective-permute-done | bytes 73760 | tf_op jit(solution)/shard_map/ppermute | solution.py:266
  11.6 0.0 copy-done
  11.6 1.4 %pair.1 = bf16[16,16,128]{2,1,0:T(8,128)(2,1)} custom-call(bf16[2,144,128]{2,1,0:T(8,128)(2,1)S(1)} %collective-permute-done.2.refs_0_, bf16[2,144,128]{2,1,0:T(8,128)(2,1)S(1)} %collective-permute-done.3.refs_1_, bf16[512,128]{1,0:T(8,128)(2,1)S(1)} %get-tuple-element.19.refs_2_, bf16[16,128]{1,0:T(8,128)(2,1)S(1)} %get-tuple-element.20.refs_3_, ...), custom_call_target="tpu_custom_call" | custom-call | tf_op jit(solution)/shard_map/pair/pallas_call | solution.py:279
Async XLA Ops:
  0.0 1.8 %collective-permute-start = (bf16[32,16,256]{2,1,0:T(8,128)(2,1)}, bf16[32,16,256]{2,1,0:T(8,128)(2,1)S(1)}, u32[]{:S(2)}, u32[]{:S(2)}) collective-permute-start(bf16[32,16,256]{2,1,0:T(8,128)(2,1)} %x_hbm.1), channel_id=1, source_target_pairs={{0,1},{1,0},{2,3},{3,2},{4,5},{5,4},{6,7},{7,6},{8,9},{9,8},{10,11... | collective-permute-start | bytes 786440 | tf_op jit(solution)/shard_map/ppermute | solution.py:231
  0.5 1.4 %collective-permute-start.1 = (s32[16,32]{1,0:T(8,128)}, s32[16,32]{1,0:T(8,128)S(1)}, u32[]{:S(2)}, u32[]{:S(2)}) collective-permute-start(s32[16,32]{1,0:T(8,128)} %bitcast.5), channel_id=1, source_target_pairs={{0,1},{1,0},{2,3},{3,2},{4,5},{5,4},{6,7},{7,6},{8,9},{9,8},{10,11... | collective-permute-start | bytes 6152 | tf_op jit(solution)/shard_map/ppermute | solution.py:231
  1.8 9.7 %copy-start = (bf16[1024,128]{1,0:T(8,128)(2,1)S(1)}, bf16[1024,128]{1,0:T(8,128)(2,1)}, u32[]{:S(2)}) copy-start(bf16[1024,128]{1,0:T(8,128)(2,1)} %refs_4_.1) | copy-start | bytes 786436
  2.6 6.3 %collective-permute-start.4 = (bf16[2,144,128]{2,1,0:T(8,128)(2,1)S(1)}, bf16[2,144,128]{2,1,0:T(8,128)(2,1)S(1)}, u32[]{:S(2)}, u32[]{:S(2)}) collective-permute-start(bf16[2,144,128]{2,1,0:T(8,128)(2,1)S(1)} %get-tuple-element.18.refs_0_), channel_id=1, source_target_pairs={{0,3},{1,2},{2,1},{3,0},{4,6},{5,7},{6,5},{7,4},{8,11},{9,10},{10,... | collective-permute-start | bytes 221192 | tf_op jit(solution)/shard_map/ppermute | solution.py:262
  5.3 5.6 %collective-permute-start.3 = (bf16[2,144,128]{2,1,0:T(8,128)(2,1)S(1)}, bf16[2,144,128]{2,1,0:T(8,128)(2,1)S(1)}, u32[]{:S(2)}, u32[]{:S(2)}) collective-permute-start(bf16[2,144,128]{2,1,0:T(8,128)(2,1)S(1)} %get-tuple-element.17), channel_id=1, source_target_pairs={{0,12},{1,8},{2,4},{3,0},{4,9},{5,13},{6,5},{7,1},{8,2},{9,6},{10,... | collective-permute-start | bytes 221192 | tf_op jit(solution)/shard_map/ppermute | solution.py:266
  8.9 2.7 %collective-permute-start.2 = (bf16[2,144,128]{2,1,0:T(8,128)(2,1)S(1)}, bf16[2,144,128]{2,1,0:T(8,128)(2,1)S(1)}, u32[]{:S(2)}, u32[]{:S(2)}) collective-permute-start(bf16[2,144,128]{2,1,0:T(8,128)(2,1)S(1)} %get-tuple-element.17), channel_id=1, source_target_pairs={{0,4},{1,0},{2,8},{3,12},{4,5},{5,1},{6,9},{7,13},{8,10},{9,14},{1... | collective-permute-start | bytes 221192 | tf_op jit(solution)/shard_map/ppermute | solution.py:266

commit v18 on v17

--- a/solution.py
+++ b/solution.py
@@ -25,10 +25,10 @@
 
 
 RIGHT = (
-    ((1, 0, 2, 3), (1, 0, 2, 3), (2, 3, 1, 0), (3, 1, 0, 2)),
-    ((3, 2, 1, 0), (2, 3, 1, 0), (0, 1, 3, 2), (2, 0, 3, 1)),
+    ((1, 0, 2, 3), (1, 0, 2, 3), (3, 1, 0, 2), (2, 1, 3, 0)),
+    ((3, 2, 0, 1), (2, 3, 0, 1), (0, 2, 3, 1), (3, 0, 1, 2)),
 )
-LEFT = ((3, 2, 1, 0), (2, 3, 1, 0), (3, 2, 0, 1), (3, 2, 1, 0))
+LEFT = ((3, 2, 1, 0), (3, 2, 0, 1), (3, 2, 1, 0), (3, 2, 0, 1))
 
 
 def right_routes(n):
@@ -54,43 +54,42 @@
     return chip
 
 
-def project_constants(seqs, rows, width, block, tiles):
-    lanes = rows * width
-    spreader = (iota((rows, lanes), 1) // width == iota((rows, lanes), 0)).astype(BF16)
-    place = iota((seqs, LANES), 1) // width
-    mine = [iota((rows, LANES), 1) // seqs + tile * (LANES // seqs) == block for tile in range(tiles)]
-    return spreader, place, mine
-
-
-def project_block(width, x_ref, flag_ref, weight, vectors, constants, left_ref, right_ref, proj_ref):
-    seqs, rows, depth = x_ref.shape
+def project_kernel(width, own_x_ref, own_flag_ref, other_x_ref, other_flag_ref, weight_ref, vector_ref,
+                   left_ref, right_ref, proj_ref):
+    seqs, rows, depth = own_x_ref.shape
     fold = LANES // width
     lanes = rows * width
     data = lanes // LANES * seqs
-    spreader, place, mine = constants
-    x = x_ref[...].astype(F32).reshape(seqs * rows, depth)
+    block = lax.axis_index("seq")
+    core = block % CORES
+
+    x = jnp.concatenate([ref[...].reshape(seqs * rows, depth) for ref in (own_x_ref, other_x_ref)], axis=0).astype(F32)
     center = jnp.mean(x, axis=-1, keepdims=True)
     x = x - center
     spread = jnp.mean(x * x, axis=-1, keepdims=True)
-    normed = x * lax.rsqrt(spread + 1e-05) * vectors[0:1] + vectors[1:2]
-    both = dot(normed.astype(BF16), weight, NT) + vectors[2:3]
+    normed = x * lax.rsqrt(spread + 1e-05) * vector_ref[0:1] + vector_ref[1:2]
+    both = dot(normed.astype(BF16), weight_ref[...], NT) + vector_ref[2:3]
     proj_ref[0] = both[:, :LANES]
     proj_ref[1] = both[:, LANES:]
 
-    flags = flag_ref[...].astype(F32)
-    mask = dot(flags.astype(BF16), spreader, TN)
-    flags = jnp.concatenate([flags] * (LANES // seqs), axis=1)
-
-    for half, out_ref in ((0, left_ref), (1, right_ref)):
-        for tile in range(rows // fold):
-            merged = proj_ref[half, pl.ds(tile * fold, seqs, stride=rows), :]
-            for k in range(1, fold):
-                part = proj_ref[half, pl.ds(tile * fold + k, seqs, stride=rows), :]
-                merged = jnp.where(place == k, part, merged)
-            merged = merged * mask[:, tile * LANES:(tile + 1) * LANES]
-            out_ref[tile * seqs:(tile + 1) * seqs, :] = merged.astype(BF16)
-        for tile, here in enumerate(mine):
-            out_ref[data + tile * rows:data + (tile + 1) * rows, :] = jnp.where(here, flags, 0.0).astype(BF16)
+    spreader = (iota((rows, lanes), 1) // width == iota((rows, lanes), 0)).astype(BF16)
+    place = iota((seqs, LANES), 1) // width
+    lane_block = iota((rows, LANES), 1) // seqs
+    for which, (flag_ref, at) in enumerate(((own_flag_ref, core), (other_flag_ref, 1 - core))):
+        flags = flag_ref[...].astype(F32)
+        mask = dot(flags.astype(BF16), spreader, TN)
+        flags = jnp.concatenate([flags] * (LANES // seqs), axis=1)
+        for half, out_ref in ((0, left_ref.at[at]), (1, right_ref.at[at])):
+            for tile in range(rows // fold):
+                first = which * seqs * rows + tile * fold
+                merged = proj_ref[half, pl.ds(first, seqs, stride=rows), :]
+                for k in range(1, fold):
+                    merged = jnp.where(place == k, proj_ref[half, pl.ds(first + k, seqs, stride=rows), :], merged)
+                merged = merged * mask[:, tile * LANES:(tile + 1) * LANES]
+                out_ref[tile * seqs:(tile + 1) * seqs, :] = merged.astype(BF16)
+            for tile in range((out_ref.shape[0] - data) // rows):
+                here = lane_block + tile * (LANES // seqs) == block - core + at
+                out_ref[data + tile * rows:data + (tile + 1) * rows, :] = jnp.where(here, flags, 0.0).astype(BF16)
 
 
 def load_kernel(x_hbm, flag_hbm, scale_hbm, shift_hbm, wl_hbm, bl_hbm, wr_hbm, br_hbm, last_hbm,
@@ -122,24 +121,6 @@
         axis=0,
     )
     copies[0].wait()
-
-
-def project_kernel(width, own_x_ref, own_flag_ref, other_x_ref, other_flag_ref, weight_ref, vector_ref,
-                   left_ref, right_ref, own_proj_ref, other_proj_ref):
-    seqs, rows, _ = own_x_ref.shape
-    block = lax.axis_index("seq")
-    core = block % CORES
-    other = 1 - core
-    tiles = (left_ref.shape[1] - rows * width // LANES * seqs) // rows
-    for x_ref, flag_ref, proj_ref, at in (
-        (own_x_ref, own_flag_ref, own_proj_ref, core),
-        (other_x_ref, other_flag_ref, other_proj_ref, other),
-    ):
-        project_block(
-            width, x_ref, flag_ref, weight_ref[...], vector_ref[...],
-            project_constants(seqs, rows, width, block - core + at, tiles),
-            left_ref.at[at], right_ref.at[at], proj_ref,
-        )
 
 
 def whole_mask(pieces, rows, data):
@@ -171,8 +152,8 @@
 
 
 def pair_kernel(seqs, rows, columns, width, *refs):
-    rights = refs[:-7]
-    turned_ref, live_ref, w_ref, vector_ref, out_ref, flat_ref, raw_ref = refs[-7:]
+    rights = refs[:-9]
+    turned_ref, live_ref, w_ref, vector_ref, out_hbm, out_ref, flat_ref, raw_ref, sems = refs[-9:]
     fold = LANES // width
     assert fold == 4
     data = rows * width // LANES * seqs
@@ -214,8 +195,16 @@
     scale = 1.0 / (1.0 + count)
     for j in range(columns):
         raw_ref[j * rows:(j + 1) * rows, :] = raw[j * rows:(j + 1) * rows, :] * scale[:, j:j + 1]
-    for i in range(rows):
-        out_ref[i] = raw_ref[pl.ds(i, columns, stride=rows), :].astype(BF16)
+    parts = sems.shape[0]
+    copies = []
+    for part in range(parts):
+        where = slice(part * rows // parts, (part + 1) * rows // parts)
+        for i in range(where.start, where.stop):
+            out_ref[i] = raw_ref[pl.ds(i, columns, stride=rows), :].astype(BF16)
+        copies.append(pltpu.make_async_copy(out_ref.at[where], out_hbm.at[where], sems.at[part]))
+        copies[-1].start()
+    for copy in copies:
+        copy.wait()
 
 
 def local(n, x, flags, scale, shift, wl, bl, wr, br, w, bias):
@@ -252,7 +241,7 @@
     left, right = pl.pallas_call(
         functools.partial(project_kernel, width),
         out_shape=(wire, wire),
-        scratch_shapes=[pltpu.VMEM((2, seqs * rows, LANES), F32)] * 2,
+        scratch_shapes=[pltpu.VMEM((2, CORES * seqs * rows, LANES), F32)],
         compiler_params=pltpu.CompilerParams(vmem_limit_bytes=16 << 20),
         name="project",
     )(own_x, own_flags, other_x, other_flags, weight, vectors)
@@ -279,9 +268,12 @@
     return pl.pallas_call(
         functools.partial(pair_kernel, seqs, rows, rows, width),
         out_shape=jax.ShapeDtypeStruct((rows, rows, outs), BF16),
+        out_specs=pl.BlockSpec(memory_space=pltpu.HBM),
         scratch_shapes=[
+            pltpu.VMEM((rows, rows, outs), BF16),
             pltpu.VMEM((rows * rows, width * width), BF16),
             pltpu.VMEM((rows * rows, outs), F32),
+            pltpu.SemaphoreType.DMA((4,)),
         ],
         compiler_params=pltpu.CompilerParams(vmem_limit_bytes=16 << 20),
         name="pair",

time: 13.2 us -> 13.2 us (level)
  no operation moved by 1% of the time
where the time goes in v18:
time: 13.2 us; the launch traced here: 13 us
  starting transfers between devices  6.76 us (51%)
  Pallas kernels  3.58 us (27%)
  waiting for transfers between devices  2.66 us (20%)
    ppermute x2, starting transfers between devices, local(): lax.ppermute(right, axes, [(a * n + p, step[a][p] * n + a) for a in range...  3.6 us
    ppermute x1, starting transfers between devices, local(): lax.ppermute(left, axes, [(a * n + p, a * n + step[a][p]) for a in range(...  2.65 us
    ppermute x2, waiting for transfers between devices, local(): lax.ppermute(right, axes, [(a * n + p, step[a][p] * n + a) for a in range...  2.38 us
    pallas_call x1, Pallas kernels, local(): pl.pallas_call(functools.partial(pair_kernel, seqs, rows, rows, width), o...  1.45 us
    pallas_call x1, Pallas kernels, local(): pl.pallas_call(load_kernel, out_shape=(jax.ShapeDtypeStruct(x.shape, x.dt...  1.04 us
    pallas_call x1, Pallas kernels, local(): pl.pallas_call(functools.partial(project_kernel, width), out_shape=(wire,...  0.81 us
    ppermute x1, starting transfers between devices, local(): lax.ppermute(x, 'seq', swap)  0.45 us
    pallas_call x1, Pallas kernels, local(): pl.pallas_call(functools.partial(left_kernel, steps, seqs, rows, width),...  0.28 us
  transfers between devices with their start and end apart: 5, of which 3 were waited for; matrix products, arithmetic and copies ran while one was open for 0% of the time, Pallas kernels for 10%

profile of v18, /device:TPU:0, one launch (start us, length us, event | category | flops | bytes accessed | tf_op | source)
XLA Modules:
  0.0 13.0 jit_solution(9233785477802492147)
XLA Ops:
  0.0 0.5 %collective-permute-start = (bf16[32,16,256]{2,1,0:T(8,128)(2,1)}, bf16[32,16,256]{2,1,0:T(8,128)(2,1)S(1)}, u32[]{:S(2)}, u32[]{:S(2)}) collective-permute-start(bf16[32,16,256]{2,1,0:T(8,128)(2,1)} %x_hbm.1), channel_id=1, source_target_pairs={{0,1},{1,0},{2,3},{3,2},{4,5},{5,4},{6,7},{7,6},{8,9},{9,8},{10,11... | collective-permute-start | bytes 786440 | tf_op jit(solution)/shard_map/ppermute | solution.py:220
  0.5 0.1 collective-permute-start.1
  0.5 1.0 %load.1 = (bf16[32,16,256]{2,1,0:T(8,128)(2,1)S(1)}, s32[16,32]{1,0:T(8,128)S(1)}, bf16[256,256]{1,0:T(8,128)(2,1)S(1)}, f32[8,256]{1,0:T(8,128)S(1)}) custom-call(bf16[32,16,256]{2,1,0:T(8,128)(2,1)} %x_hbm.1, s32[16,32]{1,0:T(8,128)} %bitcast.6, f32[256]{0:T(256)} %scale_hbm.1, f32[256]{0:T(256)} %shift_hbm.1, bf16[32,256]{1,0:T(8,128)(2,1)} %bitcast.3, ...), custom_call_target="tpu_custom_call" | custom-call | flops 33554432 | bytes 1048576 | tf_op jit(solution)/shard_map/load/pallas_call | solution.py:225
  1.6 0.3 %collective-permute-done.1.other_flag_ref = s32[16,32]{1,0:T(8,128)S(1)} collective-permute-done((s32[16,32]{1,0:T(8,128)}, s32[16,32]{1,0:T(8,128)S(1)}, u32[]{:S(2)}, u32[]{:S(2)}) %collective-permute-start.1) | collective-permute-done | bytes 2080 | tf_op jit(solution)/shard_map/ppermute | solution.py:220
  1.8 0.0 collective-permute-done.other_x_ref
  1.8 0.0 copy-start
  1.8 0.8 %project.1 = (bf16[2,144,128]{2,1,0:T(8,128)(2,1)S(1)}, bf16[2,144,128]{2,1,0:T(8,128)(2,1)S(1)}) custom-call(bf16[32,16,256]{2,1,0:T(8,128)(2,1)S(1)} %get-tuple-element.13.own_x_ref, s32[16,32]{1,0:T(8,128)S(1)} %get-tuple-element.14.own_flag_ref, bf16[32,16,256]{2,1,0:T(8,128)(2,1)S(1)} %collective-permute-done.other_x_ref, ...), custom_call_target="tpu_custom_call" | custom-call | tf_op jit(solution)/shard_map/project/pallas_call | solution.py:241
  2.7 2.7 %collective-permute-start.4 = (bf16[2,144,128]{2,1,0:T(8,128)(2,1)S(1)}, bf16[2,144,128]{2,1,0:T(8,128)(2,1)S(1)}, u32[]{:S(2)}, u32[]{:S(2)}) collective-permute-start(bf16[2,144,128]{2,1,0:T(8,128)(2,1)S(1)} %get-tuple-element.18.refs_0_), channel_id=1, source_target_pairs={{0,3},{1,2},{2,1},{3,0},{4,7},{5,6},{6,4},{7,5},{8,11},{9,10},{10,... | collective-permute-start | bytes 221192 | tf_op jit(solution)/shard_map/ppermute | solution.py:251
  5.3 3.6 %collective-permute-start.3 = (bf16[2,144,128]{2,1,0:T(8,128)(2,1)S(1)}, bf16[2,144,128]{2,1,0:T(8,128)(2,1)S(1)}, u32[]{:S(2)}, u32[]{:S(2)}) collective-permute-start(bf16[2,144,128]{2,1,0:T(8,128)(2,1)S(1)} %get-tuple-element.17), channel_id=1, source_target_pairs={{0,12},{1,8},{2,0},{3,4},{4,9},{5,13},{6,1},{7,5},{8,2},{9,10},{10... | collective-permute-start | bytes 221192 | tf_op jit(solution)/shard_map/ppermute | solution.py:255
  8.9 0.0 collective-permute-start.2
  8.9 0.0 collective-permute-done.4.refs_1_
  8.9 0.3 %turn_left.1 = (bf16[512,128]{1,0:T(8,128)(2,1)S(1)}, bf16[16,128]{1,0:T(8,128)(2,1)S(1)}) custom-call(bf16[2,144,128]{2,1,0:T(8,128)(2,1)S(1)} %get-tuple-element.18.refs_0_, bf16[2,144,128]{2,1,0:T(8,128)(2,1)S(1)} %collective-permute-done.4.refs_1_), custom_call_target="tpu_custom_call" | custom-call | tf_op jit(solution)/shard_map/turn_left/pallas_call | solution.py:258
  9.2 1.7 %collective-permute-done.3.refs_1_ = bf16[2,144,128]{2,1,0:T(8,128)(2,1)S(1)} collective-permute-done((bf16[2,144,128]{2,1,0:T(8,128)(2,1)S(1)}, bf16[2,144,128]{2,1,0:T(8,128)(2,1)S(1)}, u32[]{:S(2)}, u32[]{:S(2)}) %collective-permute-start.3) | collective-permute-done | bytes 73760 | tf_op jit(solution)/shard_map/ppermute | solution.py:255
  10.9 0.7 %collective-permute-done.2.refs_0_ = bf16[2,144,128]{2,1,0:T(8,128)(2,1)S(1)} collective-permute-done((bf16[2,144,128]{2,1,0:T(8,128)(2,1)S(1)}, bf16[2,144,128]{2,1,0:T(8,128)(2,1)S(1)}, u32[]{:S(2)}, u32[]{:S(2)}) %collective-permute-start.2) | collective-permute-done | bytes 73760 | tf_op jit(solution)/shard_map/ppermute | solution.py:255
  11.6 0.0 copy-done
  11.6 1.4 %pair.1 = bf16[16,16,128]{2,1,0:T(8,128)(2,1)} custom-call(bf16[2,144,128]{2,1,0:T(8,128)(2,1)S(1)} %collective-permute-done.2.refs_0_, bf16[2,144,128]{2,1,0:T(8,128)(2,1)S(1)} %collective-permute-done.3.refs_1_, bf16[512,128]{1,0:T(8,128)(2,1)S(1)} %get-tuple-element.19.refs_2_, bf16[16,128]{1,0:T(8,128)(2,1)S(1)} %get-tuple-element.20.refs_3_, ...), custom_call_target="tpu_custom_call" | custom-call | tf_op jit(solution)/shard_map/pair/pallas_call | solution.py:268
Async XLA Ops:
  0.0 1.8 %collective-permute-start = (bf16[32,16,256]{2,1,0:T(8,128)(2,1)}, bf16[32,16,256]{2,1,0:T(8,128)(2,1)S(1)}, u32[]{:S(2)}, u32[]{:S(2)}) collective-permute-start(bf16[32,16,256]{2,1,0:T(8,128)(2,1)} %x_hbm.1), channel_id=1, source_target_pairs={{0,1},{1,0},{2,3},{3,2},{4,5},{5,4},{6,7},{7,6},{8,9},{9,8},{10,11... | collective-permute-start | bytes 786440 | tf_op jit(solution)/shard_map/ppermute | solution.py:220
  0.5 1.4 %collective-permute-start.1 = (s32[16,32]{1,0:T(8,128)}, s32[16,32]{1,0:T(8,128)S(1)}, u32[]{:S(2)}, u32[]{:S(2)}) collective-permute-start(s32[16,32]{1,0:T(8,128)} %bitcast.5), channel_id=1, source_target_pairs={{0,1},{1,0},{2,3},{3,2},{4,5},{5,4},{6,7},{7,6},{8,9},{9,8},{10,11... | collective-permute-start | bytes 6152 | tf_op jit(solution)/shard_map/ppermute | solution.py:220
  1.8 9.7 %copy-start = (bf16[1024,128]{1,0:T(8,128)(2,1)S(1)}, bf16[1024,128]{1,0:T(8,128)(2,1)}, u32[]{:S(2)}) copy-start(bf16[1024,128]{1,0:T(8,128)(2,1)} %refs_4_.1) | copy-start | bytes 786436
  2.7 6.3 %collective-permute-start.4 = (bf16[2,144,128]{2,1,0:T(8,128)(2,1)S(1)}, bf16[2,144,128]{2,1,0:T(8,128)(2,1)S(1)}, u32[]{:S(2)}, u32[]{:S(2)}) collective-permute-start(bf16[2,144,128]{2,1,0:T(8,128)(2,1)S(1)} %get-tuple-element.18.refs_0_), channel_id=1, source_target_pairs={{0,3},{1,2},{2,1},{3,0},{4,7},{5,6},{6,4},{7,5},{8,11},{9,10},{10,... | collective-permute-start | bytes 221192 | tf_op jit(solution)/shard_map/ppermute | solution.py:251
  5.3 5.6 %collective-permute-start.3 = (bf16[2,144,128]{2,1,0:T(8,128)(2,1)S(1)}, bf16[2,144,128]{2,1,0:T(8,128)(2,1)S(1)}, u32[]{:S(2)}, u32[]{:S(2)}) collective-permute-start(bf16[2,144,128]{2,1,0:T(8,128)(2,1)S(1)} %get-tuple-element.17), channel_id=1, source_target_pairs={{0,12},{1,8},{2,0},{3,4},{4,9},{5,13},{6,1},{7,5},{8,2},{9,10},{10... | collective-permute-start | bytes 221192 | tf_op jit(solution)/shard_map/ppermute | solution.py:255
  8.9 2.7 %collective-permute-start.2 = (bf16[2,144,128]{2,1,0:T(8,128)(2,1)S(1)}, bf16[2,144,128]{2,1,0:T(8,128)(2,1)S(1)}, u32[]{:S(2)}, u32[]{:S(2)}) collective-permute-start(bf16[2,144,128]{2,1,0:T(8,128)(2,1)S(1)} %get-tuple-element.17), channel_id=1, source_target_pairs={{0,4},{1,0},{2,8},{3,12},{4,5},{5,1},{6,9},{7,13},{8,14},{9,6},{10... | collective-permute-start | bytes 221192 | tf_op jit(solution)/shard_map/ppermute | solution.py:255

commit v19 on v17

--- a/solution.py
+++ b/solution.py
@@ -185,7 +185,10 @@
         ],
         axis=0,
     )
-    outer = dot(turned_ref[...], right).astype(BF16)
+    half = width // 2 * rows
+    outer = jnp.concatenate(
+        [dot(turned_ref[k:k + half, :], right).astype(BF16) for k in (0, half)], axis=0
+    )
 
     place = (iota((rows, LANES), 1) // width).astype(BF16)
     even = [None] * fold
@@ -209,7 +212,8 @@
                 j = tile * fold + k
                 flat_ref[j * rows:(j + 1) * rows, quad * LANES:(quad + 1) * LANES] = part[k]
 
-    raw = dot(flat_ref[...], w_ref[...]) + vector_ref[3:4, :LANES]
+    half = width // 2 * width
+    raw = dot(flat_ref[:, :half], w_ref[:half, :]) + dot(flat_ref[:, half:], w_ref[half:, :]) + vector_ref[3:4, :LANES]
     count = dot(live_ref[...], whole_mask(rights, rows, data), NT)
     scale = 1.0 / (1.0 + count)
     for j in range(columns):

time: 13.2 us -> 13.2 us (level)
  no operation moved by 1% of the time
where the time goes in v19:
time: 13.2 us; the launch traced here: 13.1 us
  starting transfers between devices  6.76 us (51%)
  Pallas kernels  3.6 us (27%)
  waiting for transfers between devices  2.66 us (20%)
    ppermute x2, starting transfers between devices, local(): lax.ppermute(right, axes, [(a * n + p, step[a][p] * n + a) for a in range...  3.61 us
    ppermute x1, starting transfers between devices, local(): lax.ppermute(left, axes, [(a * n + p, a * n + step[a][p]) for a in range(...  2.65 us
    ppermute x2, waiting for transfers between devices, local(): lax.ppermute(right, axes, [(a * n + p, step[a][p] * n + a) for a in range...  2.38 us
    pallas_call x1, Pallas kernels, local(): pl.pallas_call(functools.partial(pair_kernel, seqs, rows, rows, width), o...  1.5 us
    pallas_call x1, Pallas kernels, local(): pl.pallas_call(load_kernel, out_shape=(jax.ShapeDtypeStruct(x.shape, x.dt...  1.04 us
    pallas_call x1, Pallas kernels, local(): pl.pallas_call(functools.partial(project_kernel, width), out_shape=(wire,...  0.78 us
    ppermute x1, starting transfers between devices, local(): lax.ppermute(x, 'seq', swap)  0.45 us
    pallas_call x1, Pallas kernels, local(): pl.pallas_call(functools.partial(left_kernel, steps, seqs, rows, width),...  0.28 us
  transfers between devices with their start and end apart: 5, of which 3 were waited for; matrix products, arithmetic and copies ran while one was open for 0% of the time, Pallas kernels for 10%

profile of v19, /device:TPU:0, one launch (start us, length us, event | category | flops | bytes accessed | tf_op | source)
XLA Modules:
  0.0 13.1 jit_solution(3709171515685844869)
XLA Ops:
  0.0 0.5 %collective-permute-start = (bf16[32,16,256]{2,1,0:T(8,128)(2,1)}, bf16[32,16,256]{2,1,0:T(8,128)(2,1)S(1)}, u32[]{:S(2)}, u32[]{:S(2)}) collective-permute-start(bf16[32,16,256]{2,1,0:T(8,128)(2,1)} %x_hbm.1), channel_id=1, source_target_pairs={{0,1},{1,0},{2,3},{3,2},{4,5},{5,4},{6,7},{7,6},{8,9},{9,8},{10,11... | collective-permute-start | bytes 786440 | tf_op jit(solution)/shard_map/ppermute | solution.py:235
  0.5 0.1 collective-permute-start.1
  0.5 1.0 %load.1 = (bf16[32,16,256]{2,1,0:T(8,128)(2,1)S(1)}, s32[16,32]{1,0:T(8,128)S(1)}, bf16[256,256]{1,0:T(8,128)(2,1)S(1)}, f32[8,256]{1,0:T(8,128)S(1)}) custom-call(bf16[32,16,256]{2,1,0:T(8,128)(2,1)} %x_hbm.1, s32[16,32]{1,0:T(8,128)} %bitcast.6, f32[256]{0:T(256)} %scale_hbm.1, f32[256]{0:T(256)} %shift_hbm.1, bf16[32,256]{1,0:T(8,128)(2,1)} %bitcast.3, ...), custom_call_target="tpu_custom_call" | custom-call | flops 33554432 | bytes 1048576 | tf_op jit(solution)/shard_map/load/pallas_call | solution.py:240
  1.6 0.3 %collective-permute-done.1.other_flag_ref = s32[16,32]{1,0:T(8,128)S(1)} collective-permute-done((s32[16,32]{1,0:T(8,128)}, s32[16,32]{1,0:T(8,128)S(1)}, u32[]{:S(2)}, u32[]{:S(2)}) %collective-permute-start.1) | collective-permute-done | bytes 2080 | tf_op jit(solution)/shard_map/ppermute | solution.py:235
  1.8 0.0 collective-permute-done.other_x_ref
  1.8 0.0 copy-start
  1.8 0.8 %project.1 = (bf16[2,144,128]{2,1,0:T(8,128)(2,1)S(1)}, bf16[2,144,128]{2,1,0:T(8,128)(2,1)S(1)}) custom-call(bf16[32,16,256]{2,1,0:T(8,128)(2,1)S(1)} %get-tuple-element.13.own_x_ref, s32[16,32]{1,0:T(8,128)S(1)} %get-tuple-element.14.own_flag_ref, bf16[32,16,256]{2,1,0:T(8,128)(2,1)S(1)} %collective-permute-done.other_x_ref, ...), custom_call_target="tpu_custom_call" | custom-call | tf_op jit(solution)/shard_map/project/pallas_call | solution.py:256
  2.6 2.6 %collective-permute-start.4 = (bf16[2,144,128]{2,1,0:T(8,128)(2,1)S(1)}, bf16[2,144,128]{2,1,0:T(8,128)(2,1)S(1)}, u32[]{:S(2)}, u32[]{:S(2)}) collective-permute-start(bf16[2,144,128]{2,1,0:T(8,128)(2,1)S(1)} %get-tuple-element.18.refs_0_), channel_id=1, source_target_pairs={{0,3},{1,2},{2,1},{3,0},{4,6},{5,7},{6,5},{7,4},{8,11},{9,10},{10,... | collective-permute-start | bytes 221192 | tf_op jit(solution)/shard_map/ppermute | solution.py:266
  5.3 3.6 %collective-permute-start.3 = (bf16[2,144,128]{2,1,0:T(8,128)(2,1)S(1)}, bf16[2,144,128]{2,1,0:T(8,128)(2,1)S(1)}, u32[]{:S(2)}, u32[]{:S(2)}) collective-permute-start(bf16[2,144,128]{2,1,0:T(8,128)(2,1)S(1)} %get-tuple-element.17), channel_id=1, source_target_pairs={{0,12},{1,8},{2,4},{3,0},{4,9},{5,13},{6,5},{7,1},{8,2},{9,6},{10,... | collective-permute-start | bytes 221192 | tf_op jit(solution)/shard_map/ppermute | solution.py:270
  8.9 0.0 collective-permute-start.2
  8.9 0.0 collective-permute-done.4.refs_1_
  8.9 0.3 %turn_left.1 = (bf16[512,128]{1,0:T(8,128)(2,1)S(1)}, bf16[16,128]{1,0:T(8,128)(2,1)S(1)}) custom-call(bf16[2,144,128]{2,1,0:T(8,128)(2,1)S(1)} %get-tuple-element.18.refs_0_, bf16[2,144,128]{2,1,0:T(8,128)(2,1)S(1)} %collective-permute-done.4.refs_1_), custom_call_target="tpu_custom_call" | custom-call | tf_op jit(solution)/shard_map/turn_left/pallas_call | solution.py:273
  9.2 1.7 %collective-permute-done.3.refs_1_ = bf16[2,144,128]{2,1,0:T(8,128)(2,1)S(1)} collective-permute-done((bf16[2,144,128]{2,1,0:T(8,128)(2,1)S(1)}, bf16[2,144,128]{2,1,0:T(8,128)(2,1)S(1)}, u32[]{:S(2)}, u32[]{:S(2)}) %collective-permute-start.3) | collective-permute-done | bytes 73760 | tf_op jit(solution)/shard_map/ppermute | solution.py:270
  10.9 0.7 %collective-permute-done.2.refs_0_ = bf16[2,144,128]{2,1,0:T(8,128)(2,1)S(1)} collective-permute-done((bf16[2,144,128]{2,1,0:T(8,128)(2,1)S(1)}, bf16[2,144,128]{2,1,0:T(8,128)(2,1)S(1)}, u32[]{:S(2)}, u32[]{:S(2)}) %collective-permute-start.2) | collective-permute-done | bytes 73760 | tf_op jit(solution)/shard_map/ppermute | solution.py:270
  11.6 0.0 copy-done
  11.6 1.5 %pair.1 = bf16[16,16,128]{2,1,0:T(8,128)(2,1)} custom-call(bf16[2,144,128]{2,1,0:T(8,128)(2,1)S(1)} %collective-permute-done.2.refs_0_, bf16[2,144,128]{2,1,0:T(8,128)(2,1)S(1)} %collective-permute-done.3.refs_1_, bf16[512,128]{1,0:T(8,128)(2,1)S(1)} %get-tuple-element.19.refs_2_, bf16[16,128]{1,0:T(8,128)(2,1)S(1)} %get-tuple-element.20.refs_3_, ...), custom_call_target="tpu_custom_call" | custom-call | tf_op jit(solution)/shard_map/pair/pallas_call | solution.py:283
Async XLA Ops:
  0.0 1.8 %collective-permute-start = (bf16[32,16,256]{2,1,0:T(8,128)(2,1)}, bf16[32,16,256]{2,1,0:T(8,128)(2,1)S(1)}, u32[]{:S(2)}, u32[]{:S(2)}) collective-permute-start(bf16[32,16,256]{2,1,0:T(8,128)(2,1)} %x_hbm.1), channel_id=1, source_target_pairs={{0,1},{1,0},{2,3},{3,2},{4,5},{5,4},{6,7},{7,6},{8,9},{9,8},{10,11... | collective-permute-start | bytes 786440 | tf_op jit(solution)/shard_map/ppermute | solution.py:235
  0.5 1.4 %collective-permute-start.1 = (s32[16,32]{1,0:T(8,128)}, s32[16,32]{1,0:T(8,128)S(1)}, u32[]{:S(2)}, u32[]{:S(2)}) collective-permute-start(s32[16,32]{1,0:T(8,128)} %bitcast.5), channel_id=1, source_target_pairs={{0,1},{1,0},{2,3},{3,2},{4,5},{5,4},{6,7},{7,6},{8,9},{9,8},{10,11... | collective-permute-start | bytes 6152 | tf_op jit(solution)/shard_map/ppermute | solution.py:235
  1.8 9.7 %copy-start = (bf16[1024,128]{1,0:T(8,128)(2,1)S(1)}, bf16[1024,128]{1,0:T(8,128)(2,1)}, u32[]{:S(2)}) copy-start(bf16[1024,128]{1,0:T(8,128)(2,1)} %refs_4_.1) | copy-start | bytes 786436
  2.6 6.3 %collective-permute-start.4 = (bf16[2,144,128]{2,1,0:T(8,128)(2,1)S(1)}, bf16[2,144,128]{2,1,0:T(8,128)(2,1)S(1)}, u32[]{:S(2)}, u32[]{:S(2)}) collective-permute-start(bf16[2,144,128]{2,1,0:T(8,128)(2,1)S(1)} %get-tuple-element.18.refs_0_), channel_id=1, source_target_pairs={{0,3},{1,2},{2,1},{3,0},{4,6},{5,7},{6,5},{7,4},{8,11},{9,10},{10,... | collective-permute-start | bytes 221192 | tf_op jit(solution)/shard_map/ppermute | solution.py:266
  5.3 5.6 %collective-permute-start.3 = (bf16[2,144,128]{2,1,0:T(8,128)(2,1)S(1)}, bf16[2,144,128]{2,1,0:T(8,128)(2,1)S(1)}, u32[]{:S(2)}, u32[]{:S(2)}) collective-permute-start(bf16[2,144,128]{2,1,0:T(8,128)(2,1)S(1)} %get-tuple-element.17), channel_id=1, source_target_pairs={{0,12},{1,8},{2,4},{3,0},{4,9},{5,13},{6,5},{7,1},{8,2},{9,6},{10,... | collective-permute-start | bytes 221192 | tf_op jit(solution)/shard_map/ppermute | solution.py:270
  8.9 2.7 %collective-permute-start.2 = (bf16[2,144,128]{2,1,0:T(8,128)(2,1)S(1)}, bf16[2,144,128]{2,1,0:T(8,128)(2,1)S(1)}, u32[]{:S(2)}, u32[]{:S(2)}) collective-permute-start(bf16[2,144,128]{2,1,0:T(8,128)(2,1)S(1)} %get-tuple-element.17), channel_id=1, source_target_pairs={{0,4},{1,0},{2,8},{3,12},{4,5},{5,1},{6,9},{7,13},{8,10},{9,14},{1... | collective-permute-start | bytes 221192 | tf_op jit(solution)/shard_map/ppermute | solution.py:270

commit v20 on v17

--- a/solution.py
+++ b/solution.py
@@ -54,20 +54,11 @@
     return chip
 
 
-def project_constants(seqs, rows, width, block, tiles):
-    lanes = rows * width
-    spreader = (iota((rows, lanes), 1) // width == iota((rows, lanes), 0)).astype(BF16)
-    place = iota((seqs, LANES), 1) // width
-    mine = [iota((rows, LANES), 1) // seqs + tile * (LANES // seqs) == block for tile in range(tiles)]
-    return spreader, place, mine
-
-
-def project_block(width, x_ref, flag_ref, weight, vectors, constants, left_ref, right_ref, proj_ref):
+def project_block(width, x_ref, flag_ref, weight, vectors, spreader, place, left_ref, right_ref, proj_ref):
     seqs, rows, depth = x_ref.shape
     fold = LANES // width
     lanes = rows * width
     data = lanes // LANES * seqs
-    spreader, place, mine = constants
     x = x_ref[...].astype(F32).reshape(seqs * rows, depth)
     center = jnp.mean(x, axis=-1, keepdims=True)
     x = x - center
@@ -77,10 +68,7 @@
     proj_ref[0] = both[:, :LANES]
     proj_ref[1] = both[:, LANES:]
 
-    flags = flag_ref[...].astype(F32)
-    mask = dot(flags.astype(BF16), spreader, TN)
-    flags = jnp.concatenate([flags] * (LANES // seqs), axis=1)
-
+    mask = dot(flag_ref[...].astype(F32).astype(BF16), spreader, TN)
     for half, out_ref in ((0, left_ref), (1, right_ref)):
         for tile in range(rows // fold):
             merged = proj_ref[half, pl.ds(tile * fold, seqs, stride=rows), :]
@@ -89,8 +77,6 @@
                 merged = jnp.where(place == k, part, merged)
             merged = merged * mask[:, tile * LANES:(tile + 1) * LANES]
             out_ref[tile * seqs:(tile + 1) * seqs, :] = merged.astype(BF16)
-        for tile, here in enumerate(mine):
-            out_ref[data + tile * rows:data + (tile + 1) * rows, :] = jnp.where(here, flags, 0.0).astype(BF16)
 
 
 def load_kernel(x_hbm, flag_hbm, scale_hbm, shift_hbm, wl_hbm, bl_hbm, wr_hbm, br_hbm, last_hbm,
@@ -127,23 +113,34 @@
 def project_kernel(width, own_x_ref, own_flag_ref, other_x_ref, other_flag_ref, weight_ref, vector_ref,
                    left_ref, right_ref, own_proj_ref, other_proj_ref):
     seqs, rows, _ = own_x_ref.shape
+    lanes = rows * width
+    data = lanes // LANES * seqs
     block = lax.axis_index("seq")
     core = block % CORES
-    other = 1 - core
-    tiles = (left_ref.shape[1] - rows * width // LANES * seqs) // rows
+    spreader = (iota((rows, lanes), 1) // width == iota((rows, lanes), 0)).astype(BF16)
+    place = iota((seqs, LANES), 1) // width
     for x_ref, flag_ref, proj_ref, at in (
         (own_x_ref, own_flag_ref, own_proj_ref, core),
-        (other_x_ref, other_flag_ref, other_proj_ref, other),
+        (other_x_ref, other_flag_ref, other_proj_ref, 1 - core),
     ):
+        here = pl.ds(pl.multiple_of(at * data, data), data)
         project_block(
-            width, x_ref, flag_ref, weight_ref[...], vector_ref[...],
-            project_constants(seqs, rows, width, block - core + at, tiles),
-            left_ref.at[at], right_ref.at[at], proj_ref,
+            width, x_ref, flag_ref, weight_ref[...], vector_ref[...], spreader, place,
+            left_ref.at[here], right_ref.at[here], proj_ref,
         )
+    own, other = (
+        jnp.concatenate([ref[...].astype(F32)] * (LANES // seqs), axis=1) for ref in (own_flag_ref, other_flag_ref)
+    )
+    for tile in range((left_ref.shape[0] - CORES * data) // rows):
+        lane_block = iota((rows, LANES), 1) // seqs + tile * (LANES // seqs)
+        placed = jnp.where(lane_block == block, own, jnp.where(lane_block == block + 1 - 2 * core, other, 0.0)).astype(BF16)
+        first = CORES * data + tile * rows
+        for out_ref in (left_ref, right_ref):
+            out_ref[first:first + rows, :] = placed
 
 
 def whole_mask(pieces, rows, data):
-    total = functools.reduce(jnp.add, [p[k, data:, :] for p in pieces for k in range(CORES)])
+    total = functools.reduce(jnp.add, [p[CORES * data:, :] for p in pieces])
     return jnp.concatenate([total[k:k + rows] for k in range(0, total.shape[0], rows)], axis=1)
 
 
@@ -159,7 +156,7 @@
             at = pl.multiple_of((slot * CORES + core) * seqs, seqs)
             for tile in range(data // seqs):
                 left_ref[pl.ds(at, seqs), tile * LANES:(tile + 1) * LANES] = (
-                    piece[core, tile * seqs:(tile + 1) * seqs, :]
+                    piece[core * data + tile * seqs:core * data + (tile + 1) * seqs, :]
                 )
     mask_ref[...] = whole_mask(lefts, rows, data)
     for tile in range(turned_ref.shape[0]):
@@ -179,7 +176,9 @@
 
     right = jnp.concatenate(
         [
-            jnp.concatenate([p[core, t * seqs:(t + 1) * seqs, :] for t in range(data // seqs)], axis=1)
+            jnp.concatenate(
+                [p[core * data + t * seqs:core * data + (t + 1) * seqs, :] for t in range(data // seqs)], axis=1
+            )
             for p in rights
             for core in range(CORES)
         ],
@@ -223,7 +222,7 @@
     width = wl.shape[1]
     outs = w.shape[1]
     lanes = rows * width
-    size = lanes // LANES * seqs + rows * pl.cdiv(n * seqs, LANES)
+    size = CORES * lanes // LANES * seqs + rows * pl.cdiv(n * seqs, LANES)
     axes = ("res", "seq")
     flags = flags.T
 
@@ -248,7 +247,7 @@
         cost_estimate=pl.CostEstimate(flops=1 << 25, bytes_accessed=x.size * 8, transcendentals=0),
         name="load",
     )(*operands)
-    wire = jax.ShapeDtypeStruct((CORES, size, LANES), BF16)
+    wire = jax.ShapeDtypeStruct((size, LANES), BF16)
     left, right = pl.pallas_call(
         functools.partial(project_kernel, width),
         out_shape=(wire, wire),

time: 13.2 us -> 13.1 us (level)
  no operation moved by 1% of the time
where the time goes in v20:
time: 13.1 us; the launch traced here: 12.9 us
  starting transfers between devices  6.76 us (52%)
  Pallas kernels  3.53 us (27%)
  waiting for transfers between devices  2.59 us (20%)
    ppermute x2, starting transfers between devices, local(): lax.ppermute(right, axes, [(a * n + p, step[a][p] * n + a) for a in range...  3.61 us
    ppermute x1, starting transfers between devices, local(): lax.ppermute(left, axes, [(a * n + p, a * n + step[a][p]) for a in range(...  2.65 us
    ppermute x2, waiting for transfers between devices, local(): lax.ppermute(right, axes, [(a * n + p, step[a][p] * n + a) for a in range...  2.3 us
    pallas_call x1, Pallas kernels, local(): pl.pallas_call(functools.partial(pair_kernel, seqs, rows, rows, width), o...  1.43 us
    pallas_call x1, Pallas kernels, local(): pl.pallas_call(load_kernel, out_shape=(jax.ShapeDtypeStruct(x.shape, x.dt...  1.04 us
    pallas_call x1, Pallas kernels, local(): pl.pallas_call(functools.partial(project_kernel, width), out_shape=(wire,...  0.78 us
    ppermute x1, starting transfers between devices, local(): lax.ppermute(x, 'seq', swap)  0.45 us
    pallas_call x1, Pallas kernels, local(): pl.pallas_call(functools.partial(left_kernel, steps, seqs, rows, width),...  0.28 us
  transfers between devices with their start and end apart: 5, of which 3 were waited for; matrix products, arithmetic and copies ran while one was open for 0% of the time, Pallas kernels for 10%

profile of v20, /device:TPU:0, one launch (start us, length us, event | category | flops | bytes accessed | tf_op | source)
XLA Modules:
  0.0 12.9 jit_solution(9730723911424432991)
XLA Ops:
  0.0 0.5 %collective-permute-start = (bf16[32,16,256]{2,1,0:T(8,128)(2,1)}, bf16[32,16,256]{2,1,0:T(8,128)(2,1)S(1)}, u32[]{:S(2)}, u32[]{:S(2)}) collective-permute-start(bf16[32,16,256]{2,1,0:T(8,128)(2,1)} %x_hbm.1), channel_id=1, source_target_pairs={{0,1},{1,0},{2,3},{3,2},{4,5},{5,4},{6,7},{7,6},{8,9},{9,8},{10,11... | collective-permute-start | bytes 786440 | tf_op jit(solution)/shard_map/ppermute | solution.py:230
  0.5 0.1 collective-permute-start.1
  0.5 1.0 %load.1 = (bf16[32,16,256]{2,1,0:T(8,128)(2,1)S(1)}, s32[16,32]{1,0:T(8,128)S(1)}, bf16[256,256]{1,0:T(8,128)(2,1)S(1)}, f32[8,256]{1,0:T(8,128)S(1)}) custom-call(bf16[32,16,256]{2,1,0:T(8,128)(2,1)} %x_hbm.1, s32[16,32]{1,0:T(8,128)} %bitcast.6, f32[256]{0:T(256)} %scale_hbm.1, f32[256]{0:T(256)} %shift_hbm.1, bf16[32,256]{1,0:T(8,128)(2,1)} %bitcast.3, ...), custom_call_target="tpu_custom_call" | custom-call | flops 33554432 | bytes 1048576 | tf_op jit(solution)/shard_map/load/pallas_call | solution.py:235
  1.6 0.3 %collective-permute-done.1.other_flag_ref = s32[16,32]{1,0:T(8,128)S(1)} collective-permute-done((s32[16,32]{1,0:T(8,128)}, s32[16,32]{1,0:T(8,128)S(1)}, u32[]{:S(2)}, u32[]{:S(2)}) %collective-permute-start.1) | collective-permute-done | bytes 2080 | tf_op jit(solution)/shard_map/ppermute | solution.py:230
  1.8 0.0 collective-permute-done.other_x_ref
  1.8 0.0 copy-start
  1.8 0.8 %project.1 = (bf16[272,128]{1,0:T(8,128)(2,1)S(1)}, bf16[272,128]{1,0:T(8,128)(2,1)S(1)}) custom-call(bf16[32,16,256]{2,1,0:T(8,128)(2,1)S(1)} %get-tuple-element.13.own_x_ref, s32[16,32]{1,0:T(8,128)S(1)} %get-tuple-element.14.own_flag_ref, bf16[32,16,256]{2,1,0:T(8,128)(2,1)S(1)} %collective-permute-done.other_x_ref, ...), custom_call_target="tpu_custom_call" | custom-call | tf_op jit(solution)/shard_map/project/pallas_call | solution.py:251
  2.6 2.6 %collective-permute-start.4 = (bf16[272,128]{1,0:T(8,128)(2,1)S(1)}, bf16[272,128]{1,0:T(8,128)(2,1)S(1)}, u32[]{:S(2)}, u32[]{:S(2)}) collective-permute-start(bf16[272,128]{1,0:T(8,128)(2,1)S(1)} %get-tuple-element.18.refs_0_), channel_id=1, source_target_pairs={{0,3},{1,2},{2,1},{3,0},{4,6},{5,7},{6,5},{7,4},{8,11},{9,10},{10,... | collective-permute-start | bytes 208904 | tf_op jit(solution)/shard_map/ppermute | solution.py:261
  5.3 3.6 %collective-permute-start.3 = (bf16[272,128]{1,0:T(8,128)(2,1)S(1)}, bf16[272,128]{1,0:T(8,128)(2,1)S(1)}, u32[]{:S(2)}, u32[]{:S(2)}) collective-permute-start(bf16[272,128]{1,0:T(8,128)(2,1)S(1)} %get-tuple-element.17), channel_id=1, source_target_pairs={{0,12},{1,8},{2,4},{3,0},{4,9},{5,13},{6,5},{7,1},{8,2},{9,6},{10,... | collective-permute-start | bytes 208904 | tf_op jit(solution)/shard_map/ppermute | solution.py:265
  8.9 0.0 collective-permute-start.2
  8.9 0.0 collective-permute-done.4.refs_1_
  8.9 0.3 %turn_left.1 = (bf16[512,128]{1,0:T(8,128)(2,1)S(1)}, bf16[16,128]{1,0:T(8,128)(2,1)S(1)}) custom-call(bf16[272,128]{1,0:T(8,128)(2,1)S(1)} %get-tuple-element.18.refs_0_, bf16[272,128]{1,0:T(8,128)(2,1)S(1)} %collective-permute-done.4.refs_1_), custom_call_target="tpu_custom_call" | custom-call | tf_op jit(solution)/shard_map/turn_left/pallas_call | solution.py:268
  9.2 1.6 %collective-permute-done.3.refs_1_ = bf16[272,128]{1,0:T(8,128)(2,1)S(1)} collective-permute-done((bf16[272,128]{1,0:T(8,128)(2,1)S(1)}, bf16[272,128]{1,0:T(8,128)(2,1)S(1)}, u32[]{:S(2)}, u32[]{:S(2)}) %collective-permute-start.3) | collective-permute-done | bytes 69664 | tf_op jit(solution)/shard_map/ppermute | solution.py:265
  10.8 0.7 %collective-permute-done.2.refs_0_ = bf16[272,128]{1,0:T(8,128)(2,1)S(1)} collective-permute-done((bf16[272,128]{1,0:T(8,128)(2,1)S(1)}, bf16[272,128]{1,0:T(8,128)(2,1)S(1)}, u32[]{:S(2)}, u32[]{:S(2)}) %collective-permute-start.2) | collective-permute-done | bytes 69664 | tf_op jit(solution)/shard_map/ppermute | solution.py:265
  11.5 0.0 copy-done
  11.5 1.4 %pair.1 = bf16[16,16,128]{2,1,0:T(8,128)(2,1)} custom-call(bf16[272,128]{1,0:T(8,128)(2,1)S(1)} %collective-permute-done.2.refs_0_, bf16[272,128]{1,0:T(8,128)(2,1)S(1)} %collective-permute-done.3.refs_1_, bf16[512,128]{1,0:T(8,128)(2,1)S(1)} %get-tuple-element.19.refs_2_, bf16[16,128]{1,0:T(8,128)(2,1)S(1)} %get-tuple-element.20.refs_3_, ...), custom_call_target="tpu_custom_call" | custom-call | tf_op jit(solution)/shard_map/pair/pallas_call | solution.py:278
Async XLA Ops:
  0.0 1.8 %collective-permute-start = (bf16[32,16,256]{2,1,0:T(8,128)(2,1)}, bf16[32,16,256]{2,1,0:T(8,128)(2,1)S(1)}, u32[]{:S(2)}, u32[]{:S(2)}) collective-permute-start(bf16[32,16,256]{2,1,0:T(8,128)(2,1)} %x_hbm.1), channel_id=1, source_target_pairs={{0,1},{1,0},{2,3},{3,2},{4,5},{5,4},{6,7},{7,6},{8,9},{9,8},{10,11... | collective-permute-start | bytes 786440 | tf_op jit(solution)/shard_map/ppermute | solution.py:230
  0.5 1.4 %collective-permute-start.1 = (s32[16,32]{1,0:T(8,128)}, s32[16,32]{1,0:T(8,128)S(1)}, u32[]{:S(2)}, u32[]{:S(2)}) collective-permute-start(s32[16,32]{1,0:T(8,128)} %bitcast.5), channel_id=1, source_target_pairs={{0,1},{1,0},{2,3},{3,2},{4,5},{5,4},{6,7},{7,6},{8,9},{9,8},{10,11... | collective-permute-start | bytes 6152 | tf_op jit(solution)/shard_map/ppermute | solution.py:230
  1.8 9.6 %copy-start = (bf16[1024,128]{1,0:T(8,128)(2,1)S(1)}, bf16[1024,128]{1,0:T(8,128)(2,1)}, u32[]{:S(2)}) copy-start(bf16[1024,128]{1,0:T(8,128)(2,1)} %refs_4_.1) | copy-start | bytes 786436
  2.6 6.3 %collective-permute-start.4 = (bf16[272,128]{1,0:T(8,128)(2,1)S(1)}, bf16[272,128]{1,0:T(8,128)(2,1)S(1)}, u32[]{:S(2)}, u32[]{:S(2)}) collective-permute-start(bf16[272,128]{1,0:T(8,128)(2,1)S(1)} %get-tuple-element.18.refs_0_), channel_id=1, source_target_pairs={{0,3},{1,2},{2,1},{3,0},{4,6},{5,7},{6,5},{7,4},{8,11},{9,10},{10,... | collective-permute-start | bytes 208904 | tf_op jit(solution)/shard_map/ppermute | solution.py:261
  5.3 5.5 %collective-permute-start.3 = (bf16[272,128]{1,0:T(8,128)(2,1)S(1)}, bf16[272,128]{1,0:T(8,128)(2,1)S(1)}, u32[]{:S(2)}, u32[]{:S(2)}) collective-permute-start(bf16[272,128]{1,0:T(8,128)(2,1)S(1)} %get-tuple-element.17), channel_id=1, source_target_pairs={{0,12},{1,8},{2,4},{3,0},{4,9},{5,13},{6,5},{7,1},{8,2},{9,6},{10,... | collective-permute-start | bytes 208904 | tf_op jit(solution)/shard_map/ppermute | solution.py:265
  8.9 2.6 %collective-permute-start.2 = (bf16[272,128]{1,0:T(8,128)(2,1)S(1)}, bf16[272,128]{1,0:T(8,128)(2,1)S(1)}, u32[]{:S(2)}, u32[]{:S(2)}) collective-permute-start(bf16[272,128]{1,0:T(8,128)(2,1)S(1)} %get-tuple-element.17), channel_id=1, source_target_pairs={{0,4},{1,0},{2,8},{3,12},{4,5},{5,1},{6,9},{7,13},{8,10},{9,14},{1... | collective-permute-start | bytes 208904 | tf_op jit(solution)/shard_map/ppermute | solution.py:265

commit v21 on v20

--- a/solution.py
+++ b/solution.py
@@ -54,21 +54,18 @@
     return chip
 
 
-def project_block(width, x_ref, flag_ref, weight, vectors, spreader, place, left_ref, right_ref, proj_ref):
+def norm_project(x_ref, weight, vectors):
     seqs, rows, depth = x_ref.shape
-    fold = LANES // width
-    lanes = rows * width
-    data = lanes // LANES * seqs
     x = x_ref[...].astype(F32).reshape(seqs * rows, depth)
     center = jnp.mean(x, axis=-1, keepdims=True)
     x = x - center
     spread = jnp.mean(x * x, axis=-1, keepdims=True)
     normed = x * lax.rsqrt(spread + 1e-05) * vectors[0:1] + vectors[1:2]
-    both = dot(normed.astype(BF16), weight, NT) + vectors[2:3]
-    proj_ref[0] = both[:, :LANES]
-    proj_ref[1] = both[:, LANES:]
-
-    mask = dot(flag_ref[...].astype(F32).astype(BF16), spreader, TN)
+    return dot(normed.astype(BF16), weight, NT) + vectors[2:3]
+
+
+def merge(width, seqs, rows, proj_ref, mask, place, left_ref, right_ref):
+    fold = LANES // width
     for half, out_ref in ((0, left_ref), (1, right_ref)):
         for tile in range(rows // fold):
             merged = proj_ref[half, pl.ds(tile * fold, seqs, stride=rows), :]
@@ -119,24 +116,23 @@
     core = block % CORES
     spreader = (iota((rows, lanes), 1) // width == iota((rows, lanes), 0)).astype(BF16)
     place = iota((seqs, LANES), 1) // width
-    for x_ref, flag_ref, proj_ref, at in (
-        (own_x_ref, own_flag_ref, own_proj_ref, core),
-        (other_x_ref, other_flag_ref, other_proj_ref, 1 - core),
-    ):
-        here = pl.ds(pl.multiple_of(at * data, data), data)
-        project_block(
-            width, x_ref, flag_ref, weight_ref[...], vector_ref[...], spreader, place,
-            left_ref.at[here], right_ref.at[here], proj_ref,
-        )
-    own, other = (
-        jnp.concatenate([ref[...].astype(F32)] * (LANES // seqs), axis=1) for ref in (own_flag_ref, other_flag_ref)
-    )
+    flags = [ref[...].astype(F32) for ref in (own_flag_ref, other_flag_ref)]
+    masks = [dot(f.astype(BF16), spreader, TN) for f in flags]
+    own, other = (jnp.concatenate([f] * (LANES // seqs), axis=1) for f in flags)
     for tile in range((left_ref.shape[0] - CORES * data) // rows):
         lane_block = iota((rows, LANES), 1) // seqs + tile * (LANES // seqs)
         placed = jnp.where(lane_block == block, own, jnp.where(lane_block == block + 1 - 2 * core, other, 0.0)).astype(BF16)
         first = CORES * data + tile * rows
         for out_ref in (left_ref, right_ref):
             out_ref[first:first + rows, :] = placed
+
+    for x_ref, proj_ref in ((own_x_ref, own_proj_ref), (other_x_ref, other_proj_ref)):
+        both = norm_project(x_ref, weight_ref[...], vector_ref[...])
+        proj_ref[0] = both[:, :LANES]
+        proj_ref[1] = both[:, LANES:]
+    for proj_ref, mask, at in ((own_proj_ref, masks[0], core), (other_proj_ref, masks[1], 1 - core)):
+        here = pl.ds(pl.multiple_of(at * data, data), data)
+        merge(width, seqs, rows, proj_ref, mask, place, left_ref.at[here], right_ref.at[here])
 
 
 def whole_mask(pieces, rows, data):
@@ -174,6 +170,9 @@
     assert fold == 4
     data = rows * width // LANES * seqs
 
+    count = dot(live_ref[...], whole_mask(rights, rows, data), NT)
+    scale = 1.0 / (1.0 + count)
+    scales = [jnp.broadcast_to(scale[:, j:j + 1], (rows, w_ref.shape[1])) for j in range(columns)]
     right = jnp.concatenate(
         [
             jnp.concatenate(
@@ -209,10 +208,8 @@
                 flat_ref[j * rows:(j + 1) * rows, quad * LANES:(quad + 1) * LANES] = part[k]
 
     raw = dot(flat_ref[...], w_ref[...]) + vector_ref[3:4, :LANES]
-    count = dot(live_ref[...], whole_mask(rights, rows, data), NT)
-    scale = 1.0 / (1.0 + count)
     for j in range(columns):
-        raw_ref[j * rows:(j + 1) * rows, :] = raw[j * rows:(j + 1) * rows, :] * scale[:, j:j + 1]
+        raw_ref[j * rows:(j + 1) * rows, :] = raw[j * rows:(j + 1) * rows, :] * scales[j]
     for i in range(rows):
         out_ref[i] = raw_ref[pl.ds(i, columns, stride=rows), :].astype(BF16)
 

time: 13.1 us -> 13.1 us (level)
  no operation moved by 1% of the time
where the time goes in v21:
time: 13.1 us; the launch traced here: 12.9 us
  starting transfers between devices  6.76 us (52%)
  Pallas kernels  3.54 us (27%)
  waiting for transfers between devices  2.59 us (20%)
    ppermute x2, starting transfers between devices, local(): lax.ppermute(right, axes, [(a * n + p, step[a][p] * n + a) for a in range...  3.61 us
    ppermute x1, starting transfers between devices, local(): lax.ppermute(left, axes, [(a * n + p, a * n + step[a][p]) for a in range(...  2.65 us
    ppermute x2, waiting for transfers between devices, local(): lax.ppermute(right, axes, [(a * n + p, step[a][p] * n + a) for a in range...  2.3 us
    pallas_call x1, Pallas kernels, local(): pl.pallas_call(functools.partial(pair_kernel, seqs, rows, rows, width), o...  1.35 us
    pallas_call x1, Pallas kernels, local(): pl.pallas_call(load_kernel, out_shape=(jax.ShapeDtypeStruct(x.shape, x.dt...  1.04 us
    pallas_call x1, Pallas kernels, local(): pl.pallas_call(functools.partial(project_kernel, width), out_shape=(wire,...  0.88 us
    ppermute x1, starting transfers between devices, local(): lax.ppermute(x, 'seq', swap)  0.45 us
    pallas_call x1, Pallas kernels, local(): pl.pallas_call(functools.partial(left_kernel, steps, seqs, rows, width),...  0.28 us
  transfers between devices with their start and end apart: 5, of which 3 were waited for; matrix products, arithmetic and copies ran while one was open for 0% of the time, Pallas kernels for 10%

profile of v21, /device:TPU:0, one launch (start us, length us, event | category | flops | bytes accessed | tf_op | source)
XLA Modules:
  0.0 12.9 jit_solution(6899863802290500162)
XLA Ops:
  0.0 0.5 %collective-permute-start = (bf16[32,16,256]{2,1,0:T(8,128)(2,1)}, bf16[32,16,256]{2,1,0:T(8,128)(2,1)S(1)}, u32[]{:S(2)}, u32[]{:S(2)}) collective-permute-start(bf16[32,16,256]{2,1,0:T(8,128)(2,1)} %x_hbm.1), channel_id=1, source_target_pairs={{0,1},{1,0},{2,3},{3,2},{4,5},{5,4},{6,7},{7,6},{8,9},{9,8},{10,11... | collective-permute-start | bytes 786440 | tf_op jit(solution)/shard_map/ppermute | solution.py:227
  0.5 0.1 collective-permute-start.1
  0.5 1.0 %load.1 = (bf16[32,16,256]{2,1,0:T(8,128)(2,1)S(1)}, s32[16,32]{1,0:T(8,128)S(1)}, bf16[256,256]{1,0:T(8,128)(2,1)S(1)}, f32[8,256]{1,0:T(8,128)S(1)}) custom-call(bf16[32,16,256]{2,1,0:T(8,128)(2,1)} %x_hbm.1, s32[16,32]{1,0:T(8,128)} %bitcast.6, f32[256]{0:T(256)} %scale_hbm.1, f32[256]{0:T(256)} %shift_hbm.1, bf16[32,256]{1,0:T(8,128)(2,1)} %bitcast.3, ...), custom_call_target="tpu_custom_call" | custom-call | flops 33554432 | bytes 1048576 | tf_op jit(solution)/shard_map/load/pallas_call | solution.py:232
  1.6 0.3 %collective-permute-done.1.other_flag_ref = s32[16,32]{1,0:T(8,128)S(1)} collective-permute-done((s32[16,32]{1,0:T(8,128)}, s32[16,32]{1,0:T(8,128)S(1)}, u32[]{:S(2)}, u32[]{:S(2)}) %collective-permute-start.1) | collective-permute-done | bytes 2080 | tf_op jit(solution)/shard_map/ppermute | solution.py:227
  1.8 0.0 collective-permute-done.other_x_ref
  1.8 0.0 copy-start
  1.8 0.9 %project.1 = (bf16[272,128]{1,0:T(8,128)(2,1)S(1)}, bf16[272,128]{1,0:T(8,128)(2,1)S(1)}) custom-call(bf16[32,16,256]{2,1,0:T(8,128)(2,1)S(1)} %get-tuple-element.13.own_x_ref, s32[16,32]{1,0:T(8,128)S(1)} %get-tuple-element.14.own_flag_ref, bf16[32,16,256]{2,1,0:T(8,128)(2,1)S(1)} %collective-permute-done.other_x_ref, ...), custom_call_target="tpu_custom_call" | custom-call | tf_op jit(solution)/shard_map/project/pallas_call | solution.py:248
  2.7 2.6 %collective-permute-start.4 = (bf16[272,128]{1,0:T(8,128)(2,1)S(1)}, bf16[272,128]{1,0:T(8,128)(2,1)S(1)}, u32[]{:S(2)}, u32[]{:S(2)}) collective-permute-start(bf16[272,128]{1,0:T(8,128)(2,1)S(1)} %get-tuple-element.18.refs_0_), channel_id=1, source_target_pairs={{0,3},{1,2},{2,1},{3,0},{4,6},{5,7},{6,5},{7,4},{8,11},{9,10},{10,... | collective-permute-start | bytes 208904 | tf_op jit(solution)/shard_map/ppermute | solution.py:258
  5.4 3.6 %collective-permute-start.3 = (bf16[272,128]{1,0:T(8,128)(2,1)S(1)}, bf16[272,128]{1,0:T(8,128)(2,1)S(1)}, u32[]{:S(2)}, u32[]{:S(2)}) collective-permute-start(bf16[272,128]{1,0:T(8,128)(2,1)S(1)} %get-tuple-element.17), channel_id=1, source_target_pairs={{0,12},{1,8},{2,4},{3,0},{4,9},{5,13},{6,5},{7,1},{8,2},{9,6},{10,... | collective-permute-start | bytes 208904 | tf_op jit(solution)/shard_map/ppermute | solution.py:262
  9.0 0.0 collective-permute-start.2
  9.0 0.0 collective-permute-done.4.refs_1_
  9.0 0.3 %turn_left.1 = (bf16[512,128]{1,0:T(8,128)(2,1)S(1)}, bf16[16,128]{1,0:T(8,128)(2,1)S(1)}) custom-call(bf16[272,128]{1,0:T(8,128)(2,1)S(1)} %get-tuple-element.18.refs_0_, bf16[272,128]{1,0:T(8,128)(2,1)S(1)} %collective-permute-done.4.refs_1_), custom_call_target="tpu_custom_call" | custom-call | tf_op jit(solution)/shard_map/turn_left/pallas_call | solution.py:265
  9.3 1.6 %collective-permute-done.3.refs_1_ = bf16[272,128]{1,0:T(8,128)(2,1)S(1)} collective-permute-done((bf16[272,128]{1,0:T(8,128)(2,1)S(1)}, bf16[272,128]{1,0:T(8,128)(2,1)S(1)}, u32[]{:S(2)}, u32[]{:S(2)}) %collective-permute-start.3) | collective-permute-done | bytes 69664 | tf_op jit(solution)/shard_map/ppermute | solution.py:262
  10.9 0.7 %collective-permute-done.2.refs_0_ = bf16[272,128]{1,0:T(8,128)(2,1)S(1)} collective-permute-done((bf16[272,128]{1,0:T(8,128)(2,1)S(1)}, bf16[272,128]{1,0:T(8,128)(2,1)S(1)}, u32[]{:S(2)}, u32[]{:S(2)}) %collective-permute-start.2) | collective-permute-done | bytes 69664 | tf_op jit(solution)/shard_map/ppermute | solution.py:262
  11.6 0.0 copy-done
  11.6 1.3 %pair.1 = bf16[16,16,128]{2,1,0:T(8,128)(2,1)} custom-call(bf16[272,128]{1,0:T(8,128)(2,1)S(1)} %collective-permute-done.2.refs_0_, bf16[272,128]{1,0:T(8,128)(2,1)S(1)} %collective-permute-done.3.refs_1_, bf16[512,128]{1,0:T(8,128)(2,1)S(1)} %get-tuple-element.19.refs_2_, bf16[16,128]{1,0:T(8,128)(2,1)S(1)} %get-tuple-element.20.refs_3_, ...), custom_call_target="tpu_custom_call" | custom-call | tf_op jit(solution)/shard_map/pair/pallas_call | solution.py:275
Async XLA Ops:
  0.0 1.8 %collective-permute-start = (bf16[32,16,256]{2,1,0:T(8,128)(2,1)}, bf16[32,16,256]{2,1,0:T(8,128)(2,1)S(1)}, u32[]{:S(2)}, u32[]{:S(2)}) collective-permute-start(bf16[32,16,256]{2,1,0:T(8,128)(2,1)} %x_hbm.1), channel_id=1, source_target_pairs={{0,1},{1,0},{2,3},{3,2},{4,5},{5,4},{6,7},{7,6},{8,9},{9,8},{10,11... | collective-permute-start | bytes 786440 | tf_op jit(solution)/shard_map/ppermute | solution.py:227
  0.5 1.4 %collective-permute-start.1 = (s32[16,32]{1,0:T(8,128)}, s32[16,32]{1,0:T(8,128)S(1)}, u32[]{:S(2)}, u32[]{:S(2)}) collective-permute-start(s32[16,32]{1,0:T(8,128)} %bitcast.5), channel_id=1, source_target_pairs={{0,1},{1,0},{2,3},{3,2},{4,5},{5,4},{6,7},{7,6},{8,9},{9,8},{10,11... | collective-permute-start | bytes 6152 | tf_op jit(solution)/shard_map/ppermute | solution.py:227
  1.8 9.7 %copy-start = (bf16[1024,128]{1,0:T(8,128)(2,1)S(1)}, bf16[1024,128]{1,0:T(8,128)(2,1)}, u32[]{:S(2)}) copy-start(bf16[1024,128]{1,0:T(8,128)(2,1)} %refs_4_.1) | copy-start | bytes 786436
  2.7 6.3 %collective-permute-start.4 = (bf16[272,128]{1,0:T(8,128)(2,1)S(1)}, bf16[272,128]{1,0:T(8,128)(2,1)S(1)}, u32[]{:S(2)}, u32[]{:S(2)}) collective-permute-start(bf16[272,128]{1,0:T(8,128)(2,1)S(1)} %get-tuple-element.18.refs_0_), channel_id=1, source_target_pairs={{0,3},{1,2},{2,1},{3,0},{4,6},{5,7},{6,5},{7,4},{8,11},{9,10},{10,... | collective-permute-start | bytes 208904 | tf_op jit(solution)/shard_map/ppermute | solution.py:258
  5.4 5.5 %collective-permute-start.3 = (bf16[272,128]{1,0:T(8,128)(2,1)S(1)}, bf16[272,128]{1,0:T(8,128)(2,1)S(1)}, u32[]{:S(2)}, u32[]{:S(2)}) collective-permute-start(bf16[272,128]{1,0:T(8,128)(2,1)S(1)} %get-tuple-element.17), channel_id=1, source_target_pairs={{0,12},{1,8},{2,4},{3,0},{4,9},{5,13},{6,5},{7,1},{8,2},{9,6},{10,... | collective-permute-start | bytes 208904 | tf_op jit(solution)/shard_map/ppermute | solution.py:262
  9.0 2.6 %collective-permute-start.2 = (bf16[272,128]{1,0:T(8,128)(2,1)S(1)}, bf16[272,128]{1,0:T(8,128)(2,1)S(1)}, u32[]{:S(2)}, u32[]{:S(2)}) collective-permute-start(bf16[272,128]{1,0:T(8,128)(2,1)S(1)} %get-tuple-element.17), channel_id=1, source_target_pairs={{0,4},{1,0},{2,8},{3,12},{4,5},{5,1},{6,9},{7,13},{8,10},{9,14},{1... | collective-permute-start | bytes 208904 | tf_op jit(solution)/shard_map/ppermute | solution.py:262

commit v22 on v20

--- a/solution.py
+++ b/solution.py
@@ -54,7 +54,7 @@
     return chip
 
 
-def project_block(width, x_ref, flag_ref, weight, vectors, spreader, place, left_ref, right_ref, proj_ref):
+def project_block(width, x_ref, mask_of, weight, vectors, place, left_ref, right_ref, proj_ref):
     seqs, rows, depth = x_ref.shape
     fold = LANES // width
     lanes = rows * width
@@ -68,7 +68,7 @@
     proj_ref[0] = both[:, :LANES]
     proj_ref[1] = both[:, LANES:]
 
-    mask = dot(flag_ref[...].astype(F32).astype(BF16), spreader, TN)
+    mask = mask_of()
     for half, out_ref in ((0, left_ref), (1, right_ref)):
         for tile in range(rows // fold):
             merged = proj_ref[half, pl.ds(tile * fold, seqs, stride=rows), :]
@@ -80,7 +80,7 @@
 
 
 def load_kernel(x_hbm, flag_hbm, scale_hbm, shift_hbm, wl_hbm, bl_hbm, wr_hbm, br_hbm, last_hbm,
-                x_ref, flag_ref, weight_ref, vector_ref,
+                x_ref, flag_ref, weight_ref, vector_ref, spreader_ref, mask_ref,
                 scale_ref, shift_ref, wl_ref, bl_ref, wr_ref, br_ref, last_ref, sems):
     copies = [
         pltpu.make_async_copy(src, dst, sems.at[k])
@@ -107,25 +107,31 @@
         ],
         axis=0,
     )
+    shape = spreader_ref.shape
+    spreader_ref[...] = (iota(shape, 1) // width == iota(shape, 0)).astype(BF16)
+    mask_ref[...] = spread_mask(flag_ref, spreader_ref)
     copies[0].wait()
 
 
+def spread_mask(flag_ref, spreader_ref):
+    return dot(flag_ref[...].astype(F32).astype(BF16), spreader_ref[...], TN)
+
+
 def project_kernel(width, own_x_ref, own_flag_ref, other_x_ref, other_flag_ref, weight_ref, vector_ref,
-                   left_ref, right_ref, own_proj_ref, other_proj_ref):
+                   spreader_ref, own_mask_ref, left_ref, right_ref, own_proj_ref, other_proj_ref):
     seqs, rows, _ = own_x_ref.shape
     lanes = rows * width
     data = lanes // LANES * seqs
     block = lax.axis_index("seq")
     core = block % CORES
-    spreader = (iota((rows, lanes), 1) // width == iota((rows, lanes), 0)).astype(BF16)
     place = iota((seqs, LANES), 1) // width
-    for x_ref, flag_ref, proj_ref, at in (
-        (own_x_ref, own_flag_ref, own_proj_ref, core),
-        (other_x_ref, other_flag_ref, other_proj_ref, 1 - core),
+    for x_ref, mask_of, proj_ref, at in (
+        (own_x_ref, lambda: own_mask_ref[...], own_proj_ref, core),
+        (other_x_ref, lambda: spread_mask(other_flag_ref, spreader_ref), other_proj_ref, 1 - core),
     ):
         here = pl.ds(pl.multiple_of(at * data, data), data)
         project_block(
-            width, x_ref, flag_ref, weight_ref[...], vector_ref[...], spreader, place,
+            width, x_ref, mask_of, weight_ref[...], vector_ref[...], place,
             left_ref.at[here], right_ref.at[here], proj_ref,
         )
     own, other = (
@@ -174,6 +180,9 @@
     assert fold == 4
     data = rows * width // LANES * seqs
 
+    count = dot(live_ref[...], whole_mask(rights, rows, data), NT)
+    scale = 1.0 / (1.0 + count)
+    scales = [jnp.broadcast_to(scale[:, j:j + 1], (rows, w_ref.shape[1])) for j in range(columns)]
     right = jnp.concatenate(
         [
             jnp.concatenate(
@@ -209,10 +218,8 @@
                 flat_ref[j * rows:(j + 1) * rows, quad * LANES:(quad + 1) * LANES] = part[k]
 
     raw = dot(flat_ref[...], w_ref[...]) + vector_ref[3:4, :LANES]
-    count = dot(live_ref[...], whole_mask(rights, rows, data), NT)
-    scale = 1.0 / (1.0 + count)
     for j in range(columns):
-        raw_ref[j * rows:(j + 1) * rows, :] = raw[j * rows:(j + 1) * rows, :] * scale[:, j:j + 1]
+        raw_ref[j * rows:(j + 1) * rows, :] = raw[j * rows:(j + 1) * rows, :] * scales[j]
     for i in range(rows):
         out_ref[i] = raw_ref[pl.ds(i, columns, stride=rows), :].astype(BF16)
 
@@ -232,13 +239,15 @@
     operands = [
         pltpu.with_memory_space_constraint(o, pltpu.HBM) for o in (x, flags, scale, shift, wl.T, bl, wr.T, br, bias)
     ]
-    own_x, own_flags, weight, vectors = pl.pallas_call(
+    own_x, own_flags, weight, vectors, spreader, own_mask = pl.pallas_call(
         load_kernel,
         out_shape=(
             jax.ShapeDtypeStruct(x.shape, x.dtype),
             jax.ShapeDtypeStruct(flags.shape, flags.dtype),
             jax.ShapeDtypeStruct((2 * LANES, depth), BF16),
             jax.ShapeDtypeStruct((8, 2 * LANES), F32),
+            jax.ShapeDtypeStruct((rows, lanes), BF16),
+            jax.ShapeDtypeStruct((seqs, lanes), F32),
         ),
         in_specs=[pl.BlockSpec(memory_space=pltpu.HBM)] * len(operands),
         scratch_shapes=[pltpu.VMEM(o.shape, o.dtype) for o in operands[2:]]
@@ -254,7 +263,7 @@
         scratch_shapes=[pltpu.VMEM((2, seqs * rows, LANES), F32)] * 2,
         compiler_params=pltpu.CompilerParams(vmem_limit_bytes=16 << 20),
         name="project",
-    )(own_x, own_flags, other_x, other_flags, weight, vectors)
+    )(own_x, own_flags, other_x, other_flags, weight, vectors, spreader, own_mask)
 
     steps = right_routes(n)
     lefts = [left] + [

time: 13.1 us -> 13 us (level)
  transfers between devices with their start and end apart: 5 -> 5, of which waited for: 3 -> 3; matrix products, arithmetic and copies ran while one was open for 0% -> 0% of each run, Pallas kernels for 10% -> 11%
where the time goes in v22:
time: 13 us; the launch traced here: 12.8 us
  starting transfers between devices  6.76 us (52%)
  Pallas kernels  3.54 us (27%)
  waiting for transfers between devices  2.49 us (19%)
    ppermute x2, starting transfers between devices, local(): lax.ppermute(right, axes, [(a * n + p, step[a][p] * n + a) for a in range...  3.61 us
    ppermute x1, starting transfers between devices, local(): lax.ppermute(left, axes, [(a * n + p, a * n + step[a][p]) for a in range(...  2.65 us
    ppermute x2, waiting for transfers between devices, local(): lax.ppermute(right, axes, [(a * n + p, step[a][p] * n + a) for a in range...  2.3 us
    pallas_call x1, Pallas kernels, local(): pl.pallas_call(functools.partial(pair_kernel, seqs, rows, rows, width), o...  1.35 us
    pallas_call x1, Pallas kernels, local(): pl.pallas_call(load_kernel, out_shape=(jax.ShapeDtypeStruct(x.shape, x.dt...  1.14 us
    pallas_call x1, Pallas kernels, local(): pl.pallas_call(functools.partial(project_kernel, width), out_shape=(wire,...  0.78 us
    ppermute x1, starting transfers between devices, local(): lax.ppermute(x, 'seq', swap)  0.45 us
    pallas_call x1, Pallas kernels, local(): pl.pallas_call(functools.partial(left_kernel, steps, seqs, rows, width),...  0.28 us
  transfers between devices with their start and end apart: 5, of which 3 were waited for; matrix products, arithmetic and copies ran while one was open for 0% of the time, Pallas kernels for 11%

profile of v22, /device:TPU:0, one launch (start us, length us, event | category | flops | bytes accessed | tf_op | source)
XLA Modules:
  0.0 12.8 jit_solution(11269504725160692703)
XLA Ops:
  0.0 0.5 %collective-permute-start = (bf16[32,16,256]{2,1,0:T(8,128)(2,1)}, bf16[32,16,256]{2,1,0:T(8,128)(2,1)S(1)}, u32[]{:S(2)}, u32[]{:S(2)}) collective-permute-start(bf16[32,16,256]{2,1,0:T(8,128)(2,1)} %x_hbm.1), channel_id=1, source_target_pairs={{0,1},{1,0},{2,3},{3,2},{4,5},{5,4},{6,7},{7,6},{8,9},{9,8},{10,11... | collective-permute-start | bytes 786440 | tf_op jit(solution)/shard_map/ppermute | solution.py:237
  0.5 0.1 collective-permute-start.1
  0.5 1.1 %load.1 = (bf16[32,16,256]{2,1,0:T(8,128)(2,1)S(1)}, s32[16,32]{1,0:T(8,128)S(1)}, bf16[256,256]{1,0:T(8,128)(2,1)S(1)}, f32[8,256]{1,0:T(8,128)S(1)}, bf16[16,5...) custom-call(bf16[32,16,256]{2,1,0:T(8,128)(2,1)} %x_hbm.1, s32[16,32]{1,0:T(8,128)} %bitcast.6, f32[256]{0:T(256)} %scale_hbm.1, ...), custom_call_target="tpu_custom_call" | custom-call | flops 33554432 | bytes 1048576 | tf_op jit(solution)/shard_map/load/pallas_call | solution.py:242
  1.7 0.2 %collective-permute-done.1.other_flag_ref = s32[16,32]{1,0:T(8,128)S(1)} collective-permute-done((s32[16,32]{1,0:T(8,128)}, s32[16,32]{1,0:T(8,128)S(1)}, u32[]{:S(2)}, u32[]{:S(2)}) %collective-permute-start.1) | collective-permute-done | bytes 2080 | tf_op jit(solution)/shard_map/ppermute | solution.py:237
  1.8 0.0 collective-permute-done.other_x_ref
  1.8 0.0 copy-start
  1.8 0.8 %project.1 = (bf16[272,128]{1,0:T(8,128)(2,1)S(1)}, bf16[272,128]{1,0:T(8,128)(2,1)S(1)}) custom-call(bf16[32,16,256]{2,1,0:T(8,128)(2,1)S(1)} %get-tuple-element.15.own_x_ref, s32[16,32]{1,0:T(8,128)S(1)} %get-tuple-element.16.own_flag_ref, bf16[32,16,256]{2,1,0:T(8,128)(2,1)S(1)} %collective-permute-done.other_x_ref, ...), custom_call_target="tpu_custom_call" | custom-call | tf_op jit(solution)/shard_map/project/pallas_call | solution.py:260
  2.6 2.6 %collective-permute-start.4 = (bf16[272,128]{1,0:T(8,128)(2,1)S(1)}, bf16[272,128]{1,0:T(8,128)(2,1)S(1)}, u32[]{:S(2)}, u32[]{:S(2)}) collective-permute-start(bf16[272,128]{1,0:T(8,128)(2,1)S(1)} %get-tuple-element.22.refs_0_), channel_id=1, source_target_pairs={{0,3},{1,2},{2,1},{3,0},{4,6},{5,7},{6,5},{7,4},{8,11},{9,10},{10,... | collective-permute-start | bytes 208904 | tf_op jit(solution)/shard_map/ppermute | solution.py:270
  5.3 3.6 %collective-permute-start.3 = (bf16[272,128]{1,0:T(8,128)(2,1)S(1)}, bf16[272,128]{1,0:T(8,128)(2,1)S(1)}, u32[]{:S(2)}, u32[]{:S(2)}) collective-permute-start(bf16[272,128]{1,0:T(8,128)(2,1)S(1)} %get-tuple-element.21), channel_id=1, source_target_pairs={{0,12},{1,8},{2,4},{3,0},{4,9},{5,13},{6,5},{7,1},{8,2},{9,6},{10,... | collective-permute-start | bytes 208904 | tf_op jit(solution)/shard_map/ppermute | solution.py:274
  8.9 0.0 collective-permute-start.2
  8.9 0.0 collective-permute-done.4.refs_1_
  8.9 0.3 %turn_left.1 = (bf16[512,128]{1,0:T(8,128)(2,1)S(1)}, bf16[16,128]{1,0:T(8,128)(2,1)S(1)}) custom-call(bf16[272,128]{1,0:T(8,128)(2,1)S(1)} %get-tuple-element.22.refs_0_, bf16[272,128]{1,0:T(8,128)(2,1)S(1)} %collective-permute-done.4.refs_1_), custom_call_target="tpu_custom_call" | custom-call | tf_op jit(solution)/shard_map/turn_left/pallas_call | solution.py:277
  9.2 1.6 %collective-permute-done.3.refs_1_ = bf16[272,128]{1,0:T(8,128)(2,1)S(1)} collective-permute-done((bf16[272,128]{1,0:T(8,128)(2,1)S(1)}, bf16[272,128]{1,0:T(8,128)(2,1)S(1)}, u32[]{:S(2)}, u32[]{:S(2)}) %collective-permute-start.3) | collective-permute-done | bytes 69664 | tf_op jit(solution)/shard_map/ppermute | solution.py:274
  10.8 0.7 %collective-permute-done.2.refs_0_ = bf16[272,128]{1,0:T(8,128)(2,1)S(1)} collective-permute-done((bf16[272,128]{1,0:T(8,128)(2,1)S(1)}, bf16[272,128]{1,0:T(8,128)(2,1)S(1)}, u32[]{:S(2)}, u32[]{:S(2)}) %collective-permute-start.2) | collective-permute-done | bytes 69664 | tf_op jit(solution)/shard_map/ppermute | solution.py:274
  11.5 0.0 copy-done
  11.5 1.3 %pair.1 = bf16[16,16,128]{2,1,0:T(8,128)(2,1)} custom-call(bf16[272,128]{1,0:T(8,128)(2,1)S(1)} %collective-permute-done.2.refs_0_, bf16[272,128]{1,0:T(8,128)(2,1)S(1)} %collective-permute-done.3.refs_1_, bf16[512,128]{1,0:T(8,128)(2,1)S(1)} %get-tuple-element.23.refs_2_, bf16[16,128]{1,0:T(8,128)(2,1)S(1)} %get-tuple-element.24.refs_3_, ...), custom_call_target="tpu_custom_call" | custom-call | tf_op jit(solution)/shard_map/pair/pallas_call | solution.py:287
Async XLA Ops:
  0.0 1.8 %collective-permute-start = (bf16[32,16,256]{2,1,0:T(8,128)(2,1)}, bf16[32,16,256]{2,1,0:T(8,128)(2,1)S(1)}, u32[]{:S(2)}, u32[]{:S(2)}) collective-permute-start(bf16[32,16,256]{2,1,0:T(8,128)(2,1)} %x_hbm.1), channel_id=1, source_target_pairs={{0,1},{1,0},{2,3},{3,2},{4,5},{5,4},{6,7},{7,6},{8,9},{9,8},{10,11... | collective-permute-start | bytes 786440 | tf_op jit(solution)/shard_map/ppermute | solution.py:237
  0.5 1.4 %collective-permute-start.1 = (s32[16,32]{1,0:T(8,128)}, s32[16,32]{1,0:T(8,128)S(1)}, u32[]{:S(2)}, u32[]{:S(2)}) collective-permute-start(s32[16,32]{1,0:T(8,128)} %bitcast.5), channel_id=1, source_target_pairs={{0,1},{1,0},{2,3},{3,2},{4,5},{5,4},{6,7},{7,6},{8,9},{9,8},{10,11... | collective-permute-start | bytes 6152 | tf_op jit(solution)/shard_map/ppermute | solution.py:237
  1.8 9.6 %copy-start = (bf16[1024,128]{1,0:T(8,128)(2,1)S(1)}, bf16[1024,128]{1,0:T(8,128)(2,1)}, u32[]{:S(2)}) copy-start(bf16[1024,128]{1,0:T(8,128)(2,1)} %refs_4_.1) | copy-start | bytes 786436
  2.6 6.3 %collective-permute-start.4 = (bf16[272,128]{1,0:T(8,128)(2,1)S(1)}, bf16[272,128]{1,0:T(8,128)(2,1)S(1)}, u32[]{:S(2)}, u32[]{:S(2)}) collective-permute-start(bf16[272,128]{1,0:T(8,128)(2,1)S(1)} %get-tuple-element.22.refs_0_), channel_id=1, source_target_pairs={{0,3},{1,2},{2,1},{3,0},{4,6},{5,7},{6,5},{7,4},{8,11},{9,10},{10,... | collective-permute-start | bytes 208904 | tf_op jit(solution)/shard_map/ppermute | solution.py:270
  5.3 5.5 %collective-permute-start.3 = (bf16[272,128]{1,0:T(8,128)(2,1)S(1)}, bf16[272,128]{1,0:T(8,128)(2,1)S(1)}, u32[]{:S(2)}, u32[]{:S(2)}) collective-permute-start(bf16[272,128]{1,0:T(8,128)(2,1)S(1)} %get-tuple-element.21), channel_id=1, source_target_pairs={{0,12},{1,8},{2,4},{3,0},{4,9},{5,13},{6,5},{7,1},{8,2},{9,6},{10,... | collective-permute-start | bytes 208904 | tf_op jit(solution)/shard_map/ppermute | solution.py:274
  8.9 2.6 %collective-permute-start.2 = (bf16[272,128]{1,0:T(8,128)(2,1)S(1)}, bf16[272,128]{1,0:T(8,128)(2,1)S(1)}, u32[]{:S(2)}, u32[]{:S(2)}) collective-permute-start(bf16[272,128]{1,0:T(8,128)(2,1)S(1)} %get-tuple-element.21), channel_id=1, source_target_pairs={{0,4},{1,0},{2,8},{3,12},{4,5},{5,1},{6,9},{7,13},{8,10},{9,14},{1... | collective-permute-start | bytes 208904 | tf_op jit(solution)/shard_map/ppermute | solution.py:274

commit v23 on v22

--- a/solution.py
+++ b/solution.py
@@ -25,10 +25,10 @@
 
 
 RIGHT = (
-    ((1, 0, 2, 3), (1, 0, 2, 3), (2, 3, 1, 0), (3, 1, 0, 2)),
-    ((3, 2, 1, 0), (2, 3, 1, 0), (0, 1, 3, 2), (2, 0, 3, 1)),
+    ((1, 0, 2, 3), (1, 0, 2, 3), (1, 3, 0, 2), (2, 1, 3, 0)),
+    ((3, 2, 0, 1), (2, 3, 0, 1), (0, 2, 3, 1), (3, 0, 1, 2)),
 )
-LEFT = ((3, 2, 1, 0), (2, 3, 1, 0), (3, 2, 0, 1), (3, 2, 1, 0))
+LEFT = ((2, 3, 1, 0), (3, 2, 0, 1), (3, 2, 1, 0), (3, 2, 0, 1))
 
 
 def right_routes(n):
@@ -199,8 +199,8 @@
     even = [None] * fold
     even[1] = (place == 0.0) | (place == 2.0)
     even[2] = (place == 0.0) | (place == 1.0)
-    for tile in range(columns // fold):
-        for quad in range(width // fold):
+    for quad in range(width // fold):
+        for tile in range(columns // fold):
             part = [
                 outer[(quad * fold + k) * rows:(quad * fold + k + 1) * rows, tile * LANES:(tile + 1) * LANES]
                 for k in range(fold)

time: 13 us -> 13 us (level)
    ppermute x2, starting transfers between devices: 3.61 us -> 3.34 us  [local(): lax.ppermute(right, axes, [(a * n + p, step[a][p] * n + a) for a in range...]
    ppermute x1, starting transfers between devices: 2.65 us -> 2.91 us  [local(): lax.ppermute(left, axes, [(a * n + p, a * n + step[a][p]) for a in range(...]
where the time goes in v23:
time: 13 us; the launch traced here: 12.8 us
  starting transfers between devices  6.76 us (52%)
  Pallas kernels  3.54 us (27%)
  waiting for transfers between devices  2.49 us (19%)
    ppermute x2, starting transfers between devices, local(): lax.ppermute(right, axes, [(a * n + p, step[a][p] * n + a) for a in range...  3.34 us
    ppermute x1, starting transfers between devices, local(): lax.ppermute(left, axes, [(a * n + p, a * n + step[a][p]) for a in range(...  2.91 us
    ppermute x2, waiting for transfers between devices, local(): lax.ppermute(right, axes, [(a * n + p, step[a][p] * n + a) for a in range...  2.3 us
    pallas_call x1, Pallas kernels, local(): pl.pallas_call(functools.partial(pair_kernel, seqs, rows, rows, width), o...  1.35 us
    pallas_call x1, Pallas kernels, local(): pl.pallas_call(load_kernel, out_shape=(jax.ShapeDtypeStruct(x.shape, x.dt...  1.14 us
    pallas_call x1, Pallas kernels, local(): pl.pallas_call(functools.partial(project_kernel, width), out_shape=(wire,...  0.78 us
    ppermute x1, starting transfers between devices, local(): lax.ppermute(x, 'seq', swap)  0.45 us
    pallas_call x1, Pallas kernels, local(): pl.pallas_call(functools.partial(left_kernel, steps, seqs, rows, width),...  0.28 us
  transfers between devices with their start and end apart: 5, of which 3 were waited for; matrix products, arithmetic and copies ran while one was open for 0% of the time, Pallas kernels for 11%

profile of v23, /device:TPU:0, one launch (start us, length us, event | category | flops | bytes accessed | tf_op | source)
XLA Modules:
  0.0 12.8 jit_solution(16682362613612619242)
XLA Ops:
  0.0 0.5 %collective-permute-start = (bf16[32,16,256]{2,1,0:T(8,128)(2,1)}, bf16[32,16,256]{2,1,0:T(8,128)(2,1)S(1)}, u32[]{:S(2)}, u32[]{:S(2)}) collective-permute-start(bf16[32,16,256]{2,1,0:T(8,128)(2,1)} %x_hbm.1), channel_id=1, source_target_pairs={{0,1},{1,0},{2,3},{3,2},{4,5},{5,4},{6,7},{7,6},{8,9},{9,8},{10,11... | collective-permute-start | bytes 786440 | tf_op jit(solution)/shard_map/ppermute | solution.py:237
  0.5 0.1 collective-permute-start.1
  0.5 1.1 %load.1 = (bf16[32,16,256]{2,1,0:T(8,128)(2,1)S(1)}, s32[16,32]{1,0:T(8,128)S(1)}, bf16[256,256]{1,0:T(8,128)(2,1)S(1)}, f32[8,256]{1,0:T(8,128)S(1)}, bf16[16,5...) custom-call(bf16[32,16,256]{2,1,0:T(8,128)(2,1)} %x_hbm.1, s32[16,32]{1,0:T(8,128)} %bitcast.6, f32[256]{0:T(256)} %scale_hbm.1, ...), custom_call_target="tpu_custom_call" | custom-call | flops 33554432 | bytes 1048576 | tf_op jit(solution)/shard_map/load/pallas_call | solution.py:242
  1.7 0.2 %collective-permute-done.1.other_flag_ref = s32[16,32]{1,0:T(8,128)S(1)} collective-permute-done((s32[16,32]{1,0:T(8,128)}, s32[16,32]{1,0:T(8,128)S(1)}, u32[]{:S(2)}, u32[]{:S(2)}) %collective-permute-start.1) | collective-permute-done | bytes 2080 | tf_op jit(solution)/shard_map/ppermute | solution.py:237
  1.8 0.0 collective-permute-done.other_x_ref
  1.8 0.0 copy-start
  1.8 0.8 %project.1 = (bf16[272,128]{1,0:T(8,128)(2,1)S(1)}, bf16[272,128]{1,0:T(8,128)(2,1)S(1)}) custom-call(bf16[32,16,256]{2,1,0:T(8,128)(2,1)S(1)} %get-tuple-element.15.own_x_ref, s32[16,32]{1,0:T(8,128)S(1)} %get-tuple-element.16.own_flag_ref, bf16[32,16,256]{2,1,0:T(8,128)(2,1)S(1)} %collective-permute-done.other_x_ref, ...), custom_call_target="tpu_custom_call" | custom-call | tf_op jit(solution)/shard_map/project/pallas_call | solution.py:260
  2.6 2.9 %collective-permute-start.4 = (bf16[272,128]{1,0:T(8,128)(2,1)S(1)}, bf16[272,128]{1,0:T(8,128)(2,1)S(1)}, u32[]{:S(2)}, u32[]{:S(2)}) collective-permute-start(bf16[272,128]{1,0:T(8,128)(2,1)S(1)} %get-tuple-element.22.refs_0_), channel_id=1, source_target_pairs={{0,2},{1,3},{2,1},{3,0},{4,7},{5,6},{6,4},{7,5},{8,11},{9,10},{10,... | collective-permute-start | bytes 208904 | tf_op jit(solution)/shard_map/ppermute | solution.py:270
  5.5 3.3 %collective-permute-start.3 = (bf16[272,128]{1,0:T(8,128)(2,1)S(1)}, bf16[272,128]{1,0:T(8,128)(2,1)S(1)}, u32[]{:S(2)}, u32[]{:S(2)}) collective-permute-start(bf16[272,128]{1,0:T(8,128)(2,1)S(1)} %get-tuple-element.21), channel_id=1, source_target_pairs={{0,12},{1,8},{2,0},{3,4},{4,9},{5,13},{6,1},{7,5},{8,2},{9,10},{10... | collective-permute-start | bytes 208904 | tf_op jit(solution)/shard_map/ppermute | solution.py:274
  8.9 0.0 collective-permute-start.2
  8.9 0.0 collective-permute-done.4.refs_1_
  8.9 0.3 %turn_left.1 = (bf16[512,128]{1,0:T(8,128)(2,1)S(1)}, bf16[16,128]{1,0:T(8,128)(2,1)S(1)}) custom-call(bf16[272,128]{1,0:T(8,128)(2,1)S(1)} %get-tuple-element.22.refs_0_, bf16[272,128]{1,0:T(8,128)(2,1)S(1)} %collective-permute-done.4.refs_1_), custom_call_target="tpu_custom_call" | custom-call | tf_op jit(solution)/shard_map/turn_left/pallas_call | solution.py:277
  9.2 1.6 %collective-permute-done.3.refs_1_ = bf16[272,128]{1,0:T(8,128)(2,1)S(1)} collective-permute-done((bf16[272,128]{1,0:T(8,128)(2,1)S(1)}, bf16[272,128]{1,0:T(8,128)(2,1)S(1)}, u32[]{:S(2)}, u32[]{:S(2)}) %collective-permute-start.3) | collective-permute-done | bytes 69664 | tf_op jit(solution)/shard_map/ppermute | solution.py:274
  10.8 0.7 %collective-permute-done.2.refs_0_ = bf16[272,128]{1,0:T(8,128)(2,1)S(1)} collective-permute-done((bf16[272,128]{1,0:T(8,128)(2,1)S(1)}, bf16[272,128]{1,0:T(8,128)(2,1)S(1)}, u32[]{:S(2)}, u32[]{:S(2)}) %collective-permute-start.2) | collective-permute-done | bytes 69664 | tf_op jit(solution)/shard_map/ppermute | solution.py:274
  11.5 0.0 copy-done
  11.5 1.3 %pair.1 = bf16[16,16,128]{2,1,0:T(8,128)(2,1)} custom-call(bf16[272,128]{1,0:T(8,128)(2,1)S(1)} %collective-permute-done.2.refs_0_, bf16[272,128]{1,0:T(8,128)(2,1)S(1)} %collective-permute-done.3.refs_1_, bf16[512,128]{1,0:T(8,128)(2,1)S(1)} %get-tuple-element.23.refs_2_, bf16[16,128]{1,0:T(8,128)(2,1)S(1)} %get-tuple-element.24.refs_3_, ...), custom_call_target="tpu_custom_call" | custom-call | tf_op jit(solution)/shard_map/pair/pallas_call | solution.py:287
Async XLA Ops:
  0.0 1.8 %collective-permute-start = (bf16[32,16,256]{2,1,0:T(8,128)(2,1)}, bf16[32,16,256]{2,1,0:T(8,128)(2,1)S(1)}, u32[]{:S(2)}, u32[]{:S(2)}) collective-permute-start(bf16[32,16,256]{2,1,0:T(8,128)(2,1)} %x_hbm.1), channel_id=1, source_target_pairs={{0,1},{1,0},{2,3},{3,2},{4,5},{5,4},{6,7},{7,6},{8,9},{9,8},{10,11... | collective-permute-start | bytes 786440 | tf_op jit(solution)/shard_map/ppermute | solution.py:237
  0.5 1.4 %collective-permute-start.1 = (s32[16,32]{1,0:T(8,128)}, s32[16,32]{1,0:T(8,128)S(1)}, u32[]{:S(2)}, u32[]{:S(2)}) collective-permute-start(s32[16,32]{1,0:T(8,128)} %bitcast.5), channel_id=1, source_target_pairs={{0,1},{1,0},{2,3},{3,2},{4,5},{5,4},{6,7},{7,6},{8,9},{9,8},{10,11... | collective-permute-start | bytes 6152 | tf_op jit(solution)/shard_map/ppermute | solution.py:237
  1.8 9.6 %copy-start = (bf16[1024,128]{1,0:T(8,128)(2,1)S(1)}, bf16[1024,128]{1,0:T(8,128)(2,1)}, u32[]{:S(2)}) copy-start(bf16[1024,128]{1,0:T(8,128)(2,1)} %refs_4_.1) | copy-start | bytes 786436
  2.6 6.3 %collective-permute-start.4 = (bf16[272,128]{1,0:T(8,128)(2,1)S(1)}, bf16[272,128]{1,0:T(8,128)(2,1)S(1)}, u32[]{:S(2)}, u32[]{:S(2)}) collective-permute-start(bf16[272,128]{1,0:T(8,128)(2,1)S(1)} %get-tuple-element.22.refs_0_), channel_id=1, source_target_pairs={{0,2},{1,3},{2,1},{3,0},{4,7},{5,6},{6,4},{7,5},{8,11},{9,10},{10,... | collective-permute-start | bytes 208904 | tf_op jit(solution)/shard_map/ppermute | solution.py:270
  5.5 5.3 %collective-permute-start.3 = (bf16[272,128]{1,0:T(8,128)(2,1)S(1)}, bf16[272,128]{1,0:T(8,128)(2,1)S(1)}, u32[]{:S(2)}, u32[]{:S(2)}) collective-permute-start(bf16[272,128]{1,0:T(8,128)(2,1)S(1)} %get-tuple-element.21), channel_id=1, source_target_pairs={{0,12},{1,8},{2,0},{3,4},{4,9},{5,13},{6,1},{7,5},{8,2},{9,10},{10... | collective-permute-start | bytes 208904 | tf_op jit(solution)/shard_map/ppermute | solution.py:274
  8.9 2.6 %collective-permute-start.2 = (bf16[272,128]{1,0:T(8,128)(2,1)S(1)}, bf16[272,128]{1,0:T(8,128)(2,1)S(1)}, u32[]{:S(2)}, u32[]{:S(2)}) collective-permute-start(bf16[272,128]{1,0:T(8,128)(2,1)S(1)} %get-tuple-element.21), channel_id=1, source_target_pairs={{0,4},{1,0},{2,8},{3,12},{4,5},{5,1},{6,9},{7,13},{8,6},{9,14},{10... | collective-permute-start | bytes 208904 | tf_op jit(solution)/shard_map/ppermute | solution.py:274

commit v24 on v23

--- a/solution.py
+++ b/solution.py
@@ -54,17 +54,18 @@
     return chip
 
 
-def project_block(width, x_ref, mask_of, weight, vectors, place, left_ref, right_ref, proj_ref):
+def norm(x_ref, vectors):
     seqs, rows, depth = x_ref.shape
-    fold = LANES // width
-    lanes = rows * width
-    data = lanes // LANES * seqs
     x = x_ref[...].astype(F32).reshape(seqs * rows, depth)
     center = jnp.mean(x, axis=-1, keepdims=True)
     x = x - center
     spread = jnp.mean(x * x, axis=-1, keepdims=True)
-    normed = x * lax.rsqrt(spread + 1e-05) * vectors[0:1] + vectors[1:2]
-    both = dot(normed.astype(BF16), weight, NT) + vectors[2:3]
+    return (x * lax.rsqrt(spread + 1e-05) * vectors[0:1] + vectors[1:2]).astype(BF16)
+
+
+def project_block(width, seqs, rows, normed, mask_of, weight, vectors, place, left_ref, right_ref, proj_ref):
+    fold = LANES // width
+    both = dot(normed, weight, NT) + vectors[2:3]
     proj_ref[0] = both[:, :LANES]
     proj_ref[1] = both[:, LANES:]
 
@@ -80,8 +81,8 @@
 
 
 def load_kernel(x_hbm, flag_hbm, scale_hbm, shift_hbm, wl_hbm, bl_hbm, wr_hbm, br_hbm, last_hbm,
-                x_ref, flag_ref, weight_ref, vector_ref, spreader_ref, mask_ref,
-                scale_ref, shift_ref, wl_ref, bl_ref, wr_ref, br_ref, last_ref, sems):
+                normed_ref, flag_ref, weight_ref, vector_ref, spreader_ref, mask_ref,
+                x_ref, scale_ref, shift_ref, wl_ref, bl_ref, wr_ref, br_ref, last_ref, sems):
     copies = [
         pltpu.make_async_copy(src, dst, sems.at[k])
         for k, (src, dst) in enumerate((
@@ -111,27 +112,31 @@
     spreader_ref[...] = (iota(shape, 1) // width == iota(shape, 0)).astype(BF16)
     mask_ref[...] = spread_mask(flag_ref, spreader_ref)
     copies[0].wait()
+    normed_ref[...] = norm(x_ref, vector_ref[...])
 
 
 def spread_mask(flag_ref, spreader_ref):
     return dot(flag_ref[...].astype(F32).astype(BF16), spreader_ref[...], TN)
 
 
-def project_kernel(width, own_x_ref, own_flag_ref, other_x_ref, other_flag_ref, weight_ref, vector_ref,
+def project_kernel(width, own_normed_ref, own_flag_ref, other_x_ref, other_flag_ref, weight_ref, vector_ref,
                    spreader_ref, own_mask_ref, left_ref, right_ref, own_proj_ref, other_proj_ref):
-    seqs, rows, _ = own_x_ref.shape
+    seqs, rows, _ = other_x_ref.shape
     lanes = rows * width
     data = lanes // LANES * seqs
     block = lax.axis_index("seq")
     core = block % CORES
     place = iota((seqs, LANES), 1) // width
-    for x_ref, mask_of, proj_ref, at in (
-        (own_x_ref, lambda: own_mask_ref[...], own_proj_ref, core),
-        (other_x_ref, lambda: spread_mask(other_flag_ref, spreader_ref), other_proj_ref, 1 - core),
+    for normed_of, mask_of, proj_ref, at in (
+        (lambda: own_normed_ref[...], lambda: own_mask_ref[...], own_proj_ref, core),
+        (
+            lambda: norm(other_x_ref, vector_ref[...]), lambda: spread_mask(other_flag_ref, spreader_ref),
+            other_proj_ref, 1 - core,
+        ),
     ):
         here = pl.ds(pl.multiple_of(at * data, data), data)
         project_block(
-            width, x_ref, mask_of, weight_ref[...], vector_ref[...], place,
+            width, seqs, rows, normed_of(), mask_of, weight_ref[...], vector_ref[...], place,
             left_ref.at[here], right_ref.at[here], proj_ref,
         )
     own, other = (
@@ -239,10 +244,10 @@
     operands = [
         pltpu.with_memory_space_constraint(o, pltpu.HBM) for o in (x, flags, scale, shift, wl.T, bl, wr.T, br, bias)
     ]
-    own_x, own_flags, weight, vectors, spreader, own_mask = pl.pallas_call(
+    own_normed, own_flags, weight, vectors, spreader, own_mask = pl.pallas_call(
         load_kernel,
         out_shape=(
-            jax.ShapeDtypeStruct(x.shape, x.dtype),
+            jax.ShapeDtypeStruct((seqs * rows, depth), BF16),
             jax.ShapeDtypeStruct(flags.shape, flags.dtype),
             jax.ShapeDtypeStruct((2 * LANES, depth), BF16),
             jax.ShapeDtypeStruct((8, 2 * LANES), F32),
@@ -250,7 +255,7 @@
             jax.ShapeDtypeStruct((seqs, lanes), F32),
         ),
         in_specs=[pl.BlockSpec(memory_space=pltpu.HBM)] * len(operands),
-        scratch_shapes=[pltpu.VMEM(o.shape, o.dtype) for o in operands[2:]]
+        scratch_shapes=[pltpu.VMEM(o.shape, o.dtype) for o in (operands[0], *operands[2:])]
         + [pltpu.SemaphoreType.DMA((len(operands),))],
         compiler_params=pltpu.CompilerParams(vmem_limit_bytes=16 << 20),
         cost_estimate=pl.CostEstimate(flops=1 << 25, bytes_accessed=x.size * 8, transcendentals=0),
@@ -263,7 +268,7 @@
         scratch_shapes=[pltpu.VMEM((2, seqs * rows, LANES), F32)] * 2,
         compiler_params=pltpu.CompilerParams(vmem_limit_bytes=16 << 20),
         name="project",
-    )(own_x, own_flags, other_x, other_flags, weight, vectors, spreader, own_mask)
+    )(own_normed, own_flags, other_x, other_flags, weight, vectors, spreader, own_mask)
 
     steps = right_routes(n)
     lefts = [left] + [

time: 13 us -> 12.9 us (level)
  waiting for transfers between devices: 2.49 us -> 2.31 us
  Pallas kernels: 3.54 us -> 3.71 us
    pallas_call x1, Pallas kernels: 1.14 us -> 1.39 us  [local(): pl.pallas_call(load_kernel, out_shape=(jax.ShapeDtypeStruct((seqs * rows,...]
    ppermute x1, waiting for transfers between devices: 0.18 us -> 0.01 us  [local(): lax.ppermute(flags, 'seq', swap)]
    ppermute x2, starting transfers between devices: 3.34 us -> 3.21 us  [local(): lax.ppermute(right, axes, [(a * n + p, step[a][p] * n + a) for a in range...]
  transfers between devices with their start and end apart: 5 -> 5, of which waited for: 3 -> 2; matrix products, arithmetic and copies ran while one was open for 0% -> 0% of each run, Pallas kernels for 11% -> 13%
where the time goes in v24:
time: 12.9 us; the launch traced here: 12.8 us
  starting transfers between devices  6.71 us (52%)
  Pallas kernels  3.71 us (29%)
  waiting for transfers between devices  2.31 us (18%)
    ppermute x2, starting transfers between devices, local(): lax.ppermute(right, axes, [(a * n + p, step[a][p] * n + a) for a in range...  3.21 us
    ppermute x1, starting transfers between devices, local(): lax.ppermute(left, axes, [(a * n + p, a * n + step[a][p]) for a in range(...  2.99 us
    ppermute x2, waiting for transfers between devices, local(): lax.ppermute(right, axes, [(a * n + p, step[a][p] * n + a) for a in range...  2.3 us
    pallas_call x1, Pallas kernels, local(): pl.pallas_call(load_kernel, out_shape=(jax.ShapeDtypeStruct((seqs * rows,...  1.39 us
    pallas_call x1, Pallas kernels, local(): pl.pallas_call(functools.partial(pair_kernel, seqs, rows, rows, width), o...  1.35 us
    pallas_call x1, Pallas kernels, local(): pl.pallas_call(functools.partial(project_kernel, width), out_shape=(wire,...  0.69 us
    ppermute x1, starting transfers between devices, local(): lax.ppermute(x, 'seq', swap)  0.45 us
    pallas_call x1, Pallas kernels, local(): pl.pallas_call(functools.partial(left_kernel, steps, seqs, rows, width),...  0.28 us
  transfers between devices with their start and end apart: 5, of which 2 were waited for; matrix products, arithmetic and copies ran while one was open for 0% of the time, Pallas kernels for 13%

profile of v24, /device:TPU:0, one launch (start us, length us, event | category | flops | bytes accessed | tf_op | source)
XLA Modules:
  0.0 12.8 jit_solution(13544940088797304272)
XLA Ops:
  0.0 0.5 %collective-permute-start = (bf16[32,16,256]{2,1,0:T(8,128)(2,1)}, bf16[32,16,256]{2,1,0:T(8,128)(2,1)S(1)}, u32[]{:S(2)}, u32[]{:S(2)}) collective-permute-start(bf16[32,16,256]{2,1,0:T(8,128)(2,1)} %x_hbm.1), channel_id=1, source_target_pairs={{0,1},{1,0},{2,3},{3,2},{4,5},{5,4},{6,7},{7,6},{8,9},{9,8},{10,11... | collective-permute-start | bytes 786440 | tf_op jit(solution)/shard_map/ppermute | solution.py:242
  0.5 0.1 collective-permute-start.1
  0.5 1.4 %load.1 = (bf16[512,256]{1,0:T(8,128)(2,1)S(1)}, s32[16,32]{1,0:T(8,128)S(1)}, bf16[256,256]{1,0:T(8,128)(2,1)S(1)}, f32[8,256]{1,0:T(8,128)S(1)}, bf16[16,512]{1,0:T(8,128)(2,1)S(1)}, /*index=5*/f32[32,512]{1,0:T(8,128)S(1)}) custom-call(bf16[32,16,256]{2,1,0:T(8,128)(2,1)} %x_hbm.1, s32[16,32]{1,0:T(8,128)} %bitcast.6, f32[256]{0:T(256)} %scale_hbm.1, ...), custom_call_target="tpu_custom_call" | custom-call | flops 33554432 | bytes 1048576 | tf_op jit(solution)/shard_map/load/pallas_call | solution.py:247
  1.9 0.0 collective-permute-done.1.other_flag_ref
  1.9 0.0 collective-permute-done.other_x_ref
  1.9 0.0 copy-start
  1.9 0.7 %project.1 = (bf16[272,128]{1,0:T(8,128)(2,1)S(1)}, bf16[272,128]{1,0:T(8,128)(2,1)S(1)}) custom-call(bf16[512,256]{1,0:T(8,128)(2,1)S(1)} %get-tuple-element.15.own_normed_ref, s32[16,32]{1,0:T(8,128)S(1)} %get-tuple-element.16.own_flag_ref, bf16[32,16,256]{2,1,0:T(8,128)(2,1)S(1)} %collective-permute-done.other_x_ref, ...), custom_call_target="tpu_custom_call" | custom-call | tf_op jit(solution)/shard_map/project/pallas_call | solution.py:265
  2.6 3.0 %collective-permute-start.4 = (bf16[272,128]{1,0:T(8,128)(2,1)S(1)}, bf16[272,128]{1,0:T(8,128)(2,1)S(1)}, u32[]{:S(2)}, u32[]{:S(2)}) collective-permute-start(bf16[272,128]{1,0:T(8,128)(2,1)S(1)} %get-tuple-element.22.refs_0_), channel_id=1, source_target_pairs={{0,2},{1,3},{2,1},{3,0},{4,7},{5,6},{6,4},{7,5},{8,11},{9,10},{10,... | collective-permute-start | bytes 208904 | tf_op jit(solution)/shard_map/ppermute | solution.py:275
  5.6 3.2 %collective-permute-start.3 = (bf16[272,128]{1,0:T(8,128)(2,1)S(1)}, bf16[272,128]{1,0:T(8,128)(2,1)S(1)}, u32[]{:S(2)}, u32[]{:S(2)}) collective-permute-start(bf16[272,128]{1,0:T(8,128)(2,1)S(1)} %get-tuple-element.21), channel_id=1, source_target_pairs={{0,12},{1,8},{2,0},{3,4},{4,9},{5,13},{6,1},{7,5},{8,2},{9,10},{10... | collective-permute-start | bytes 208904 | tf_op jit(solution)/shard_map/ppermute | solution.py:279
  8.8 0.0 collective-permute-start.2
  8.8 0.0 collective-permute-done.4.refs_1_
  8.8 0.3 %turn_left.1 = (bf16[512,128]{1,0:T(8,128)(2,1)S(1)}, bf16[16,128]{1,0:T(8,128)(2,1)S(1)}) custom-call(bf16[272,128]{1,0:T(8,128)(2,1)S(1)} %get-tuple-element.22.refs_0_, bf16[272,128]{1,0:T(8,128)(2,1)S(1)} %collective-permute-done.4.refs_1_), custom_call_target="tpu_custom_call" | custom-call | tf_op jit(solution)/shard_map/turn_left/pallas_call | solution.py:282
  9.1 1.6 %collective-permute-done.3.refs_1_ = bf16[272,128]{1,0:T(8,128)(2,1)S(1)} collective-permute-done((bf16[272,128]{1,0:T(8,128)(2,1)S(1)}, bf16[272,128]{1,0:T(8,128)(2,1)S(1)}, u32[]{:S(2)}, u32[]{:S(2)}) %collective-permute-start.3) | collective-permute-done | bytes 69664 | tf_op jit(solution)/shard_map/ppermute | solution.py:279
  10.8 0.7 %collective-permute-done.2.refs_0_ = bf16[272,128]{1,0:T(8,128)(2,1)S(1)} collective-permute-done((bf16[272,128]{1,0:T(8,128)(2,1)S(1)}, bf16[272,128]{1,0:T(8,128)(2,1)S(1)}, u32[]{:S(2)}, u32[]{:S(2)}) %collective-permute-start.2) | collective-permute-done | bytes 69664 | tf_op jit(solution)/shard_map/ppermute | solution.py:279
  11.4 0.0 copy-done
  11.4 1.3 %pair.1 = bf16[16,16,128]{2,1,0:T(8,128)(2,1)} custom-call(bf16[272,128]{1,0:T(8,128)(2,1)S(1)} %collective-permute-done.2.refs_0_, bf16[272,128]{1,0:T(8,128)(2,1)S(1)} %collective-permute-done.3.refs_1_, bf16[512,128]{1,0:T(8,128)(2,1)S(1)} %get-tuple-element.23.refs_2_, bf16[16,128]{1,0:T(8,128)(2,1)S(1)} %get-tuple-element.24.refs_3_, ...), custom_call_target="tpu_custom_call" | custom-call | tf_op jit(solution)/shard_map/pair/pallas_call | solution.py:292
Async XLA Ops:
  0.0 1.9 %collective-permute-start = (bf16[32,16,256]{2,1,0:T(8,128)(2,1)}, bf16[32,16,256]{2,1,0:T(8,128)(2,1)S(1)}, u32[]{:S(2)}, u32[]{:S(2)}) collective-permute-start(bf16[32,16,256]{2,1,0:T(8,128)(2,1)} %x_hbm.1), channel_id=1, source_target_pairs={{0,1},{1,0},{2,3},{3,2},{4,5},{5,4},{6,7},{7,6},{8,9},{9,8},{10,11... | collective-permute-start | bytes 786440 | tf_op jit(solution)/shard_map/ppermute | solution.py:242
  0.5 1.5 %collective-permute-start.1 = (s32[16,32]{1,0:T(8,128)}, s32[16,32]{1,0:T(8,128)S(1)}, u32[]{:S(2)}, u32[]{:S(2)}) collective-permute-start(s32[16,32]{1,0:T(8,128)} %bitcast.5), channel_id=1, source_target_pairs={{0,1},{1,0},{2,3},{3,2},{4,5},{5,4},{6,7},{7,6},{8,9},{9,8},{10,11... | collective-permute-start | bytes 6152 | tf_op jit(solution)/shard_map/ppermute | solution.py:242
  1.9 9.5 %copy-start = (bf16[1024,128]{1,0:T(8,128)(2,1)S(1)}, bf16[1024,128]{1,0:T(8,128)(2,1)}, u32[]{:S(2)}) copy-start(bf16[1024,128]{1,0:T(8,128)(2,1)} %refs_4_.1) | copy-start | bytes 786436
  2.6 6.2 %collective-permute-start.4 = (bf16[272,128]{1,0:T(8,128)(2,1)S(1)}, bf16[272,128]{1,0:T(8,128)(2,1)S(1)}, u32[]{:S(2)}, u32[]{:S(2)}) collective-permute-start(bf16[272,128]{1,0:T(8,128)(2,1)S(1)} %get-tuple-element.22.refs_0_), channel_id=1, source_target_pairs={{0,2},{1,3},{2,1},{3,0},{4,7},{5,6},{6,4},{7,5},{8,11},{9,10},{10,... | collective-permute-start | bytes 208904 | tf_op jit(solution)/shard_map/ppermute | solution.py:275
  5.6 5.2 %collective-permute-start.3 = (bf16[272,128]{1,0:T(8,128)(2,1)S(1)}, bf16[272,128]{1,0:T(8,128)(2,1)S(1)}, u32[]{:S(2)}, u32[]{:S(2)}) collective-permute-start(bf16[272,128]{1,0:T(8,128)(2,1)S(1)} %get-tuple-element.21), channel_id=1, source_target_pairs={{0,12},{1,8},{2,0},{3,4},{4,9},{5,13},{6,1},{7,5},{8,2},{9,10},{10... | collective-permute-start | bytes 208904 | tf_op jit(solution)/shard_map/ppermute | solution.py:279
  8.8 2.6 %collective-permute-start.2 = (bf16[272,128]{1,0:T(8,128)(2,1)S(1)}, bf16[272,128]{1,0:T(8,128)(2,1)S(1)}, u32[]{:S(2)}, u32[]{:S(2)}) collective-permute-start(bf16[272,128]{1,0:T(8,128)(2,1)S(1)} %get-tuple-element.21), channel_id=1, source_target_pairs={{0,4},{1,0},{2,8},{3,12},{4,5},{5,1},{6,9},{7,13},{8,6},{9,14},{10... | collective-permute-start | bytes 208904 | tf_op jit(solution)/shard_map/ppermute | solution.py:279

commit v25 on v23

--- a/solution.py
+++ b/solution.py
@@ -174,8 +174,8 @@
 
 
 def pair_kernel(seqs, rows, columns, width, *refs):
-    rights = refs[:-7]
-    turned_ref, live_ref, w_ref, vector_ref, out_ref, flat_ref, raw_ref = refs[-7:]
+    rights = refs[:-6]
+    turned_ref, live_ref, w_ref, vector_ref, out_ref, flat_ref = refs[-6:]
     fold = LANES // width
     assert fold == 4
     data = rows * width // LANES * seqs
@@ -218,10 +218,8 @@
                 flat_ref[j * rows:(j + 1) * rows, quad * LANES:(quad + 1) * LANES] = part[k]
 
     raw = dot(flat_ref[...], w_ref[...]) + vector_ref[3:4, :LANES]
-    for j in range(columns):
-        raw_ref[j * rows:(j + 1) * rows, :] = raw[j * rows:(j + 1) * rows, :] * scales[j]
-    for i in range(rows):
-        out_ref[i] = raw_ref[pl.ds(i, columns, stride=rows), :].astype(BF16)
+    scaled = [raw[j * rows:(j + 1) * rows, :] * scales[j] for j in range(columns)]
+    out_ref[...] = jnp.swapaxes(jnp.stack(scaled, axis=0), 0, 1).astype(BF16)
 
 
 def local(n, x, flags, scale, shift, wl, bl, wr, br, w, bias):
@@ -289,7 +287,6 @@
         out_shape=jax.ShapeDtypeStruct((rows, rows, outs), BF16),
         scratch_shapes=[
             pltpu.VMEM((rows * rows, width * width), BF16),
-            pltpu.VMEM((rows * rows, outs), F32),
         ],
         compiler_params=pltpu.CompilerParams(vmem_limit_bytes=16 << 20),
         name="pair",

time: 13 us -> 13 us (level)
  no operation moved by 1% of the time
where the time goes in v25:
time: 13 us; the launch traced here: 12.8 us
  starting transfers between devices  6.76 us (52%)
  Pallas kernels  3.54 us (27%)
  waiting for transfers between devices  2.49 us (19%)
    ppermute x2, starting transfers between devices, local(): lax.ppermute(right, axes, [(a * n + p, step[a][p] * n + a) for a in range...  3.34 us
    ppermute x1, starting transfers between devices, local(): lax.ppermute(left, axes, [(a * n + p, a * n + step[a][p]) for a in range(...  2.91 us
    ppermute x2, waiting for transfers between devices, local(): lax.ppermute(right, axes, [(a * n + p, step[a][p] * n + a) for a in range...  2.3 us
    pallas_call x1, Pallas kernels, local(): pl.pallas_call(functools.partial(pair_kernel, seqs, rows, rows, width), o...  1.34 us
    pallas_call x1, Pallas kernels, local(): pl.pallas_call(load_kernel, out_shape=(jax.ShapeDtypeStruct(x.shape, x.dt...  1.14 us
    pallas_call x1, Pallas kernels, local(): pl.pallas_call(functools.partial(project_kernel, width), out_shape=(wire,...  0.78 us
    ppermute x1, starting transfers between devices, local(): lax.ppermute(x, 'seq', swap)  0.45 us
    pallas_call x1, Pallas kernels, local(): pl.pallas_call(functools.partial(left_kernel, steps, seqs, rows, width),...  0.28 us
  transfers between devices with their start and end apart: 5, of which 3 were waited for; matrix products, arithmetic and copies ran while one was open for 0% of the time, Pallas kernels for 11%

profile of v25, /device:TPU:0, one launch (start us, length us, event | category | flops | bytes accessed | tf_op | source)
XLA Modules:
  0.0 12.8 jit_solution(7341297455464897660)
XLA Ops:
  0.0 0.5 %collective-permute-start = (bf16[32,16,256]{2,1,0:T(8,128)(2,1)}, bf16[32,16,256]{2,1,0:T(8,128)(2,1)S(1)}, u32[]{:S(2)}, u32[]{:S(2)}) collective-permute-start(bf16[32,16,256]{2,1,0:T(8,128)(2,1)} %x_hbm.1), channel_id=1, source_target_pairs={{0,1},{1,0},{2,3},{3,2},{4,5},{5,4},{6,7},{7,6},{8,9},{9,8},{10,11... | collective-permute-start | bytes 786440 | tf_op jit(solution)/shard_map/ppermute | solution.py:235
  0.5 0.1 collective-permute-start.1
  0.5 1.1 %load.1 = (bf16[32,16,256]{2,1,0:T(8,128)(2,1)S(1)}, s32[16,32]{1,0:T(8,128)S(1)}, bf16[256,256]{1,0:T(8,128)(2,1)S(1)}, f32[8,256]{1,0:T(8,128)S(1)}, bf16[16,5...) custom-call(bf16[32,16,256]{2,1,0:T(8,128)(2,1)} %x_hbm.1, s32[16,32]{1,0:T(8,128)} %bitcast.6, f32[256]{0:T(256)} %scale_hbm.1, ...), custom_call_target="tpu_custom_call" | custom-call | flops 33554432 | bytes 1048576 | tf_op jit(solution)/shard_map/load/pallas_call | solution.py:240
  1.7 0.2 %collective-permute-done.1.other_flag_ref = s32[16,32]{1,0:T(8,128)S(1)} collective-permute-done((s32[16,32]{1,0:T(8,128)}, s32[16,32]{1,0:T(8,128)S(1)}, u32[]{:S(2)}, u32[]{:S(2)}) %collective-permute-start.1) | collective-permute-done | bytes 2080 | tf_op jit(solution)/shard_map/ppermute | solution.py:235
  1.8 0.0 collective-permute-done.other_x_ref
  1.8 0.0 copy-start
  1.8 0.8 %project.1 = (bf16[272,128]{1,0:T(8,128)(2,1)S(1)}, bf16[272,128]{1,0:T(8,128)(2,1)S(1)}) custom-call(bf16[32,16,256]{2,1,0:T(8,128)(2,1)S(1)} %get-tuple-element.15.own_x_ref, s32[16,32]{1,0:T(8,128)S(1)} %get-tuple-element.16.own_flag_ref, bf16[32,16,256]{2,1,0:T(8,128)(2,1)S(1)} %collective-permute-done.other_x_ref, ...), custom_call_target="tpu_custom_call" | custom-call | tf_op jit(solution)/shard_map/project/pallas_call | solution.py:258
  2.6 2.9 %collective-permute-start.4 = (bf16[272,128]{1,0:T(8,128)(2,1)S(1)}, bf16[272,128]{1,0:T(8,128)(2,1)S(1)}, u32[]{:S(2)}, u32[]{:S(2)}) collective-permute-start(bf16[272,128]{1,0:T(8,128)(2,1)S(1)} %get-tuple-element.22.refs_0_), channel_id=1, source_target_pairs={{0,2},{1,3},{2,1},{3,0},{4,7},{5,6},{6,4},{7,5},{8,11},{9,10},{10,... | collective-permute-start | bytes 208904 | tf_op jit(solution)/shard_map/ppermute | solution.py:268
  5.5 3.3 %collective-permute-start.3 = (bf16[272,128]{1,0:T(8,128)(2,1)S(1)}, bf16[272,128]{1,0:T(8,128)(2,1)S(1)}, u32[]{:S(2)}, u32[]{:S(2)}) collective-permute-start(bf16[272,128]{1,0:T(8,128)(2,1)S(1)} %get-tuple-element.21), channel_id=1, source_target_pairs={{0,12},{1,8},{2,0},{3,4},{4,9},{5,13},{6,1},{7,5},{8,2},{9,10},{10... | collective-permute-start | bytes 208904 | tf_op jit(solution)/shard_map/ppermute | solution.py:272
  8.9 0.0 collective-permute-start.2
  8.9 0.0 collective-permute-done.4.refs_1_
  8.9 0.3 %turn_left.1 = (bf16[512,128]{1,0:T(8,128)(2,1)S(1)}, bf16[16,128]{1,0:T(8,128)(2,1)S(1)}) custom-call(bf16[272,128]{1,0:T(8,128)(2,1)S(1)} %get-tuple-element.22.refs_0_, bf16[272,128]{1,0:T(8,128)(2,1)S(1)} %collective-permute-done.4.refs_1_), custom_call_target="tpu_custom_call" | custom-call | tf_op jit(solution)/shard_map/turn_left/pallas_call | solution.py:275
  9.2 1.6 %collective-permute-done.3.refs_1_ = bf16[272,128]{1,0:T(8,128)(2,1)S(1)} collective-permute-done((bf16[272,128]{1,0:T(8,128)(2,1)S(1)}, bf16[272,128]{1,0:T(8,128)(2,1)S(1)}, u32[]{:S(2)}, u32[]{:S(2)}) %collective-permute-start.3) | collective-permute-done | bytes 69664 | tf_op jit(solution)/shard_map/ppermute | solution.py:272
  10.8 0.7 %collective-permute-done.2.refs_0_ = bf16[272,128]{1,0:T(8,128)(2,1)S(1)} collective-permute-done((bf16[272,128]{1,0:T(8,128)(2,1)S(1)}, bf16[272,128]{1,0:T(8,128)(2,1)S(1)}, u32[]{:S(2)}, u32[]{:S(2)}) %collective-permute-start.2) | collective-permute-done | bytes 69664 | tf_op jit(solution)/shard_map/ppermute | solution.py:272
  11.5 0.0 copy-done
  11.5 1.3 %pair.1 = bf16[16,16,128]{2,1,0:T(8,128)(2,1)} custom-call(bf16[272,128]{1,0:T(8,128)(2,1)S(1)} %collective-permute-done.2.refs_0_, bf16[272,128]{1,0:T(8,128)(2,1)S(1)} %collective-permute-done.3.refs_1_, bf16[512,128]{1,0:T(8,128)(2,1)S(1)} %get-tuple-element.23.refs_2_, bf16[16,128]{1,0:T(8,128)(2,1)S(1)} %get-tuple-element.24.refs_3_, ...), custom_call_target="tpu_custom_call" | custom-call | tf_op jit(solution)/shard_map/pair/pallas_call | solution.py:285
Async XLA Ops:
  0.0 1.8 %collective-permute-start = (bf16[32,16,256]{2,1,0:T(8,128)(2,1)}, bf16[32,16,256]{2,1,0:T(8,128)(2,1)S(1)}, u32[]{:S(2)}, u32[]{:S(2)}) collective-permute-start(bf16[32,16,256]{2,1,0:T(8,128)(2,1)} %x_hbm.1), channel_id=1, source_target_pairs={{0,1},{1,0},{2,3},{3,2},{4,5},{5,4},{6,7},{7,6},{8,9},{9,8},{10,11... | collective-permute-start | bytes 786440 | tf_op jit(solution)/shard_map/ppermute | solution.py:235
  0.5 1.4 %collective-permute-start.1 = (s32[16,32]{1,0:T(8,128)}, s32[16,32]{1,0:T(8,128)S(1)}, u32[]{:S(2)}, u32[]{:S(2)}) collective-permute-start(s32[16,32]{1,0:T(8,128)} %bitcast.5), channel_id=1, source_target_pairs={{0,1},{1,0},{2,3},{3,2},{4,5},{5,4},{6,7},{7,6},{8,9},{9,8},{10,11... | collective-permute-start | bytes 6152 | tf_op jit(solution)/shard_map/ppermute | solution.py:235
  1.8 9.6 %copy-start = (bf16[1024,128]{1,0:T(8,128)(2,1)S(1)}, bf16[1024,128]{1,0:T(8,128)(2,1)}, u32[]{:S(2)}) copy-start(bf16[1024,128]{1,0:T(8,128)(2,1)} %refs_4_.1) | copy-start | bytes 786436
  2.6 6.3 %collective-permute-start.4 = (bf16[272,128]{1,0:T(8,128)(2,1)S(1)}, bf16[272,128]{1,0:T(8,128)(2,1)S(1)}, u32[]{:S(2)}, u32[]{:S(2)}) collective-permute-start(bf16[272,128]{1,0:T(8,128)(2,1)S(1)} %get-tuple-element.22.refs_0_), channel_id=1, source_target_pairs={{0,2},{1,3},{2,1},{3,0},{4,7},{5,6},{6,4},{7,5},{8,11},{9,10},{10,... | collective-permute-start | bytes 208904 | tf_op jit(solution)/shard_map/ppermute | solution.py:268
  5.5 5.3 %collective-permute-start.3 = (bf16[272,128]{1,0:T(8,128)(2,1)S(1)}, bf16[272,128]{1,0:T(8,128)(2,1)S(1)}, u32[]{:S(2)}, u32[]{:S(2)}) collective-permute-start(bf16[272,128]{1,0:T(8,128)(2,1)S(1)} %get-tuple-element.21), channel_id=1, source_target_pairs={{0,12},{1,8},{2,0},{3,4},{4,9},{5,13},{6,1},{7,5},{8,2},{9,10},{10... | collective-permute-start | bytes 208904 | tf_op jit(solution)/shard_map/ppermute | solution.py:272
  8.9 2.6 %collective-permute-start.2 = (bf16[272,128]{1,0:T(8,128)(2,1)S(1)}, bf16[272,128]{1,0:T(8,128)(2,1)S(1)}, u32[]{:S(2)}, u32[]{:S(2)}) collective-permute-start(bf16[272,128]{1,0:T(8,128)(2,1)S(1)} %get-tuple-element.21), channel_id=1, source_target_pairs={{0,4},{1,0},{2,8},{3,12},{4,5},{5,1},{6,9},{7,13},{8,6},{9,14},{10... | collective-permute-start | bytes 208904 | tf_op jit(solution)/shard_map/ppermute | solution.py:272

commit v26 on v25

--- a/solution.py
+++ b/solution.py
@@ -124,6 +124,16 @@
     data = lanes // LANES * seqs
     block = lax.axis_index("seq")
     core = block % CORES
+    own, other = (
+        jnp.concatenate([ref[...].astype(F32)] * (LANES // seqs), axis=1) for ref in (own_flag_ref, other_flag_ref)
+    )
+    for tile in range((left_ref.shape[0] - CORES * data) // rows):
+        lane_block = iota((rows, LANES), 1) // seqs + tile * (LANES // seqs)
+        placed = jnp.where(lane_block == block, own, jnp.where(lane_block == block + 1 - 2 * core, other, 0.0)).astype(BF16)
+        first = CORES * data + tile * rows
+        for out_ref in (left_ref, right_ref):
+            out_ref[first:first + rows, :] = placed
+
     place = iota((seqs, LANES), 1) // width
     for x_ref, mask_of, proj_ref, at in (
         (own_x_ref, lambda: own_mask_ref[...], own_proj_ref, core),
@@ -134,15 +144,6 @@
             width, x_ref, mask_of, weight_ref[...], vector_ref[...], place,
             left_ref.at[here], right_ref.at[here], proj_ref,
         )
-    own, other = (
-        jnp.concatenate([ref[...].astype(F32)] * (LANES // seqs), axis=1) for ref in (own_flag_ref, other_flag_ref)
-    )
-    for tile in range((left_ref.shape[0] - CORES * data) // rows):
-        lane_block = iota((rows, LANES), 1) // seqs + tile * (LANES // seqs)
-        placed = jnp.where(lane_block == block, own, jnp.where(lane_block == block + 1 - 2 * core, other, 0.0)).astype(BF16)
-        first = CORES * data + tile * rows
-        for out_ref in (left_ref, right_ref):
-            out_ref[first:first + rows, :] = placed
 
 
 def whole_mask(pieces, rows, data):

time: 13 us -> 13 us (level)
  no operation moved by 1% of the time
where the time goes in v26:
time: 13 us; the launch traced here: 12.8 us
  starting transfers between devices  6.76 us (52%)
  Pallas kernels  3.55 us (27%)
  waiting for transfers between devices  2.49 us (19%)
    ppermute x2, starting transfers between devices, local(): lax.ppermute(right, axes, [(a * n + p, step[a][p] * n + a) for a in range...  3.34 us
    ppermute x1, starting transfers between devices, local(): lax.ppermute(left, axes, [(a * n + p, a * n + step[a][p]) for a in range(...  2.91 us
    ppermute x2, waiting for transfers between devices, local(): lax.ppermute(right, axes, [(a * n + p, step[a][p] * n + a) for a in range...  2.3 us
    pallas_call x1, Pallas kernels, local(): pl.pallas_call(functools.partial(pair_kernel, seqs, rows, rows, width), o...  1.34 us
    pallas_call x1, Pallas kernels, local(): pl.pallas_call(load_kernel, out_shape=(jax.ShapeDtypeStruct(x.shape, x.dt...  1.14 us
    pallas_call x1, Pallas kernels, local(): pl.pallas_call(functools.partial(project_kernel, width), out_shape=(wire,...  0.78 us
    ppermute x1, starting transfers between devices, local(): lax.ppermute(x, 'seq', swap)  0.45 us
    pallas_call x1, Pallas kernels, local(): pl.pallas_call(functools.partial(left_kernel, steps, seqs, rows, width),...  0.28 us
  transfers between devices with their start and end apart: 5, of which 3 were waited for; matrix products, arithmetic and copies ran while one was open for 0% of the time, Pallas kernels for 11%

profile of v26, /device:TPU:0, one launch (start us, length us, event | category | flops | bytes accessed | tf_op | source)
XLA Modules:
  0.0 12.8 jit_solution(7542761518214526467)
XLA Ops:
  0.0 0.5 %collective-permute-start = (bf16[32,16,256]{2,1,0:T(8,128)(2,1)}, bf16[32,16,256]{2,1,0:T(8,128)(2,1)S(1)}, u32[]{:S(2)}, u32[]{:S(2)}) collective-permute-start(bf16[32,16,256]{2,1,0:T(8,128)(2,1)} %x_hbm.1), channel_id=1, source_target_pairs={{0,1},{1,0},{2,3},{3,2},{4,5},{5,4},{6,7},{7,6},{8,9},{9,8},{10,11... | collective-permute-start | bytes 786440 | tf_op jit(solution)/shard_map/ppermute | solution.py:236
  0.5 0.1 collective-permute-start.1
  0.5 1.1 %load.1 = (bf16[32,16,256]{2,1,0:T(8,128)(2,1)S(1)}, s32[16,32]{1,0:T(8,128)S(1)}, bf16[256,256]{1,0:T(8,128)(2,1)S(1)}, f32[8,256]{1,0:T(8,128)S(1)}, bf16[16,5...) custom-call(bf16[32,16,256]{2,1,0:T(8,128)(2,1)} %x_hbm.1, s32[16,32]{1,0:T(8,128)} %bitcast.6, f32[256]{0:T(256)} %scale_hbm.1, ...), custom_call_target="tpu_custom_call" | custom-call | flops 33554432 | bytes 1048576 | tf_op jit(solution)/shard_map/load/pallas_call | solution.py:241
  1.7 0.2 %collective-permute-done.1.other_flag_ref = s32[16,32]{1,0:T(8,128)S(1)} collective-permute-done((s32[16,32]{1,0:T(8,128)}, s32[16,32]{1,0:T(8,128)S(1)}, u32[]{:S(2)}, u32[]{:S(2)}) %collective-permute-start.1) | collective-permute-done | bytes 2080 | tf_op jit(solution)/shard_map/ppermute | solution.py:236
  1.8 0.0 collective-permute-done.other_x_ref
  1.8 0.0 copy-start
  1.8 0.8 %project.1 = (bf16[272,128]{1,0:T(8,128)(2,1)S(1)}, bf16[272,128]{1,0:T(8,128)(2,1)S(1)}) custom-call(bf16[32,16,256]{2,1,0:T(8,128)(2,1)S(1)} %get-tuple-element.15.own_x_ref, s32[16,32]{1,0:T(8,128)S(1)} %get-tuple-element.16.own_flag_ref, bf16[32,16,256]{2,1,0:T(8,128)(2,1)S(1)} %collective-permute-done.other_x_ref, ...), custom_call_target="tpu_custom_call" | custom-call | tf_op jit(solution)/shard_map/project/pallas_call | solution.py:259
  2.6 2.9 %collective-permute-start.4 = (bf16[272,128]{1,0:T(8,128)(2,1)S(1)}, bf16[272,128]{1,0:T(8,128)(2,1)S(1)}, u32[]{:S(2)}, u32[]{:S(2)}) collective-permute-start(bf16[272,128]{1,0:T(8,128)(2,1)S(1)} %get-tuple-element.22.refs_0_), channel_id=1, source_target_pairs={{0,2},{1,3},{2,1},{3,0},{4,7},{5,6},{6,4},{7,5},{8,11},{9,10},{10,... | collective-permute-start | bytes 208904 | tf_op jit(solution)/shard_map/ppermute | solution.py:269
  5.5 3.3 %collective-permute-start.3 = (bf16[272,128]{1,0:T(8,128)(2,1)S(1)}, bf16[272,128]{1,0:T(8,128)(2,1)S(1)}, u32[]{:S(2)}, u32[]{:S(2)}) collective-permute-start(bf16[272,128]{1,0:T(8,128)(2,1)S(1)} %get-tuple-element.21), channel_id=1, source_target_pairs={{0,12},{1,8},{2,0},{3,4},{4,9},{5,13},{6,1},{7,5},{8,2},{9,10},{10... | collective-permute-start | bytes 208904 | tf_op jit(solution)/shard_map/ppermute | solution.py:273
  8.9 0.0 collective-permute-start.2
  8.9 0.0 collective-permute-done.4.refs_1_
  8.9 0.3 %turn_left.1 = (bf16[512,128]{1,0:T(8,128)(2,1)S(1)}, bf16[16,128]{1,0:T(8,128)(2,1)S(1)}) custom-call(bf16[272,128]{1,0:T(8,128)(2,1)S(1)} %get-tuple-element.22.refs_0_, bf16[272,128]{1,0:T(8,128)(2,1)S(1)} %collective-permute-done.4.refs_1_), custom_call_target="tpu_custom_call" | custom-call | tf_op jit(solution)/shard_map/turn_left/pallas_call | solution.py:276
  9.2 1.6 %collective-permute-done.3.refs_1_ = bf16[272,128]{1,0:T(8,128)(2,1)S(1)} collective-permute-done((bf16[272,128]{1,0:T(8,128)(2,1)S(1)}, bf16[272,128]{1,0:T(8,128)(2,1)S(1)}, u32[]{:S(2)}, u32[]{:S(2)}) %collective-permute-start.3) | collective-permute-done | bytes 69664 | tf_op jit(solution)/shard_map/ppermute | solution.py:273
  10.8 0.7 %collective-permute-done.2.refs_0_ = bf16[272,128]{1,0:T(8,128)(2,1)S(1)} collective-permute-done((bf16[272,128]{1,0:T(8,128)(2,1)S(1)}, bf16[272,128]{1,0:T(8,128)(2,1)S(1)}, u32[]{:S(2)}, u32[]{:S(2)}) %collective-permute-start.2) | collective-permute-done | bytes 69664 | tf_op jit(solution)/shard_map/ppermute | solution.py:273
  11.5 0.0 copy-done
  11.5 1.3 %pair.1 = bf16[16,16,128]{2,1,0:T(8,128)(2,1)} custom-call(bf16[272,128]{1,0:T(8,128)(2,1)S(1)} %collective-permute-done.2.refs_0_, bf16[272,128]{1,0:T(8,128)(2,1)S(1)} %collective-permute-done.3.refs_1_, bf16[512,128]{1,0:T(8,128)(2,1)S(1)} %get-tuple-element.23.refs_2_, bf16[16,128]{1,0:T(8,128)(2,1)S(1)} %get-tuple-element.24.refs_3_, ...), custom_call_target="tpu_custom_call" | custom-call | tf_op jit(solution)/shard_map/pair/pallas_call | solution.py:286
Async XLA Ops:
  0.0 1.8 %collective-permute-start = (bf16[32,16,256]{2,1,0:T(8,128)(2,1)}, bf16[32,16,256]{2,1,0:T(8,128)(2,1)S(1)}, u32[]{:S(2)}, u32[]{:S(2)}) collective-permute-start(bf16[32,16,256]{2,1,0:T(8,128)(2,1)} %x_hbm.1), channel_id=1, source_target_pairs={{0,1},{1,0},{2,3},{3,2},{4,5},{5,4},{6,7},{7,6},{8,9},{9,8},{10,11... | collective-permute-start | bytes 786440 | tf_op jit(solution)/shard_map/ppermute | solution.py:236
  0.5 1.4 %collective-permute-start.1 = (s32[16,32]{1,0:T(8,128)}, s32[16,32]{1,0:T(8,128)S(1)}, u32[]{:S(2)}, u32[]{:S(2)}) collective-permute-start(s32[16,32]{1,0:T(8,128)} %bitcast.5), channel_id=1, source_target_pairs={{0,1},{1,0},{2,3},{3,2},{4,5},{5,4},{6,7},{7,6},{8,9},{9,8},{10,11... | collective-permute-start | bytes 6152 | tf_op jit(solution)/shard_map/ppermute | solution.py:236
  1.8 9.6 %copy-start = (bf16[1024,128]{1,0:T(8,128)(2,1)S(1)}, bf16[1024,128]{1,0:T(8,128)(2,1)}, u32[]{:S(2)}) copy-start(bf16[1024,128]{1,0:T(8,128)(2,1)} %refs_4_.1) | copy-start | bytes 786436
  2.6 6.3 %collective-permute-start.4 = (bf16[272,128]{1,0:T(8,128)(2,1)S(1)}, bf16[272,128]{1,0:T(8,128)(2,1)S(1)}, u32[]{:S(2)}, u32[]{:S(2)}) collective-permute-start(bf16[272,128]{1,0:T(8,128)(2,1)S(1)} %get-tuple-element.22.refs_0_), channel_id=1, source_target_pairs={{0,2},{1,3},{2,1},{3,0},{4,7},{5,6},{6,4},{7,5},{8,11},{9,10},{10,... | collective-permute-start | bytes 208904 | tf_op jit(solution)/shard_map/ppermute | solution.py:269
  5.5 5.3 %collective-permute-start.3 = (bf16[272,128]{1,0:T(8,128)(2,1)S(1)}, bf16[272,128]{1,0:T(8,128)(2,1)S(1)}, u32[]{:S(2)}, u32[]{:S(2)}) collective-permute-start(bf16[272,128]{1,0:T(8,128)(2,1)S(1)} %get-tuple-element.21), channel_id=1, source_target_pairs={{0,12},{1,8},{2,0},{3,4},{4,9},{5,13},{6,1},{7,5},{8,2},{9,10},{10... | collective-permute-start | bytes 208904 | tf_op jit(solution)/shard_map/ppermute | solution.py:273
  8.9 2.6 %collective-permute-start.2 = (bf16[272,128]{1,0:T(8,128)(2,1)S(1)}, bf16[272,128]{1,0:T(8,128)(2,1)S(1)}, u32[]{:S(2)}, u32[]{:S(2)}) collective-permute-start(bf16[272,128]{1,0:T(8,128)(2,1)S(1)} %get-tuple-element.21), channel_id=1, source_target_pairs={{0,4},{1,0},{2,8},{3,12},{4,5},{5,1},{6,9},{7,13},{8,6},{9,14},{10... | collective-permute-start | bytes 208904 | tf_op jit(solution)/shard_map/ppermute | solution.py:273

commit v27 on v26

--- a/solution.py
+++ b/solution.py
@@ -136,8 +136,8 @@
 
     place = iota((seqs, LANES), 1) // width
     for x_ref, mask_of, proj_ref, at in (
+        (other_x_ref, lambda: spread_mask(other_flag_ref, spreader_ref), other_proj_ref, 1 - core),
         (own_x_ref, lambda: own_mask_ref[...], own_proj_ref, core),
-        (other_x_ref, lambda: spread_mask(other_flag_ref, spreader_ref), other_proj_ref, 1 - core),
     ):
         here = pl.ds(pl.multiple_of(at * data, data), data)
         project_block(

time: 13 us -> 13 us (level)
  no operation moved by 1% of the time
where the time goes in v27:
time: 13 us; the launch traced here: 12.9 us
  starting transfers between devices  6.76 us (52%)
  Pallas kernels  3.59 us (28%)
  waiting for transfers between devices  2.49 us (19%)
    ppermute x2, starting transfers between devices, local(): lax.ppermute(right, axes, [(a * n + p, step[a][p] * n + a) for a in range...  3.34 us
    ppermute x1, starting transfers between devices, local(): lax.ppermute(left, axes, [(a * n + p, a * n + step[a][p]) for a in range(...  2.91 us
    ppermute x2, waiting for transfers between devices, local(): lax.ppermute(right, axes, [(a * n + p, step[a][p] * n + a) for a in range...  2.3 us
    pallas_call x1, Pallas kernels, local(): pl.pallas_call(functools.partial(pair_kernel, seqs, rows, rows, width), o...  1.34 us
    pallas_call x1, Pallas kernels, local(): pl.pallas_call(load_kernel, out_shape=(jax.ShapeDtypeStruct(x.shape, x.dt...  1.14 us
    pallas_call x1, Pallas kernels, local(): pl.pallas_call(functools.partial(project_kernel, width), out_shape=(wire,...  0.82 us
    ppermute x1, starting transfers between devices, local(): lax.ppermute(x, 'seq', swap)  0.45 us
    pallas_call x1, Pallas kernels, local(): pl.pallas_call(functools.partial(left_kernel, steps, seqs, rows, width),...  0.28 us
  transfers between devices with their start and end apart: 5, of which 3 were waited for; matrix products, arithmetic and copies ran while one was open for 0% of the time, Pallas kernels for 11%

profile of v27, /device:TPU:0, one launch (start us, length us, event | category | flops | bytes accessed | tf_op | source)
XLA Modules:
  0.0 12.9 jit_solution(13450262545612092399)
XLA Ops:
  0.0 0.5 %collective-permute-start = (bf16[32,16,256]{2,1,0:T(8,128)(2,1)}, bf16[32,16,256]{2,1,0:T(8,128)(2,1)S(1)}, u32[]{:S(2)}, u32[]{:S(2)}) collective-permute-start(bf16[32,16,256]{2,1,0:T(8,128)(2,1)} %x_hbm.1), channel_id=1, source_target_pairs={{0,1},{1,0},{2,3},{3,2},{4,5},{5,4},{6,7},{7,6},{8,9},{9,8},{10,11... | collective-permute-start | bytes 786440 | tf_op jit(solution)/shard_map/ppermute | solution.py:236
  0.5 0.1 collective-permute-start.1
  0.5 1.1 %load.1 = (bf16[32,16,256]{2,1,0:T(8,128)(2,1)S(1)}, s32[16,32]{1,0:T(8,128)S(1)}, bf16[256,256]{1,0:T(8,128)(2,1)S(1)}, f32[8,256]{1,0:T(8,128)S(1)}, bf16[16,5...) custom-call(bf16[32,16,256]{2,1,0:T(8,128)(2,1)} %x_hbm.1, s32[16,32]{1,0:T(8,128)} %bitcast.6, f32[256]{0:T(256)} %scale_hbm.1, ...), custom_call_target="tpu_custom_call" | custom-call | flops 33554432 | bytes 1048576 | tf_op jit(solution)/shard_map/load/pallas_call | solution.py:241
  1.7 0.2 %collective-permute-done.1.other_flag_ref = s32[16,32]{1,0:T(8,128)S(1)} collective-permute-done((s32[16,32]{1,0:T(8,128)}, s32[16,32]{1,0:T(8,128)S(1)}, u32[]{:S(2)}, u32[]{:S(2)}) %collective-permute-start.1) | collective-permute-done | bytes 2080 | tf_op jit(solution)/shard_map/ppermute | solution.py:236
  1.8 0.0 collective-permute-done.other_x_ref
  1.8 0.0 copy-start
  1.8 0.8 %project.1 = (bf16[272,128]{1,0:T(8,128)(2,1)S(1)}, bf16[272,128]{1,0:T(8,128)(2,1)S(1)}) custom-call(bf16[32,16,256]{2,1,0:T(8,128)(2,1)S(1)} %get-tuple-element.15.own_x_ref, s32[16,32]{1,0:T(8,128)S(1)} %get-tuple-element.16.own_flag_ref, bf16[32,16,256]{2,1,0:T(8,128)(2,1)S(1)} %collective-permute-done.other_x_ref, ...), custom_call_target="tpu_custom_call" | custom-call | tf_op jit(solution)/shard_map/project/pallas_call | solution.py:259
  2.7 2.9 %collective-permute-start.4 = (bf16[272,128]{1,0:T(8,128)(2,1)S(1)}, bf16[272,128]{1,0:T(8,128)(2,1)S(1)}, u32[]{:S(2)}, u32[]{:S(2)}) collective-permute-start(bf16[272,128]{1,0:T(8,128)(2,1)S(1)} %get-tuple-element.22.refs_0_), channel_id=1, source_target_pairs={{0,2},{1,3},{2,1},{3,0},{4,7},{5,6},{6,4},{7,5},{8,11},{9,10},{10,... | collective-permute-start | bytes 208904 | tf_op jit(solution)/shard_map/ppermute | solution.py:269
  5.6 3.3 %collective-permute-start.3 = (bf16[272,128]{1,0:T(8,128)(2,1)S(1)}, bf16[272,128]{1,0:T(8,128)(2,1)S(1)}, u32[]{:S(2)}, u32[]{:S(2)}) collective-permute-start(bf16[272,128]{1,0:T(8,128)(2,1)S(1)} %get-tuple-element.21), channel_id=1, source_target_pairs={{0,12},{1,8},{2,0},{3,4},{4,9},{5,13},{6,1},{7,5},{8,2},{9,10},{10... | collective-permute-start | bytes 208904 | tf_op jit(solution)/shard_map/ppermute | solution.py:273
  8.9 0.0 collective-permute-start.2
  8.9 0.0 collective-permute-done.4.refs_1_
  8.9 0.3 %turn_left.1 = (bf16[512,128]{1,0:T(8,128)(2,1)S(1)}, bf16[16,128]{1,0:T(8,128)(2,1)S(1)}) custom-call(bf16[272,128]{1,0:T(8,128)(2,1)S(1)} %get-tuple-element.22.refs_0_, bf16[272,128]{1,0:T(8,128)(2,1)S(1)} %collective-permute-done.4.refs_1_), custom_call_target="tpu_custom_call" | custom-call | tf_op jit(solution)/shard_map/turn_left/pallas_call | solution.py:276
  9.2 1.6 %collective-permute-done.3.refs_1_ = bf16[272,128]{1,0:T(8,128)(2,1)S(1)} collective-permute-done((bf16[272,128]{1,0:T(8,128)(2,1)S(1)}, bf16[272,128]{1,0:T(8,128)(2,1)S(1)}, u32[]{:S(2)}, u32[]{:S(2)}) %collective-permute-start.3) | collective-permute-done | bytes 69664 | tf_op jit(solution)/shard_map/ppermute | solution.py:273
  10.9 0.7 %collective-permute-done.2.refs_0_ = bf16[272,128]{1,0:T(8,128)(2,1)S(1)} collective-permute-done((bf16[272,128]{1,0:T(8,128)(2,1)S(1)}, bf16[272,128]{1,0:T(8,128)(2,1)S(1)}, u32[]{:S(2)}, u32[]{:S(2)}) %collective-permute-start.2) | collective-permute-done | bytes 69664 | tf_op jit(solution)/shard_map/ppermute | solution.py:273
  11.5 0.0 copy-done
  11.5 1.3 %pair.1 = bf16[16,16,128]{2,1,0:T(8,128)(2,1)} custom-call(bf16[272,128]{1,0:T(8,128)(2,1)S(1)} %collective-permute-done.2.refs_0_, bf16[272,128]{1,0:T(8,128)(2,1)S(1)} %collective-permute-done.3.refs_1_, bf16[512,128]{1,0:T(8,128)(2,1)S(1)} %get-tuple-element.23.refs_2_, bf16[16,128]{1,0:T(8,128)(2,1)S(1)} %get-tuple-element.24.refs_3_, ...), custom_call_target="tpu_custom_call" | custom-call | tf_op jit(solution)/shard_map/pair/pallas_call | solution.py:286
Async XLA Ops:
  0.0 1.8 %collective-permute-start = (bf16[32,16,256]{2,1,0:T(8,128)(2,1)}, bf16[32,16,256]{2,1,0:T(8,128)(2,1)S(1)}, u32[]{:S(2)}, u32[]{:S(2)}) collective-permute-start(bf16[32,16,256]{2,1,0:T(8,128)(2,1)} %x_hbm.1), channel_id=1, source_target_pairs={{0,1},{1,0},{2,3},{3,2},{4,5},{5,4},{6,7},{7,6},{8,9},{9,8},{10,11... | collective-permute-start | bytes 786440 | tf_op jit(solution)/shard_map/ppermute | solution.py:236
  0.5 1.4 %collective-permute-start.1 = (s32[16,32]{1,0:T(8,128)}, s32[16,32]{1,0:T(8,128)S(1)}, u32[]{:S(2)}, u32[]{:S(2)}) collective-permute-start(s32[16,32]{1,0:T(8,128)} %bitcast.5), channel_id=1, source_target_pairs={{0,1},{1,0},{2,3},{3,2},{4,5},{5,4},{6,7},{7,6},{8,9},{9,8},{10,11... | collective-permute-start | bytes 6152 | tf_op jit(solution)/shard_map/ppermute | solution.py:236
  1.8 9.7 %copy-start = (bf16[1024,128]{1,0:T(8,128)(2,1)S(1)}, bf16[1024,128]{1,0:T(8,128)(2,1)}, u32[]{:S(2)}) copy-start(bf16[1024,128]{1,0:T(8,128)(2,1)} %refs_4_.1) | copy-start | bytes 786436
  2.7 6.3 %collective-permute-start.4 = (bf16[272,128]{1,0:T(8,128)(2,1)S(1)}, bf16[272,128]{1,0:T(8,128)(2,1)S(1)}, u32[]{:S(2)}, u32[]{:S(2)}) collective-permute-start(bf16[272,128]{1,0:T(8,128)(2,1)S(1)} %get-tuple-element.22.refs_0_), channel_id=1, source_target_pairs={{0,2},{1,3},{2,1},{3,0},{4,7},{5,6},{6,4},{7,5},{8,11},{9,10},{10,... | collective-permute-start | bytes 208904 | tf_op jit(solution)/shard_map/ppermute | solution.py:269
  5.6 5.3 %collective-permute-start.3 = (bf16[272,128]{1,0:T(8,128)(2,1)S(1)}, bf16[272,128]{1,0:T(8,128)(2,1)S(1)}, u32[]{:S(2)}, u32[]{:S(2)}) collective-permute-start(bf16[272,128]{1,0:T(8,128)(2,1)S(1)} %get-tuple-element.21), channel_id=1, source_target_pairs={{0,12},{1,8},{2,0},{3,4},{4,9},{5,13},{6,1},{7,5},{8,2},{9,10},{10... | collective-permute-start | bytes 208904 | tf_op jit(solution)/shard_map/ppermute | solution.py:273
  8.9 2.6 %collective-permute-start.2 = (bf16[272,128]{1,0:T(8,128)(2,1)S(1)}, bf16[272,128]{1,0:T(8,128)(2,1)S(1)}, u32[]{:S(2)}, u32[]{:S(2)}) collective-permute-start(bf16[272,128]{1,0:T(8,128)(2,1)S(1)} %get-tuple-element.21), channel_id=1, source_target_pairs={{0,4},{1,0},{2,8},{3,12},{4,5},{5,1},{6,9},{7,13},{8,6},{9,14},{10... | collective-permute-start | bytes 208904 | tf_op jit(solution)/shard_map/ppermute | solution.py:273

commit v28 on v26

--- a/solution.py
+++ b/solution.py
@@ -219,8 +219,8 @@
                 flat_ref[j * rows:(j + 1) * rows, quad * LANES:(quad + 1) * LANES] = part[k]
 
     raw = dot(flat_ref[...], w_ref[...]) + vector_ref[3:4, :LANES]
-    scaled = [raw[j * rows:(j + 1) * rows, :] * scales[j] for j in range(columns)]
-    out_ref[...] = jnp.swapaxes(jnp.stack(scaled, axis=0), 0, 1).astype(BF16)
+    scaled = [(raw[j * rows:(j + 1) * rows, :] * scales[j]).astype(BF16) for j in range(columns)]
+    out_ref[...] = jnp.swapaxes(jnp.stack(scaled, axis=0), 0, 1)
 
 
 def local(n, x, flags, scale, shift, wl, bl, wr, br, w, bias):

time: 13 us -> 13 us (level)
  no operation moved by 1% of the time
where the time goes in v28:
time: 13 us; the launch traced here: 12.8 us
  starting transfers between devices  6.76 us (52%)
  Pallas kernels  3.54 us (27%)
  waiting for transfers between devices  2.49 us (19%)
    ppermute x2, starting transfers between devices, local(): lax.ppermute(right, axes, [(a * n + p, step[a][p] * n + a) for a in range...  3.34 us
    ppermute x1, starting transfers between devices, local(): lax.ppermute(left, axes, [(a * n + p, a * n + step[a][p]) for a in range(...  2.91 us
    ppermute x2, waiting for transfers between devices, local(): lax.ppermute(right, axes, [(a * n + p, step[a][p] * n + a) for a in range...  2.3 us
    pallas_call x1, Pallas kernels, local(): pl.pallas_call(functools.partial(pair_kernel, seqs, rows, rows, width), o...  1.33 us
    pallas_call x1, Pallas kernels, local(): pl.pallas_call(load_kernel, out_shape=(jax.ShapeDtypeStruct(x.shape, x.dt...  1.14 us
    pallas_call x1, Pallas kernels, local(): pl.pallas_call(functools.partial(project_kernel, width), out_shape=(wire,...  0.78 us
    ppermute x1, starting transfers between devices, local(): lax.ppermute(x, 'seq', swap)  0.45 us
    pallas_call x1, Pallas kernels, local(): pl.pallas_call(functools.partial(left_kernel, steps, seqs, rows, width),...  0.28 us
  transfers between devices with their start and end apart: 5, of which 3 were waited for; matrix products, arithmetic and copies ran while one was open for 0% of the time, Pallas kernels for 11%

profile of v28, /device:TPU:0, one launch (start us, length us, event | category | flops | bytes accessed | tf_op | source)
XLA Modules:
  0.0 12.8 jit_solution(15919388601572813427)
XLA Ops:
  0.0 0.5 %collective-permute-start = (bf16[32,16,256]{2,1,0:T(8,128)(2,1)}, bf16[32,16,256]{2,1,0:T(8,128)(2,1)S(1)}, u32[]{:S(2)}, u32[]{:S(2)}) collective-permute-start(bf16[32,16,256]{2,1,0:T(8,128)(2,1)} %x_hbm.1), channel_id=1, source_target_pairs={{0,1},{1,0},{2,3},{3,2},{4,5},{5,4},{6,7},{7,6},{8,9},{9,8},{10,11... | collective-permute-start | bytes 786440 | tf_op jit(solution)/shard_map/ppermute | solution.py:236
  0.5 0.1 collective-permute-start.1
  0.5 1.1 %load.1 = (bf16[32,16,256]{2,1,0:T(8,128)(2,1)S(1)}, s32[16,32]{1,0:T(8,128)S(1)}, bf16[256,256]{1,0:T(8,128)(2,1)S(1)}, f32[8,256]{1,0:T(8,128)S(1)}, bf16[16,5...) custom-call(bf16[32,16,256]{2,1,0:T(8,128)(2,1)} %x_hbm.1, s32[16,32]{1,0:T(8,128)} %bitcast.6, f32[256]{0:T(256)} %scale_hbm.1, ...), custom_call_target="tpu_custom_call" | custom-call | flops 33554432 | bytes 1048576 | tf_op jit(solution)/shard_map/load/pallas_call | solution.py:241
  1.7 0.2 %collective-permute-done.1.other_flag_ref = s32[16,32]{1,0:T(8,128)S(1)} collective-permute-done((s32[16,32]{1,0:T(8,128)}, s32[16,32]{1,0:T(8,128)S(1)}, u32[]{:S(2)}, u32[]{:S(2)}) %collective-permute-start.1) | collective-permute-done | bytes 2080 | tf_op jit(solution)/shard_map/ppermute | solution.py:236
  1.8 0.0 collective-permute-done.other_x_ref
  1.8 0.0 copy-start
  1.8 0.8 %project.1 = (bf16[272,128]{1,0:T(8,128)(2,1)S(1)}, bf16[272,128]{1,0:T(8,128)(2,1)S(1)}) custom-call(bf16[32,16,256]{2,1,0:T(8,128)(2,1)S(1)} %get-tuple-element.15.own_x_ref, s32[16,32]{1,0:T(8,128)S(1)} %get-tuple-element.16.own_flag_ref, bf16[32,16,256]{2,1,0:T(8,128)(2,1)S(1)} %collective-permute-done.other_x_ref, ...), custom_call_target="tpu_custom_call" | custom-call | tf_op jit(solution)/shard_map/project/pallas_call | solution.py:259
  2.6 2.9 %collective-permute-start.4 = (bf16[272,128]{1,0:T(8,128)(2,1)S(1)}, bf16[272,128]{1,0:T(8,128)(2,1)S(1)}, u32[]{:S(2)}, u32[]{:S(2)}) collective-permute-start(bf16[272,128]{1,0:T(8,128)(2,1)S(1)} %get-tuple-element.22.refs_0_), channel_id=1, source_target_pairs={{0,2},{1,3},{2,1},{3,0},{4,7},{5,6},{6,4},{7,5},{8,11},{9,10},{10,... | collective-permute-start | bytes 208904 | tf_op jit(solution)/shard_map/ppermute | solution.py:269
  5.5 3.3 %collective-permute-start.3 = (bf16[272,128]{1,0:T(8,128)(2,1)S(1)}, bf16[272,128]{1,0:T(8,128)(2,1)S(1)}, u32[]{:S(2)}, u32[]{:S(2)}) collective-permute-start(bf16[272,128]{1,0:T(8,128)(2,1)S(1)} %get-tuple-element.21), channel_id=1, source_target_pairs={{0,12},{1,8},{2,0},{3,4},{4,9},{5,13},{6,1},{7,5},{8,2},{9,10},{10... | collective-permute-start | bytes 208904 | tf_op jit(solution)/shard_map/ppermute | solution.py:273
  8.9 0.0 collective-permute-start.2
  8.9 0.0 collective-permute-done.4.refs_1_
  8.9 0.3 %turn_left.1 = (bf16[512,128]{1,0:T(8,128)(2,1)S(1)}, bf16[16,128]{1,0:T(8,128)(2,1)S(1)}) custom-call(bf16[272,128]{1,0:T(8,128)(2,1)S(1)} %get-tuple-element.22.refs_0_, bf16[272,128]{1,0:T(8,128)(2,1)S(1)} %collective-permute-done.4.refs_1_), custom_call_target="tpu_custom_call" | custom-call | tf_op jit(solution)/shard_map/turn_left/pallas_call | solution.py:276
  9.2 1.6 %collective-permute-done.3.refs_1_ = bf16[272,128]{1,0:T(8,128)(2,1)S(1)} collective-permute-done((bf16[272,128]{1,0:T(8,128)(2,1)S(1)}, bf16[272,128]{1,0:T(8,128)(2,1)S(1)}, u32[]{:S(2)}, u32[]{:S(2)}) %collective-permute-start.3) | collective-permute-done | bytes 69664 | tf_op jit(solution)/shard_map/ppermute | solution.py:273
  10.8 0.7 %collective-permute-done.2.refs_0_ = bf16[272,128]{1,0:T(8,128)(2,1)S(1)} collective-permute-done((bf16[272,128]{1,0:T(8,128)(2,1)S(1)}, bf16[272,128]{1,0:T(8,128)(2,1)S(1)}, u32[]{:S(2)}, u32[]{:S(2)}) %collective-permute-start.2) | collective-permute-done | bytes 69664 | tf_op jit(solution)/shard_map/ppermute | solution.py:273
  11.5 0.0 copy-done
  11.5 1.3 %pair.1 = bf16[16,16,128]{2,1,0:T(8,128)(2,1)} custom-call(bf16[272,128]{1,0:T(8,128)(2,1)S(1)} %collective-permute-done.2.refs_0_, bf16[272,128]{1,0:T(8,128)(2,1)S(1)} %collective-permute-done.3.refs_1_, bf16[512,128]{1,0:T(8,128)(2,1)S(1)} %get-tuple-element.23.refs_2_, bf16[16,128]{1,0:T(8,128)(2,1)S(1)} %get-tuple-element.24.refs_3_, ...), custom_call_target="tpu_custom_call" | custom-call | tf_op jit(solution)/shard_map/pair/pallas_call | solution.py:286
Async XLA Ops:
  0.0 1.8 %collective-permute-start = (bf16[32,16,256]{2,1,0:T(8,128)(2,1)}, bf16[32,16,256]{2,1,0:T(8,128)(2,1)S(1)}, u32[]{:S(2)}, u32[]{:S(2)}) collective-permute-start(bf16[32,16,256]{2,1,0:T(8,128)(2,1)} %x_hbm.1), channel_id=1, source_target_pairs={{0,1},{1,0},{2,3},{3,2},{4,5},{5,4},{6,7},{7,6},{8,9},{9,8},{10,11... | collective-permute-start | bytes 786440 | tf_op jit(solution)/shard_map/ppermute | solution.py:236
  0.5 1.4 %collective-permute-start.1 = (s32[16,32]{1,0:T(8,128)}, s32[16,32]{1,0:T(8,128)S(1)}, u32[]{:S(2)}, u32[]{:S(2)}) collective-permute-start(s32[16,32]{1,0:T(8,128)} %bitcast.5), channel_id=1, source_target_pairs={{0,1},{1,0},{2,3},{3,2},{4,5},{5,4},{6,7},{7,6},{8,9},{9,8},{10,11... | collective-permute-start | bytes 6152 | tf_op jit(solution)/shard_map/ppermute | solution.py:236
  1.8 9.6 %copy-start = (bf16[1024,128]{1,0:T(8,128)(2,1)S(1)}, bf16[1024,128]{1,0:T(8,128)(2,1)}, u32[]{:S(2)}) copy-start(bf16[1024,128]{1,0:T(8,128)(2,1)} %refs_4_.1) | copy-start | bytes 786436
  2.6 6.3 %collective-permute-start.4 = (bf16[272,128]{1,0:T(8,128)(2,1)S(1)}, bf16[272,128]{1,0:T(8,128)(2,1)S(1)}, u32[]{:S(2)}, u32[]{:S(2)}) collective-permute-start(bf16[272,128]{1,0:T(8,128)(2,1)S(1)} %get-tuple-element.22.refs_0_), channel_id=1, source_target_pairs={{0,2},{1,3},{2,1},{3,0},{4,7},{5,6},{6,4},{7,5},{8,11},{9,10},{10,... | collective-permute-start | bytes 208904 | tf_op jit(solution)/shard_map/ppermute | solution.py:269
  5.5 5.3 %collective-permute-start.3 = (bf16[272,128]{1,0:T(8,128)(2,1)S(1)}, bf16[272,128]{1,0:T(8,128)(2,1)S(1)}, u32[]{:S(2)}, u32[]{:S(2)}) collective-permute-start(bf16[272,128]{1,0:T(8,128)(2,1)S(1)} %get-tuple-element.21), channel_id=1, source_target_pairs={{0,12},{1,8},{2,0},{3,4},{4,9},{5,13},{6,1},{7,5},{8,2},{9,10},{10... | collective-permute-start | bytes 208904 | tf_op jit(solution)/shard_map/ppermute | solution.py:273
  8.9 2.6 %collective-permute-start.2 = (bf16[272,128]{1,0:T(8,128)(2,1)S(1)}, bf16[272,128]{1,0:T(8,128)(2,1)S(1)}, u32[]{:S(2)}, u32[]{:S(2)}) collective-permute-start(bf16[272,128]{1,0:T(8,128)(2,1)S(1)} %get-tuple-element.21), channel_id=1, source_target_pairs={{0,4},{1,0},{2,8},{3,12},{4,5},{5,1},{6,9},{7,13},{8,6},{9,14},{10... | collective-permute-start | bytes 208904 | tf_op jit(solution)/shard_map/ppermute | solution.py:273
